TPU v7x, 256 devices: a whole 4x4x8 slice. The times are simulated.
256 devices in a mesh: dp: 4 (over x), out: 16 (over z, y_lo), in: 4 (over y_hi, core).
Axes of the slice: x: 4, y: 4 (y_hi: 2, y_lo: 2; y = y_hi * 2 + y_lo), z: 8, core: 2. Of those that a mesh axis runs over, the one named last changes fastest.
Arguments:
- activations: bfloat16 [8192, 8192], P(('dp', 'out'), 'in'), may hold values from -0.23925781 to 0.23925781
- out_grad: bfloat16 [8192, 10240], P('dp', 'out'), may hold values from -2.390625 to 2.390625
- weight: bfloat16 [4, 2048, 10240], P('in', 'dp', 'out'), may hold values from -0.0625 to 0.0625
Outputs:
- input_grad: bfloat16 [8192, 8192], P(('dp', 'out'), 'in')
- weight_grad: float32 [4, 2048, 10240], P('in', 'dp', 'out')
All inputs are finite; a program needn't handle non-finite values.
Results may differ from a plain program's by a relative error of at most 0.001.
Values may be sent and summed in bfloat16 or wider, within the bound.
No kernel may reach another device: no remote copies, remote signals or barrier semaphores. Data moves between devices by JAX's collectives and lax.ppermute only.
A program may use at most 128 MiB of HBM per device.

v0:
```python
import functools

import jax
import jax.numpy as jnp
from jax import lax
from jax.experimental import pallas as pl
from jax.experimental.pallas import tpu as pltpu
from jax.sharding import Mesh, PartitionSpec as P

F32 = jnp.float32
BF16 = jnp.bfloat16
LANES = 128
TILE = 16
SQUARINGS = 4
TOP = 2.0**7.75
TINY = 1e-30
MIB = 1024 * 1024


def encode(v, s):
    a = jnp.abs(v) * s
    for _ in range(SQUARINGS):
        a = a * a
    return jnp.where(v < 0, -a, a).astype(BF16)


def decode(y, inv):
    y = y.astype(F32)
    a = jnp.exp2(jnp.log2(jnp.abs(y)) * 0.5**SQUARINGS) * inv
    return jnp.where(y < 0, -a, a)


def inverse_scale(ref):
    return 1.0 / ref[ref.shape[0] - TILE :, :].astype(F32)


def for_tiles(rows, body, init):
    return lax.fori_loop(0, rows // TILE, lambda i, x: body(pl.multiple_of(i * TILE, TILE), x), init, unroll=2)


def write_coded(v_ref, blocks, amax, out_ref):
    rows = v_ref.shape[0]
    coded = (TOP / jnp.maximum(amax, TINY)).astype(BF16)
    s = coded.astype(F32)
    out_ref[blocks * rows :, :] = coded

    def body(r, x):
        for j in range(blocks):
            at = j * LANES
            out_ref[pl.ds(j * rows + r, TILE), :] = encode(v_ref[pl.ds(r, TILE), at : at + LANES], s)
        return x

    for_tiles(rows, body, 0)


def summed_tile(own_ref, got, invs, r, j):
    rows = own_ref.shape[0]
    v = own_ref[pl.ds(r, TILE), j * LANES : (j + 1) * LANES]
    for ref, inv in zip(got, invs):
        v = v + decode(ref[pl.ds(j * rows + r, TILE), :], inv)
    return v


def hop_kernel(n_got, idx_ref, *refs):
    got, (own_ref, out_ref, v_ref) = refs[:n_got], refs[n_got:]
    blocks = v_ref.shape[1] // LANES
    invs = [inverse_scale(ref) for ref in got]

    def body(r, amax):
        for j in range(blocks):
            v = summed_tile(own_ref, got, invs, r, j)
            v_ref[pl.ds(r, TILE), j * LANES : (j + 1) * LANES] = v
            amax = jnp.maximum(amax, jnp.abs(v))
        return amax

    amax = for_tiles(v_ref.shape[0], body, jnp.zeros((TILE, LANES), F32))
    write_coded(v_ref, blocks, amax, out_ref)


def tokens_kernel(idx_ref, f_ref, b_ref, own_ref, out_ref):
    invs = [inverse_scale(f_ref), inverse_scale(b_ref)]
    rows = out_ref.shape[0]
    at = idx_ref[1] * rows

    def body(r, x):
        for j in range(own_ref.shape[1] // LANES):
            v = own_ref[pl.ds(r, TILE), j * LANES : (j + 1) * LANES]
            for ref, inv in zip((f_ref, b_ref), invs):
                row = pl.multiple_of(j * 2 * rows + at + r, TILE)
                v = v + decode(ref[pl.ds(row, TILE), :], inv)
            out_ref[pl.ds(r, TILE), j * LANES : (j + 1) * LANES] = v.astype(BF16)
        return x

    for_tiles(rows, body, 0)


def columns_kernel(half, h_ref, mine_ref, got_ref, out_ref):
    for j in range(mine_ref.shape[1] // half):
        at = slice(j * half, (j + 1) * half)
        mine_at = pl.multiple_of((2 * j + h_ref[0]) * half, LANES)
        got_at = pl.multiple_of((2 * j + 1 - h_ref[0]) * half, LANES)
        out_ref[:, pl.ds(mine_at, half)] = mine_ref[:, at]
        out_ref[:, pl.ds(got_at, half)] = got_ref[:, at]


def owned_kernel(idx_ref, f_ref, b_ref, own_ref, mine_ref, out_ref, v_ref):
    invs = [inverse_scale(f_ref), inverse_scale(b_ref)]
    blocks = v_ref.shape[1] // LANES

    def body(r, amax):
        for j in range(2 * blocks):
            v = summed_tile(own_ref, (f_ref, b_ref), invs, r, j)
            if j < blocks:
                mine_ref[pl.ds(r, TILE), j * LANES : (j + 1) * LANES] = v
            else:
                v_ref[pl.ds(r, TILE), (j - blocks) * LANES : (j - blocks + 1) * LANES] = v
                amax = jnp.maximum(amax, jnp.abs(v))
        return amax

    amax = for_tiles(own_ref.shape[0], body, jnp.zeros((TILE, LANES), F32))
    write_coded(v_ref, blocks, amax, out_ref)


def rows_kernel(h_ref, mine_ref, got_ref, out_ref):
    rows = mine_ref.shape[0]
    inv = inverse_scale(got_ref)
    mine_at, got_at = h_ref[0] * rows, (1 - h_ref[0]) * rows

    def body(r, x):
        out_ref[pl.ds(pl.multiple_of(mine_at + r, TILE), TILE), :] = mine_ref[pl.ds(r, TILE), :]
        for j in range(mine_ref.shape[1] // LANES):
            v = decode(got_ref[pl.ds(j * rows + r, TILE), :], inv)
            out_ref[pl.ds(pl.multiple_of(got_at + r, TILE), TILE), j * LANES : (j + 1) * LANES] = v
        return x

    for_tiles(rows, body, 0)


def whole(shape):
    return pl.BlockSpec(shape, lambda i, idx: (0,) * len(shape))


def call(kernel, idx, wholes, block, out_shapes, scratch=()):
    in_specs, args = [whole(a.shape) for a in wholes], list(wholes)
    if block is not None:
        in_specs.append(pl.BlockSpec((block[1], block[0].shape[1]), lambda i, idx: (idx[0], 0)))
        args.append(block[0])
    size = sum(a.size * 4 for a in args) + sum(s.size * 4 for s in out_shapes)
    return pl.pallas_call(
        kernel,
        grid_spec=pltpu.PrefetchScalarGridSpec(
            num_scalar_prefetch=1,
            grid=(1,),
            in_specs=in_specs,
            out_specs=[whole(s.shape) for s in out_shapes],
            scratch_shapes=[pltpu.VMEM(s, F32) for s in scratch],
        ),
        out_shape=out_shapes,
        compiler_params=pltpu.CompilerParams(vmem_limit_bytes=10 * MIB),
        cost_estimate=pl.CostEstimate(flops=size * 8, bytes_accessed=size, transcendentals=0),
    )(jnp.stack(idx).astype(jnp.int32), *args)


def placed_kernel(pieces, at_ref, *refs):
    srcs, out_ref, sems = refs[:-2], refs[-2], refs[-1]
    copies = []
    for i, (src, row, rows, col) in enumerate(pieces):
        ref = srcs[src]
        to = out_ref.at[pl.ds(pl.multiple_of(at_ref[i], LANES), rows), col : col + ref.shape[1]]
        copies.append(pltpu.make_async_copy(ref.at[row : row + rows], to, sems.at[i]))
    for copy in copies:
        copy.start()
    for copy in copies:
        copy.wait()


def placed(arrays, pieces, shape):
    fixed = [p[:4] for p in pieces]
    size = 2 * shape[0] * shape[1]
    return pl.pallas_call(
        functools.partial(placed_kernel, fixed),
        grid_spec=pltpu.PrefetchScalarGridSpec(
            num_scalar_prefetch=1,
            grid=(1,),
            in_specs=[pl.BlockSpec(memory_space=pltpu.VMEM)] * len(arrays),
            out_specs=pl.BlockSpec(memory_space=pltpu.VMEM),
            scratch_shapes=[pltpu.SemaphoreType.DMA((len(pieces),))],
        ),
        out_shape=jax.ShapeDtypeStruct(shape, BF16),
        compiler_params=pltpu.CompilerParams(vmem_limit_bytes=4 * MIB),
        cost_estimate=pl.CostEstimate(flops=0, bytes_accessed=2 * size, transcendentals=0),
    )(jnp.stack([jnp.int32(p[4]) for p in pieces]), *arrays)


def coded_shape(rows, width):
    return jax.ShapeDtypeStruct((width // LANES * rows + TILE, LANES), BF16)


def hop(got, mine):
    kernel = functools.partial(hop_kernel, len(got))
    return call(kernel, [jnp.int32(0)], got + [mine], None, [coded_shape(*mine.shape)], [mine.shape])[0]


def swap(a, axis):
    return lax.ppermute(a, axis, [(0, 1), (1, 0)])


def y_ring(a):
    perm = []
    for y in range(4):
        for c in range(2):
            t = (y + (1 if c == 0 else -1)) % 4
            perm.append((((y % 2) * 2 + y // 2) * 2 + c, ((t % 2) * 2 + t // 2) * 2 + c))
    return lax.ppermute(a, ("yl", "yh", "c"), perm)


def ring(a, axis, way):
    n = lax.axis_size(axis)
    perm = [(i * 2 + c, (i + (way if c == 0 else -way)) % n * 2 + c) for i in range(n) for c in range(2)]
    return lax.ppermute(a, (axis, "c"), perm)


def gathered(parts, axis, order, joint, hold=()):
    n, me = lax.axis_size(axis), lax.axis_index(axis)
    step = 1 - 2 * lax.axis_index("c")
    count, (rows, width) = len(parts), parts[0].shape
    blocks = {0: parts}
    ahead = back = parts
    for k in range(1, n // 2 + 1):
        if k == joint:
            ahead, back = [jnp.concatenate(ahead)], [jnp.concatenate(back)]
            hold = after(*ahead, *back, *hold)[2:]
        ahead = blocks[-k] = [ring(p, axis, 1) for p in ahead]
        if k < n - n // 2:
            back = blocks[k] = [ring(p, axis, -1) for p in back]
    arrays, pieces = [], []
    for k, got in blocks.items():
        at = lax.rem(me + step * k + n, n) * count
        for i, place in enumerate(order):
            src, row = (i, 0) if len(got) == count else (0, i * rows)
            pieces.append((len(arrays) + src, row, rows, 0, (at + place) * rows))
        arrays += got
    return arrays, pieces, (n * count * rows, width), hold


def outgoing(share, axis):
    n, me = lax.axis_size(axis), lax.axis_index(axis)
    step = 1 - 2 * lax.axis_index("c")
    ahead, back = n // 2, n - n // 2 - 1
    return hop([], share(lax.rem(me + step * ahead + n, n))), hop([], share(lax.rem(me - step * back + n, n)))


def scattered(share, axis, first):
    n, me = lax.axis_size(axis), lax.axis_index(axis)
    step = 1 - 2 * lax.axis_index("c")
    came = []
    for way, hops, got in ((1, n // 2, first[0]), (-1, n - n // 2 - 1, first[1])):
        got = ring(got, axis, way)
        for k in range(hops - 1, 0, -1):
            got = ring(hop([got], share(lax.rem(me + way * step * k + n, n))), axis, way)
        came.append(got)
    return came


def dot(a, b, dims):
    return lax.dot_general(a, b, (dims, ((), ())), preferred_element_type=F32)


def after(first, *rest):
    return lax.optimization_barrier((first,) + rest)


def on_device(activations, out_grad, weight):
    h = lax.axis_index("yl")
    c = lax.axis_index("c")
    tokens, width = out_grad.shape
    own_tokens, features = activations.shape
    rows = weight.shape[1]
    half = rows // 2
    owners = features // rows

    low = jnp.concatenate([activations[:, d * rows : d * rows + half] for d in range(owners)], axis=1)
    high = jnp.concatenate([activations[:, d * rows + half : (d + 1) * rows] for d in range(owners)], axis=1)
    acts_mine, acts_sent = jnp.where(h == 0, low, high), jnp.where(h == 0, high, low)
    acts_sent, acts_mine, weight, out_grad = after(acts_sent, acts_mine, weight, out_grad)
    acts_got = swap(acts_sent, "yl")

    w_mine = lax.dynamic_slice_in_dim(weight[0], h * half, half, 0)
    w_sent = lax.dynamic_slice_in_dim(weight[0], (1 - h) * half, half, 0)
    w_got = swap(w_sent, "yl")
    w_all = placed(*gathered([jnp.concatenate([w_mine, w_got], axis=1)], "x", (0,), 0)[:3])

    part = tokens // 2
    g_sent = lax.dynamic_slice_in_dim(out_grad, c * part, part, 0)
    hold = [y_ring(g_sent)]
    arrays, acts_pieces, shape, (g_got,) = gathered([acts_mine, acts_got], "z", (h, 1 - h), 3, hold)
    g_rest = swap(g_got, "c")
    pieces = [(0, 0, tokens, 0, 0), (1, 0, part, width, c * part), (2, 0, part, width, (1 - c) * part)]
    g_pair = placed([out_grad, g_got, g_rest], pieces, (tokens, 2 * width))

    def of_tokens(i):
        count = 2 * own_tokens
        return dot(lax.dynamic_slice_in_dim(g_pair, i * count, count, 0), w_all, ((1,), (1,)))

    first = outgoing(of_tokens, "z")
    acts_all = placed(after(*first, *arrays)[2:], acts_pieces, shape)
    came = scattered(of_tokens, "z", first)
    mine = of_tokens(lax.axis_index("z"))

    def finished(of):
        shape = jax.ShapeDtypeStruct((own_tokens, features // 2), BF16)
        return call(tokens_kernel, [of, of], came, (mine, own_tokens), [shape])[0]

    s_got = swap(finished(1 - h), "yl")
    shape = jax.ShapeDtypeStruct((own_tokens, features), BF16)
    input_grad = call(functools.partial(columns_kernel, half), [h], [finished(h), s_got], None, [shape])[0]

    def of_rows(i):
        acts = lax.dynamic_slice_in_dim(acts_all, i * half, half, 1)
        return dot(acts, g_pair, ((0,), (0,)))

    came = scattered(of_rows, "x", outgoing(of_rows, "x"))
    mine = of_rows(lax.axis_index("x"))
    shapes = [jax.ShapeDtypeStruct((half, width), F32), coded_shape(half, width)]
    owned, coded = call(owned_kernel, [jnp.int32(0)], came + [mine], None, shapes, [(half, width)])
    shape = jax.ShapeDtypeStruct((rows, width), F32)
    weight_grad = call(rows_kernel, [h], [owned, swap(coded, "yl")], None, [shape])[0]
    return input_grad, weight_grad[None]


def solution(mesh):
    dp, out, in_ = mesh.devices.shape
    fine = Mesh(mesh.devices.reshape(dp, out // 2, 2, 2, in_ // 2), ("x", "z", "yl", "yh", "c"))
    tokens, split = P(("x", "z", "yl"), ("yh", "c")), P(("yh", "c"), "x", ("z", "yl"))
    return jax.shard_map(
        on_device,
        mesh=fine,
        in_specs=(tokens, P("x", ("z", "yl")), split),
        out_specs=(tokens, split),
        check_vma=False,
    )
```

profile of v0, /device:TPU:4, one launch (start us, length us, event | category | flops | bytes accessed | tf_op | source)
XLA Modules:
  0.0 151.8 jit_solution(16107686708884382987)
XLA Ops:
  0.6 1.2 fusion.36
  1.9 2.6 %constant_dynamic-slice_fusion = bf16[1024,640]{1,0:T(8,128)(2,1)} fusion(bf16[2048,640]{1,0:T(8,128)(2,1)} %refs_0_, s32[]{:T(128)S(6)} %select_n.60), kind=kLoop, calls=%fused_computation.47 | loop fusion | bytes 2621444 | tf_op jit(solution)/shard_map/dynamic_slice | solution.py:294
  4.5 1.6 %collective-permute-start.9 = (bf16[1024,640]{1,0:T(8,128)(2,1)}, bf16[1024,640]{1,0:T(8,128)(2,1)S(1)}, u32[]{:S(2)}, u32[]{:S(2)}) collective-permute-start(bf16[1024,640]{1,0:T(8,128)(2,1)} %constant_dynamic-slice_fusion), channel_id=1, source_target_pairs={{0,4},{1,7},{4,2},{5,1},{2,6},{3,5},{6,0},{7,3},{8,12},{9,15},{12,... | collective-permute-start | bytes 3932168 | tf_op jit(solution)/shard_map/ppermute | solution.py:214
  6.1 1.6 %collective-permute-start.2 = (bf16[128,1024]{1,0:T(8,128)(2,1)S(1)}, bf16[128,1024]{1,0:T(8,128)(2,1)S(1)}, u32[]{:S(2)}, u32[]{:S(2)}) collective-permute-start(bf16[128,1024]{1,0:T(8,128)(2,1)S(1)} %get-tuple-element.24), channel_id=1, source_target_pairs={{0,4},{4,0},{1,5},{5,1},{2,6},{6,2},{3,7},{7,3},{8,12},{12,8},{9,1... | collective-permute-start | bytes 786440 | tf_op jit(solution)/shard_map/ppermute | solution.py:205
  8.3 1.9 %collective-permute-start = (bf16[128,1024]{1,0:T(8,128)(2,1)S(1)}, bf16[128,1024]{1,0:T(8,128)(2,1)S(1)}, u32[]{:S(2)}, u32[]{:S(2)}) collective-permute-start(bf16[128,1024]{1,0:T(8,128)(2,1)S(1)} %get-tuple-element.27.refs_0_), channel_id=1, source_target_pairs={{0,8},{1,57},{8,16},{9,1},{16,24},{17,9},{24,32},{25,17},{32,40},{... | collective-permute-start | bytes 786440 | tf_op jit(solution)/shard_map/ppermute | solution.py:220
  10.2 3.9 %collective-permute-start.5 = (bf16[128,1024]{1,0:T(8,128)(2,1)S(1)}, bf16[128,1024]{1,0:T(8,128)(2,1)S(1)}, u32[]{:S(2)}, u32[]{:S(2)}) collective-permute-start(bf16[128,1024]{1,0:T(8,128)(2,1)S(1)} %get-tuple-element.27.refs_0_), channel_id=1, source_target_pairs={{0,56},{1,9},{8,0},{9,17},{16,8},{17,25},{24,16},{25,33},{32,24},{... | collective-permute-start | bytes 786440 | tf_op jit(solution)/shard_map/ppermute | solution.py:220
  14.1 16.4 %collective-permute-done.2.refs_1_ = bf16[128,1024]{1,0:T(8,128)(2,1)S(1)} collective-permute-done((bf16[128,1024]{1,0:T(8,128)(2,1)S(1)}, bf16[128,1024]{1,0:T(8,128)(2,1)S(1)}, u32[]{:S(2)}, u32[]{:S(2)}) %collective-permute-start.2) | collective-permute-done | bytes 262176 | tf_op jit(solution)/shard_map/ppermute | solution.py:205
  30.6 1.9 %collective-permute-start.3 = (bf16[128,1024]{1,0:T(8,128)(2,1)S(1)}, bf16[128,1024]{1,0:T(8,128)(2,1)S(1)}, u32[]{:S(2)}, u32[]{:S(2)}) collective-permute-start(bf16[128,1024]{1,0:T(8,128)(2,1)S(1)} %collective-permute-done.2.refs_1_), channel_id=1, source_target_pairs={{0,8},{1,57},{8,16},{9,1},{16,24},{17,9},{24,32},{25,17},{32,40},{... | collective-permute-start | bytes 786440 | tf_op jit(solution)/shard_map/ppermute | solution.py:220
  32.5 1.9 %collective-permute-start.1 = (bf16[128,1024]{1,0:T(8,128)(2,1)S(1)}, bf16[128,1024]{1,0:T(8,128)(2,1)S(1)}, u32[]{:S(2)}, u32[]{:S(2)}) collective-permute-start(bf16[128,1024]{1,0:T(8,128)(2,1)S(1)} %collective-permute-done.refs_2_), channel_id=1, source_target_pairs={{0,8},{1,57},{8,16},{9,1},{16,24},{17,9},{24,32},{25,17},{32,40},{... | collective-permute-start | bytes 786440 | tf_op jit(solution)/shard_map/ppermute | solution.py:220
  34.4 2.2 %collective-permute-start.7 = (bf16[128,1024]{1,0:T(8,128)(2,1)S(1)}, bf16[128,1024]{1,0:T(8,128)(2,1)S(1)}, u32[]{:S(2)}, u32[]{:S(2)}) collective-permute-start(bf16[128,1024]{1,0:T(8,128)(2,1)S(1)} %collective-permute-done.2.refs_1_), channel_id=1, source_target_pairs={{0,56},{1,9},{8,0},{9,17},{16,8},{17,25},{24,16},{25,33},{32,24},{... | collective-permute-start | bytes 786440 | tf_op jit(solution)/shard_map/ppermute | solution.py:220
  36.6 3.3 %collective-permute-start.6 = (bf16[128,1024]{1,0:T(8,128)(2,1)S(1)}, bf16[128,1024]{1,0:T(8,128)(2,1)S(1)}, u32[]{:S(2)}, u32[]{:S(2)}) collective-permute-start(bf16[128,1024]{1,0:T(8,128)(2,1)S(1)} %collective-permute-done.5.refs_4_), channel_id=1, source_target_pairs={{0,56},{1,9},{8,0},{9,17},{16,8},{17,25},{24,16},{25,33},{32,24},{... | collective-permute-start | bytes 786440 | tf_op jit(solution)/shard_map/ppermute | solution.py:220
  39.9 1.3 collective-permute-done.3.refs_3_
  41.3 5.5 %collective-permute-done.1.refs_6_ = bf16[128,1024]{1,0:T(8,128)(2,1)S(1)} collective-permute-done((bf16[128,1024]{1,0:T(8,128)(2,1)S(1)}, bf16[128,1024]{1,0:T(8,128)(2,1)S(1)}, u32[]{:S(2)}, u32[]{:S(2)}) %collective-permute-start.1) | collective-permute-done | bytes 262176 | tf_op jit(solution)/shard_map/ppermute | solution.py:220
  46.8 1.2 collective-permute-start.12
  48.0 4.4 %collective-permute-start.8 = (bf16[128,1024]{1,0:T(8,128)(2,1)S(1)}, bf16[128,1024]{1,0:T(8,128)(2,1)S(1)}, u32[]{:S(2)}, u32[]{:S(2)}) collective-permute-start(bf16[128,1024]{1,0:T(8,128)(2,1)S(1)} %collective-permute-done.7.refs_5_), channel_id=1, source_target_pairs={{0,56},{1,9},{8,0},{9,17},{16,8},{17,25},{24,16},{25,33},{32,24},{... | collective-permute-start | bytes 786440 | tf_op jit(solution)/shard_map/ppermute | solution.py:220
  54.0 2.3 %collective-permute-done.8.refs_9_ = bf16[128,1024]{1,0:T(8,128)(2,1)S(1)} collective-permute-done((bf16[128,1024]{1,0:T(8,128)(2,1)S(1)}, bf16[128,1024]{1,0:T(8,128)(2,1)S(1)}, u32[]{:S(2)}, u32[]{:S(2)}) %collective-permute-start.8) | collective-permute-done | bytes 262176 | tf_op jit(solution)/shard_map/ppermute | solution.py:220
  57.0 0.9 collective-permute-start.13
  58.0 1.2 collective-permute-start.14
  59.6 3.9 %collective-permute-start.24 = (bf16[256,1024]{1,0:T(8,128)(2,1)}, bf16[256,1024]{1,0:T(8,128)(2,1)S(1)}, u32[]{:S(2)}, u32[]{:S(2)}) collective-permute-start(bf16[256,1024]{1,0:T(8,128)(2,1)} %copy-done.20), channel_id=1, source_target_pairs={{0,56},{1,9},{8,0},{9,17},{16,8},{17,25},{24,16},{25,33},{32,24},{... | collective-permute-start | bytes 1572872 | tf_op jit(solution)/shard_map/ppermute | solution.py:220
  63.6 10.5 %collective-permute-done.23.refs_10_ = bf16[256,1024]{1,0:T(8,128)(2,1)} collective-permute-done((bf16[256,1024]{1,0:T(8,128)(2,1)}, bf16[256,1024]{1,0:T(8,128)(2,1)}, u32[]{:S(2)}, u32[]{:S(2)}) %collective-permute-start.23) | collective-permute-done | bytes 524320 | tf_op jit(solution)/shard_map/ppermute | solution.py:220
  74.7 2.9 %shard_map.51 = bf16[1024,1280]{1,0:T(8,128)(2,1)S(1)} custom-call(s32[4]{0:T(128)S(1)} %pad_add_fusion.2.at_ref, bf16[256,1280]{1,0:T(8,128)(2,1)S(1)} %pad_maximum_fusion.refs_0_, bf16[256,1280]{1,0:T(8,128)(2,1)} %collective-permute-done.12.refs_1_, bf16[256,1280]{1,0:T(8,128)(2,1)} %collective-permute-done.13.refs_2_, ...), custom_call_target="tpu_custom_call" | custom-call | bytes 5242880 | tf_op jit(solution)/shard_map/pallas_call | solution.py:180
  77.6 1.0 shard_map.50
  82.1 3.4 %collective-permute-start.19 = (bf16[2064,128]{1,0:T(8,128)(2,1)S(1)}, bf16[2064,128]{1,0:T(8,128)(2,1)S(1)}, u32[]{:S(2)}, u32[]{:S(2)}) collective-permute-start(bf16[2064,128]{1,0:T(8,128)(2,1)S(1)} %shard_map.56), channel_id=1, source_target_pairs={{0,56},{1,9},{8,0},{9,17},{16,8},{17,25},{24,16},{25,33},{32,24},{... | collective-permute-start | bytes 1585160 | tf_op jit(solution)/shard_map/ppermute | solution.py:220
  85.6 2.1 %shard_map.62 = bf16[2048,1024]{1,0:T(8,128)(2,1)S(1)} custom-call(s32[16]{0:T(128)S(1)} %stack.119.at_ref, bf16[128,1024]{1,0:T(8,128)(2,1)S(1)} %copy-done.8, bf16[128,1024]{1,0:T(8,128)(2,1)S(1)} %copy-done.10, bf16[128,1024]{1,0:T(8,128)(2,1)S(1)} %copy-done.12, bf16[128,1024]{1,0:T(8,128)(2,1)S(1)} %copy-done.16, bf16[128,1024]{1,0:T(8,128)(2,1)S(1)} %copy-done.14, ...), custom_call_target="tpu_custom_call" | custom-call | bytes 8388608 | tf_op jit(solution)/shard_map/pallas_call | solution.py:180
  87.7 1.6 %fusion.6.refs_0_ = f32[256,1280]{1,0:T(8,128)S(1)} fusion(bf16[2048,1280]{1,0:T(8,128)(2,1)S(1)} %shard_map.50, bf16[2048,1024]{1,0:T(8,128)(2,1)S(1)} %shard_map.62, s32[]{:T(128)S(6)} %select_n.71), kind=kOutput, calls=%fused_computation.6 | convolution fusion | flops 1342177280 | bytes 7602180 | tf_op jit(solution)/shard_map/dot_general | solution.py:266
  89.9 2.2 %collective-permute-start.26 = (bf16[2576,128]{1,0:T(8,128)(2,1)S(1)}, bf16[2576,128]{1,0:T(8,128)(2,1)S(1)}, u32[]{:S(2)}, u32[]{:S(2)}) collective-permute-start(bf16[2576,128]{1,0:T(8,128)(2,1)S(1)} %shard_map.63), channel_id=1, source_target_pairs={{0,64},{1,193},{64,128},{65,1},{128,192},{129,65},{192,0},{193,129... | collective-permute-start | bytes 1978376 | tf_op jit(solution)/shard_map/ppermute | solution.py:220
  92.1 1.6 %fusion.4.refs_1_ = f32[256,1280]{1,0:T(8,128)S(1)} fusion(bf16[2048,1280]{1,0:T(8,128)(2,1)S(1)} %shard_map.50, bf16[2048,1024]{1,0:T(8,128)(2,1)S(1)} %shard_map.62, s32[]{:T(128)S(6)} %select_n.72), kind=kOutput, calls=%fused_computation.4 | convolution fusion | flops 1342177280 | bytes 7602180 | tf_op jit(solution)/shard_map/dot_general | solution.py:266
  94.6 1.6 %fusion.2.refs_0_ = f32[256,1280]{1,0:T(8,128)S(1)} fusion(bf16[2048,1280]{1,0:T(8,128)(2,1)S(1)} %shard_map.50, bf16[2048,1024]{1,0:T(8,128)(2,1)S(1)} %shard_map.62, s32[]{:T(128)S(6)} %select_n.73), kind=kOutput, calls=%fused_computation.2 | convolution fusion | flops 1342177280 | bytes 7602180 | tf_op jit(solution)/shard_map/dot_general | solution.py:266
  96.2 0.9 shard_map.53
  100.4 0.9 shard_map.57
  101.3 2.8 %collective-permute-start.20 = (bf16[2064,128]{1,0:T(8,128)(2,1)S(1)}, bf16[2064,128]{1,0:T(8,128)(2,1)S(1)}, u32[]{:S(2)}, u32[]{:S(2)}) collective-permute-start(bf16[2064,128]{1,0:T(8,128)(2,1)S(1)} %shard_map.57), channel_id=1, source_target_pairs={{0,56},{1,9},{8,0},{9,17},{16,8},{17,25},{24,16},{25,33},{32,24},{... | collective-permute-start | bytes 1585160 | tf_op jit(solution)/shard_map/ppermute | solution.py:220
  104.1 5.1 %collective-permute-done.16.refs_0_ = bf16[2064,128]{1,0:T(8,128)(2,1)S(1)} collective-permute-done((bf16[2064,128]{1,0:T(8,128)(2,1)S(1)}, bf16[2064,128]{1,0:T(8,128)(2,1)S(1)}, u32[]{:S(2)}, u32[]{:S(2)}) %collective-permute-start.16) | collective-permute-done | bytes 528416 | tf_op jit(solution)/shard_map/ppermute | solution.py:220
  109.2 0.9 shard_map.54
  111.8 1.1 shard_map.64
  112.9 2.3 %collective-permute-start.27 = (bf16[2576,128]{1,0:T(8,128)(2,1)S(1)}, bf16[2576,128]{1,0:T(8,128)(2,1)S(1)}, u32[]{:S(2)}, u32[]{:S(2)}) collective-permute-start(bf16[2576,128]{1,0:T(8,128)(2,1)S(1)} %shard_map.64), channel_id=1, source_target_pairs={{0,64},{1,193},{64,128},{65,1},{128,192},{129,65},{192,0},{193,129... | collective-permute-start | bytes 1978376 | tf_op jit(solution)/shard_map/ppermute | solution.py:220
  116.1 0.9 shard_map.58
  117.0 1.3 collective-permute-start.21
  118.3 4.8 %collective-permute-done.17.refs_0_ = bf16[2064,128]{1,0:T(8,128)(2,1)S(1)} collective-permute-done((bf16[2064,128]{1,0:T(8,128)(2,1)S(1)}, bf16[2064,128]{1,0:T(8,128)(2,1)S(1)}, u32[]{:S(2)}, u32[]{:S(2)}) %collective-permute-start.17) | collective-permute-done | bytes 528416 | tf_op jit(solution)/shard_map/ppermute | solution.py:220
  123.1 0.9 shard_map.55
  124.0 2.7 %collective-permute-start.18 = (bf16[2064,128]{1,0:T(8,128)(2,1)S(1)}, bf16[2064,128]{1,0:T(8,128)(2,1)S(1)}, u32[]{:S(2)}, u32[]{:S(2)}) collective-permute-start(bf16[2064,128]{1,0:T(8,128)(2,1)S(1)} %shard_map.55), channel_id=1, source_target_pairs={{0,8},{1,57},{8,16},{9,1},{16,24},{17,9},{24,32},{25,17},{32,40},{... | collective-permute-start | bytes 1585160 | tf_op jit(solution)/shard_map/ppermute | solution.py:220
  126.7 1.6 %fusion.own_ref = f32[256,1280]{1,0:T(8,128)S(1)} fusion(bf16[2048,1280]{1,0:T(8,128)(2,1)S(1)} %shard_map.50, bf16[2048,1024]{1,0:T(8,128)(2,1)S(1)} %shard_map.62, s32[]{:T(128)S(6)} %select_n.74), kind=kOutput, calls=%fused_computation | convolution fusion | flops 1342177280 | bytes 7602180 | tf_op jit(solution)/shard_map/dot_general | solution.py:266
  128.3 1.3 shard_map.66
  129.6 8.6 %collective-permute-start.29 = (bf16[1296,128]{1,0:T(8,128)(2,1)S(1)}, bf16[1296,128]{1,0:T(8,128)(2,1)S(1)}, u32[]{:S(2)}, u32[]{:S(2)}) collective-permute-start(bf16[1296,128]{1,0:T(8,128)(2,1)S(1)} %get-tuple-element.41), channel_id=1, source_target_pairs={{0,4},{4,0},{1,5},{5,1},{2,6},{6,2},{3,7},{7,3},{8,12},{12,8},{9,1... | collective-permute-start | bytes 995336 | tf_op jit(solution)/shard_map/ppermute | solution.py:205
  139.1 1.0 shard_map.60
  140.0 6.6 %collective-permute-start.22 = (bf16[128,1024]{1,0:T(8,128)(2,1)S(1)}, bf16[128,1024]{1,0:T(8,128)(2,1)S(1)}, u32[]{:S(2)}, u32[]{:S(2)}) collective-permute-start(bf16[128,1024]{1,0:T(8,128)(2,1)S(1)} %shard_map.60), channel_id=1, source_target_pairs={{0,4},{4,0},{1,5},{5,1},{2,6},{6,2},{3,7},{7,3},{8,12},{12,8},{9,1... | collective-permute-start | bytes 786440 | tf_op jit(solution)/shard_map/ppermute | solution.py:205
  146.7 1.4 shard_map.67
  148.1 1.0 shard_map.59.mine_ref
  149.1 1.9 %collective-permute-done.22.got_ref = bf16[128,1024]{1,0:T(8,128)(2,1)S(1)} collective-permute-done((bf16[128,1024]{1,0:T(8,128)(2,1)S(1)}, bf16[128,1024]{1,0:T(8,128)(2,1)S(1)}, u32[]{:S(2)}, u32[]{:S(2)}) %collective-permute-start.22) | collective-permute-done | bytes 262176 | tf_op jit(solution)/shard_map/ppermute | solution.py:205
  (98 shorter events, 16.6 us)
Async XLA Ops:
  0.6 7.1 %copy-start.19 = (bf16[1,512,640]{2,1,0:T(8,128)(2,1)S(1)}, bf16[1,512,640]{2,1,0:T(8,128)(2,1)}, u32[]{:S(2)}) copy-start(bf16[1,512,640]{2,1,0:T(8,128)(2,1)} %param.5) | copy-start | bytes 1966084
  1.9 39.3 %copy-start.7 = (bf16[128,1024]{1,0:T(8,128)(2,1)}, bf16[128,1024]{1,0:T(8,128)(2,1)S(1)}, u32[]{:S(2)}) copy-start(bf16[128,1024]{1,0:T(8,128)(2,1)S(1)} %get-tuple-element.27.refs_0_) | copy-start | bytes 786436
  4.5 52.5 %collective-permute-start.9 = (bf16[1024,640]{1,0:T(8,128)(2,1)}, bf16[1024,640]{1,0:T(8,128)(2,1)S(1)}, u32[]{:S(2)}, u32[]{:S(2)}) collective-permute-start(bf16[1024,640]{1,0:T(8,128)(2,1)} %constant_dynamic-slice_fusion), channel_id=1, source_target_pairs={{0,4},{1,7},{4,2},{5,1},{2,6},{3,5},{6,0},{7,3},{8,12},{9,15},{12,... | collective-permute-start | bytes 3932168 | tf_op jit(solution)/shard_map/ppermute | solution.py:214
  6.1 24.5 %collective-permute-start.2 = (bf16[128,1024]{1,0:T(8,128)(2,1)S(1)}, bf16[128,1024]{1,0:T(8,128)(2,1)S(1)}, u32[]{:S(2)}, u32[]{:S(2)}) collective-permute-start(bf16[128,1024]{1,0:T(8,128)(2,1)S(1)} %get-tuple-element.24), channel_id=1, source_target_pairs={{0,4},{4,0},{1,5},{5,1},{2,6},{6,2},{3,7},{7,3},{8,12},{12,8},{9,1... | collective-permute-start | bytes 786440 | tf_op jit(solution)/shard_map/ppermute | solution.py:205
  7.7 28.9 %collective-permute-start.11 = (bf16[256,640]{1,0:T(8,128)(2,1)S(1)}, bf16[256,640]{1,0:T(8,128)(2,1)S(1)}, u32[]{:S(2)}, u32[]{:S(2)}) collective-permute-start(bf16[256,640]{1,0:T(8,128)(2,1)S(1)} %get-tuple-element.43), channel_id=1, source_target_pairs={{0,4},{4,0},{1,5},{5,1},{2,6},{6,2},{3,7},{7,3},{8,12},{12,8},{9,1... | collective-permute-start | bytes 983048 | tf_op jit(solution)/shard_map/ppermute | solution.py:205
  8.3 24.2 %collective-permute-start = (bf16[128,1024]{1,0:T(8,128)(2,1)S(1)}, bf16[128,1024]{1,0:T(8,128)(2,1)S(1)}, u32[]{:S(2)}, u32[]{:S(2)}) collective-permute-start(bf16[128,1024]{1,0:T(8,128)(2,1)S(1)} %get-tuple-element.27.refs_0_), channel_id=1, source_target_pairs={{0,8},{1,57},{8,16},{9,1},{16,24},{17,9},{24,32},{25,17},{32,40},{... | collective-permute-start | bytes 786440 | tf_op jit(solution)/shard_map/ppermute | solution.py:220
  10.2 24.2 %collective-permute-start.5 = (bf16[128,1024]{1,0:T(8,128)(2,1)S(1)}, bf16[128,1024]{1,0:T(8,128)(2,1)S(1)}, u32[]{:S(2)}, u32[]{:S(2)}) collective-permute-start(bf16[128,1024]{1,0:T(8,128)(2,1)S(1)} %get-tuple-element.27.refs_0_), channel_id=1, source_target_pairs={{0,56},{1,9},{8,0},{9,17},{16,8},{17,25},{24,16},{25,33},{32,24},{... | collective-permute-start | bytes 786440 | tf_op jit(solution)/shard_map/ppermute | solution.py:220
  30.6 17.5 %copy-start.9 = (bf16[128,1024]{1,0:T(8,128)(2,1)}, bf16[128,1024]{1,0:T(8,128)(2,1)S(1)}, u32[]{:S(2)}) copy-start(bf16[128,1024]{1,0:T(8,128)(2,1)S(1)} %collective-permute-done.2.refs_1_) | copy-start | bytes 786436
  30.6 10.6 %collective-permute-start.3 = (bf16[128,1024]{1,0:T(8,128)(2,1)S(1)}, bf16[128,1024]{1,0:T(8,128)(2,1)S(1)}, u32[]{:S(2)}, u32[]{:S(2)}) collective-permute-start(bf16[128,1024]{1,0:T(8,128)(2,1)S(1)} %collective-permute-done.2.refs_1_), channel_id=1, source_target_pairs={{0,8},{1,57},{8,16},{9,1},{16,24},{17,9},{24,32},{25,17},{32,40},{... | collective-permute-start | bytes 786440 | tf_op jit(solution)/shard_map/ppermute | solution.py:220
  32.5 23.8 %copy-start.11 = (bf16[128,1024]{1,0:T(8,128)(2,1)}, bf16[128,1024]{1,0:T(8,128)(2,1)S(1)}, u32[]{:S(2)}) copy-start(bf16[128,1024]{1,0:T(8,128)(2,1)S(1)} %collective-permute-done.refs_2_) | copy-start | bytes 786436
  32.5 14.3 %collective-permute-start.1 = (bf16[128,1024]{1,0:T(8,128)(2,1)S(1)}, bf16[128,1024]{1,0:T(8,128)(2,1)S(1)}, u32[]{:S(2)}, u32[]{:S(2)}) collective-permute-start(bf16[128,1024]{1,0:T(8,128)(2,1)S(1)} %collective-permute-done.refs_2_), channel_id=1, source_target_pairs={{0,8},{1,57},{8,16},{9,1},{16,24},{17,9},{24,32},{25,17},{32,40},{... | collective-permute-start | bytes 786440 | tf_op jit(solution)/shard_map/ppermute | solution.py:220
  34.4 21.9 %copy-start.13 = (bf16[128,1024]{1,0:T(8,128)(2,1)}, bf16[128,1024]{1,0:T(8,128)(2,1)S(1)}, u32[]{:S(2)}) copy-start(bf16[128,1024]{1,0:T(8,128)(2,1)S(1)} %collective-permute-done.5.refs_4_) | copy-start | bytes 786436
  34.4 13.6 %collective-permute-start.7 = (bf16[128,1024]{1,0:T(8,128)(2,1)S(1)}, bf16[128,1024]{1,0:T(8,128)(2,1)S(1)}, u32[]{:S(2)}, u32[]{:S(2)}) collective-permute-start(bf16[128,1024]{1,0:T(8,128)(2,1)S(1)} %collective-permute-done.2.refs_1_), channel_id=1, source_target_pairs={{0,56},{1,9},{8,0},{9,17},{16,8},{17,25},{24,16},{25,33},{32,24},{... | collective-permute-start | bytes 786440 | tf_op jit(solution)/shard_map/ppermute | solution.py:220
  36.6 16.5 %collective-permute-start.6 = (bf16[128,1024]{1,0:T(8,128)(2,1)S(1)}, bf16[128,1024]{1,0:T(8,128)(2,1)S(1)}, u32[]{:S(2)}, u32[]{:S(2)}) collective-permute-start(bf16[128,1024]{1,0:T(8,128)(2,1)S(1)} %collective-permute-done.5.refs_4_), channel_id=1, source_target_pairs={{0,56},{1,9},{8,0},{9,17},{16,8},{17,25},{24,16},{25,33},{32,24},{... | collective-permute-start | bytes 786440 | tf_op jit(solution)/shard_map/ppermute | solution.py:220
  41.2 16.7 %copy-start.15 = (bf16[128,1024]{1,0:T(8,128)(2,1)}, bf16[128,1024]{1,0:T(8,128)(2,1)S(1)}, u32[]{:S(2)}) copy-start(bf16[128,1024]{1,0:T(8,128)(2,1)S(1)} %collective-permute-done.3.refs_3_) | copy-start | bytes 786436
  41.2 12.0 %collective-permute-start.4 = (bf16[128,1024]{1,0:T(8,128)(2,1)S(1)}, bf16[128,1024]{1,0:T(8,128)(2,1)S(1)}, u32[]{:S(2)}, u32[]{:S(2)}) collective-permute-start(bf16[128,1024]{1,0:T(8,128)(2,1)S(1)} %collective-permute-done.3.refs_3_), channel_id=1, source_target_pairs={{0,8},{1,57},{8,16},{9,1},{16,24},{17,9},{24,32},{25,17},{32,40},{... | collective-permute-start | bytes 786440 | tf_op jit(solution)/shard_map/ppermute | solution.py:220
  46.8 11.1 %collective-permute-start.12 = (bf16[256,1280]{1,0:T(8,128)(2,1)S(1)}, bf16[256,1280]{1,0:T(8,128)(2,1)}, u32[]{:S(2)}, u32[]{:S(2)}) collective-permute-start(bf16[256,1280]{1,0:T(8,128)(2,1)S(1)} %pad_maximum_fusion.refs_0_), channel_id=1, source_target_pairs={{0,64},{1,193},{64,128},{65,1},{128,192},{129,65},{192,0},{193,129... | collective-permute-start | bytes 1966088 | tf_op jit(solution)/shard_map/ppermute | solution.py:220
  48.0 11.1 %copy-start.17 = (bf16[128,1024]{1,0:T(8,128)(2,1)}, bf16[128,1024]{1,0:T(8,128)(2,1)S(1)}, u32[]{:S(2)}) copy-start(bf16[128,1024]{1,0:T(8,128)(2,1)S(1)} %collective-permute-done.7.refs_5_) | copy-start | bytes 786436
  48.0 8.3 %collective-permute-start.8 = (bf16[128,1024]{1,0:T(8,128)(2,1)S(1)}, bf16[128,1024]{1,0:T(8,128)(2,1)S(1)}, u32[]{:S(2)}, u32[]{:S(2)}) collective-permute-start(bf16[128,1024]{1,0:T(8,128)(2,1)S(1)} %collective-permute-done.7.refs_5_), channel_id=1, source_target_pairs={{0,56},{1,9},{8,0},{9,17},{16,8},{17,25},{24,16},{25,33},{32,24},{... | collective-permute-start | bytes 786440 | tf_op jit(solution)/shard_map/ppermute | solution.py:220
  53.1 3.2 %copy-start.1 = (bf16[128,1024]{1,0:T(8,128)(2,1)}, bf16[128,1024]{1,0:T(8,128)(2,1)S(1)}, u32[]{:S(2)}) copy-start(bf16[128,1024]{1,0:T(8,128)(2,1)S(1)} %collective-permute-done.6.refs_8_) | copy-start | bytes 786436
  57.0 20.6 %collective-permute-start.10 = (bf16[1024,640]{1,0:T(8,128)(2,1)S(1)}, bf16[1024,640]{1,0:T(8,128)(2,1)S(1)}, u32[]{:S(2)}, u32[]{:S(2)}) collective-permute-start(bf16[1024,640]{1,0:T(8,128)(2,1)S(1)} %collective-permute-done.9.refs_1_), channel_id=1, source_target_pairs={{0,1},{1,0},{2,3},{3,2},{4,5},{5,4},{6,7},{7,6},{8,9},{9,8},{10,11... | collective-permute-start | bytes 3932168 | tf_op jit(solution)/shard_map/ppermute | solution.py:205
  57.0 17.7 %collective-permute-start.13 = (bf16[256,1280]{1,0:T(8,128)(2,1)S(1)}, bf16[256,1280]{1,0:T(8,128)(2,1)}, u32[]{:S(2)}, u32[]{:S(2)}) collective-permute-start(bf16[256,1280]{1,0:T(8,128)(2,1)S(1)} %pad_maximum_fusion.refs_0_), channel_id=1, source_target_pairs={{0,192},{1,65},{64,0},{65,129},{128,64},{129,193},{192,128},{193,1... | collective-permute-start | bytes 1966088 | tf_op jit(solution)/shard_map/ppermute | solution.py:220
  58.0 16.8 %collective-permute-start.14 = (bf16[256,1280]{1,0:T(8,128)(2,1)}, bf16[256,1280]{1,0:T(8,128)(2,1)}, u32[]{:S(2)}, u32[]{:S(2)}) collective-permute-start(bf16[256,1280]{1,0:T(8,128)(2,1)} %collective-permute-done.12.refs_1_), channel_id=1, source_target_pairs={{0,64},{1,193},{64,128},{65,1},{128,192},{129,65},{192,0},{193,129... | collective-permute-start | bytes 1966088 | tf_op jit(solution)/shard_map/ppermute | solution.py:220
  59.2 14.9 %collective-permute-start.23 = (bf16[256,1024]{1,0:T(8,128)(2,1)}, bf16[256,1024]{1,0:T(8,128)(2,1)}, u32[]{:S(2)}, u32[]{:S(2)}) collective-permute-start(bf16[256,1024]{1,0:T(8,128)(2,1)} %constant_dynamic-update-slice_fusion), channel_id=1, source_target_pairs={{0,8},{1,57},{8,16},{9,1},{16,24},{17,9},{24,32},{25,17},{32,40},{... | collective-permute-start | bytes 1572872 | tf_op jit(solution)/shard_map/ppermute | solution.py:220
  59.6 18.0 %copy-start = (bf16[2048,640]{1,0:T(8,128)(2,1)S(1)}, bf16[2048,640]{1,0:T(8,128)(2,1)}, u32[]{:S(2)}) copy-start(bf16[2048,640]{1,0:T(8,128)(2,1)} %refs_0_) | copy-start | bytes 7864324
  59.6 25.8 %collective-permute-start.24 = (bf16[256,1024]{1,0:T(8,128)(2,1)}, bf16[256,1024]{1,0:T(8,128)(2,1)S(1)}, u32[]{:S(2)}, u32[]{:S(2)}) collective-permute-start(bf16[256,1024]{1,0:T(8,128)(2,1)} %copy-done.20), channel_id=1, source_target_pairs={{0,56},{1,9},{8,0},{9,17},{16,8},{17,25},{24,16},{25,33},{32,24},{... | collective-permute-start | bytes 1572872 | tf_op jit(solution)/shard_map/ppermute | solution.py:220
  74.1 11.4 %collective-permute-start.25 = (bf16[256,1024]{1,0:T(8,128)(2,1)}, bf16[256,1024]{1,0:T(8,128)(2,1)S(1)}, u32[]{:S(2)}, u32[]{:S(2)}) collective-permute-start(bf16[256,1024]{1,0:T(8,128)(2,1)} %collective-permute-done.23.refs_10_), channel_id=1, source_target_pairs={{0,8},{1,57},{8,16},{9,1},{16,24},{17,9},{24,32},{25,17},{32,40},{... | collective-permute-start | bytes 1572872 | tf_op jit(solution)/shard_map/ppermute | solution.py:220
  80.1 5.4 %copy-start.2 = (bf16[128,1024]{1,0:T(8,128)(2,1)S(1)}, bf16[128,1024]{1,0:T(8,128)(2,1)}, u32[]{:S(2)}) copy-start(bf16[128,1024]{1,0:T(8,128)(2,1)} %copy-done.1) | copy-start | bytes 786436
  80.1 5.4 %copy-start.4 = (bf16[128,1024]{1,0:T(8,128)(2,1)S(1)}, bf16[128,1024]{1,0:T(8,128)(2,1)}, u32[]{:S(2)}) copy-start(bf16[128,1024]{1,0:T(8,128)(2,1)} %copy-done.3) | copy-start | bytes 786436
  80.1 5.4 %copy-start.6 = (bf16[128,1024]{1,0:T(8,128)(2,1)S(1)}, bf16[128,1024]{1,0:T(8,128)(2,1)}, u32[]{:S(2)}) copy-start(bf16[128,1024]{1,0:T(8,128)(2,1)} %copy-done.5) | copy-start | bytes 786436
  80.1 5.4 %copy-start.8 = (bf16[128,1024]{1,0:T(8,128)(2,1)S(1)}, bf16[128,1024]{1,0:T(8,128)(2,1)}, u32[]{:S(2)}) copy-start(bf16[128,1024]{1,0:T(8,128)(2,1)} %copy-done.7) | copy-start | bytes 786436
  80.1 5.4 %copy-start.10 = (bf16[128,1024]{1,0:T(8,128)(2,1)S(1)}, bf16[128,1024]{1,0:T(8,128)(2,1)}, u32[]{:S(2)}) copy-start(bf16[128,1024]{1,0:T(8,128)(2,1)} %copy-done.9) | copy-start | bytes 786436
  80.1 5.4 %copy-start.12 = (bf16[128,1024]{1,0:T(8,128)(2,1)S(1)}, bf16[128,1024]{1,0:T(8,128)(2,1)}, u32[]{:S(2)}) copy-start(bf16[128,1024]{1,0:T(8,128)(2,1)} %copy-done.11) | copy-start | bytes 786436
  80.2 5.4 %copy-start.14 = (bf16[128,1024]{1,0:T(8,128)(2,1)S(1)}, bf16[128,1024]{1,0:T(8,128)(2,1)}, u32[]{:S(2)}) copy-start(bf16[128,1024]{1,0:T(8,128)(2,1)} %copy-done.13) | copy-start | bytes 786436
  80.2 5.4 %copy-start.16 = (bf16[128,1024]{1,0:T(8,128)(2,1)S(1)}, bf16[128,1024]{1,0:T(8,128)(2,1)}, u32[]{:S(2)}) copy-start(bf16[128,1024]{1,0:T(8,128)(2,1)} %copy-done.15) | copy-start | bytes 786436
  80.2 5.4 %copy-start.18 = (bf16[128,1024]{1,0:T(8,128)(2,1)S(1)}, bf16[128,1024]{1,0:T(8,128)(2,1)}, u32[]{:S(2)}) copy-start(bf16[128,1024]{1,0:T(8,128)(2,1)} %copy-done.17) | copy-start | bytes 786436
  80.2 16.0 %collective-permute-start.15 = (bf16[2064,128]{1,0:T(8,128)(2,1)S(1)}, bf16[2064,128]{1,0:T(8,128)(2,1)S(1)}, u32[]{:S(2)}, u32[]{:S(2)}) collective-permute-start(bf16[2064,128]{1,0:T(8,128)(2,1)S(1)} %shard_map.52), channel_id=1, source_target_pairs={{0,8},{1,57},{8,16},{9,1},{16,24},{17,9},{24,32},{25,17},{32,40},{... | collective-permute-start | bytes 1585160 | tf_op jit(solution)/shard_map/ppermute | solution.py:220
  82.1 18.3 %collective-permute-start.19 = (bf16[2064,128]{1,0:T(8,128)(2,1)S(1)}, bf16[2064,128]{1,0:T(8,128)(2,1)S(1)}, u32[]{:S(2)}, u32[]{:S(2)}) collective-permute-start(bf16[2064,128]{1,0:T(8,128)(2,1)S(1)} %shard_map.56), channel_id=1, source_target_pairs={{0,56},{1,9},{8,0},{9,17},{16,8},{17,25},{24,16},{25,33},{32,24},{... | collective-permute-start | bytes 1585160 | tf_op jit(solution)/shard_map/ppermute | solution.py:220
  89.9 21.9 %collective-permute-start.26 = (bf16[2576,128]{1,0:T(8,128)(2,1)S(1)}, bf16[2576,128]{1,0:T(8,128)(2,1)S(1)}, u32[]{:S(2)}, u32[]{:S(2)}) collective-permute-start(bf16[2576,128]{1,0:T(8,128)(2,1)S(1)} %shard_map.63), channel_id=1, source_target_pairs={{0,64},{1,193},{64,128},{65,1},{128,192},{129,65},{192,0},{193,129... | collective-permute-start | bytes 1978376 | tf_op jit(solution)/shard_map/ppermute | solution.py:220
  97.1 12.1 %collective-permute-start.16 = (bf16[2064,128]{1,0:T(8,128)(2,1)S(1)}, bf16[2064,128]{1,0:T(8,128)(2,1)S(1)}, u32[]{:S(2)}, u32[]{:S(2)}) collective-permute-start(bf16[2064,128]{1,0:T(8,128)(2,1)S(1)} %shard_map.53), channel_id=1, source_target_pairs={{0,8},{1,57},{8,16},{9,1},{16,24},{17,9},{24,32},{25,17},{32,40},{... | collective-permute-start | bytes 1585160 | tf_op jit(solution)/shard_map/ppermute | solution.py:220
  98.9 29.3 %collective-permute-start.28 = (bf16[2576,128]{1,0:T(8,128)(2,1)S(1)}, bf16[2576,128]{1,0:T(8,128)(2,1)S(1)}, u32[]{:S(2)}, u32[]{:S(2)}) collective-permute-start(bf16[2576,128]{1,0:T(8,128)(2,1)S(1)} %shard_map.65), channel_id=1, source_target_pairs={{0,192},{1,65},{64,0},{65,129},{128,64},{129,193},{192,128},{193,1... | collective-permute-start | bytes 1978376 | tf_op jit(solution)/shard_map/ppermute | solution.py:220
  101.3 14.7 %collective-permute-start.20 = (bf16[2064,128]{1,0:T(8,128)(2,1)S(1)}, bf16[2064,128]{1,0:T(8,128)(2,1)S(1)}, u32[]{:S(2)}, u32[]{:S(2)}) collective-permute-start(bf16[2064,128]{1,0:T(8,128)(2,1)S(1)} %shard_map.57), channel_id=1, source_target_pairs={{0,56},{1,9},{8,0},{9,17},{16,8},{17,25},{24,16},{25,33},{32,24},{... | collective-permute-start | bytes 1585160 | tf_op jit(solution)/shard_map/ppermute | solution.py:220
  110.1 13.0 %collective-permute-start.17 = (bf16[2064,128]{1,0:T(8,128)(2,1)S(1)}, bf16[2064,128]{1,0:T(8,128)(2,1)S(1)}, u32[]{:S(2)}, u32[]{:S(2)}) collective-permute-start(bf16[2064,128]{1,0:T(8,128)(2,1)S(1)} %shard_map.54), channel_id=1, source_target_pairs={{0,8},{1,57},{8,16},{9,1},{16,24},{17,9},{24,32},{25,17},{32,40},{... | collective-permute-start | bytes 1585160 | tf_op jit(solution)/shard_map/ppermute | solution.py:220
  112.9 15.4 %collective-permute-start.27 = (bf16[2576,128]{1,0:T(8,128)(2,1)S(1)}, bf16[2576,128]{1,0:T(8,128)(2,1)S(1)}, u32[]{:S(2)}, u32[]{:S(2)}) collective-permute-start(bf16[2576,128]{1,0:T(8,128)(2,1)S(1)} %shard_map.64), channel_id=1, source_target_pairs={{0,64},{1,193},{64,128},{65,1},{128,192},{129,65},{192,0},{193,129... | collective-permute-start | bytes 1978376 | tf_op jit(solution)/shard_map/ppermute | solution.py:220
  117.0 22.1 %collective-permute-start.21 = (bf16[2064,128]{1,0:T(8,128)(2,1)S(1)}, bf16[2064,128]{1,0:T(8,128)(2,1)S(1)}, u32[]{:S(2)}, u32[]{:S(2)}) collective-permute-start(bf16[2064,128]{1,0:T(8,128)(2,1)S(1)} %shard_map.58), channel_id=1, source_target_pairs={{0,56},{1,9},{8,0},{9,17},{16,8},{17,25},{24,16},{25,33},{32,24},{... | collective-permute-start | bytes 1585160 | tf_op jit(solution)/shard_map/ppermute | solution.py:220
  124.0 15.0 %collective-permute-start.18 = (bf16[2064,128]{1,0:T(8,128)(2,1)S(1)}, bf16[2064,128]{1,0:T(8,128)(2,1)S(1)}, u32[]{:S(2)}, u32[]{:S(2)}) collective-permute-start(bf16[2064,128]{1,0:T(8,128)(2,1)S(1)} %shard_map.55), channel_id=1, source_target_pairs={{0,8},{1,57},{8,16},{9,1},{16,24},{17,9},{24,32},{25,17},{32,40},{... | collective-permute-start | bytes 1585160 | tf_op jit(solution)/shard_map/ppermute | solution.py:220
  129.6 17.1 %collective-permute-start.29 = (bf16[1296,128]{1,0:T(8,128)(2,1)S(1)}, bf16[1296,128]{1,0:T(8,128)(2,1)S(1)}, u32[]{:S(2)}, u32[]{:S(2)}) collective-permute-start(bf16[1296,128]{1,0:T(8,128)(2,1)S(1)} %get-tuple-element.41), channel_id=1, source_target_pairs={{0,4},{4,0},{1,5},{5,1},{2,6},{6,2},{3,7},{7,3},{8,12},{12,8},{9,1... | collective-permute-start | bytes 995336 | tf_op jit(solution)/shard_map/ppermute | solution.py:205
  140.0 10.9 %collective-permute-start.22 = (bf16[128,1024]{1,0:T(8,128)(2,1)S(1)}, bf16[128,1024]{1,0:T(8,128)(2,1)S(1)}, u32[]{:S(2)}, u32[]{:S(2)}) collective-permute-start(bf16[128,1024]{1,0:T(8,128)(2,1)S(1)} %shard_map.60), channel_id=1, source_target_pairs={{0,4},{4,0},{1,5},{5,1},{2,6},{6,2},{3,7},{7,3},{8,12},{12,8},{9,1... | collective-permute-start | bytes 786440 | tf_op jit(solution)/shard_map/ppermute | solution.py:205
  (3 other events, 6.0 us)
where the time goes:
time: 153 us; the launch traced here: 152 us
  starting transfers between devices  62.4 us (41%)
  waiting for transfers between devices  48.4 us (32%)
  Pallas kernels  19.7 us (13%)
  matrix products  13.2 us (9%)
  local copies, waits for them, and re-layouts  6.25 us (4%)
    ppermute x24, starting transfers between devices, ring(): return lax.ppermute(a, (axis, 'c'), perm)  43.6 us
    ppermute x24, waiting for transfers between devices, ring(): return lax.ppermute(a, (axis, 'c'), perm)  30.1 us
    ppermute x5, waiting for transfers between devices, swap(): return lax.ppermute(a, axis, [(0, 1), (1, 0)])  18.3 us
    ppermute x5, starting transfers between devices, swap(): return lax.ppermute(a, axis, [(0, 1), (1, 0)])  17.3 us
    pallas_call x15, Pallas kernels, call(): pl.pallas_call(kernel, grid_spec=pltpu.PrefetchScalarGridSpec(num_scalar_...  13.7 us
    dot_general x12, matrix products, dot(): return lax.dot_general(a, b, (dims, ((), ())), preferred_element_type=F32)  13.2 us
    pallas_call x3, Pallas kernels, placed(): pl.pallas_call(functools.partial(placed_kernel, fixed), grid_spec=pltpu.P...  6 us
  transfers between devices with their start and end apart: 30, of which 9 were waited for; matrix products, arithmetic and copies ran while one was open for 10% of the time, Pallas kernels for 12%

commit v1 on v0

v1 whole, which is shorter than its diff:
```python
import functools

import jax
import jax.numpy as jnp
from jax import lax
from jax.experimental import pallas as pl
from jax.experimental.pallas import tpu as pltpu
from jax.sharding import Mesh, PartitionSpec as P

F32 = jnp.float32
BF16 = jnp.bfloat16
LANES = 128
TILE = 16
SQUARINGS = 4
TOP = 2.0**7.75
TINY = 1e-30
MIB = 1024 * 1024


def encode(v, s):
    a = jnp.abs(v) * s
    for _ in range(SQUARINGS):
        a = a * a
    return jnp.where(v < 0, -a, a).astype(BF16)


def decode(y, inv):
    y = y.astype(F32)
    a = jnp.exp2(jnp.log2(jnp.abs(y)) * 0.5**SQUARINGS) * inv
    return jnp.where(y < 0, -a, a)


def inverse_scale(ref):
    return 1.0 / ref[ref.shape[0] - TILE :, :].astype(F32)


def for_tiles(rows, body, init):
    return lax.fori_loop(0, rows // TILE, lambda i, x: body(pl.multiple_of(i * TILE, TILE), x), init, unroll=2)


def write_coded(v_ref, blocks, amax, out_ref):
    rows = v_ref.shape[0]
    coded = (TOP / jnp.maximum(amax, TINY)).astype(BF16)
    s = coded.astype(F32)
    out_ref[blocks * rows :, :] = coded

    def body(r, x):
        for j in range(blocks):
            at = j * LANES
            out_ref[pl.ds(j * rows + r, TILE), :] = encode(v_ref[pl.ds(r, TILE), at : at + LANES], s)
        return x

    for_tiles(rows, body, 0)


def fetch(at_ref, own_ref, v_ref, sem):
    rows = pl.ds(pl.multiple_of(at_ref[0], LANES), v_ref.shape[0])
    copy = pltpu.make_async_copy(own_ref.at[rows], v_ref, sem)
    copy.start()
    copy.wait()


def summed_tile(v_ref, got, invs, r, j):
    rows = v_ref.shape[0]
    v = v_ref[pl.ds(r, TILE), j * LANES : (j + 1) * LANES]
    for ref, inv in zip(got, invs):
        v = v + decode(ref[pl.ds(j * rows + r, TILE), :], inv)
    return v


def hop_kernel(n_got, at_ref, *refs):
    got, (own_ref, out_ref, v_ref, sem) = refs[:n_got], refs[n_got:]
    blocks = v_ref.shape[1] // LANES
    invs = [inverse_scale(ref) for ref in got]
    fetch(at_ref, own_ref, v_ref, sem)

    def body(r, amax):
        for j in range(blocks):
            v = summed_tile(v_ref, got, invs, r, j)
            if got:
                v_ref[pl.ds(r, TILE), j * LANES : (j + 1) * LANES] = v
            amax = jnp.maximum(amax, jnp.abs(v))
        return amax

    amax = for_tiles(v_ref.shape[0], body, jnp.zeros((TILE, LANES), F32))
    write_coded(v_ref, blocks, amax, out_ref)


def tokens_kernel(at_ref, f_ref, b_ref, own_ref, out_ref, v_ref, sem):
    invs = [inverse_scale(f_ref), inverse_scale(b_ref)]
    rows = out_ref.shape[0]
    fetch(at_ref, own_ref, v_ref, sem)

    def body(r, x):
        for j in range(v_ref.shape[1] // LANES):
            v = v_ref[pl.ds(r, TILE), j * LANES : (j + 1) * LANES]
            for ref, inv in zip((f_ref, b_ref), invs):
                row = pl.multiple_of(j * 2 * rows + at_ref[1] + r, TILE)
                v = v + decode(ref[pl.ds(row, TILE), :], inv)
            out_ref[pl.ds(r, TILE), j * LANES : (j + 1) * LANES] = v.astype(BF16)
        return x

    for_tiles(rows, body, 0)


def columns_kernel(half, h_ref, mine_ref, got_ref, out_ref):
    for j in range(mine_ref.shape[1] // half):
        at = slice(j * half, (j + 1) * half)
        mine_at = pl.multiple_of((2 * j + h_ref[0]) * half, LANES)
        got_at = pl.multiple_of((2 * j + 1 - h_ref[0]) * half, LANES)
        out_ref[:, pl.ds(mine_at, half)] = mine_ref[:, at]
        out_ref[:, pl.ds(got_at, half)] = got_ref[:, at]


def owned_kernel(at_ref, f_ref, b_ref, own_ref, mine_ref, out_ref, v_ref, sem):
    invs = [inverse_scale(f_ref), inverse_scale(b_ref)]
    blocks = v_ref.shape[1] // LANES
    kept = blocks // 2
    fetch(at_ref, own_ref, v_ref, sem)

    def body(r, amax):
        for j in range(blocks):
            v = summed_tile(v_ref, (f_ref, b_ref), invs, r, j)
            if j < kept:
                mine_ref[pl.ds(r, TILE), j * LANES : (j + 1) * LANES] = v
            else:
                v_ref[pl.ds(r, TILE), (j - kept) * LANES : (j - kept + 1) * LANES] = v
                amax = jnp.maximum(amax, jnp.abs(v))
        return amax

    amax = for_tiles(v_ref.shape[0], body, jnp.zeros((TILE, LANES), F32))
    write_coded(v_ref, blocks - kept, amax, out_ref)


def rows_kernel(h_ref, mine_ref, got_ref, out_ref):
    rows = mine_ref.shape[0]
    inv = inverse_scale(got_ref)
    mine_at, got_at = h_ref[0] * rows, (1 - h_ref[0]) * rows

    def body(r, x):
        out_ref[pl.ds(pl.multiple_of(mine_at + r, TILE), TILE), :] = mine_ref[pl.ds(r, TILE), :]
        for j in range(mine_ref.shape[1] // LANES):
            v = decode(got_ref[pl.ds(j * rows + r, TILE), :], inv)
            out_ref[pl.ds(pl.multiple_of(got_at + r, TILE), TILE), j * LANES : (j + 1) * LANES] = v
        return x

    for_tiles(rows, body, 0)


def whole(shape):
    return pl.BlockSpec(shape, lambda i, idx: (0,) * len(shape))


def call(kernel, at, wholes, own, out_shapes, rows=0):
    in_specs, args, scratch = [whole(a.shape) for a in wholes], list(wholes), []
    if own is not None:
        in_specs.append(pl.BlockSpec(memory_space=pl.ANY))
        args.append(own)
        scratch = [pltpu.VMEM((rows, own.shape[1]), F32), pltpu.SemaphoreType.DMA]
    size = sum(a.size * 4 for a in wholes) + sum(s.size * 4 for s in out_shapes)
    return pl.pallas_call(
        kernel,
        grid_spec=pltpu.PrefetchScalarGridSpec(
            num_scalar_prefetch=1,
            grid=(1,),
            in_specs=in_specs,
            out_specs=[whole(s.shape) for s in out_shapes],
            scratch_shapes=scratch,
        ),
        out_shape=out_shapes,
        compiler_params=pltpu.CompilerParams(vmem_limit_bytes=10 * MIB),
        cost_estimate=pl.CostEstimate(flops=size * 8, bytes_accessed=size, transcendentals=0),
    )(jnp.stack([jnp.int32(i) for i in at]), *args)


def placed_kernel(pieces, at_ref, *refs):
    srcs, out_ref, sems = refs[:-2], refs[-2], refs[-1]

    def place(i, j, size):
        fixed = pieces[i][1 + j]
        if fixed is None:
            fixed = pl.multiple_of(at_ref[i], LANES)
        return pl.ds(fixed, size)

    copies = []
    for i, (src, _, _, _, _, rows, cols) in enumerate(pieces):
        here = srcs[src].at[place(i, 0, rows), place(i, 1, cols)]
        there = out_ref.at[place(i, 2, rows), place(i, 3, cols)]
        copies.append(pltpu.make_async_copy(here, there, sems.at[i]))
    for copy in copies:
        copy.start()
    for copy in copies:
        copy.wait()


def placed(arrays, pieces, shape, space=pltpu.VMEM):
    known = [tuple(None if isinstance(p, jax.Array) else p for p in piece) for piece in pieces]
    at = [next((p for p in piece if isinstance(p, jax.Array)), jnp.int32(0)) for piece in pieces]
    size = 2 * shape[0] * shape[1]
    return pl.pallas_call(
        functools.partial(placed_kernel, known),
        grid_spec=pltpu.PrefetchScalarGridSpec(
            num_scalar_prefetch=1,
            grid=(1,),
            in_specs=[pl.BlockSpec(memory_space=space)] * len(arrays),
            out_specs=pl.BlockSpec(memory_space=pltpu.VMEM),
            scratch_shapes=[pltpu.SemaphoreType.DMA((len(pieces),))],
        ),
        out_shape=jax.ShapeDtypeStruct(shape, BF16),
        compiler_params=pltpu.CompilerParams(vmem_limit_bytes=4 * MIB),
        cost_estimate=pl.CostEstimate(flops=0, bytes_accessed=2 * size, transcendentals=0),
    )(jnp.stack(at), *arrays)


def coded_shape(rows, width):
    return jax.ShapeDtypeStruct((width // LANES * rows + TILE, LANES), BF16)


def hop(got, shares, at, rows):
    shape = (rows, shares.shape[1])
    return call(functools.partial(hop_kernel, len(got)), [at], got, shares, [coded_shape(*shape)], rows)[0]


def swap(a, axis):
    return lax.ppermute(a, axis, [(0, 1), (1, 0)])


def y_ring(a):
    perm = []
    for y in range(4):
        for c in range(2):
            t = (y + (1 if c == 0 else -1)) % 4
            perm.append((((y % 2) * 2 + y // 2) * 2 + c, ((t % 2) * 2 + t // 2) * 2 + c))
    return lax.ppermute(a, ("yl", "yh", "c"), perm)


def ring(a, axis, way):
    n = lax.axis_size(axis)
    perm = [(i * 2 + c, (i + (way if c == 0 else -way)) % n * 2 + c) for i in range(n) for c in range(2)]
    return lax.ppermute(a, (axis, "c"), perm)


def block_at(axis, k):
    n = lax.axis_size(axis)
    return lax.rem(lax.axis_index(axis) + (1 - 2 * lax.axis_index("c")) * k + n, n)


def around(parts, axis, joint, before):
    n = lax.axis_size(axis)
    blocks = {0: parts}
    ahead = back = parts
    for k in range(1, n // 2 + 1):
        if k == joint:
            ahead, back = [jnp.concatenate(ahead)], [jnp.concatenate(back)]
        for held in before.get(k, []):
            *ahead, held = after(*ahead, held)
            *back, held = after(*back, held)
        ahead = blocks[-k] = [ring(p, axis, 1) for p in ahead]
        if k < n - n // 2:
            back = blocks[k] = [ring(p, axis, -1) for p in back]
    return blocks


def scattered(share, axis, first):
    n = lax.axis_size(axis)
    came = []
    for way, hops, got in ((1, n // 2, first[0]), (-1, n - n // 2 - 1, first[1])):
        got = ring(got, axis, way)
        for k in range(hops - 1, 0, -1):
            got = ring(share([got], way * k), axis, way)
        came.append(got)
    return came


def dot_kernel(dims, a_ref, b_ref, out_ref):
    out_ref[...] = lax.dot_general(a_ref[...], b_ref[...], (dims, ((), ())), preferred_element_type=F32)


def blocked_dot(a, block, at, count, b, dims):
    rows, cols = block[1 - dims[0][0]], b.shape[1 - dims[1][0]]
    along = [i for i in range(2) if i != dims[0][0]][0]
    size = 2 * count * block[0] * block[1] + 2 * b.size + 4 * count * rows * cols
    return pl.pallas_call(
        functools.partial(dot_kernel, dims),
        grid=(count,),
        in_specs=[
            pl.BlockSpec(block, lambda i: (at + i, 0) if along == 0 else (0, at + i)),
            pl.BlockSpec(memory_space=pltpu.VMEM),
        ],
        out_specs=pl.BlockSpec((rows, cols), lambda i: (i, 0)),
        out_shape=jax.ShapeDtypeStruct((count * rows, cols), F32),
        compiler_params=pltpu.CompilerParams(vmem_limit_bytes=16 * MIB),
        cost_estimate=pl.CostEstimate(
            flops=2 * count * rows * cols * block[dims[0][0]], bytes_accessed=size, transcendentals=0
        ),
    )(a, b)


def after(first, *rest):
    return lax.optimization_barrier((first,) + rest)


def on_device(activations, out_grad, weight):
    h = lax.axis_index("yl")
    c = lax.axis_index("c")
    tokens, width = out_grad.shape
    own_tokens, features = activations.shape
    rows = weight.shape[1]
    half = rows // 2
    owners = features // rows

    def acts_half(i):
        return [(0, 0, (2 * d + i) * half, 0, d * half, own_tokens, half) for d in range(owners)]

    weight = weight[0]
    split = features // 2
    cuts = half // own_tokens
    pieces = acts_half(1 - h)
    for j in range(cuts):
        pieces.append((1, (1 - h) * half + j * own_tokens, 0, 0, split + j * width, own_tokens, width))
    sent = placed([activations, weight], pieces, (own_tokens, split + cuts * width), pltpu.HBM)
    acts_mine = placed([activations], acts_half(h), (own_tokens, split), pltpu.HBM)
    sent, acts_mine, weight, out_grad = after(sent, acts_mine, weight, out_grad)
    got = swap(sent, "yl")

    w_mine = placed([weight], [(0, h * half, 0, 0, 0, half, width)], (half, width), pltpu.HBM)
    w_own = around([w_mine], "x", 0, {})
    acts_ahead = ring(acts_mine, "z", 1)
    acts_back = ring(acts_mine, "z", -1)
    blocks = {0: [acts_mine], -1: [acts_ahead], 1: [acts_back]}
    acts_ahead, acts_back = ring(acts_ahead, "z", 1), ring(acts_back, "z", -1)
    blocks[-2], blocks[2] = [acts_ahead], [acts_back]
    got = after(acts_ahead, acts_back, w_own[-1][0], w_own[1][0], got)[-1]

    pieces = [(0, 0, split + j * width, j * own_tokens, 0, own_tokens, width) for j in range(cuts)]
    w_other = around([placed([got], pieces, (half, width))], "x", 0, {})
    acts_got = got[:, :split]
    other_ahead, other_back = ring(acts_got, "z", 1), ring(acts_got, "z", -1)
    blocks[0], blocks[-1], blocks[1] = (blocks[k] + [p] for k, p in ((0, acts_got), (-1, other_ahead), (1, other_back)))
    other_ahead, other_back, *held = after(other_ahead, other_back, w_own[-2][0])
    other_ahead, other_back = ring(other_ahead, "z", 1), ring(other_back, "z", -1)
    blocks[-2], blocks[2] = blocks[-2] + [other_ahead], blocks[2] + [other_back]
    ahead, back = jnp.concatenate(blocks[-2]), jnp.concatenate(blocks[2])

    part = tokens // 2
    g_sent = after(acts_got, out_grad)[1]
    g_got = y_ring(placed([g_sent], [(0, c * part, 0, 0, 0, part, width)], (part, width), pltpu.HBM))
    g_got = after(ahead, back, w_other[-1][0], w_other[1][0], g_got)[-1]
    g_rest = swap(g_got, "c")

    ahead, back, *held = after(ahead, back, w_other[-1][0], w_other[1][0])
    ahead, back = ring(ahead, "z", 1), ring(back, "z", -1)
    blocks[-3], blocks[3] = [ahead], [back]
    blocks[-4] = [ring(after(w_other[-2][0], ahead)[-1], "z", 1)]

    arrays, pieces = [], []
    for col, of in ((0, w_own), (width, w_other)):
        for k, (block,) in of.items():
            pieces.append((len(arrays), 0, 0, block_at("x", k) * half, col, half, width))
            arrays.append(block)
    w_all = placed(arrays, pieces, (owners * half, 2 * width))

    count = 2 * own_tokens
    order = [4, -3, 3, -2, 2, -1, 1, 0]
    pieces = []
    for i, k in enumerate(order):
        at = block_at("z", k) * count
        pieces.append((0, at, 0, i * count, 0, count, width))
    other = placed([g_got, g_rest], [(0, 0, 0, c * part, 0, part, width), (1, 0, 0, (1 - c) * part, 0, part, width)], (tokens, width))
    for i, k in enumerate(order):
        at = block_at("z", k) * count
        pieces.append((1, at, 0, i * count, width, count, width))
    g_pair = placed([out_grad, other], pieces, (tokens, 2 * width))

    block = (count, 2 * width)
    shares = [blocked_dot(g_pair, block, at, n, w_all, ((1,), (1,))) for at, n in ((0, 2), (2, len(order) - 2))]

    def of_tokens(got, k):
        i = order.index(k)
        return hop(got, shares[i >= 2], (i - 2 * (i >= 2)) * count, count)

    first = [of_tokens([], k) for k in order[:2]]
    came = scattered(of_tokens, "z", first)

    def finished(of):
        shape = jax.ShapeDtypeStruct((own_tokens, split), BF16)
        at = [(order.index(0) - 2) * count + of * own_tokens, of * own_tokens]
        return call(tokens_kernel, at, came, shares[1], [shape], own_tokens)[0]

    s_got = swap(finished(1 - h), "yl")
    shape = jax.ShapeDtypeStruct((own_tokens, features), BF16)
    input_grad = call(functools.partial(columns_kernel, half), [h], [finished(h), s_got], None, [shape])[0]

    arrays, pieces = [], []
    for k, parts in blocks.items():
        at = order.index(k if k != -4 else 4) * count
        for i, place in enumerate((h, 1 - h)):
            src, row = (i, 0) if len(parts) == 2 else (0, i * own_tokens)
            pieces.append((len(arrays) + src, row, 0, at + place * own_tokens, 0, own_tokens, split))
        arrays += parts
    acts_all = placed(after(*first, *arrays)[2:], pieces, (tokens, split))
    folded = blocked_dot(acts_all, (tokens, half), 0, owners, g_pair, ((0,), (0,)))

    def of_rows(got, k):
        return hop(got, folded, block_at("x", k) * half, half)

    came = scattered(of_rows, "x", [of_rows([], 2), of_rows([], -1)])
    shapes = [jax.ShapeDtypeStruct((half, width), F32), coded_shape(half, width)]
    owned, coded = call(owned_kernel, [block_at("x", 0) * half], came, folded, shapes, half)
    shape = jax.ShapeDtypeStruct((rows, width), F32)
    weight_grad = call(rows_kernel, [h], [owned, swap(coded, "yl")], None, [shape])[0]
    return input_grad, weight_grad[None]


def solution(mesh):
    dp, out, in_ = mesh.devices.shape
    fine = Mesh(mesh.devices.reshape(dp, out // 2, 2, 2, in_ // 2), ("x", "z", "yl", "yh", "c"))
    tokens, split = P(("x", "z", "yl"), ("yh", "c")), P(("yh", "c"), "x", ("z", "yl"))
    return jax.shard_map(
        on_device,
        mesh=fine,
        in_specs=(tokens, P("x", ("z", "yl")), split),
        out_specs=(tokens, split),
        check_vma=False,
    )
```

time: 153 us -> 158 us (1.033); the launches traced: 152 us -> 155 us
  Pallas kernels: 19.7 us -> 41.8 us
  starting transfers between devices: 62.4 us -> 47.3 us
  matrix products: 13.2 us -> 0 us
  local copies, waits for them, and re-layouts: 6.25 us -> 18.6 us
  waiting for transfers between devices: 48.4 us -> 45.8 us
    pallas_call x3 -> x12, Pallas kernels: 6 us -> 26.3 us  [the longest x3 13.9 us: blocked_dot(): pl.pallas_call(functools.partial(dot_kernel, dims), grid=(count,), in_spe...]
    unnamed x44 -> x62, local copies, waits for them, and re-layouts: 1.47 us -> 17.4 us
    ppermute x5 -> x4, waiting for transfers between devices: 18.3 us -> 2.47 us  [swap(): return lax.ppermute(a, axis, [(0, 1), (1, 0)])]
    dot_general x12 -> x0, matrix products: 13.2 us -> none  [dot(): return lax.dot_general(a, b, (dims, ((), ())), preferred_element_type=F32)]
    ppermute x24 -> x27, waiting for transfers between devices: 30.1 us -> 43.4 us  [ring(): return lax.ppermute(a, (axis, 'c'), perm)]
    ppermute x5 -> x4, starting transfers between devices: 17.3 us -> 5.45 us  [swap(): return lax.ppermute(a, axis, [(0, 1), (1, 0)])]
    dynamic_slice x2 -> x0, local copies, waits for them, and re-layouts: 2.64 us -> none  [the longest x1 2.58 us: on_device(): g_sent = lax.dynamic_slice_in_dim(out_grad, c * part, part, 0)]
    ppermute x24 -> x27, starting transfers between devices: 43.6 us -> 41.3 us  [ring(): return lax.ppermute(a, (axis, 'c'), perm)]
  transfers between devices with their start and end apart: 30 -> 32, of which waited for: 9 -> 18; matrix products, arithmetic and copies ran while one was open for 10% -> 3% of each run, Pallas kernels for 12% -> 24%
where the time goes in v1:
time: 158 us; the launch traced here: 155 us
  starting transfers between devices  47.3 us (30%)
  waiting for transfers between devices  45.8 us (29%)
  Pallas kernels  41.8 us (26%)
  local copies, waits for them, and re-layouts  18.6 us (12%)
    ppermute x27, waiting for transfers between devices, ring(): return lax.ppermute(a, (axis, 'c'), perm)  43.4 us
    ppermute x27, starting transfers between devices, ring(): return lax.ppermute(a, (axis, 'c'), perm)  41.3 us
    unnamed x62, local copies, waits for them, and re-layouts  17.4 us
    pallas_call x15, Pallas kernels, call(): pl.pallas_call(kernel, grid_spec=pltpu.PrefetchScalarGridSpec(num_scalar_...  15.4 us
    pallas_call x3, Pallas kernels, blocked_dot(): pl.pallas_call(functools.partial(dot_kernel, dims), grid=(count,), in_spe...  13.9 us
    pallas_call x9, Pallas kernels, placed(): pl.pallas_call(functools.partial(placed_kernel, known), grid_spec=pltpu.P...  12.4 us
    ppermute x4, starting transfers between devices, swap(): return lax.ppermute(a, axis, [(0, 1), (1, 0)])  5.45 us
  transfers between devices with their start and end apart: 32, of which 18 were waited for; matrix products, arithmetic and copies ran while one was open for 3% of the time, Pallas kernels for 24%

profile of v1, /device:TPU:4, one launch (start us, length us, event | category | flops | bytes accessed | tf_op | source)
XLA Modules:
  0.0 154.9 jit_solution(124557551035281444)
XLA Ops:
  0.7 1.2 copy-done.6
  1.9 1.4 shard_map.51.refs_0_
  3.4 1.1 copy-done.4
  5.5 1.5 shard_map.50
  7.0 1.7 %collective-permute-start.6 = (bf16[128,2304]{1,0:T(8,128)(2,1)}, bf16[128,2304]{1,0:T(8,128)(2,1)S(1)}, u32[]{:S(2)}, u32[]{:S(2)}) collective-permute-start(bf16[128,2304]{1,0:T(8,128)(2,1)} %shard_map.50), channel_id=1, source_target_pairs={{0,4},{4,0},{1,5},{5,1},{2,6},{6,2},{3,7},{7,3},{8,12},{12,8},{9,1... | collective-permute-start | bytes 1769480 | tf_op jit(solution)/shard_map/ppermute | solution.py:225
  8.7 1.9 %collective-permute-start = (bf16[128,1024]{1,0:T(8,128)(2,1)}, bf16[128,1024]{1,0:T(8,128)(2,1)}, u32[]{:S(2)}, u32[]{:S(2)}) collective-permute-start(bf16[128,1024]{1,0:T(8,128)(2,1)} %shard_map.51.refs_0_), channel_id=1, source_target_pairs={{0,8},{1,57},{8,16},{9,1},{16,24},{17,9},{24,32},{25,17},{32,40},{... | collective-permute-start | bytes 786440 | tf_op jit(solution)/shard_map/ppermute | solution.py:240
  10.6 3.9 %collective-permute-start.2 = (bf16[128,1024]{1,0:T(8,128)(2,1)}, bf16[128,1024]{1,0:T(8,128)(2,1)}, u32[]{:S(2)}, u32[]{:S(2)}) collective-permute-start(bf16[128,1024]{1,0:T(8,128)(2,1)} %shard_map.51.refs_0_), channel_id=1, source_target_pairs={{0,56},{1,9},{8,0},{9,17},{16,8},{17,25},{24,16},{25,33},{32,24},{... | collective-permute-start | bytes 786440 | tf_op jit(solution)/shard_map/ppermute | solution.py:240
  14.6 1.1 copy-done.5
  15.8 1.3 collective-permute-start.4
  17.9 2.6 %collective-permute-done.refs_2_ = bf16[128,1024]{1,0:T(8,128)(2,1)} collective-permute-done((bf16[128,1024]{1,0:T(8,128)(2,1)}, bf16[128,1024]{1,0:T(8,128)(2,1)}, u32[]{:S(2)}, u32[]{:S(2)}) %collective-permute-start) | collective-permute-done | bytes 262176 | tf_op jit(solution)/shard_map/ppermute | solution.py:240
  20.4 3.4 %collective-permute-start.3 = (bf16[128,1024]{1,0:T(8,128)(2,1)}, bf16[128,1024]{1,0:T(8,128)(2,1)}, u32[]{:S(2)}, u32[]{:S(2)}) collective-permute-start(bf16[128,1024]{1,0:T(8,128)(2,1)} %collective-permute-done.2.refs_4_), channel_id=1, source_target_pairs={{0,56},{1,9},{8,0},{9,17},{16,8},{17,25},{24,16},{25,33},{32,24},{... | collective-permute-start | bytes 786440 | tf_op jit(solution)/shard_map/ppermute | solution.py:240
  23.8 1.2 collective-permute-done.4.refs_1_
  25.1 5.2 %collective-permute-done.1.refs_6_ = bf16[128,1024]{1,0:T(8,128)(2,1)} collective-permute-done((bf16[128,1024]{1,0:T(8,128)(2,1)}, bf16[128,1024]{1,0:T(8,128)(2,1)}, u32[]{:S(2)}, u32[]{:S(2)}) %collective-permute-start.1) | collective-permute-done | bytes 262176 | tf_op jit(solution)/shard_map/ppermute | solution.py:240
  31.0 1.2 collective-permute-start.9
  32.2 3.2 %collective-permute-start.8 = (bf16[128,1024]{1,0:T(8,128)(2,1)S(1)}, bf16[128,1024]{1,0:T(8,128)(2,1)S(1)}, u32[]{:S(2)}, u32[]{:S(2)}) collective-permute-start(bf16[128,1024]{1,0:T(8,128)(2,1)S(1)} %slice.3.refs_1_), channel_id=1, source_target_pairs={{0,56},{1,9},{8,0},{9,17},{16,8},{17,25},{24,16},{25,33},{32,24},{... | collective-permute-start | bytes 786440 | tf_op jit(solution)/shard_map/ppermute | solution.py:240
  35.5 2.9 %collective-permute-done.9.refs_3_ = bf16[256,640]{1,0:T(8,128)(2,1)S(1)} collective-permute-done((bf16[256,640]{1,0:T(8,128)(2,1)}, bf16[256,640]{1,0:T(8,128)(2,1)S(1)}, u32[]{:S(2)}, u32[]{:S(2)}) %collective-permute-start.9) | collective-permute-done | bytes 327712 | tf_op jit(solution)/shard_map/ppermute | solution.py:240
  39.0 3.4 %collective-permute-done.7.refs_3_ = bf16[128,1024]{1,0:T(8,128)(2,1)S(1)} collective-permute-done((bf16[128,1024]{1,0:T(8,128)(2,1)S(1)}, bf16[128,1024]{1,0:T(8,128)(2,1)S(1)}, u32[]{:S(2)}, u32[]{:S(2)}) %collective-permute-start.7) | collective-permute-done | bytes 262176 | tf_op jit(solution)/shard_map/ppermute | solution.py:240
  43.0 1.5 collective-permute-start.10
  44.6 1.7 %constant_dynamic-update-slice_fusion.3 = bf16[256,1024]{1,0:T(8,128)(2,1)} fusion(bf16[128,1024]{1,0:T(8,128)(2,1)} %collective-permute-done.3.refs_8_), kind=kLoop, calls=%fused_computation.3 | loop fusion | bytes 524288
  46.2 1.1 copy-done.9
  48.0 2.0 %collective-permute-start.13 = (bf16[256,640]{1,0:T(8,128)(2,1)S(1)}, bf16[256,640]{1,0:T(8,128)(2,1)S(1)}, u32[]{:S(2)}, u32[]{:S(2)}) collective-permute-start(bf16[256,640]{1,0:T(8,128)(2,1)S(1)} %shard_map.53.refs_4_), channel_id=1, source_target_pairs={{0,192},{1,65},{64,0},{65,129},{128,64},{129,193},{192,128},{193,1... | collective-permute-start | bytes 983048 | tf_op jit(solution)/shard_map/ppermute | solution.py:240
  52.3 6.1 %collective-permute-done.12.refs_5_ = bf16[256,640]{1,0:T(8,128)(2,1)S(1)} collective-permute-done((bf16[256,640]{1,0:T(8,128)(2,1)S(1)}, bf16[256,640]{1,0:T(8,128)(2,1)S(1)}, u32[]{:S(2)}, u32[]{:S(2)}) %collective-permute-start.12) | collective-permute-done | bytes 327712 | tf_op jit(solution)/shard_map/ppermute | solution.py:240
  59.4 1.8 %collective-permute-start.16 = (bf16[256,640]{1,0:T(8,128)(2,1)S(1)}, bf16[256,640]{1,0:T(8,128)(2,1)S(1)}, u32[]{:S(2)}, u32[]{:S(2)}) collective-permute-start(bf16[256,640]{1,0:T(8,128)(2,1)S(1)} %collective-permute-done.12.refs_5_), channel_id=1, source_target_pairs={{0,64},{1,193},{64,128},{65,1},{128,192},{129,65},{192,0},{193,129... | collective-permute-start | bytes 983048 | tf_op jit(solution)/shard_map/ppermute | solution.py:240
  61.9 3.1 %collective-permute-start.26 = (bf16[256,1024]{1,0:T(8,128)(2,1)}, bf16[256,1024]{1,0:T(8,128)(2,1)}, u32[]{:S(2)}, u32[]{:S(2)}) collective-permute-start(bf16[256,1024]{1,0:T(8,128)(2,1)} %constant_dynamic-update-slice_fusion.2), channel_id=1, source_target_pairs={{0,56},{1,9},{8,0},{9,17},{16,8},{17,25},{24,16},{25,33},{32,24},{... | collective-permute-start | bytes 1572872 | tf_op jit(solution)/shard_map/ppermute | solution.py:240
  65.0 1.5 collective-permute-done.16.refs_7_
  67.3 6.9 %collective-permute-done.25.refs_10_ = bf16[256,1024]{1,0:T(8,128)(2,1)} collective-permute-done((bf16[256,1024]{1,0:T(8,128)(2,1)S(1)}, bf16[256,1024]{1,0:T(8,128)(2,1)}, u32[]{:S(2)}, u32[]{:S(2)}) %collective-permute-start.25) | collective-permute-done | bytes 524320 | tf_op jit(solution)/shard_map/ppermute | solution.py:240
  78.4 1.9 %shard_map.57.b_ref = bf16[1024,1280]{1,0:T(8,128)(2,1)S(1)} custom-call(s32[8]{0:T(128)S(1)} %stack.201.at_ref, bf16[256,640]{1,0:T(8,128)(2,1)S(1)} %shard_map.52.refs_0_, bf16[256,640]{1,0:T(8,128)(2,1)} %collective-permute-done.4.refs_1_, bf16[256,640]{1,0:T(8,128)(2,1)} %collective-permute-done.5.refs_2_, bf16[256,640]{1,0:T(8,128)(2,1)S(1)} %copy-done.17, ...), custom_call_target="tpu_custom_call" | custom-call | bytes 5242880 | tf_op jit(solution)/shard_map/pallas_call | solution.py:200
  80.4 2.8 %shard_map.55.refs_1_ = bf16[2048,640]{1,0:T(8,128)(2,1)S(1)} custom-call(s32[2]{0:T(128)S(1)} %pad_add_fusion.2.at_ref, bf16[1024,640]{1,0:T(8,128)(2,1)} %collective-permute-done.14.refs_0_, bf16[1024,640]{1,0:T(8,128)(2,1)} %collective-permute-done.15.refs_1_), custom_call_target="tpu_custom_call" | custom-call | bytes 5242880 | tf_op jit(solution)/shard_map/pallas_call | solution.py:200
  83.2 1.2 shard_map.56.a_ref.b_ref
  84.4 1.8 %shard_map.58.refs_0_ = f32[512,1024]{1,0:T(8,128)S(1)} custom-call(bf16[2048,1280]{1,0:T(8,128)(2,1)S(1)} %shard_map.56.a_ref.b_ref, bf16[1024,1280]{1,0:T(8,128)(2,1)S(1)} %shard_map.57.b_ref), custom_call_target="tpu_custom_call" | custom-call | flops 1342177280 | bytes 6029312 | tf_op jit(solution)/shard_map/pallas_call | solution.py:283
  86.7 1.4 shard_map.59
  89.1 3.3 %collective-permute-start.21 = (bf16[2064,128]{1,0:T(8,128)(2,1)S(1)}, bf16[2064,128]{1,0:T(8,128)(2,1)S(1)}, u32[]{:S(2)}, u32[]{:S(2)}) collective-permute-start(bf16[2064,128]{1,0:T(8,128)(2,1)S(1)} %shard_map.64), channel_id=1, source_target_pairs={{0,56},{1,9},{8,0},{9,17},{16,8},{17,25},{24,16},{25,33},{32,24},{... | collective-permute-start | bytes 1585160 | tf_op jit(solution)/shard_map/ppermute | solution.py:240
  94.3 2.8 %shard_map.70.a_ref = bf16[2048,1024]{1,0:T(8,128)(2,1)S(1)} custom-call(s32[16]{0:T(128)S(1)} %stack.218.at_ref, bf16[128,1024]{1,0:T(8,128)(2,1)} %shard_map.51.refs_0_, bf16[128,1024]{1,0:T(8,128)(2,1)S(1)} %copy-done.11, bf16[128,1024]{1,0:T(8,128)(2,1)} %collective-permute-done.refs_2_, bf16[128,1024]{1,0:T(8,128)(2,1)S(1)} %copy-done.25, ...), custom_call_target="tpu_custom_call" | custom-call | bytes 8388608 | tf_op jit(solution)/shard_map/pallas_call | solution.py:200
  97.1 5.3 %shard_map.60.refs_1_.own_ref = f32[1536,1024]{1,0:T(8,128)S(1)} custom-call(bf16[2048,1280]{1,0:T(8,128)(2,1)S(1)} %bitcast.44, bf16[1024,1280]{1,0:T(8,128)(2,1)S(1)} %copy-done.3), custom_call_target="tpu_custom_call" | custom-call | flops 4026531840 | bytes 12845056 | tf_op jit(solution)/shard_map/pallas_call | solution.py:283
  103.5 6.9 %shard_map.71.refs_0_.refs_1_.own_ref = f32[1024,1280]{1,0:T(8,128)S(1)} custom-call(bf16[2048,1024]{1,0:T(8,128)(2,1)S(1)} %shard_map.70.a_ref, bf16[2048,1280]{1,0:T(8,128)(2,1)S(1)} %bitcast.44), custom_call_target="tpu_custom_call" | custom-call | flops 5368709120 | bytes 14680064 | tf_op jit(solution)/shard_map/pallas_call | solution.py:283
  111.1 1.5 collective-permute-start.28
  113.6 3.0 %collective-permute-start.22 = (bf16[2064,128]{1,0:T(8,128)(2,1)S(1)}, bf16[2064,128]{1,0:T(8,128)(2,1)S(1)}, u32[]{:S(2)}, u32[]{:S(2)}) collective-permute-start(bf16[2064,128]{1,0:T(8,128)(2,1)S(1)} %shard_map.65), channel_id=1, source_target_pairs={{0,56},{1,9},{8,0},{9,17},{16,8},{17,25},{24,16},{25,33},{32,24},{... | collective-permute-start | bytes 1585160 | tf_op jit(solution)/shard_map/ppermute | solution.py:240
  119.7 6.0 %collective-permute-done.28.refs_0_ = bf16[2576,128]{1,0:T(8,128)(2,1)S(1)} collective-permute-done((bf16[2576,128]{1,0:T(8,128)(2,1)S(1)}, bf16[2576,128]{1,0:T(8,128)(2,1)S(1)}, u32[]{:S(2)}, u32[]{:S(2)}) %collective-permute-start.28) | collective-permute-done | bytes 659488 | tf_op jit(solution)/shard_map/ppermute | solution.py:240
  125.7 1.2 shard_map.73
  126.9 2.6 %collective-permute-start.29 = (bf16[2576,128]{1,0:T(8,128)(2,1)S(1)}, bf16[2576,128]{1,0:T(8,128)(2,1)S(1)}, u32[]{:S(2)}, u32[]{:S(2)}) collective-permute-start(bf16[2576,128]{1,0:T(8,128)(2,1)S(1)} %shard_map.73), channel_id=1, source_target_pairs={{0,64},{1,193},{64,128},{65,1},{128,192},{129,65},{192,0},{193,129... | collective-permute-start | bytes 1978376 | tf_op jit(solution)/shard_map/ppermute | solution.py:240
  130.5 4.5 %collective-permute-start.23 = (bf16[2064,128]{1,0:T(8,128)(2,1)S(1)}, bf16[2064,128]{1,0:T(8,128)(2,1)S(1)}, u32[]{:S(2)}, u32[]{:S(2)}) collective-permute-start(bf16[2064,128]{1,0:T(8,128)(2,1)S(1)} %shard_map.66), channel_id=1, source_target_pairs={{0,56},{1,9},{8,0},{9,17},{16,8},{17,25},{24,16},{25,33},{32,24},{... | collective-permute-start | bytes 1585160 | tf_op jit(solution)/shard_map/ppermute | solution.py:240
  136.2 1.4 collective-permute-done.29.f_ref
  137.6 1.4 shard_map.75
  139.0 2.2 %collective-permute-start.31 = (bf16[1296,128]{1,0:T(8,128)(2,1)S(1)}, bf16[1296,128]{1,0:T(8,128)(2,1)S(1)}, u32[]{:S(2)}, u32[]{:S(2)}) collective-permute-start(bf16[1296,128]{1,0:T(8,128)(2,1)S(1)} %get-tuple-element.55), channel_id=1, source_target_pairs={{0,4},{4,0},{1,5},{5,1},{2,6},{6,2},{3,7},{7,3},{8,12},{12,8},{9,1... | collective-permute-start | bytes 995336 | tf_op jit(solution)/shard_map/ppermute | solution.py:225
  141.8 4.8 %collective-permute-done.20.f_ref = bf16[2064,128]{1,0:T(8,128)(2,1)S(1)} collective-permute-done((bf16[2064,128]{1,0:T(8,128)(2,1)S(1)}, bf16[2064,128]{1,0:T(8,128)(2,1)S(1)}, u32[]{:S(2)}, u32[]{:S(2)}) %collective-permute-start.20) | collective-permute-done | bytes 528416 | tf_op jit(solution)/shard_map/ppermute | solution.py:240
  147.6 1.4 collective-permute-start.24
  150.0 1.4 shard_map.76
  152.5 1.6 %collective-permute-done.24.got_ref = bf16[128,1024]{1,0:T(8,128)(2,1)S(1)} collective-permute-done((bf16[128,1024]{1,0:T(8,128)(2,1)S(1)}, bf16[128,1024]{1,0:T(8,128)(2,1)S(1)}, u32[]{:S(2)}, u32[]{:S(2)}) %collective-permute-start.24) | collective-permute-done | bytes 262176 | tf_op jit(solution)/shard_map/ppermute | solution.py:225
  (118 shorter events, 29.5 us)
Async XLA Ops:
  0.6 29.7 %copy-start.1 = (bf16[2048,640]{1,0:T(8,128)(2,1)S(1)}, bf16[2048,640]{1,0:T(8,128)(2,1)}, u32[]{:S(2)}) copy-start(bf16[2048,640]{1,0:T(8,128)(2,1)} %refs_0_.5) | copy-start | bytes 7864324
  0.7 1.2 copy-start.6
  7.0 23.3 %collective-permute-start.6 = (bf16[128,2304]{1,0:T(8,128)(2,1)}, bf16[128,2304]{1,0:T(8,128)(2,1)S(1)}, u32[]{:S(2)}, u32[]{:S(2)}) collective-permute-start(bf16[128,2304]{1,0:T(8,128)(2,1)} %shard_map.50), channel_id=1, source_target_pairs={{0,4},{4,0},{1,5},{5,1},{2,6},{6,2},{3,7},{7,3},{8,12},{12,8},{9,1... | collective-permute-start | bytes 1769480 | tf_op jit(solution)/shard_map/ppermute | solution.py:225
  8.7 11.7 %collective-permute-start = (bf16[128,1024]{1,0:T(8,128)(2,1)}, bf16[128,1024]{1,0:T(8,128)(2,1)}, u32[]{:S(2)}, u32[]{:S(2)}) collective-permute-start(bf16[128,1024]{1,0:T(8,128)(2,1)} %shard_map.51.refs_0_), channel_id=1, source_target_pairs={{0,8},{1,57},{8,16},{9,1},{16,24},{17,9},{24,32},{25,17},{32,40},{... | collective-permute-start | bytes 786440 | tf_op jit(solution)/shard_map/ppermute | solution.py:240
  10.6 9.8 %collective-permute-start.2 = (bf16[128,1024]{1,0:T(8,128)(2,1)}, bf16[128,1024]{1,0:T(8,128)(2,1)}, u32[]{:S(2)}, u32[]{:S(2)}) collective-permute-start(bf16[128,1024]{1,0:T(8,128)(2,1)} %shard_map.51.refs_0_), channel_id=1, source_target_pairs={{0,56},{1,9},{8,0},{9,17},{16,8},{17,25},{24,16},{25,33},{32,24},{... | collective-permute-start | bytes 786440 | tf_op jit(solution)/shard_map/ppermute | solution.py:240
  15.8 9.3 %collective-permute-start.4 = (bf16[256,640]{1,0:T(8,128)(2,1)S(1)}, bf16[256,640]{1,0:T(8,128)(2,1)}, u32[]{:S(2)}, u32[]{:S(2)}) collective-permute-start(bf16[256,640]{1,0:T(8,128)(2,1)S(1)} %shard_map.52.refs_0_), channel_id=1, source_target_pairs={{0,64},{1,193},{64,128},{65,1},{128,192},{129,65},{192,0},{193,129... | collective-permute-start | bytes 983048 | tf_op jit(solution)/shard_map/ppermute | solution.py:240
  17.0 8.1 %collective-permute-start.5 = (bf16[256,640]{1,0:T(8,128)(2,1)S(1)}, bf16[256,640]{1,0:T(8,128)(2,1)}, u32[]{:S(2)}, u32[]{:S(2)}) collective-permute-start(bf16[256,640]{1,0:T(8,128)(2,1)S(1)} %shard_map.52.refs_0_), channel_id=1, source_target_pairs={{0,192},{1,65},{64,0},{65,129},{128,64},{129,193},{192,128},{193,1... | collective-permute-start | bytes 983048 | tf_op jit(solution)/shard_map/ppermute | solution.py:240
  20.4 9.9 %collective-permute-start.1 = (bf16[128,1024]{1,0:T(8,128)(2,1)}, bf16[128,1024]{1,0:T(8,128)(2,1)}, u32[]{:S(2)}, u32[]{:S(2)}) collective-permute-start(bf16[128,1024]{1,0:T(8,128)(2,1)} %collective-permute-done.refs_2_), channel_id=1, source_target_pairs={{0,8},{1,57},{8,16},{9,1},{16,24},{17,9},{24,32},{25,17},{32,40},{... | collective-permute-start | bytes 786440 | tf_op jit(solution)/shard_map/ppermute | solution.py:240
  20.4 9.9 %collective-permute-start.3 = (bf16[128,1024]{1,0:T(8,128)(2,1)}, bf16[128,1024]{1,0:T(8,128)(2,1)}, u32[]{:S(2)}, u32[]{:S(2)}) collective-permute-start(bf16[128,1024]{1,0:T(8,128)(2,1)} %collective-permute-done.2.refs_4_), channel_id=1, source_target_pairs={{0,56},{1,9},{8,0},{9,17},{16,8},{17,25},{24,16},{25,33},{32,24},{... | collective-permute-start | bytes 786440 | tf_op jit(solution)/shard_map/ppermute | solution.py:240
  30.3 15.9 %copy-start.8 = (bf16[128,2304]{1,0:T(8,128)(2,1)}, bf16[128,2304]{1,0:T(8,128)(2,1)S(1)}, u32[]{:S(2)}) copy-start(bf16[128,2304]{1,0:T(8,128)(2,1)S(1)} %collective-permute-done.6.refs_0_) | copy-start | bytes 1769476
  30.4 17.5 %copy-start.10 = (bf16[128,1024]{1,0:T(8,128)(2,1)}, bf16[128,1024]{1,0:T(8,128)(2,1)S(1)}, u32[]{:S(2)}) copy-start(bf16[128,1024]{1,0:T(8,128)(2,1)S(1)} %slice.3.refs_1_) | copy-start | bytes 786436
  30.5 28.8 %collective-permute-start.14 = (bf16[1024,640]{1,0:T(8,128)(2,1)S(1)}, bf16[1024,640]{1,0:T(8,128)(2,1)}, u32[]{:S(2)}, u32[]{:S(2)}) collective-permute-start(bf16[1024,640]{1,0:T(8,128)(2,1)S(1)} %shard_map.54), channel_id=1, source_target_pairs={{0,4},{1,7},{4,2},{5,1},{2,6},{3,5},{6,0},{7,3},{8,12},{9,15},{12,... | collective-permute-start | bytes 3932168 | tf_op jit(solution)/shard_map/ppermute | solution.py:234
  31.0 7.3 %collective-permute-start.9 = (bf16[256,640]{1,0:T(8,128)(2,1)}, bf16[256,640]{1,0:T(8,128)(2,1)S(1)}, u32[]{:S(2)}, u32[]{:S(2)}) collective-permute-start(bf16[256,640]{1,0:T(8,128)(2,1)} %collective-permute-done.4.refs_1_), channel_id=1, source_target_pairs={{0,64},{1,193},{64,128},{65,1},{128,192},{129,65},{192,0},{193,129... | collective-permute-start | bytes 983048 | tf_op jit(solution)/shard_map/ppermute | solution.py:240
  32.2 10.2 %collective-permute-start.7 = (bf16[128,1024]{1,0:T(8,128)(2,1)S(1)}, bf16[128,1024]{1,0:T(8,128)(2,1)S(1)}, u32[]{:S(2)}, u32[]{:S(2)}) collective-permute-start(bf16[128,1024]{1,0:T(8,128)(2,1)S(1)} %slice.3.refs_1_), channel_id=1, source_target_pairs={{0,8},{1,57},{8,16},{9,1},{16,24},{17,9},{24,32},{25,17},{32,40},{... | collective-permute-start | bytes 786440 | tf_op jit(solution)/shard_map/ppermute | solution.py:240
  32.2 10.2 %collective-permute-start.8 = (bf16[128,1024]{1,0:T(8,128)(2,1)S(1)}, bf16[128,1024]{1,0:T(8,128)(2,1)S(1)}, u32[]{:S(2)}, u32[]{:S(2)}) collective-permute-start(bf16[128,1024]{1,0:T(8,128)(2,1)S(1)} %slice.3.refs_1_), channel_id=1, source_target_pairs={{0,56},{1,9},{8,0},{9,17},{16,8},{17,25},{24,16},{25,33},{32,24},{... | collective-permute-start | bytes 786440 | tf_op jit(solution)/shard_map/ppermute | solution.py:240
  42.5 24.1 %copy-start.24 = (bf16[128,1024]{1,0:T(8,128)(2,1)}, bf16[128,1024]{1,0:T(8,128)(2,1)S(1)}, u32[]{:S(2)}) copy-start(bf16[128,1024]{1,0:T(8,128)(2,1)S(1)} %collective-permute-done.7.refs_3_) | copy-start | bytes 786436
  42.5 31.8 %copy-start.26 = (bf16[128,1024]{1,0:T(8,128)(2,1)}, bf16[128,1024]{1,0:T(8,128)(2,1)S(1)}, u32[]{:S(2)}) copy-start(bf16[128,1024]{1,0:T(8,128)(2,1)S(1)} %collective-permute-done.8.refs_5_) | copy-start | bytes 786436
  42.5 8.6 %collective-permute-start.11 = (bf16[128,1024]{1,0:T(8,128)(2,1)S(1)}, bf16[128,1024]{1,0:T(8,128)(2,1)S(1)}, u32[]{:S(2)}, u32[]{:S(2)}) collective-permute-start(bf16[128,1024]{1,0:T(8,128)(2,1)S(1)} %collective-permute-done.8.refs_5_), channel_id=1, source_target_pairs={{0,56},{1,9},{8,0},{9,17},{16,8},{17,25},{24,16},{25,33},{32,24},{... | collective-permute-start | bytes 786440 | tf_op jit(solution)/shard_map/ppermute | solution.py:240
  43.0 9.2 %collective-permute-start.10 = (bf16[128,1024]{1,0:T(8,128)(2,1)S(1)}, bf16[128,1024]{1,0:T(8,128)(2,1)S(1)}, u32[]{:S(2)}, u32[]{:S(2)}) collective-permute-start(bf16[128,1024]{1,0:T(8,128)(2,1)S(1)} %collective-permute-done.7.refs_3_), channel_id=1, source_target_pairs={{0,8},{1,57},{8,16},{9,1},{16,24},{17,9},{24,32},{25,17},{32,40},{... | collective-permute-start | bytes 786440 | tf_op jit(solution)/shard_map/ppermute | solution.py:240
  47.9 10.4 %collective-permute-start.12 = (bf16[256,640]{1,0:T(8,128)(2,1)S(1)}, bf16[256,640]{1,0:T(8,128)(2,1)S(1)}, u32[]{:S(2)}, u32[]{:S(2)}) collective-permute-start(bf16[256,640]{1,0:T(8,128)(2,1)S(1)} %shard_map.53.refs_4_), channel_id=1, source_target_pairs={{0,64},{1,193},{64,128},{65,1},{128,192},{129,65},{192,0},{193,129... | collective-permute-start | bytes 983048 | tf_op jit(solution)/shard_map/ppermute | solution.py:240
  48.0 10.5 %collective-permute-start.13 = (bf16[256,640]{1,0:T(8,128)(2,1)S(1)}, bf16[256,640]{1,0:T(8,128)(2,1)S(1)}, u32[]{:S(2)}, u32[]{:S(2)}) collective-permute-start(bf16[256,640]{1,0:T(8,128)(2,1)S(1)} %shard_map.53.refs_4_), channel_id=1, source_target_pairs={{0,192},{1,65},{64,0},{65,129},{128,64},{129,193},{192,128},{193,1... | collective-permute-start | bytes 983048 | tf_op jit(solution)/shard_map/ppermute | solution.py:240
  51.1 8.2 %copy-start.12 = (bf16[128,1024]{1,0:T(8,128)(2,1)}, bf16[128,1024]{1,0:T(8,128)(2,1)S(1)}, u32[]{:S(2)}) copy-start(bf16[128,1024]{1,0:T(8,128)(2,1)S(1)} %collective-permute-done.11.refs_9_) | copy-start | bytes 786436
  52.3 7.2 %copy-start.14 = (bf16[128,1024]{1,0:T(8,128)(2,1)}, bf16[128,1024]{1,0:T(8,128)(2,1)S(1)}, u32[]{:S(2)}) copy-start(bf16[128,1024]{1,0:T(8,128)(2,1)S(1)} %collective-permute-done.10.refs_7_) | copy-start | bytes 786436
  59.3 21.1 %collective-permute-start.15 = (bf16[1024,640]{1,0:T(8,128)(2,1)}, bf16[1024,640]{1,0:T(8,128)(2,1)}, u32[]{:S(2)}, u32[]{:S(2)}) collective-permute-start(bf16[1024,640]{1,0:T(8,128)(2,1)} %collective-permute-done.14.refs_0_), channel_id=1, source_target_pairs={{0,1},{1,0},{2,3},{3,2},{4,5},{5,4},{6,7},{7,6},{8,9},{9,8},{10,11... | collective-permute-start | bytes 3932168 | tf_op jit(solution)/shard_map/ppermute | solution.py:225
  59.4 14.8 %collective-permute-start.25 = (bf16[256,1024]{1,0:T(8,128)(2,1)S(1)}, bf16[256,1024]{1,0:T(8,128)(2,1)}, u32[]{:S(2)}, u32[]{:S(2)}) collective-permute-start(bf16[256,1024]{1,0:T(8,128)(2,1)S(1)} %constant_dynamic-update-slice_fusion), channel_id=1, source_target_pairs={{0,8},{1,57},{8,16},{9,1},{16,24},{17,9},{24,32},{25,17},{32,40},{... | collective-permute-start | bytes 1572872 | tf_op jit(solution)/shard_map/ppermute | solution.py:240
  59.4 7.1 %collective-permute-start.16 = (bf16[256,640]{1,0:T(8,128)(2,1)S(1)}, bf16[256,640]{1,0:T(8,128)(2,1)S(1)}, u32[]{:S(2)}, u32[]{:S(2)}) collective-permute-start(bf16[256,640]{1,0:T(8,128)(2,1)S(1)} %collective-permute-done.12.refs_5_), channel_id=1, source_target_pairs={{0,64},{1,193},{64,128},{65,1},{128,192},{129,65},{192,0},{193,129... | collective-permute-start | bytes 983048 | tf_op jit(solution)/shard_map/ppermute | solution.py:240
  61.9 30.5 %collective-permute-start.26 = (bf16[256,1024]{1,0:T(8,128)(2,1)}, bf16[256,1024]{1,0:T(8,128)(2,1)}, u32[]{:S(2)}, u32[]{:S(2)}) collective-permute-start(bf16[256,1024]{1,0:T(8,128)(2,1)} %constant_dynamic-update-slice_fusion.2), channel_id=1, source_target_pairs={{0,56},{1,9},{8,0},{9,17},{16,8},{17,25},{24,16},{25,33},{32,24},{... | collective-permute-start | bytes 1572872 | tf_op jit(solution)/shard_map/ppermute | solution.py:240
  74.2 18.1 %collective-permute-start.27 = (bf16[256,1024]{1,0:T(8,128)(2,1)}, bf16[256,1024]{1,0:T(8,128)(2,1)}, u32[]{:S(2)}, u32[]{:S(2)}) collective-permute-start(bf16[256,1024]{1,0:T(8,128)(2,1)} %collective-permute-done.25.refs_10_), channel_id=1, source_target_pairs={{0,8},{1,57},{8,16},{9,1},{16,24},{17,9},{24,32},{25,17},{32,40},{... | collective-permute-start | bytes 1572872 | tf_op jit(solution)/shard_map/ppermute | solution.py:240
  80.3 4.0 %copy-start.2 = (bf16[1024,1280]{1,0:T(8,128)(2,1)}, bf16[1024,1280]{1,0:T(8,128)(2,1)S(1)}, u32[]{:S(2)}) copy-start(bf16[1024,1280]{1,0:T(8,128)(2,1)S(1)} %shard_map.57.b_ref) | copy-start | bytes 7864324
  84.4 2.3 %copy-start = (bf16[2048,1280]{1,0:T(8,128)(2,1)}, bf16[2048,1280]{1,0:T(8,128)(2,1)S(1)}, u32[]{:S(2)}) copy-start(bf16[2048,1280]{1,0:T(8,128)(2,1)S(1)} %shard_map.56.a_ref.b_ref) | copy-start | bytes 15728644
  86.7 5.6 %copy-start.11 = (bf16[128,1024]{1,0:T(8,128)(2,1)S(1)}, bf16[128,1024]{1,0:T(8,128)(2,1)}, u32[]{:S(2)}) copy-start(bf16[128,1024]{1,0:T(8,128)(2,1)} %copy-done.10) | copy-start | bytes 786436
  86.7 5.6 %copy-start.13 = (bf16[128,1024]{1,0:T(8,128)(2,1)S(1)}, bf16[128,1024]{1,0:T(8,128)(2,1)}, u32[]{:S(2)}) copy-start(bf16[128,1024]{1,0:T(8,128)(2,1)} %copy-done.12) | copy-start | bytes 786436
  86.7 5.6 %copy-start.15 = (bf16[128,1024]{1,0:T(8,128)(2,1)S(1)}, bf16[128,1024]{1,0:T(8,128)(2,1)}, u32[]{:S(2)}) copy-start(bf16[128,1024]{1,0:T(8,128)(2,1)} %copy-done.14) | copy-start | bytes 786436
  88.2 14.2 %collective-permute-start.17 = (bf16[2064,128]{1,0:T(8,128)(2,1)}, bf16[2064,128]{1,0:T(8,128)(2,1)S(1)}, u32[]{:S(2)}, u32[]{:S(2)}) collective-permute-start(bf16[2064,128]{1,0:T(8,128)(2,1)} %shard_map.59), channel_id=1, source_target_pairs={{0,8},{1,57},{8,16},{9,1},{16,24},{17,9},{24,32},{25,17},{32,40},{... | collective-permute-start | bytes 1585160 | tf_op jit(solution)/shard_map/ppermute | solution.py:240
  88.4 8.7 %slice-start = ((s8[5242880]{0:T(1024)(128)(4,1)}), s8[4194304]{0:T(1024)(128)(4,1)S(1)}, s32[]{:S(2)}) async-start(s8[5242880]{0:T(1024)(128)(4,1)} %bitcast.43), calls=%async_computation | async-start | bytes 8388608
  89.0 8.1 %slice-start.1 = ((s8[5242880]{0:T(1024)(128)(4,1)}), s8[1048576]{0:T(1024)(128)(4,1)S(1)}, s32[]{:S(2)}) async-start(s8[5242880]{0:T(1024)(128)(4,1)} %bitcast.43), calls=%async_computation.1 | async-start | bytes 2097152
  89.0 8.1 %copy-start.3 = (bf16[1024,1280]{1,0:T(8,128)(2,1)S(1)}, bf16[1024,1280]{1,0:T(8,128)(2,1)}, u32[]{:S(2)}) copy-start(bf16[1024,1280]{1,0:T(8,128)(2,1)} %copy-done.2) | copy-start | bytes 7864324
  89.1 23.6 %collective-permute-start.21 = (bf16[2064,128]{1,0:T(8,128)(2,1)S(1)}, bf16[2064,128]{1,0:T(8,128)(2,1)S(1)}, u32[]{:S(2)}, u32[]{:S(2)}) collective-permute-start(bf16[2064,128]{1,0:T(8,128)(2,1)S(1)} %shard_map.64), channel_id=1, source_target_pairs={{0,56},{1,9},{8,0},{9,17},{16,8},{17,25},{24,16},{25,33},{32,24},{... | collective-permute-start | bytes 1585160 | tf_op jit(solution)/shard_map/ppermute | solution.py:240
  103.4 13.2 %collective-permute-start.18 = (bf16[2064,128]{1,0:T(8,128)(2,1)S(1)}, bf16[2064,128]{1,0:T(8,128)(2,1)S(1)}, u32[]{:S(2)}, u32[]{:S(2)}) collective-permute-start(bf16[2064,128]{1,0:T(8,128)(2,1)S(1)} %shard_map.61), channel_id=1, source_target_pairs={{0,8},{1,57},{8,16},{9,1},{16,24},{17,9},{24,32},{25,17},{32,40},{... | collective-permute-start | bytes 1585160 | tf_op jit(solution)/shard_map/ppermute | solution.py:240
  111.1 14.6 %collective-permute-start.28 = (bf16[2576,128]{1,0:T(8,128)(2,1)S(1)}, bf16[2576,128]{1,0:T(8,128)(2,1)S(1)}, u32[]{:S(2)}, u32[]{:S(2)}) collective-permute-start(bf16[2576,128]{1,0:T(8,128)(2,1)S(1)} %shard_map.72), channel_id=1, source_target_pairs={{0,64},{1,193},{64,128},{65,1},{128,192},{129,65},{192,0},{193,129... | collective-permute-start | bytes 1978376 | tf_op jit(solution)/shard_map/ppermute | solution.py:240
  113.6 15.9 %collective-permute-start.22 = (bf16[2064,128]{1,0:T(8,128)(2,1)S(1)}, bf16[2064,128]{1,0:T(8,128)(2,1)S(1)}, u32[]{:S(2)}, u32[]{:S(2)}) collective-permute-start(bf16[2064,128]{1,0:T(8,128)(2,1)S(1)} %shard_map.65), channel_id=1, source_target_pairs={{0,56},{1,9},{8,0},{9,17},{16,8},{17,25},{24,16},{25,33},{32,24},{... | collective-permute-start | bytes 1585160 | tf_op jit(solution)/shard_map/ppermute | solution.py:240
  117.7 17.4 %collective-permute-start.19 = (bf16[2064,128]{1,0:T(8,128)(2,1)S(1)}, bf16[2064,128]{1,0:T(8,128)(2,1)S(1)}, u32[]{:S(2)}, u32[]{:S(2)}) collective-permute-start(bf16[2064,128]{1,0:T(8,128)(2,1)S(1)} %shard_map.62), channel_id=1, source_target_pairs={{0,8},{1,57},{8,16},{9,1},{16,24},{17,9},{24,32},{25,17},{32,40},{... | collective-permute-start | bytes 1585160 | tf_op jit(solution)/shard_map/ppermute | solution.py:240
  118.7 17.5 %collective-permute-start.30 = (bf16[2576,128]{1,0:T(8,128)(2,1)S(1)}, bf16[2576,128]{1,0:T(8,128)(2,1)S(1)}, u32[]{:S(2)}, u32[]{:S(2)}) collective-permute-start(bf16[2576,128]{1,0:T(8,128)(2,1)S(1)} %shard_map.74), channel_id=1, source_target_pairs={{0,192},{1,65},{64,0},{65,129},{128,64},{129,193},{192,128},{193,1... | collective-permute-start | bytes 1978376 | tf_op jit(solution)/shard_map/ppermute | solution.py:240
  126.9 10.7 %collective-permute-start.29 = (bf16[2576,128]{1,0:T(8,128)(2,1)S(1)}, bf16[2576,128]{1,0:T(8,128)(2,1)S(1)}, u32[]{:S(2)}, u32[]{:S(2)}) collective-permute-start(bf16[2576,128]{1,0:T(8,128)(2,1)S(1)} %shard_map.73), channel_id=1, source_target_pairs={{0,64},{1,193},{64,128},{65,1},{128,192},{129,65},{192,0},{193,129... | collective-permute-start | bytes 1978376 | tf_op jit(solution)/shard_map/ppermute | solution.py:240
  130.5 11.3 %collective-permute-start.23 = (bf16[2064,128]{1,0:T(8,128)(2,1)S(1)}, bf16[2064,128]{1,0:T(8,128)(2,1)S(1)}, u32[]{:S(2)}, u32[]{:S(2)}) collective-permute-start(bf16[2064,128]{1,0:T(8,128)(2,1)S(1)} %shard_map.66), channel_id=1, source_target_pairs={{0,56},{1,9},{8,0},{9,17},{16,8},{17,25},{24,16},{25,33},{32,24},{... | collective-permute-start | bytes 1585160 | tf_op jit(solution)/shard_map/ppermute | solution.py:240
  136.0 10.5 %collective-permute-start.20 = (bf16[2064,128]{1,0:T(8,128)(2,1)S(1)}, bf16[2064,128]{1,0:T(8,128)(2,1)S(1)}, u32[]{:S(2)}, u32[]{:S(2)}) collective-permute-start(bf16[2064,128]{1,0:T(8,128)(2,1)S(1)} %shard_map.63), channel_id=1, source_target_pairs={{0,8},{1,57},{8,16},{9,1},{16,24},{17,9},{24,32},{25,17},{32,40},{... | collective-permute-start | bytes 1585160 | tf_op jit(solution)/shard_map/ppermute | solution.py:240
  139.0 11.0 %collective-permute-start.31 = (bf16[1296,128]{1,0:T(8,128)(2,1)S(1)}, bf16[1296,128]{1,0:T(8,128)(2,1)S(1)}, u32[]{:S(2)}, u32[]{:S(2)}) collective-permute-start(bf16[1296,128]{1,0:T(8,128)(2,1)S(1)} %get-tuple-element.55), channel_id=1, source_target_pairs={{0,4},{4,0},{1,5},{5,1},{2,6},{6,2},{3,7},{7,3},{8,12},{12,8},{9,1... | collective-permute-start | bytes 995336 | tf_op jit(solution)/shard_map/ppermute | solution.py:225
  147.6 6.5 %collective-permute-start.24 = (bf16[128,1024]{1,0:T(8,128)(2,1)S(1)}, bf16[128,1024]{1,0:T(8,128)(2,1)S(1)}, u32[]{:S(2)}, u32[]{:S(2)}) collective-permute-start(bf16[128,1024]{1,0:T(8,128)(2,1)S(1)} %shard_map.68), channel_id=1, source_target_pairs={{0,4},{4,0},{1,5},{5,1},{2,6},{6,2},{3,7},{7,3},{8,12},{12,8},{9,1... | collective-permute-start | bytes 786440 | tf_op jit(solution)/shard_map/ppermute | solution.py:225
  (14 other events, 13.0 us)

commit v2 on v0

--- a/solution.py
+++ b/solution.py
@@ -220,7 +220,7 @@
     return lax.ppermute(a, (axis, "c"), perm)
 
 
-def gathered(parts, axis, order, joint, hold=()):
+def gathered(parts, axis, order, joint, before, out=()):
     n, me = lax.axis_size(axis), lax.axis_index(axis)
     step = 1 - 2 * lax.axis_index("c")
     count, (rows, width) = len(parts), parts[0].shape
@@ -229,7 +229,12 @@
     for k in range(1, n // 2 + 1):
         if k == joint:
             ahead, back = [jnp.concatenate(ahead)], [jnp.concatenate(back)]
-            hold = after(*ahead, *back, *hold)[2:]
+        if k in before:
+            ahead, back, *_ = after(*ahead, *back, *before[k])
+            ahead, back = [ahead], [back]
+        if k == 1 and count == 2:
+            ahead, back = blocks[-1], blocks[1] = [[f, ring(parts[1], axis, w)] for f, w in zip(out, (1, -1))]
+            continue
         ahead = blocks[-k] = [ring(p, axis, 1) for p in ahead]
         if k < n - n // 2:
             back = blocks[k] = [ring(p, axis, -1) for p in back]
@@ -240,7 +245,7 @@
             src, row = (i, 0) if len(got) == count else (0, i * rows)
             pieces.append((len(arrays) + src, row, rows, 0, (at + place) * rows))
         arrays += got
-    return arrays, pieces, (n * count * rows, width), hold
+    return arrays, pieces, (n * count * rows, width), blocks
 
 
 def outgoing(share, axis):
@@ -287,13 +292,18 @@
 
     w_mine = lax.dynamic_slice_in_dim(weight[0], h * half, half, 0)
     w_sent = lax.dynamic_slice_in_dim(weight[0], (1 - h) * half, half, 0)
-    w_got = swap(w_sent, "yl")
-    w_all = placed(*gathered([jnp.concatenate([w_mine, w_got], axis=1)], "x", (0,), 0)[:3])
+    out = [ring(acts_mine, "z", 1), ring(acts_mine, "z", -1)]
+    *_, acts_got, w_got = after(*out, acts_got, swap(w_sent, "yl"))
+    arrays, pieces, shape, blocks = gathered([jnp.concatenate([w_mine, w_got], axis=1)], "x", (0,), 0, {2: []})
+    w_all = placed(arrays, pieces, shape)
+
+    before = {2: [w_got], 3: [blocks[-1][0], blocks[1][0]]}
+    arrays, acts_pieces, shape, blocks = gathered([acts_mine, acts_got], "z", (h, 1 - h), 2, before, out)
 
     part = tokens // 2
     g_sent = lax.dynamic_slice_in_dim(out_grad, c * part, part, 0)
-    hold = [y_ring(g_sent)]
-    arrays, acts_pieces, shape, (g_got,) = gathered([acts_mine, acts_got], "z", (h, 1 - h), 3, hold)
+    g_sent = after(acts_got, w_got, g_sent)[2]
+    g_got = after(*blocks[-2], *blocks[2], y_ring(g_sent))[-1]
     g_rest = swap(g_got, "c")
     pieces = [(0, 0, tokens, 0, 0), (1, 0, part, width, c * part), (2, 0, part, width, (1 - c) * part)]
     g_pair = placed([out_grad, g_got, g_rest], pieces, (tokens, 2 * width))

time: 153 us -> 150 us (0.980)
  starting transfers between devices: 62.4 us -> 41 us
  waiting for transfers between devices: 48.4 us -> 65.6 us
  other arithmetic: 0.46 us -> 2.22 us
  Pallas kernels: 19.7 us -> 21.4 us
    ppermute x24 -> x22, waiting for transfers between devices: 30.1 us -> 59.3 us  [ring(): return lax.ppermute(a, (axis, 'c'), perm)]
    ppermute x5, starting transfers between devices: 17.3 us -> 3.58 us  [swap(): return lax.ppermute(a, axis, [(0, 1), (1, 0)])]
    ppermute x5, waiting for transfers between devices: 18.3 us -> 6.26 us  [swap(): return lax.ppermute(a, axis, [(0, 1), (1, 0)])]
    ppermute x24 -> x22, starting transfers between devices: 43.6 us -> 35.8 us  [ring(): return lax.ppermute(a, (axis, 'c'), perm)]
    dynamic_slice x1, local copies, waits for them, and re-layouts: 2.58 us -> 0.11 us  [on_device(): g_sent = lax.dynamic_slice_in_dim(out_grad, c * part, part, 0)]
    dynamic_slice x1, local copies, waits for them, and re-layouts: 0.06 us -> 1.96 us  [on_device(): w_mine = lax.dynamic_slice_in_dim(weight[0], h * half, half, 0)]
    pallas_call x3, Pallas kernels: 6 us -> 7.73 us  [placed(): pl.pallas_call(functools.partial(placed_kernel, fixed), grid_spec=pltpu.P...]
  transfers between devices with their start and end apart: 30 -> 28, of which waited for: 9 -> 12; matrix products, arithmetic and copies ran while one was open for 10% -> 10% of each run, Pallas kernels for 12% -> 14%
where the time goes in v2:
time: 150 us
  waiting for transfers between devices  65.6 us (44%)
  starting transfers between devices  41 us (27%)
  Pallas kernels  21.4 us (14%)
  matrix products  13.3 us (9%)
  local copies, waits for them, and re-layouts  5.39 us (4%)
  other arithmetic  2.22 us (1%)
    ppermute x22, waiting for transfers between devices, ring(): return lax.ppermute(a, (axis, 'c'), perm)  59.3 us
    ppermute x22, starting transfers between devices, ring(): return lax.ppermute(a, (axis, 'c'), perm)  35.8 us
    pallas_call x15, Pallas kernels, call(): pl.pallas_call(kernel, grid_spec=pltpu.PrefetchScalarGridSpec(num_scalar_...  13.7 us
    dot_general x12, matrix products, dot(): return lax.dot_general(a, b, (dims, ((), ())), preferred_element_type=F32)  13.3 us
    pallas_call x3, Pallas kernels, placed(): pl.pallas_call(functools.partial(placed_kernel, fixed), grid_spec=pltpu.P...  7.73 us
    ppermute x5, waiting for transfers between devices, swap(): return lax.ppermute(a, axis, [(0, 1), (1, 0)])  6.26 us
    ppermute x5, starting transfers between devices, swap(): return lax.ppermute(a, axis, [(0, 1), (1, 0)])  3.58 us
  transfers between devices with their start and end apart: 28, of which 12 were waited for; matrix products, arithmetic and copies ran while one was open for 10% of the time, Pallas kernels for 14%

profile of v2, /device:TPU:4, one launch (start us, length us, event | category | flops | bytes accessed | tf_op | source)
XLA Modules:
  0.0 150.0 jit_solution(1579888525818630285)
XLA Ops:
  0.6 1.3 fusion.36
  2.7 2.0 %dynamic-slice_bitcast_fusion = (bf16[256,640]{1,0:T(8,128)(2,1)}, bf16[256,640]{1,0:T(8,128)(2,1)}) fusion(bf16[1,512,640]{2,1,0:T(8,128)(2,1)} %param.5, s32[]{:T(128)S(6)} %select_n.63, s32[]{:T(128)S(6)} %select_n.60), kind=kLoop, calls=%fused_computation.27 | loop fusion | bytes 1310728 | tf_op jit(solution)/shard_map/dynamic_slice | solution.py:293
  4.7 1.6 %collective-permute-start.3 = (bf16[256,640]{1,0:T(8,128)(2,1)}, bf16[256,640]{1,0:T(8,128)(2,1)}, u32[]{:S(2)}, u32[]{:S(2)}) collective-permute-start(bf16[256,640]{1,0:T(8,128)(2,1)} %get-tuple-element.55), channel_id=1, source_target_pairs={{0,4},{4,0},{1,5},{5,1},{2,6},{6,2},{3,7},{7,3},{8,12},{12,8},{9,1... | collective-permute-start | bytes 983048 | tf_op jit(solution)/shard_map/ppermute | solution.py:205
  6.3 1.9 %collective-permute-start = (bf16[128,1024]{1,0:T(8,128)(2,1)S(1)}, bf16[128,1024]{1,0:T(8,128)(2,1)S(1)}, u32[]{:S(2)}, u32[]{:S(2)}) collective-permute-start(bf16[128,1024]{1,0:T(8,128)(2,1)S(1)} %get-tuple-element.41.refs_0_), channel_id=1, source_target_pairs={{0,8},{1,57},{8,16},{9,1},{16,24},{17,9},{24,32},{25,17},{32,40},{... | collective-permute-start | bytes 786440 | tf_op jit(solution)/shard_map/ppermute | solution.py:220
  8.2 3.9 %collective-permute-start.1 = (bf16[128,1024]{1,0:T(8,128)(2,1)S(1)}, bf16[128,1024]{1,0:T(8,128)(2,1)S(1)}, u32[]{:S(2)}, u32[]{:S(2)}) collective-permute-start(bf16[128,1024]{1,0:T(8,128)(2,1)S(1)} %get-tuple-element.41.refs_0_), channel_id=1, source_target_pairs={{0,56},{1,9},{8,0},{9,17},{16,8},{17,25},{24,16},{25,33},{32,24},{... | collective-permute-start | bytes 786440 | tf_op jit(solution)/shard_map/ppermute | solution.py:220
  12.7 5.0 %collective-permute-done.refs_2_ = bf16[128,1024]{1,0:T(8,128)(2,1)S(1)} collective-permute-done((bf16[128,1024]{1,0:T(8,128)(2,1)S(1)}, bf16[128,1024]{1,0:T(8,128)(2,1)S(1)}, u32[]{:S(2)}, u32[]{:S(2)}) %collective-permute-start) | collective-permute-done | bytes 262176 | tf_op jit(solution)/shard_map/ppermute | solution.py:220
  17.7 2.4 %collective-permute-done.2.refs_1_ = bf16[128,1024]{1,0:T(8,128)(2,1)} collective-permute-done((bf16[128,1024]{1,0:T(8,128)(2,1)}, bf16[128,1024]{1,0:T(8,128)(2,1)}, u32[]{:S(2)}, u32[]{:S(2)}) %collective-permute-start.2) | collective-permute-done | bytes 262176 | tf_op jit(solution)/shard_map/ppermute | solution.py:205
  20.1 1.6 %collective-permute-start.8 = (bf16[1024,640]{1,0:T(8,128)(2,1)S(1)}, bf16[1024,640]{1,0:T(8,128)(2,1)}, u32[]{:S(2)}, u32[]{:S(2)}) collective-permute-start(bf16[1024,640]{1,0:T(8,128)(2,1)S(1)} %constant_dynamic-slice_fusion), channel_id=1, source_target_pairs={{0,4},{1,7},{4,2},{5,1},{2,6},{3,5},{6,0},{7,3},{8,12},{9,15},{12,... | collective-permute-start | bytes 3932168 | tf_op jit(solution)/shard_map/ppermute | solution.py:214
  21.7 1.9 %collective-permute-start.4 = (bf16[128,1024]{1,0:T(8,128)(2,1)}, bf16[128,1024]{1,0:T(8,128)(2,1)S(1)}, u32[]{:S(2)}, u32[]{:S(2)}) collective-permute-start(bf16[128,1024]{1,0:T(8,128)(2,1)} %collective-permute-done.2.refs_1_), channel_id=1, source_target_pairs={{0,8},{1,57},{8,16},{9,1},{16,24},{17,9},{24,32},{25,17},{32,40},{... | collective-permute-start | bytes 786440 | tf_op jit(solution)/shard_map/ppermute | solution.py:220
  23.6 3.9 %collective-permute-start.5 = (bf16[128,1024]{1,0:T(8,128)(2,1)}, bf16[128,1024]{1,0:T(8,128)(2,1)S(1)}, u32[]{:S(2)}, u32[]{:S(2)}) collective-permute-start(bf16[128,1024]{1,0:T(8,128)(2,1)} %collective-permute-done.2.refs_1_), channel_id=1, source_target_pairs={{0,56},{1,9},{8,0},{9,17},{16,8},{17,25},{24,16},{25,33},{32,24},{... | collective-permute-start | bytes 786440 | tf_op jit(solution)/shard_map/ppermute | solution.py:220
  27.5 5.2 %collective-permute-done.4.refs_3_ = bf16[128,1024]{1,0:T(8,128)(2,1)S(1)} collective-permute-done((bf16[128,1024]{1,0:T(8,128)(2,1)}, bf16[128,1024]{1,0:T(8,128)(2,1)S(1)}, u32[]{:S(2)}, u32[]{:S(2)}) %collective-permute-start.4) | collective-permute-done | bytes 262176 | tf_op jit(solution)/shard_map/ppermute | solution.py:220
  32.7 0.9 collective-permute-done.5.refs_5_
  33.8 3.7 %collective-permute-start.7 = (bf16[256,1024]{1,0:T(8,128)(2,1)S(1)}, bf16[256,1024]{1,0:T(8,128)(2,1)S(1)}, u32[]{:S(2)}, u32[]{:S(2)}) collective-permute-start(bf16[256,1024]{1,0:T(8,128)(2,1)S(1)} %pad_maximum_fusion.2), channel_id=1, source_target_pairs={{0,56},{1,9},{8,0},{9,17},{16,8},{17,25},{24,16},{25,33},{32,24},{... | collective-permute-start | bytes 1572872 | tf_op jit(solution)/shard_map/ppermute | solution.py:220
  37.5 1.0 pad_maximum_fusion.refs_0_
  38.5 1.3 collective-permute-start.10
  40.6 8.0 %collective-permute-done.6.refs_6_ = bf16[256,1024]{1,0:T(8,128)(2,1)} collective-permute-done((bf16[256,1024]{1,0:T(8,128)(2,1)S(1)}, bf16[256,1024]{1,0:T(8,128)(2,1)}, u32[]{:S(2)}, u32[]{:S(2)}) %collective-permute-start.6) | collective-permute-done | bytes 524320 | tf_op jit(solution)/shard_map/ppermute | solution.py:220
  48.6 1.4 collective-permute-start.9
  50.0 4.8 %collective-permute-done.10.refs_1_ = bf16[256,1280]{1,0:T(8,128)(2,1)} collective-permute-done((bf16[256,1280]{1,0:T(8,128)(2,1)S(1)}, bf16[256,1280]{1,0:T(8,128)(2,1)}, u32[]{:S(2)}, u32[]{:S(2)}) %collective-permute-start.10) | collective-permute-done | bytes 655392 | tf_op jit(solution)/shard_map/ppermute | solution.py:220
  55.7 2.0 %collective-permute-start.12 = (bf16[256,1280]{1,0:T(8,128)(2,1)}, bf16[256,1280]{1,0:T(8,128)(2,1)}, u32[]{:S(2)}, u32[]{:S(2)}) collective-permute-start(bf16[256,1280]{1,0:T(8,128)(2,1)} %collective-permute-done.10.refs_1_), channel_id=1, source_target_pairs={{0,64},{1,193},{64,128},{65,1},{128,192},{129,65},{192,0},{193,129... | collective-permute-start | bytes 1966088 | tf_op jit(solution)/shard_map/ppermute | solution.py:220
  58.3 3.0 %collective-permute-start.22 = (bf16[256,1024]{1,0:T(8,128)(2,1)}, bf16[256,1024]{1,0:T(8,128)(2,1)S(1)}, u32[]{:S(2)}, u32[]{:S(2)}) collective-permute-start(bf16[256,1024]{1,0:T(8,128)(2,1)} %copy-done.11), channel_id=1, source_target_pairs={{0,56},{1,9},{8,0},{9,17},{16,8},{17,25},{24,16},{25,33},{32,24},{... | collective-permute-start | bytes 1572872 | tf_op jit(solution)/shard_map/ppermute | solution.py:220
  61.3 12.4 %collective-permute-done.21.refs_8_ = bf16[256,1024]{1,0:T(8,128)(2,1)} collective-permute-done((bf16[256,1024]{1,0:T(8,128)(2,1)}, bf16[256,1024]{1,0:T(8,128)(2,1)}, u32[]{:S(2)}, u32[]{:S(2)}) %collective-permute-start.21) | collective-permute-done | bytes 524320 | tf_op jit(solution)/shard_map/ppermute | solution.py:220
  73.7 1.1 copy-done.10
  74.8 2.7 %shard_map.51 = bf16[1024,1280]{1,0:T(8,128)(2,1)S(1)} custom-call(s32[4]{0:T(128)S(1)} %pad_add_fusion.2.at_ref, bf16[256,1280]{1,0:T(8,128)(2,1)S(1)} %pad_maximum_fusion.refs_0_, bf16[256,1280]{1,0:T(8,128)(2,1)} %collective-permute-done.10.refs_1_, bf16[256,1280]{1,0:T(8,128)(2,1)S(1)} %copy-done.10, bf16[256,1280]{1,0:T(8,128)(2,1)} %collective-permute-done.12.refs_3_), custom_call_target="tpu_custom_call" | custom-call | bytes 5242880 | tf_op jit(solution)/shard_map/pallas_call | solution.py:180
  77.5 2.7 %shard_map.50 = bf16[2048,1280]{1,0:T(8,128)(2,1)S(1)} custom-call(s32[3]{0:T(128)S(1)} %pad_add_fusion.1.at_ref, bf16[2048,640]{1,0:T(8,128)(2,1)S(1)} %copy-done, bf16[1024,640]{1,0:T(8,128)(2,1)} %collective-permute-done.8.refs_1_, bf16[1024,640]{1,0:T(8,128)(2,1)} %collective-permute-done.9.refs_2_), custom_call_target="tpu_custom_call" | custom-call | bytes 10485760 | tf_op jit(solution)/shard_map/pallas_call | solution.py:180
  83.3 3.3 %collective-permute-start.17 = (bf16[2064,128]{1,0:T(8,128)(2,1)S(1)}, bf16[2064,128]{1,0:T(8,128)(2,1)S(1)}, u32[]{:S(2)}, u32[]{:S(2)}) collective-permute-start(bf16[2064,128]{1,0:T(8,128)(2,1)S(1)} %shard_map.56), channel_id=1, source_target_pairs={{0,56},{1,9},{8,0},{9,17},{16,8},{17,25},{24,16},{25,33},{32,24},{... | collective-permute-start | bytes 1585160 | tf_op jit(solution)/shard_map/ppermute | solution.py:220
  86.7 2.3 %shard_map.62 = bf16[2048,1024]{1,0:T(8,128)(2,1)S(1)} custom-call(s32[16]{0:T(128)S(1)} %stack.119.at_ref, bf16[128,1024]{1,0:T(8,128)(2,1)S(1)} %get-tuple-element.41.refs_0_, bf16[128,1024]{1,0:T(8,128)(2,1)} %collective-permute-done.2.refs_1_, bf16[128,1024]{1,0:T(8,128)(2,1)S(1)} %copy-done.2, bf16[128,1024]{1,0:T(8,128)(2,1)S(1)} %copy-done.6, ...), custom_call_target="tpu_custom_call" | custom-call | bytes 8388608 | tf_op jit(solution)/shard_map/pallas_call | solution.py:180
  89.0 1.6 %fusion.6.refs_0_ = f32[256,1280]{1,0:T(8,128)S(1)} fusion(bf16[2048,1280]{1,0:T(8,128)(2,1)S(1)} %shard_map.50, bf16[2048,1024]{1,0:T(8,128)(2,1)S(1)} %shard_map.62, s32[]{:T(128)S(6)} %select_n.71), kind=kOutput, calls=%fused_computation.6 | convolution fusion | flops 1342177280 | bytes 7602180 | tf_op jit(solution)/shard_map/dot_general | solution.py:271
  91.2 1.9 %collective-permute-start.24 = (bf16[2576,128]{1,0:T(8,128)(2,1)S(1)}, bf16[2576,128]{1,0:T(8,128)(2,1)S(1)}, u32[]{:S(2)}, u32[]{:S(2)}) collective-permute-start(bf16[2576,128]{1,0:T(8,128)(2,1)S(1)} %shard_map.63), channel_id=1, source_target_pairs={{0,64},{1,193},{64,128},{65,1},{128,192},{129,65},{192,0},{193,129... | collective-permute-start | bytes 1978376 | tf_op jit(solution)/shard_map/ppermute | solution.py:220
  93.1 1.6 %fusion.4.refs_1_ = f32[256,1280]{1,0:T(8,128)S(1)} fusion(bf16[2048,1280]{1,0:T(8,128)(2,1)S(1)} %shard_map.50, bf16[2048,1024]{1,0:T(8,128)(2,1)S(1)} %shard_map.62, s32[]{:T(128)S(6)} %select_n.72), kind=kOutput, calls=%fused_computation.4 | convolution fusion | flops 1342177280 | bytes 7602180 | tf_op jit(solution)/shard_map/dot_general | solution.py:271
  95.6 1.6 %fusion.2.refs_0_ = f32[256,1280]{1,0:T(8,128)S(1)} fusion(bf16[2048,1280]{1,0:T(8,128)(2,1)S(1)} %shard_map.50, bf16[2048,1024]{1,0:T(8,128)(2,1)S(1)} %shard_map.62, s32[]{:T(128)S(6)} %select_n.73), kind=kOutput, calls=%fused_computation.2 | convolution fusion | flops 1342177280 | bytes 7602180 | tf_op jit(solution)/shard_map/dot_general | solution.py:271
  97.2 0.9 shard_map.53
  101.1 0.9 shard_map.57
  102.0 3.3 %collective-permute-start.18 = (bf16[2064,128]{1,0:T(8,128)(2,1)S(1)}, bf16[2064,128]{1,0:T(8,128)(2,1)S(1)}, u32[]{:S(2)}, u32[]{:S(2)}) collective-permute-start(bf16[2064,128]{1,0:T(8,128)(2,1)S(1)} %shard_map.57), channel_id=1, source_target_pairs={{0,56},{1,9},{8,0},{9,17},{16,8},{17,25},{24,16},{25,33},{32,24},{... | collective-permute-start | bytes 1585160 | tf_op jit(solution)/shard_map/ppermute | solution.py:220
  105.3 8.3 %collective-permute-done.14.refs_0_ = bf16[2064,128]{1,0:T(8,128)(2,1)S(1)} collective-permute-done((bf16[2064,128]{1,0:T(8,128)(2,1)S(1)}, bf16[2064,128]{1,0:T(8,128)(2,1)S(1)}, u32[]{:S(2)}, u32[]{:S(2)}) %collective-permute-start.14) | collective-permute-done | bytes 528416 | tf_op jit(solution)/shard_map/ppermute | solution.py:220
  113.6 0.9 shard_map.54
  115.5 1.1 shard_map.64
  117.6 0.9 shard_map.58
  118.5 3.5 %collective-permute-start.19 = (bf16[2064,128]{1,0:T(8,128)(2,1)S(1)}, bf16[2064,128]{1,0:T(8,128)(2,1)S(1)}, u32[]{:S(2)}, u32[]{:S(2)}) collective-permute-start(bf16[2064,128]{1,0:T(8,128)(2,1)S(1)} %shard_map.58), channel_id=1, source_target_pairs={{0,56},{1,9},{8,0},{9,17},{16,8},{17,25},{24,16},{25,33},{32,24},{... | collective-permute-start | bytes 1585160 | tf_op jit(solution)/shard_map/ppermute | solution.py:220
  122.1 8.2 %collective-permute-done.15.refs_0_ = bf16[2064,128]{1,0:T(8,128)(2,1)S(1)} collective-permute-done((bf16[2064,128]{1,0:T(8,128)(2,1)S(1)}, bf16[2064,128]{1,0:T(8,128)(2,1)S(1)}, u32[]{:S(2)}, u32[]{:S(2)}) %collective-permute-start.15) | collective-permute-done | bytes 528416 | tf_op jit(solution)/shard_map/ppermute | solution.py:220
  130.2 0.9 shard_map.55
  131.2 1.6 %fusion.own_ref = f32[256,1280]{1,0:T(8,128)S(1)} fusion(bf16[2048,1280]{1,0:T(8,128)(2,1)S(1)} %shard_map.50, bf16[2048,1024]{1,0:T(8,128)(2,1)S(1)} %shard_map.62, s32[]{:T(128)S(6)} %select_n.74), kind=kOutput, calls=%fused_computation | convolution fusion | flops 1342177280 | bytes 7602180 | tf_op jit(solution)/shard_map/dot_general | solution.py:271
  132.9 1.3 shard_map.66
  134.3 0.9 fusion.8.own_ref
  135.2 6.5 %collective-permute-done.16.f_ref = bf16[2064,128]{1,0:T(8,128)(2,1)S(1)} collective-permute-done((bf16[2064,128]{1,0:T(8,128)(2,1)S(1)}, bf16[2064,128]{1,0:T(8,128)(2,1)S(1)}, u32[]{:S(2)}, u32[]{:S(2)}) %collective-permute-start.16) | collective-permute-done | bytes 528416 | tf_op jit(solution)/shard_map/ppermute | solution.py:220
  141.6 1.0 shard_map.60
  143.0 1.4 shard_map.67
  144.4 1.0 shard_map.59.mine_ref
  145.4 3.7 %collective-permute-done.20.got_ref = bf16[128,1024]{1,0:T(8,128)(2,1)S(1)} collective-permute-done((bf16[128,1024]{1,0:T(8,128)(2,1)S(1)}, bf16[128,1024]{1,0:T(8,128)(2,1)S(1)}, u32[]{:S(2)}, u32[]{:S(2)}) %collective-permute-start.20) | collective-permute-done | bytes 262176 | tf_op jit(solution)/shard_map/ppermute | solution.py:205
  (78 shorter events, 14.6 us)
Async XLA Ops:
  0.6 11.9 %copy-start = (bf16[2048,640]{1,0:T(8,128)(2,1)S(1)}, bf16[2048,640]{1,0:T(8,128)(2,1)}, u32[]{:S(2)}) copy-start(bf16[2048,640]{1,0:T(8,128)(2,1)} %refs_0_) | copy-start | bytes 7864324
  4.7 15.4 %collective-permute-start.3 = (bf16[256,640]{1,0:T(8,128)(2,1)}, bf16[256,640]{1,0:T(8,128)(2,1)}, u32[]{:S(2)}, u32[]{:S(2)}) collective-permute-start(bf16[256,640]{1,0:T(8,128)(2,1)} %get-tuple-element.55), channel_id=1, source_target_pairs={{0,4},{4,0},{1,5},{5,1},{2,6},{6,2},{3,7},{7,3},{8,12},{12,8},{9,1... | collective-permute-start | bytes 983048 | tf_op jit(solution)/shard_map/ppermute | solution.py:205
  6.3 11.4 %collective-permute-start = (bf16[128,1024]{1,0:T(8,128)(2,1)S(1)}, bf16[128,1024]{1,0:T(8,128)(2,1)S(1)}, u32[]{:S(2)}, u32[]{:S(2)}) collective-permute-start(bf16[128,1024]{1,0:T(8,128)(2,1)S(1)} %get-tuple-element.41.refs_0_), channel_id=1, source_target_pairs={{0,8},{1,57},{8,16},{9,1},{16,24},{17,9},{24,32},{25,17},{32,40},{... | collective-permute-start | bytes 786440 | tf_op jit(solution)/shard_map/ppermute | solution.py:220
  8.2 9.5 %collective-permute-start.1 = (bf16[128,1024]{1,0:T(8,128)(2,1)S(1)}, bf16[128,1024]{1,0:T(8,128)(2,1)S(1)}, u32[]{:S(2)}, u32[]{:S(2)}) collective-permute-start(bf16[128,1024]{1,0:T(8,128)(2,1)S(1)} %get-tuple-element.41.refs_0_), channel_id=1, source_target_pairs={{0,56},{1,9},{8,0},{9,17},{16,8},{17,25},{24,16},{25,33},{32,24},{... | collective-permute-start | bytes 786440 | tf_op jit(solution)/shard_map/ppermute | solution.py:220
  12.1 7.9 %collective-permute-start.2 = (bf16[128,1024]{1,0:T(8,128)(2,1)}, bf16[128,1024]{1,0:T(8,128)(2,1)}, u32[]{:S(2)}, u32[]{:S(2)}) collective-permute-start(bf16[128,1024]{1,0:T(8,128)(2,1)} %get-tuple-element.30), channel_id=1, source_target_pairs={{0,4},{4,0},{1,5},{5,1},{2,6},{6,2},{3,7},{7,3},{8,12},{12,8},{9,1... | collective-permute-start | bytes 786440 | tf_op jit(solution)/shard_map/ppermute | solution.py:205
  12.6 24.9 %copy-start.13 = (bf16[256,640]{1,0:T(8,128)(2,1)S(1)}, bf16[256,640]{1,0:T(8,128)(2,1)}, u32[]{:S(2)}) copy-start(bf16[256,640]{1,0:T(8,128)(2,1)} %get-tuple-element.54) | copy-start | bytes 983044
  17.7 19.8 %copy-start.1 = (bf16[128,1024]{1,0:T(8,128)(2,1)}, bf16[128,1024]{1,0:T(8,128)(2,1)S(1)}, u32[]{:S(2)}) copy-start(bf16[128,1024]{1,0:T(8,128)(2,1)S(1)} %collective-permute-done.refs_2_) | copy-start | bytes 786436
  17.7 19.8 %copy-start.3 = (bf16[128,1024]{1,0:T(8,128)(2,1)}, bf16[128,1024]{1,0:T(8,128)(2,1)S(1)}, u32[]{:S(2)}) copy-start(bf16[128,1024]{1,0:T(8,128)(2,1)S(1)} %collective-permute-done.1.refs_4_) | copy-start | bytes 786436
  20.1 28.5 %collective-permute-start.8 = (bf16[1024,640]{1,0:T(8,128)(2,1)S(1)}, bf16[1024,640]{1,0:T(8,128)(2,1)}, u32[]{:S(2)}, u32[]{:S(2)}) collective-permute-start(bf16[1024,640]{1,0:T(8,128)(2,1)S(1)} %constant_dynamic-slice_fusion), channel_id=1, source_target_pairs={{0,4},{1,7},{4,2},{5,1},{2,6},{3,5},{6,0},{7,3},{8,12},{9,15},{12,... | collective-permute-start | bytes 3932168 | tf_op jit(solution)/shard_map/ppermute | solution.py:214
  21.7 11.1 %collective-permute-start.4 = (bf16[128,1024]{1,0:T(8,128)(2,1)}, bf16[128,1024]{1,0:T(8,128)(2,1)S(1)}, u32[]{:S(2)}, u32[]{:S(2)}) collective-permute-start(bf16[128,1024]{1,0:T(8,128)(2,1)} %collective-permute-done.2.refs_1_), channel_id=1, source_target_pairs={{0,8},{1,57},{8,16},{9,1},{16,24},{17,9},{24,32},{25,17},{32,40},{... | collective-permute-start | bytes 786440 | tf_op jit(solution)/shard_map/ppermute | solution.py:220
  23.6 10.1 %collective-permute-start.5 = (bf16[128,1024]{1,0:T(8,128)(2,1)}, bf16[128,1024]{1,0:T(8,128)(2,1)S(1)}, u32[]{:S(2)}, u32[]{:S(2)}) collective-permute-start(bf16[128,1024]{1,0:T(8,128)(2,1)} %collective-permute-done.2.refs_1_), channel_id=1, source_target_pairs={{0,56},{1,9},{8,0},{9,17},{16,8},{17,25},{24,16},{25,33},{32,24},{... | collective-permute-start | bytes 786440 | tf_op jit(solution)/shard_map/ppermute | solution.py:220
  32.7 22.1 %copy-start.5 = (bf16[128,1024]{1,0:T(8,128)(2,1)}, bf16[128,1024]{1,0:T(8,128)(2,1)S(1)}, u32[]{:S(2)}) copy-start(bf16[128,1024]{1,0:T(8,128)(2,1)S(1)} %collective-permute-done.4.refs_3_) | copy-start | bytes 786436
  33.7 24.1 %copy-start.7 = (bf16[128,1024]{1,0:T(8,128)(2,1)}, bf16[128,1024]{1,0:T(8,128)(2,1)S(1)}, u32[]{:S(2)}) copy-start(bf16[128,1024]{1,0:T(8,128)(2,1)S(1)} %collective-permute-done.5.refs_5_) | copy-start | bytes 786436
  33.7 14.9 %collective-permute-start.6 = (bf16[256,1024]{1,0:T(8,128)(2,1)S(1)}, bf16[256,1024]{1,0:T(8,128)(2,1)}, u32[]{:S(2)}, u32[]{:S(2)}) collective-permute-start(bf16[256,1024]{1,0:T(8,128)(2,1)S(1)} %pad_maximum_fusion.1), channel_id=1, source_target_pairs={{0,8},{1,57},{8,16},{9,1},{16,24},{17,9},{24,32},{25,17},{32,40},{... | collective-permute-start | bytes 1572872 | tf_op jit(solution)/shard_map/ppermute | solution.py:220
  33.8 14.8 %collective-permute-start.7 = (bf16[256,1024]{1,0:T(8,128)(2,1)S(1)}, bf16[256,1024]{1,0:T(8,128)(2,1)S(1)}, u32[]{:S(2)}, u32[]{:S(2)}) collective-permute-start(bf16[256,1024]{1,0:T(8,128)(2,1)S(1)} %pad_maximum_fusion.2), channel_id=1, source_target_pairs={{0,56},{1,9},{8,0},{9,17},{16,8},{17,25},{24,16},{25,33},{32,24},{... | collective-permute-start | bytes 1572872 | tf_op jit(solution)/shard_map/ppermute | solution.py:220
  38.5 16.3 %collective-permute-start.10 = (bf16[256,1280]{1,0:T(8,128)(2,1)S(1)}, bf16[256,1280]{1,0:T(8,128)(2,1)}, u32[]{:S(2)}, u32[]{:S(2)}) collective-permute-start(bf16[256,1280]{1,0:T(8,128)(2,1)S(1)} %pad_maximum_fusion.refs_0_), channel_id=1, source_target_pairs={{0,64},{1,193},{64,128},{65,1},{128,192},{129,65},{192,0},{193,129... | collective-permute-start | bytes 1966088 | tf_op jit(solution)/shard_map/ppermute | solution.py:220
  39.8 15.1 %collective-permute-start.11 = (bf16[256,1280]{1,0:T(8,128)(2,1)S(1)}, bf16[256,1280]{1,0:T(8,128)(2,1)S(1)}, u32[]{:S(2)}, u32[]{:S(2)}) collective-permute-start(bf16[256,1280]{1,0:T(8,128)(2,1)S(1)} %pad_maximum_fusion.refs_0_), channel_id=1, source_target_pairs={{0,192},{1,65},{64,0},{65,129},{128,64},{129,193},{192,128},{193,1... | collective-permute-start | bytes 1966088 | tf_op jit(solution)/shard_map/ppermute | solution.py:220
  48.6 9.1 %copy-start.11 = (bf16[256,1024]{1,0:T(8,128)(2,1)}, bf16[256,1024]{1,0:T(8,128)(2,1)S(1)}, u32[]{:S(2)}) copy-start(bf16[256,1024]{1,0:T(8,128)(2,1)S(1)} %collective-permute-done.7.refs_7_) | copy-start | bytes 1572868
  48.6 28.9 %collective-permute-start.9 = (bf16[1024,640]{1,0:T(8,128)(2,1)}, bf16[1024,640]{1,0:T(8,128)(2,1)}, u32[]{:S(2)}, u32[]{:S(2)}) collective-permute-start(bf16[1024,640]{1,0:T(8,128)(2,1)} %collective-permute-done.8.refs_1_), channel_id=1, source_target_pairs={{0,1},{1,0},{2,3},{3,2},{4,5},{5,4},{6,7},{7,6},{8,9},{9,8},{10,11... | collective-permute-start | bytes 3932168 | tf_op jit(solution)/shard_map/ppermute | solution.py:205
  54.8 0.8 copy-start.9
  55.7 18.1 %collective-permute-start.12 = (bf16[256,1280]{1,0:T(8,128)(2,1)}, bf16[256,1280]{1,0:T(8,128)(2,1)}, u32[]{:S(2)}, u32[]{:S(2)}) collective-permute-start(bf16[256,1280]{1,0:T(8,128)(2,1)} %collective-permute-done.10.refs_1_), channel_id=1, source_target_pairs={{0,64},{1,193},{64,128},{65,1},{128,192},{129,65},{192,0},{193,129... | collective-permute-start | bytes 1966088 | tf_op jit(solution)/shard_map/ppermute | solution.py:220
  57.7 16.0 %collective-permute-start.21 = (bf16[256,1024]{1,0:T(8,128)(2,1)}, bf16[256,1024]{1,0:T(8,128)(2,1)}, u32[]{:S(2)}, u32[]{:S(2)}) collective-permute-start(bf16[256,1024]{1,0:T(8,128)(2,1)} %collective-permute-done.6.refs_6_), channel_id=1, source_target_pairs={{0,8},{1,57},{8,16},{9,1},{16,24},{17,9},{24,32},{25,17},{32,40},{... | collective-permute-start | bytes 1572872 | tf_op jit(solution)/shard_map/ppermute | solution.py:220
  58.3 28.3 %collective-permute-start.22 = (bf16[256,1024]{1,0:T(8,128)(2,1)}, bf16[256,1024]{1,0:T(8,128)(2,1)S(1)}, u32[]{:S(2)}, u32[]{:S(2)}) collective-permute-start(bf16[256,1024]{1,0:T(8,128)(2,1)} %copy-done.11), channel_id=1, source_target_pairs={{0,56},{1,9},{8,0},{9,17},{16,8},{17,25},{24,16},{25,33},{32,24},{... | collective-permute-start | bytes 1572872 | tf_op jit(solution)/shard_map/ppermute | solution.py:220
  73.7 12.9 %collective-permute-start.23 = (bf16[256,1024]{1,0:T(8,128)(2,1)}, bf16[256,1024]{1,0:T(8,128)(2,1)S(1)}, u32[]{:S(2)}, u32[]{:S(2)}) collective-permute-start(bf16[256,1024]{1,0:T(8,128)(2,1)} %collective-permute-done.21.refs_8_), channel_id=1, source_target_pairs={{0,8},{1,57},{8,16},{9,1},{16,24},{17,9},{24,32},{25,17},{32,40},{... | collective-permute-start | bytes 1572872 | tf_op jit(solution)/shard_map/ppermute | solution.py:220
  73.7 1.1 copy-start.10
  81.7 4.9 %copy-start.2 = (bf16[128,1024]{1,0:T(8,128)(2,1)S(1)}, bf16[128,1024]{1,0:T(8,128)(2,1)}, u32[]{:S(2)}) copy-start(bf16[128,1024]{1,0:T(8,128)(2,1)} %copy-done.1) | copy-start | bytes 786436
  81.7 4.9 %copy-start.4 = (bf16[128,1024]{1,0:T(8,128)(2,1)S(1)}, bf16[128,1024]{1,0:T(8,128)(2,1)}, u32[]{:S(2)}) copy-start(bf16[128,1024]{1,0:T(8,128)(2,1)} %copy-done.3) | copy-start | bytes 786436
  81.7 4.9 %copy-start.6 = (bf16[128,1024]{1,0:T(8,128)(2,1)S(1)}, bf16[128,1024]{1,0:T(8,128)(2,1)}, u32[]{:S(2)}) copy-start(bf16[128,1024]{1,0:T(8,128)(2,1)} %copy-done.5) | copy-start | bytes 786436
  81.7 4.9 %copy-start.8 = (bf16[128,1024]{1,0:T(8,128)(2,1)S(1)}, bf16[128,1024]{1,0:T(8,128)(2,1)}, u32[]{:S(2)}) copy-start(bf16[128,1024]{1,0:T(8,128)(2,1)} %copy-done.7) | copy-start | bytes 786436
  81.8 4.9 %copy-start.12 = (bf16[256,1024]{1,0:T(8,128)(2,1)S(1)}, bf16[256,1024]{1,0:T(8,128)(2,1)}, u32[]{:S(2)}) copy-start(bf16[256,1024]{1,0:T(8,128)(2,1)} %copy-done.11) | copy-start | bytes 1572868
  81.8 15.4 %collective-permute-start.13 = (bf16[2064,128]{1,0:T(8,128)(2,1)S(1)}, bf16[2064,128]{1,0:T(8,128)(2,1)S(1)}, u32[]{:S(2)}, u32[]{:S(2)}) collective-permute-start(bf16[2064,128]{1,0:T(8,128)(2,1)S(1)} %shard_map.52), channel_id=1, source_target_pairs={{0,8},{1,57},{8,16},{9,1},{16,24},{17,9},{24,32},{25,17},{32,40},{... | collective-permute-start | bytes 1585160 | tf_op jit(solution)/shard_map/ppermute | solution.py:220
  83.3 17.8 %collective-permute-start.17 = (bf16[2064,128]{1,0:T(8,128)(2,1)S(1)}, bf16[2064,128]{1,0:T(8,128)(2,1)S(1)}, u32[]{:S(2)}, u32[]{:S(2)}) collective-permute-start(bf16[2064,128]{1,0:T(8,128)(2,1)S(1)} %shard_map.56), channel_id=1, source_target_pairs={{0,56},{1,9},{8,0},{9,17},{16,8},{17,25},{24,16},{25,33},{32,24},{... | collective-permute-start | bytes 1585160 | tf_op jit(solution)/shard_map/ppermute | solution.py:220
  91.2 24.3 %collective-permute-start.24 = (bf16[2576,128]{1,0:T(8,128)(2,1)S(1)}, bf16[2576,128]{1,0:T(8,128)(2,1)S(1)}, u32[]{:S(2)}, u32[]{:S(2)}) collective-permute-start(bf16[2576,128]{1,0:T(8,128)(2,1)S(1)} %shard_map.63), channel_id=1, source_target_pairs={{0,64},{1,193},{64,128},{65,1},{128,192},{129,65},{192,0},{193,129... | collective-permute-start | bytes 1978376 | tf_op jit(solution)/shard_map/ppermute | solution.py:220
  98.1 15.5 %collective-permute-start.14 = (bf16[2064,128]{1,0:T(8,128)(2,1)S(1)}, bf16[2064,128]{1,0:T(8,128)(2,1)S(1)}, u32[]{:S(2)}, u32[]{:S(2)}) collective-permute-start(bf16[2064,128]{1,0:T(8,128)(2,1)S(1)} %shard_map.53), channel_id=1, source_target_pairs={{0,8},{1,57},{8,16},{9,1},{16,24},{17,9},{24,32},{25,17},{32,40},{... | collective-permute-start | bytes 1585160 | tf_op jit(solution)/shard_map/ppermute | solution.py:220
  99.7 33.1 %collective-permute-start.26 = (bf16[2576,128]{1,0:T(8,128)(2,1)S(1)}, bf16[2576,128]{1,0:T(8,128)(2,1)S(1)}, u32[]{:S(2)}, u32[]{:S(2)}) collective-permute-start(bf16[2576,128]{1,0:T(8,128)(2,1)S(1)} %shard_map.65), channel_id=1, source_target_pairs={{0,192},{1,65},{64,0},{65,129},{128,64},{129,193},{192,128},{193,1... | collective-permute-start | bytes 1978376 | tf_op jit(solution)/shard_map/ppermute | solution.py:220
  102.0 15.6 %collective-permute-start.18 = (bf16[2064,128]{1,0:T(8,128)(2,1)S(1)}, bf16[2064,128]{1,0:T(8,128)(2,1)S(1)}, u32[]{:S(2)}, u32[]{:S(2)}) collective-permute-start(bf16[2064,128]{1,0:T(8,128)(2,1)S(1)} %shard_map.57), channel_id=1, source_target_pairs={{0,56},{1,9},{8,0},{9,17},{16,8},{17,25},{24,16},{25,33},{32,24},{... | collective-permute-start | bytes 1585160 | tf_op jit(solution)/shard_map/ppermute | solution.py:220
  114.5 15.7 %collective-permute-start.15 = (bf16[2064,128]{1,0:T(8,128)(2,1)S(1)}, bf16[2064,128]{1,0:T(8,128)(2,1)S(1)}, u32[]{:S(2)}, u32[]{:S(2)}) collective-permute-start(bf16[2064,128]{1,0:T(8,128)(2,1)S(1)} %shard_map.54), channel_id=1, source_target_pairs={{0,8},{1,57},{8,16},{9,1},{16,24},{17,9},{24,32},{25,17},{32,40},{... | collective-permute-start | bytes 1585160 | tf_op jit(solution)/shard_map/ppermute | solution.py:220
  116.6 16.2 %collective-permute-start.25 = (bf16[2576,128]{1,0:T(8,128)(2,1)S(1)}, bf16[2576,128]{1,0:T(8,128)(2,1)S(1)}, u32[]{:S(2)}, u32[]{:S(2)}) collective-permute-start(bf16[2576,128]{1,0:T(8,128)(2,1)S(1)} %shard_map.64), channel_id=1, source_target_pairs={{0,64},{1,193},{64,128},{65,1},{128,192},{129,65},{192,0},{193,129... | collective-permute-start | bytes 1978376 | tf_op jit(solution)/shard_map/ppermute | solution.py:220
  118.5 16.6 %collective-permute-start.19 = (bf16[2064,128]{1,0:T(8,128)(2,1)S(1)}, bf16[2064,128]{1,0:T(8,128)(2,1)S(1)}, u32[]{:S(2)}, u32[]{:S(2)}) collective-permute-start(bf16[2064,128]{1,0:T(8,128)(2,1)S(1)} %shard_map.58), channel_id=1, source_target_pairs={{0,56},{1,9},{8,0},{9,17},{16,8},{17,25},{24,16},{25,33},{32,24},{... | collective-permute-start | bytes 1585160 | tf_op jit(solution)/shard_map/ppermute | solution.py:220
  131.1 10.5 %collective-permute-start.16 = (bf16[2064,128]{1,0:T(8,128)(2,1)S(1)}, bf16[2064,128]{1,0:T(8,128)(2,1)S(1)}, u32[]{:S(2)}, u32[]{:S(2)}) collective-permute-start(bf16[2064,128]{1,0:T(8,128)(2,1)S(1)} %shard_map.55), channel_id=1, source_target_pairs={{0,8},{1,57},{8,16},{9,1},{16,24},{17,9},{24,32},{25,17},{32,40},{... | collective-permute-start | bytes 1585160 | tf_op jit(solution)/shard_map/ppermute | solution.py:220
  134.2 8.8 %collective-permute-start.27 = (bf16[1296,128]{1,0:T(8,128)(2,1)S(1)}, bf16[1296,128]{1,0:T(8,128)(2,1)S(1)}, u32[]{:S(2)}, u32[]{:S(2)}) collective-permute-start(bf16[1296,128]{1,0:T(8,128)(2,1)S(1)} %get-tuple-element.53), channel_id=1, source_target_pairs={{0,4},{4,0},{1,5},{5,1},{2,6},{6,2},{3,7},{7,3},{8,12},{12,8},{9,1... | collective-permute-start | bytes 995336 | tf_op jit(solution)/shard_map/ppermute | solution.py:205
  142.6 6.5 %collective-permute-start.20 = (bf16[128,1024]{1,0:T(8,128)(2,1)S(1)}, bf16[128,1024]{1,0:T(8,128)(2,1)S(1)}, u32[]{:S(2)}, u32[]{:S(2)}) collective-permute-start(bf16[128,1024]{1,0:T(8,128)(2,1)S(1)} %shard_map.60), channel_id=1, source_target_pairs={{0,4},{4,0},{1,5},{5,1},{2,6},{6,2},{3,7},{7,3},{8,12},{12,8},{9,1... | collective-permute-start | bytes 786440 | tf_op jit(solution)/shard_map/ppermute | solution.py:205

commit v3 on v2

--- a/solution.py
+++ b/solution.py
@@ -94,13 +94,64 @@
     for_tiles(rows, body, 0)
 
 
-def columns_kernel(half, h_ref, mine_ref, got_ref, out_ref):
+def columns_kernel(half, at_ref, mine_ref, got_ref, out_ref):
     for j in range(mine_ref.shape[1] // half):
         at = slice(j * half, (j + 1) * half)
-        mine_at = pl.multiple_of((2 * j + h_ref[0]) * half, LANES)
-        got_at = pl.multiple_of((2 * j + 1 - h_ref[0]) * half, LANES)
+        mine_at = pl.multiple_of((2 * at_ref[1 + j] + at_ref[0]) * half, LANES)
+        got_at = pl.multiple_of((2 * at_ref[1 + j] + 1 - at_ref[0]) * half, LANES)
         out_ref[:, pl.ds(mine_at, half)] = mine_ref[:, at]
         out_ref[:, pl.ds(got_at, half)] = got_ref[:, at]
+
+
+def first_kernel(at_ref, own_ref, got_ref, rest_ref, *refs):
+    ws, (out_ref, other_ref, v_ref) = refs[:-3], refs[-3:]
+    width, half = own_ref.shape[1], ws[0].shape[0]
+
+    @pl.when(at_ref[2] == 1)
+    def _():
+        other_ref[...] = got_ref[...]
+
+    @pl.when(at_ref[2] != 1)
+    def _():
+        other_ref[...] = rest_ref[...]
+
+    for j, w in enumerate(ws):
+        v_ref[:, j * half : (j + 1) * half] = dot(own_ref[...], w[:, :width], ((1,), (1,))) + dot(
+            other_ref[...], w[:, width:], ((1,), (1,))
+        )
+
+    def body(r, amax):
+        for j in range(v_ref.shape[1] // LANES):
+            amax = jnp.maximum(amax, jnp.abs(v_ref[pl.ds(r, TILE), j * LANES : (j + 1) * LANES]))
+        return amax
+
+    amax = for_tiles(v_ref.shape[0], body, jnp.zeros((TILE, LANES), F32))
+    write_coded(v_ref, v_ref.shape[1] // LANES, amax, out_ref)
+
+
+def first_sum(i, rows, core, own, got, rest, ws):
+    per = got.shape[0] // rows
+    width = own.shape[1]
+    shape = (rows, len(ws) * ws[0].shape[0])
+    out = coded_shape(*shape)
+    vmem = pl.BlockSpec(memory_space=pltpu.VMEM)
+    part = pl.BlockSpec((rows, width), lambda j, at: (at[1], 0))
+    at = [i, lax.rem(i, per), jnp.where(lax.div(i, per) == core, 1, 0)]
+    return pl.pallas_call(
+        first_kernel,
+        grid_spec=pltpu.PrefetchScalarGridSpec(
+            num_scalar_prefetch=1,
+            grid=(1,),
+            in_specs=[pl.BlockSpec((rows, width), lambda j, at: (at[0], 0)), part, part] + [vmem] * len(ws),
+            out_specs=whole(out.shape),
+            scratch_shapes=[pltpu.VMEM((rows, width), BF16), pltpu.VMEM(shape, F32)],
+        ),
+        out_shape=out,
+        compiler_params=pltpu.CompilerParams(vmem_limit_bytes=10 * MIB),
+        cost_estimate=pl.CostEstimate(
+            flops=4 * width * shape[0] * shape[1], bytes_accessed=4 * out.size, transcendentals=0
+        ),
+    )(jnp.stack([jnp.int32(k) for k in at]), own, got, rest, *ws)
 
 
 def owned_kernel(idx_ref, f_ref, b_ref, own_ref, mine_ref, out_ref, v_ref):
@@ -158,7 +209,7 @@
         out_shape=out_shapes,
         compiler_params=pltpu.CompilerParams(vmem_limit_bytes=10 * MIB),
         cost_estimate=pl.CostEstimate(flops=size * 8, bytes_accessed=size, transcendentals=0),
-    )(jnp.stack(idx).astype(jnp.int32), *args)
+    )(jnp.stack([jnp.int32(i) for i in idx]), *args)
 
 
 def placed_kernel(pieces, at_ref, *refs):
@@ -230,8 +281,12 @@
         if k == joint:
             ahead, back = [jnp.concatenate(ahead)], [jnp.concatenate(back)]
         if k in before:
-            ahead, back, *_ = after(*ahead, *back, *before[k])
-            ahead, back = [ahead], [back]
+            held = before[k](blocks)
+            if k < n - n // 2:
+                ahead, back, *_ = after(*ahead, *back, *held)
+                ahead, back = [ahead], [back]
+            else:
+                ahead = [after(*ahead, *held)[0]]
         if k == 1 and count == 2:
             ahead, back = blocks[-1], blocks[1] = [[f, ring(parts[1], axis, w)] for f, w in zip(out, (1, -1))]
             continue
@@ -248,11 +303,9 @@
     return arrays, pieces, (n * count * rows, width), blocks
 
 
-def outgoing(share, axis):
-    n, me = lax.axis_size(axis), lax.axis_index(axis)
-    step = 1 - 2 * lax.axis_index("c")
-    ahead, back = n // 2, n - n // 2 - 1
-    return hop([], share(lax.rem(me + step * ahead + n, n))), hop([], share(lax.rem(me - step * back + n, n)))
+def block_at(axis, k):
+    n = lax.axis_size(axis)
+    return lax.rem(lax.axis_index(axis) + (1 - 2 * lax.axis_index("c")) * k + n, n)
 
 
 def scattered(share, axis, first):
@@ -294,25 +347,35 @@
     w_sent = lax.dynamic_slice_in_dim(weight[0], (1 - h) * half, half, 0)
     out = [ring(acts_mine, "z", 1), ring(acts_mine, "z", -1)]
     *_, acts_got, w_got = after(*out, acts_got, swap(w_sent, "yl"))
-    arrays, pieces, shape, blocks = gathered([jnp.concatenate([w_mine, w_got], axis=1)], "x", (0,), 0, {2: []})
-    w_all = placed(arrays, pieces, shape)
-
-    before = {2: [w_got], 3: [blocks[-1][0], blocks[1][0]]}
-    arrays, acts_pieces, shape, blocks = gathered([acts_mine, acts_got], "z", (h, 1 - h), 2, before, out)
+    w_pair = jnp.concatenate([w_mine, w_got], axis=1)
+    *_, blocks = gathered([w_pair], "x", (0,), 0, {2: lambda b: b[1]})
+    near = [0, -1, 1, -2]
+    ws = [blocks[k][0] for k in near]
 
     part = tokens // 2
     g_sent = lax.dynamic_slice_in_dim(out_grad, c * part, part, 0)
-    g_sent = after(acts_got, w_got, g_sent)[2]
-    g_got = after(*blocks[-2], *blocks[2], y_ring(g_sent))[-1]
-    g_rest = swap(g_got, "c")
+    g_got = y_ring(after(acts_got, w_got, g_sent)[2])
+    first, gs = [], []
+
+    def first_sums(blocks):
+        got = after(*blocks[-2], *blocks[2], ws[-1], g_got)[-1]
+        gs.extend([out_grad, got, swap(got, "c")])
+        first.extend(first_sum(block_at("z", k), 2 * own_tokens, c, *gs, ws) for k in (4, -3))
+        return first
+
+    before = {2: lambda b: [w_got], 3: lambda b: [ws[-1]], 4: first_sums}
+    arrays, acts_pieces, shape, blocks = gathered([acts_mine, acts_got], "z", (h, 1 - h), 2, before, out)
+
+    ws = after(*first, *ws)[2:]
+    pieces = [(i, 0, half, 0, i * half) for i in range(owners)]
+    w_all = placed(ws, pieces, (owners * half, 2 * width))
     pieces = [(0, 0, tokens, 0, 0), (1, 0, part, width, c * part), (2, 0, part, width, (1 - c) * part)]
-    g_pair = placed([out_grad, g_got, g_rest], pieces, (tokens, 2 * width))
+    g_pair = placed(after(*first, *gs)[2:], pieces, (tokens, 2 * width))
 
     def of_tokens(i):
         count = 2 * own_tokens
         return dot(lax.dynamic_slice_in_dim(g_pair, i * count, count, 0), w_all, ((1,), (1,)))
 
-    first = outgoing(of_tokens, "z")
     acts_all = placed(after(*first, *arrays)[2:], acts_pieces, shape)
     came = scattered(of_tokens, "z", first)
     mine = of_tokens(lax.axis_index("z"))
@@ -323,13 +386,13 @@
 
     s_got = swap(finished(1 - h), "yl")
     shape = jax.ShapeDtypeStruct((own_tokens, features), BF16)
-    input_grad = call(functools.partial(columns_kernel, half), [h], [finished(h), s_got], None, [shape])[0]
+    input_grad = call(functools.partial(columns_kernel, half), [h] + [block_at("x", k) for k in near], [finished(h), s_got], None, [shape])[0]
 
     def of_rows(i):
         acts = lax.dynamic_slice_in_dim(acts_all, i * half, half, 1)
         return dot(acts, g_pair, ((0,), (0,)))
 
-    came = scattered(of_rows, "x", outgoing(of_rows, "x"))
+    came = scattered(of_rows, "x", [hop([], of_rows(block_at("x", k))) for k in (2, -1)])
     mine = of_rows(lax.axis_index("x"))
     shapes = [jax.ShapeDtypeStruct((half, width), F32), coded_shape(half, width)]
     owned, coded = call(owned_kernel, [jnp.int32(0)], came + [mine], None, shapes, [(half, width)])

time: 150 us -> 150 us (level); the launches traced: 150 us -> 147 us
  waiting for transfers between devices: 65.6 us -> 49 us
  Pallas kernels: 21.4 us -> 27.6 us
  starting transfers between devices: 41 us -> 46.4 us
  local copies, waits for them, and re-layouts: 5.39 us -> 9.33 us
  matrix products: 13.3 us -> 11.5 us
    ppermute x22, waiting for transfers between devices: 59.3 us -> 41.8 us  [ring(): return lax.ppermute(a, (axis, 'c'), perm)]
    pallas_call x0 -> x2, Pallas kernels: none -> 6.6 us  [first_sum(): pl.pallas_call(first_kernel, grid_spec=pltpu.PrefetchScalarGridSpec(num_s...]
    unnamed x28 -> x34, local copies, waits for them, and re-layouts: 1.97 us -> 5.82 us
    ppermute x22, starting transfers between devices: 35.8 us -> 38.7 us  [ring(): return lax.ppermute(a, (axis, 'c'), perm)]
    ppermute x5, starting transfers between devices: 3.58 us -> 6.04 us  [swap(): return lax.ppermute(a, axis, [(0, 1), (1, 0)])]
    dot_general x12 -> x10, matrix products: 13.3 us -> 11.5 us  [dot(): return lax.dot_general(a, b, (dims, ((), ())), preferred_element_type=F32)]
    pallas_call x15 -> x13, Pallas kernels: 13.7 us -> 14.5 us  [call(): pl.pallas_call(kernel, grid_spec=pltpu.PrefetchScalarGridSpec(num_scalar_...]
  transfers between devices with their start and end apart: 28 -> 28, of which waited for: 12 -> 10; matrix products, arithmetic and copies ran while one was open for 10% -> 8% of each run, Pallas kernels for 14% -> 18%
where the time goes in v3:
time: 150 us; the launch traced here: 147 us
  waiting for transfers between devices  49 us (33%)
  starting transfers between devices  46.4 us (31%)
  Pallas kernels  27.6 us (18%)
  matrix products  11.5 us (8%)
  local copies, waits for them, and re-layouts  9.33 us (6%)
  other arithmetic  2.44 us (2%)
    ppermute x22, waiting for transfers between devices, ring(): return lax.ppermute(a, (axis, 'c'), perm)  41.8 us
    ppermute x22, starting transfers between devices, ring(): return lax.ppermute(a, (axis, 'c'), perm)  38.7 us
    pallas_call x13, Pallas kernels, call(): pl.pallas_call(kernel, grid_spec=pltpu.PrefetchScalarGridSpec(num_scalar_...  14.5 us
    dot_general x10, matrix products, dot(): return lax.dot_general(a, b, (dims, ((), ())), preferred_element_type=F32)  11.5 us
    ppermute x5, waiting for transfers between devices, swap(): return lax.ppermute(a, axis, [(0, 1), (1, 0)])  7.21 us
    pallas_call x2, Pallas kernels, first_sum(): pl.pallas_call(first_kernel, grid_spec=pltpu.PrefetchScalarGridSpec(num_s...  6.6 us
    pallas_call x3, Pallas kernels, placed(): pl.pallas_call(functools.partial(placed_kernel, fixed), grid_spec=pltpu.P...  6.46 us
    ppermute x5, starting transfers between devices, swap(): return lax.ppermute(a, axis, [(0, 1), (1, 0)])  6.04 us
  transfers between devices with their start and end apart: 28, of which 10 were waited for; matrix products, arithmetic and copies ran while one was open for 8% of the time, Pallas kernels for 18%

profile of v3, /device:TPU:4, one launch (start us, length us, event | category | flops | bytes accessed | tf_op | source)
XLA Modules:
  0.0 147.4 jit_solution(13289172345414547551)
XLA Ops:
  0.6 1.3 fusion.30
  2.7 2.0 %dynamic-slice_bitcast_fusion = (bf16[256,640]{1,0:T(8,128)(2,1)}, bf16[256,640]{1,0:T(8,128)(2,1)}) fusion(bf16[1,512,640]{2,1,0:T(8,128)(2,1)} %param.5, s32[]{:T(128)S(6)} %select_n.63, s32[]{:T(128)S(6)} %select_n.62), kind=kLoop, calls=%fused_computation.23 | loop fusion | bytes 1310728 | tf_op jit(solution)/shard_map/dynamic_slice | solution.py:346
  4.7 1.6 %collective-permute-start.3 = (bf16[256,640]{1,0:T(8,128)(2,1)}, bf16[256,640]{1,0:T(8,128)(2,1)}, u32[]{:S(2)}, u32[]{:S(2)}) collective-permute-start(bf16[256,640]{1,0:T(8,128)(2,1)} %get-tuple-element.71), channel_id=1, source_target_pairs={{0,4},{4,0},{1,5},{5,1},{2,6},{6,2},{3,7},{7,3},{8,12},{12,8},{9,1... | collective-permute-start | bytes 983048 | tf_op jit(solution)/shard_map/ppermute | solution.py:256
  6.3 1.9 %collective-permute-start = (bf16[128,1024]{1,0:T(8,128)(2,1)S(1)}, bf16[128,1024]{1,0:T(8,128)(2,1)S(1)}, u32[]{:S(2)}, u32[]{:S(2)}) collective-permute-start(bf16[128,1024]{1,0:T(8,128)(2,1)S(1)} %get-tuple-element.57.refs_0_), channel_id=1, source_target_pairs={{0,8},{1,57},{8,16},{9,1},{16,24},{17,9},{24,32},{25,17},{32,40},{... | collective-permute-start | bytes 786440 | tf_op jit(solution)/shard_map/ppermute | solution.py:271
  8.2 3.9 %collective-permute-start.1 = (bf16[128,1024]{1,0:T(8,128)(2,1)S(1)}, bf16[128,1024]{1,0:T(8,128)(2,1)S(1)}, u32[]{:S(2)}, u32[]{:S(2)}) collective-permute-start(bf16[128,1024]{1,0:T(8,128)(2,1)S(1)} %get-tuple-element.57.refs_0_), channel_id=1, source_target_pairs={{0,56},{1,9},{8,0},{9,17},{16,8},{17,25},{24,16},{25,33},{32,24},{... | collective-permute-start | bytes 786440 | tf_op jit(solution)/shard_map/ppermute | solution.py:271
  12.6 5.1 %collective-permute-done.refs_2_ = bf16[128,1024]{1,0:T(8,128)(2,1)S(1)} collective-permute-done((bf16[128,1024]{1,0:T(8,128)(2,1)S(1)}, bf16[128,1024]{1,0:T(8,128)(2,1)S(1)}, u32[]{:S(2)}, u32[]{:S(2)}) %collective-permute-start) | collective-permute-done | bytes 262176 | tf_op jit(solution)/shard_map/ppermute | solution.py:271
  17.7 2.4 %collective-permute-done.2.refs_1_ = bf16[128,1024]{1,0:T(8,128)(2,1)} collective-permute-done((bf16[128,1024]{1,0:T(8,128)(2,1)}, bf16[128,1024]{1,0:T(8,128)(2,1)}, u32[]{:S(2)}, u32[]{:S(2)}) %collective-permute-start.2) | collective-permute-done | bytes 262176 | tf_op jit(solution)/shard_map/ppermute | solution.py:256
  20.1 1.2 pad_maximum_fusion.refs_0_
  21.3 1.3 collective-permute-start.8
  23.5 1.7 %collective-permute-start.11 = (bf16[1024,640]{1,0:T(8,128)(2,1)S(1)}, bf16[1024,640]{1,0:T(8,128)(2,1)}, u32[]{:S(2)}, u32[]{:S(2)}) collective-permute-start(bf16[1024,640]{1,0:T(8,128)(2,1)S(1)} %constant_dynamic-slice_fusion), channel_id=1, source_target_pairs={{0,4},{1,7},{4,2},{5,1},{2,6},{3,5},{6,0},{7,3},{8,12},{9,15},{12,... | collective-permute-start | bytes 3932168 | tf_op jit(solution)/shard_map/ppermute | solution.py:265
  25.2 1.9 %collective-permute-start.4 = (bf16[128,1024]{1,0:T(8,128)(2,1)}, bf16[128,1024]{1,0:T(8,128)(2,1)S(1)}, u32[]{:S(2)}, u32[]{:S(2)}) collective-permute-start(bf16[128,1024]{1,0:T(8,128)(2,1)} %collective-permute-done.2.refs_1_), channel_id=1, source_target_pairs={{0,8},{1,57},{8,16},{9,1},{16,24},{17,9},{24,32},{25,17},{32,40},{... | collective-permute-start | bytes 786440 | tf_op jit(solution)/shard_map/ppermute | solution.py:271
  27.1 3.9 %collective-permute-start.5 = (bf16[128,1024]{1,0:T(8,128)(2,1)}, bf16[128,1024]{1,0:T(8,128)(2,1)S(1)}, u32[]{:S(2)}, u32[]{:S(2)}) collective-permute-start(bf16[128,1024]{1,0:T(8,128)(2,1)} %collective-permute-done.2.refs_1_), channel_id=1, source_target_pairs={{0,56},{1,9},{8,0},{9,17},{16,8},{17,25},{24,16},{25,33},{32,24},{... | collective-permute-start | bytes 786440 | tf_op jit(solution)/shard_map/ppermute | solution.py:271
  31.0 7.0 %collective-permute-done.8.refs_1_ = bf16[256,1280]{1,0:T(8,128)(2,1)S(1)} collective-permute-done((bf16[256,1280]{1,0:T(8,128)(2,1)S(1)}, bf16[256,1280]{1,0:T(8,128)(2,1)S(1)}, u32[]{:S(2)}, u32[]{:S(2)}) %collective-permute-start.8) | collective-permute-done | bytes 655392 | tf_op jit(solution)/shard_map/ppermute | solution.py:271
  38.8 2.1 %collective-permute-start.10 = (bf16[256,1280]{1,0:T(8,128)(2,1)S(1)}, bf16[256,1280]{1,0:T(8,128)(2,1)S(1)}, u32[]{:S(2)}, u32[]{:S(2)}) collective-permute-start(bf16[256,1280]{1,0:T(8,128)(2,1)S(1)} %collective-permute-done.8.refs_1_), channel_id=1, source_target_pairs={{0,64},{1,193},{64,128},{65,1},{128,192},{129,65},{192,0},{193,129... | collective-permute-start | bytes 1966088 | tf_op jit(solution)/shard_map/ppermute | solution.py:271
  41.9 1.2 collective-permute-start.6
  43.2 4.0 %collective-permute-start.7 = (bf16[256,1024]{1,0:T(8,128)(2,1)S(1)}, bf16[256,1024]{1,0:T(8,128)(2,1)}, u32[]{:S(2)}, u32[]{:S(2)}) collective-permute-start(bf16[256,1024]{1,0:T(8,128)(2,1)S(1)} %pad_maximum_fusion.2), channel_id=1, source_target_pairs={{0,56},{1,9},{8,0},{9,17},{16,8},{17,25},{24,16},{25,33},{32,24},{... | collective-permute-start | bytes 1572872 | tf_op jit(solution)/shard_map/ppermute | solution.py:271
  47.2 12.2 %collective-permute-done.6.refs_6_ = bf16[256,1024]{1,0:T(8,128)(2,1)} collective-permute-done((bf16[256,1024]{1,0:T(8,128)(2,1)S(1)}, bf16[256,1024]{1,0:T(8,128)(2,1)}, u32[]{:S(2)}, u32[]{:S(2)}) %collective-permute-start.6) | collective-permute-done | bytes 524320 | tf_op jit(solution)/shard_map/ppermute | solution.py:271
  61.1 3.2 %collective-permute-start.22 = (bf16[256,1024]{1,0:T(8,128)(2,1)}, bf16[256,1024]{1,0:T(8,128)(2,1)S(1)}, u32[]{:S(2)}, u32[]{:S(2)}) collective-permute-start(bf16[256,1024]{1,0:T(8,128)(2,1)} %collective-permute-done.7.refs_7_), channel_id=1, source_target_pairs={{0,56},{1,9},{8,0},{9,17},{16,8},{17,25},{24,16},{25,33},{32,24},{... | collective-permute-start | bytes 1572872 | tf_op jit(solution)/shard_map/ppermute | solution.py:271
  64.3 1.1 copy-done.2
  65.4 1.1 copy-done.4
  66.5 1.1 copy-done.6
  67.6 3.4 %shard_map.50 = bf16[2064,128]{1,0:T(8,128)(2,1)S(1)} custom-call(s32[3]{0:T(128)S(1)} %pad_add_fusion.1.at_ref, bf16[2048,640]{1,0:T(8,128)(2,1)S(1)} %copy-done, bf16[1024,640]{1,0:T(8,128)(2,1)} %collective-permute-done.11.got_ref.refs_1_, bf16[1024,640]{1,0:T(8,128)(2,1)} %collective-permute-done.12.rest_ref.refs_2_, ...), custom_call_target="tpu_custom_call" | custom-call | flops 671088640 | bytes 1056768 | tf_op jit(solution)/shard_map/pallas_call | solution.py:140
  71.1 3.2 %shard_map.51 = bf16[2064,128]{1,0:T(8,128)(2,1)S(1)} custom-call(s32[3]{0:T(128)S(1)} %pad_add_fusion.3.at_ref, bf16[2048,640]{1,0:T(8,128)(2,1)S(1)} %copy-done, bf16[1024,640]{1,0:T(8,128)(2,1)} %collective-permute-done.11.got_ref.refs_1_, bf16[1024,640]{1,0:T(8,128)(2,1)} %collective-permute-done.12.rest_ref.refs_2_, ...), custom_call_target="tpu_custom_call" | custom-call | flops 671088640 | bytes 1056768 | tf_op jit(solution)/shard_map/pallas_call | solution.py:140
  74.3 3.3 %collective-permute-start.17 = (bf16[2064,128]{1,0:T(8,128)(2,1)S(1)}, bf16[2064,128]{1,0:T(8,128)(2,1)S(1)}, u32[]{:S(2)}, u32[]{:S(2)}) collective-permute-start(bf16[2064,128]{1,0:T(8,128)(2,1)S(1)} %shard_map.51), channel_id=1, source_target_pairs={{0,56},{1,9},{8,0},{9,17},{16,8},{17,25},{24,16},{25,33},{32,24},{... | collective-permute-start | bytes 1585160 | tf_op jit(solution)/shard_map/ppermute | solution.py:271
  77.6 2.7 %shard_map.52 = bf16[2048,1280]{1,0:T(8,128)(2,1)S(1)} custom-call(s32[3]{0:T(128)S(1)} %pad_add_fusion.2.at_ref, bf16[2048,640]{1,0:T(8,128)(2,1)S(1)} %copy-done, bf16[1024,640]{1,0:T(8,128)(2,1)} %collective-permute-done.11.got_ref.refs_1_, bf16[1024,640]{1,0:T(8,128)(2,1)} %collective-permute-done.12.rest_ref.refs_2_), custom_call_target="tpu_custom_call" | custom-call | bytes 10485760 | tf_op jit(solution)/shard_map/pallas_call | solution.py:231
  80.3 1.4 shard_map.53
  85.4 8.8 %collective-permute-done.23.refs_10_ = bf16[256,1024]{1,0:T(8,128)(2,1)S(1)} collective-permute-done((bf16[256,1024]{1,0:T(8,128)(2,1)S(1)}, bf16[256,1024]{1,0:T(8,128)(2,1)S(1)}, u32[]{:S(2)}, u32[]{:S(2)}) %collective-permute-start.23) | collective-permute-done | bytes 524320 | tf_op jit(solution)/shard_map/ppermute | solution.py:271
  94.3 2.3 %shard_map.62 = bf16[2048,1024]{1,0:T(8,128)(2,1)S(1)} custom-call(s32[16]{0:T(128)S(1)} %stack.151.at_ref, bf16[128,1024]{1,0:T(8,128)(2,1)S(1)} %get-tuple-element.57.refs_0_, bf16[128,1024]{1,0:T(8,128)(2,1)} %collective-permute-done.2.refs_1_, bf16[128,1024]{1,0:T(8,128)(2,1)S(1)} %copy-done.9, bf16[128,1024]{1,0:T(8,128)(2,1)S(1)} %copy-done.14, ...), custom_call_target="tpu_custom_call" | custom-call | bytes 8388608 | tf_op jit(solution)/shard_map/pallas_call | solution.py:231
  97.6 1.6 %fusion.6.refs_0_ = f32[256,1280]{1,0:T(8,128)S(1)} fusion(bf16[2048,1280]{1,0:T(8,128)(2,1)S(1)} %shard_map.52, bf16[2048,1024]{1,0:T(8,128)(2,1)S(1)} %shard_map.62, s32[]{:T(128)S(6)} %select_n.72), kind=kOutput, calls=%fused_computation.6 | convolution fusion | flops 1342177280 | bytes 7602180 | tf_op jit(solution)/shard_map/dot_general | solution.py:324
  99.9 1.1 collective-permute-start.24
  100.9 1.6 %fusion.4.refs_1_ = f32[256,1280]{1,0:T(8,128)S(1)} fusion(bf16[2048,1280]{1,0:T(8,128)(2,1)S(1)} %shard_map.52, bf16[2048,1024]{1,0:T(8,128)(2,1)S(1)} %shard_map.62, s32[]{:T(128)S(6)} %select_n.73), kind=kOutput, calls=%fused_computation.4 | convolution fusion | flops 1342177280 | bytes 7602180 | tf_op jit(solution)/shard_map/dot_general | solution.py:324
  103.5 3.5 %collective-permute-start.18 = (bf16[2064,128]{1,0:T(8,128)(2,1)S(1)}, bf16[2064,128]{1,0:T(8,128)(2,1)S(1)}, u32[]{:S(2)}, u32[]{:S(2)}) collective-permute-start(bf16[2064,128]{1,0:T(8,128)(2,1)S(1)} %shard_map.57), channel_id=1, source_target_pairs={{0,56},{1,9},{8,0},{9,17},{16,8},{17,25},{24,16},{25,33},{32,24},{... | collective-permute-start | bytes 1585160 | tf_op jit(solution)/shard_map/ppermute | solution.py:271
  107.0 1.1 collective-permute-done.14.refs_0_
  109.1 1.6 %fusion.2.refs_0_ = f32[256,1280]{1,0:T(8,128)S(1)} fusion(bf16[2048,1280]{1,0:T(8,128)(2,1)S(1)} %shard_map.52, bf16[2048,1024]{1,0:T(8,128)(2,1)S(1)} %shard_map.62, s32[]{:T(128)S(6)} %select_n.74), kind=kOutput, calls=%fused_computation.2 | convolution fusion | flops 1342177280 | bytes 7602180 | tf_op jit(solution)/shard_map/dot_general | solution.py:324
  111.4 1.1 shard_map.64
  112.5 2.1 %collective-permute-start.25 = (bf16[2576,128]{1,0:T(8,128)(2,1)S(1)}, bf16[2576,128]{1,0:T(8,128)(2,1)S(1)}, u32[]{:S(2)}, u32[]{:S(2)}) collective-permute-start(bf16[2576,128]{1,0:T(8,128)(2,1)S(1)} %shard_map.64), channel_id=1, source_target_pairs={{0,64},{1,193},{64,128},{65,1},{128,192},{129,65},{192,0},{193,129... | collective-permute-start | bytes 1978376 | tf_op jit(solution)/shard_map/ppermute | solution.py:271
  115.5 3.6 %collective-permute-done.18.refs_0_ = bf16[2064,128]{1,0:T(8,128)(2,1)S(1)} collective-permute-done((bf16[2064,128]{1,0:T(8,128)(2,1)S(1)}, bf16[2064,128]{1,0:T(8,128)(2,1)S(1)}, u32[]{:S(2)}, u32[]{:S(2)}) %collective-permute-start.18) | collective-permute-done | bytes 528416 | tf_op jit(solution)/shard_map/ppermute | solution.py:271
  120.0 3.8 %collective-permute-start.19 = (bf16[2064,128]{1,0:T(8,128)(2,1)S(1)}, bf16[2064,128]{1,0:T(8,128)(2,1)S(1)}, u32[]{:S(2)}, u32[]{:S(2)}) collective-permute-start(bf16[2064,128]{1,0:T(8,128)(2,1)S(1)} %shard_map.58), channel_id=1, source_target_pairs={{0,56},{1,9},{8,0},{9,17},{16,8},{17,25},{24,16},{25,33},{32,24},{... | collective-permute-start | bytes 1585160 | tf_op jit(solution)/shard_map/ppermute | solution.py:271
  124.7 1.6 %fusion.own_ref = f32[256,1280]{1,0:T(8,128)S(1)} fusion(bf16[2048,1280]{1,0:T(8,128)(2,1)S(1)} %shard_map.52, bf16[2048,1024]{1,0:T(8,128)(2,1)S(1)} %shard_map.62, s32[]{:T(128)S(6)} %select_n.75), kind=kOutput, calls=%fused_computation | convolution fusion | flops 1342177280 | bytes 7602180 | tf_op jit(solution)/shard_map/dot_general | solution.py:324
  126.3 1.1 collective-permute-done.26.b_ref
  127.4 2.0 %shard_map.66 = (f32[256,640]{1,0:T(8,128)S(1)}, bf16[1296,128]{1,0:T(8,128)(2,1)}) custom-call(s32[1]{0:T(128)} %constant.82.clone.1.idx_ref, bf16[2576,128]{1,0:T(8,128)(2,1)S(1)} %collective-permute-done.25.f_ref, bf16[2576,128]{1,0:T(8,128)(2,1)S(1)} %collective-permute-done.26.b_ref, f32[256,1280]{1,0:T(8,128)S(1)} %fusion.own_ref), custom_call_target="tpu_custom_call" | custom-call | flops 42139648 | bytes 5267456 | tf_op jit(solution)/shard_map/pallas_call | solution.py:200
  129.5 2.1 %collective-permute-start.27 = (bf16[1296,128]{1,0:T(8,128)(2,1)}, bf16[1296,128]{1,0:T(8,128)(2,1)S(1)}, u32[]{:S(2)}, u32[]{:S(2)}) collective-permute-start(bf16[1296,128]{1,0:T(8,128)(2,1)} %get-tuple-element.69), channel_id=1, source_target_pairs={{0,4},{4,0},{1,5},{5,1},{2,6},{6,2},{3,7},{7,3},{8,12},{12,8},{9,1... | collective-permute-start | bytes 995336 | tf_op jit(solution)/shard_map/ppermute | solution.py:256
  132.4 2.9 %collective-permute-done.19.b_ref = bf16[2064,128]{1,0:T(8,128)(2,1)S(1)} collective-permute-done((bf16[2064,128]{1,0:T(8,128)(2,1)S(1)}, bf16[2064,128]{1,0:T(8,128)(2,1)S(1)}, u32[]{:S(2)}, u32[]{:S(2)}) %collective-permute-start.19) | collective-permute-done | bytes 528416 | tf_op jit(solution)/shard_map/ppermute | solution.py:271
  135.3 1.7 %shard_map.60 = bf16[128,1024]{1,0:T(8,128)(2,1)} custom-call(s32[2]{0:T(128)S(1)} %pad_add_fusion.4.idx_ref, bf16[2064,128]{1,0:T(8,128)(2,1)S(1)} %collective-permute-done.16.f_ref, bf16[2064,128]{1,0:T(8,128)(2,1)S(1)} %collective-permute-done.19.b_ref, f32[256,1024]{1,0:T(8,128)S(1)} %fusion.8.own_ref), custom_call_target="tpu_custom_call" | custom-call | flops 29491200 | bytes 3686400 | tf_op jit(solution)/shard_map/pallas_call | solution.py:200
  137.0 1.6 %collective-permute-start.20 = (bf16[128,1024]{1,0:T(8,128)(2,1)}, bf16[128,1024]{1,0:T(8,128)(2,1)S(1)}, u32[]{:S(2)}, u32[]{:S(2)}) collective-permute-start(bf16[128,1024]{1,0:T(8,128)(2,1)} %shard_map.60), channel_id=1, source_target_pairs={{0,4},{4,0},{1,5},{5,1},{2,6},{6,2},{3,7},{7,3},{8,12},{12,8},{9,1... | collective-permute-start | bytes 786440 | tf_op jit(solution)/shard_map/ppermute | solution.py:256
  139.8 1.4 shard_map.67
  141.2 4.8 %collective-permute-done.20.got_ref = bf16[128,1024]{1,0:T(8,128)(2,1)S(1)} collective-permute-done((bf16[128,1024]{1,0:T(8,128)(2,1)}, bf16[128,1024]{1,0:T(8,128)(2,1)S(1)}, u32[]{:S(2)}, u32[]{:S(2)}) %collective-permute-start.20) | collective-permute-done | bytes 262176 | tf_op jit(solution)/shard_map/ppermute | solution.py:256
  146.0 1.4 shard_map.61
  (85 shorter events, 18.4 us)
Async XLA Ops:
  0.6 22.8 %copy-start = (bf16[2048,640]{1,0:T(8,128)(2,1)S(1)}, bf16[2048,640]{1,0:T(8,128)(2,1)}, u32[]{:S(2)}) copy-start(bf16[2048,640]{1,0:T(8,128)(2,1)} %refs_0_) | copy-start | bytes 7864324
  4.7 15.4 %collective-permute-start.3 = (bf16[256,640]{1,0:T(8,128)(2,1)}, bf16[256,640]{1,0:T(8,128)(2,1)}, u32[]{:S(2)}, u32[]{:S(2)}) collective-permute-start(bf16[256,640]{1,0:T(8,128)(2,1)} %get-tuple-element.71), channel_id=1, source_target_pairs={{0,4},{4,0},{1,5},{5,1},{2,6},{6,2},{3,7},{7,3},{8,12},{12,8},{9,1... | collective-permute-start | bytes 983048 | tf_op jit(solution)/shard_map/ppermute | solution.py:256
  6.3 11.4 %collective-permute-start = (bf16[128,1024]{1,0:T(8,128)(2,1)S(1)}, bf16[128,1024]{1,0:T(8,128)(2,1)S(1)}, u32[]{:S(2)}, u32[]{:S(2)}) collective-permute-start(bf16[128,1024]{1,0:T(8,128)(2,1)S(1)} %get-tuple-element.57.refs_0_), channel_id=1, source_target_pairs={{0,8},{1,57},{8,16},{9,1},{16,24},{17,9},{24,32},{25,17},{32,40},{... | collective-permute-start | bytes 786440 | tf_op jit(solution)/shard_map/ppermute | solution.py:271
  8.2 9.5 %collective-permute-start.1 = (bf16[128,1024]{1,0:T(8,128)(2,1)S(1)}, bf16[128,1024]{1,0:T(8,128)(2,1)S(1)}, u32[]{:S(2)}, u32[]{:S(2)}) collective-permute-start(bf16[128,1024]{1,0:T(8,128)(2,1)S(1)} %get-tuple-element.57.refs_0_), channel_id=1, source_target_pairs={{0,56},{1,9},{8,0},{9,17},{16,8},{17,25},{24,16},{25,33},{32,24},{... | collective-permute-start | bytes 786440 | tf_op jit(solution)/shard_map/ppermute | solution.py:271
  12.1 7.9 %collective-permute-start.2 = (bf16[128,1024]{1,0:T(8,128)(2,1)}, bf16[128,1024]{1,0:T(8,128)(2,1)}, u32[]{:S(2)}, u32[]{:S(2)}) collective-permute-start(bf16[128,1024]{1,0:T(8,128)(2,1)} %get-tuple-element.38), channel_id=1, source_target_pairs={{0,4},{4,0},{1,5},{5,1},{2,6},{6,2},{3,7},{7,3},{8,12},{12,8},{9,1... | collective-permute-start | bytes 786440 | tf_op jit(solution)/shard_map/ppermute | solution.py:256
  17.7 2.4 %copy-start.7 = (bf16[128,1024]{1,0:T(8,128)(2,1)}, bf16[128,1024]{1,0:T(8,128)(2,1)S(1)}, u32[]{:S(2)}) copy-start(bf16[128,1024]{1,0:T(8,128)(2,1)S(1)} %collective-permute-done.refs_2_) | copy-start | bytes 786436
  17.7 2.4 %copy-start.10 = (bf16[128,1024]{1,0:T(8,128)(2,1)}, bf16[128,1024]{1,0:T(8,128)(2,1)S(1)}, u32[]{:S(2)}) copy-start(bf16[128,1024]{1,0:T(8,128)(2,1)S(1)} %collective-permute-done.1.refs_4_) | copy-start | bytes 786436
  20.1 21.7 %copy-start.8 = (bf16[128,1024]{1,0:T(8,128)(2,1)S(1)}, bf16[128,1024]{1,0:T(8,128)(2,1)}, u32[]{:S(2)}) copy-start(bf16[128,1024]{1,0:T(8,128)(2,1)} %copy-done.7) | copy-start | bytes 786436
  20.1 21.8 %copy-start.11 = (bf16[128,1024]{1,0:T(8,128)(2,1)S(1)}, bf16[128,1024]{1,0:T(8,128)(2,1)}, u32[]{:S(2)}) copy-start(bf16[128,1024]{1,0:T(8,128)(2,1)} %copy-done.10) | copy-start | bytes 786436
  21.3 16.7 %collective-permute-start.8 = (bf16[256,1280]{1,0:T(8,128)(2,1)S(1)}, bf16[256,1280]{1,0:T(8,128)(2,1)S(1)}, u32[]{:S(2)}, u32[]{:S(2)}) collective-permute-start(bf16[256,1280]{1,0:T(8,128)(2,1)S(1)} %pad_maximum_fusion.refs_0_), channel_id=1, source_target_pairs={{0,64},{1,193},{64,128},{65,1},{128,192},{129,65},{192,0},{193,129... | collective-permute-start | bytes 1966088 | tf_op jit(solution)/shard_map/ppermute | solution.py:271
  22.6 15.4 %collective-permute-start.9 = (bf16[256,1280]{1,0:T(8,128)(2,1)S(1)}, bf16[256,1280]{1,0:T(8,128)(2,1)S(1)}, u32[]{:S(2)}, u32[]{:S(2)}) collective-permute-start(bf16[256,1280]{1,0:T(8,128)(2,1)S(1)} %pad_maximum_fusion.refs_0_), channel_id=1, source_target_pairs={{0,192},{1,65},{64,0},{65,129},{128,64},{129,193},{192,128},{193,1... | collective-permute-start | bytes 1966088 | tf_op jit(solution)/shard_map/ppermute | solution.py:271
  23.5 36.8 %collective-permute-start.11 = (bf16[1024,640]{1,0:T(8,128)(2,1)S(1)}, bf16[1024,640]{1,0:T(8,128)(2,1)}, u32[]{:S(2)}, u32[]{:S(2)}) collective-permute-start(bf16[1024,640]{1,0:T(8,128)(2,1)S(1)} %constant_dynamic-slice_fusion), channel_id=1, source_target_pairs={{0,4},{1,7},{4,2},{5,1},{2,6},{3,5},{6,0},{7,3},{8,12},{9,15},{12,... | collective-permute-start | bytes 3932168 | tf_op jit(solution)/shard_map/ppermute | solution.py:265
  25.2 16.7 %collective-permute-start.4 = (bf16[128,1024]{1,0:T(8,128)(2,1)}, bf16[128,1024]{1,0:T(8,128)(2,1)S(1)}, u32[]{:S(2)}, u32[]{:S(2)}) collective-permute-start(bf16[128,1024]{1,0:T(8,128)(2,1)} %collective-permute-done.2.refs_1_), channel_id=1, source_target_pairs={{0,8},{1,57},{8,16},{9,1},{16,24},{17,9},{24,32},{25,17},{32,40},{... | collective-permute-start | bytes 786440 | tf_op jit(solution)/shard_map/ppermute | solution.py:271
  27.1 14.8 %collective-permute-start.5 = (bf16[128,1024]{1,0:T(8,128)(2,1)}, bf16[128,1024]{1,0:T(8,128)(2,1)S(1)}, u32[]{:S(2)}, u32[]{:S(2)}) collective-permute-start(bf16[128,1024]{1,0:T(8,128)(2,1)} %collective-permute-done.2.refs_1_), channel_id=1, source_target_pairs={{0,56},{1,9},{8,0},{9,17},{16,8},{17,25},{24,16},{25,33},{32,24},{... | collective-permute-start | bytes 786440 | tf_op jit(solution)/shard_map/ppermute | solution.py:271
  38.0 0.9 copy-start.3
  38.8 20.6 %collective-permute-start.10 = (bf16[256,1280]{1,0:T(8,128)(2,1)S(1)}, bf16[256,1280]{1,0:T(8,128)(2,1)S(1)}, u32[]{:S(2)}, u32[]{:S(2)}) collective-permute-start(bf16[256,1280]{1,0:T(8,128)(2,1)S(1)} %collective-permute-done.8.refs_1_), channel_id=1, source_target_pairs={{0,64},{1,193},{64,128},{65,1},{128,192},{129,65},{192,0},{193,129... | collective-permute-start | bytes 1966088 | tf_op jit(solution)/shard_map/ppermute | solution.py:271
  41.0 0.8 copy-start.1
  41.8 17.6 %copy-start.13 = (bf16[128,1024]{1,0:T(8,128)(2,1)}, bf16[128,1024]{1,0:T(8,128)(2,1)S(1)}, u32[]{:S(2)}) copy-start(bf16[128,1024]{1,0:T(8,128)(2,1)S(1)} %collective-permute-done.4.refs_3_) | copy-start | bytes 786436
  41.9 18.4 %copy-start.15 = (bf16[128,1024]{1,0:T(8,128)(2,1)}, bf16[128,1024]{1,0:T(8,128)(2,1)S(1)}, u32[]{:S(2)}) copy-start(bf16[128,1024]{1,0:T(8,128)(2,1)S(1)} %collective-permute-done.5.refs_5_) | copy-start | bytes 786436
  41.9 17.5 %collective-permute-start.6 = (bf16[256,1024]{1,0:T(8,128)(2,1)S(1)}, bf16[256,1024]{1,0:T(8,128)(2,1)}, u32[]{:S(2)}, u32[]{:S(2)}) collective-permute-start(bf16[256,1024]{1,0:T(8,128)(2,1)S(1)} %pad_maximum_fusion.1), channel_id=1, source_target_pairs={{0,8},{1,57},{8,16},{9,1},{16,24},{17,9},{24,32},{25,17},{32,40},{... | collective-permute-start | bytes 1572872 | tf_op jit(solution)/shard_map/ppermute | solution.py:271
  43.2 16.3 %collective-permute-start.7 = (bf16[256,1024]{1,0:T(8,128)(2,1)S(1)}, bf16[256,1024]{1,0:T(8,128)(2,1)}, u32[]{:S(2)}, u32[]{:S(2)}) collective-permute-start(bf16[256,1024]{1,0:T(8,128)(2,1)S(1)} %pad_maximum_fusion.2), channel_id=1, source_target_pairs={{0,56},{1,9},{8,0},{9,17},{16,8},{17,25},{24,16},{25,33},{32,24},{... | collective-permute-start | bytes 1572872 | tf_op jit(solution)/shard_map/ppermute | solution.py:271
  59.4 0.8 copy-start.5
  60.3 4.0 %collective-permute-start.12 = (bf16[1024,640]{1,0:T(8,128)(2,1)}, bf16[1024,640]{1,0:T(8,128)(2,1)}, u32[]{:S(2)}, u32[]{:S(2)}) collective-permute-start(bf16[1024,640]{1,0:T(8,128)(2,1)} %collective-permute-done.11.got_ref.refs_1_), channel_id=1, source_target_pairs={{0,1},{1,0},{2,3},{3,2},{4,5},{5,4},{6,7},{7,6},{8,9},{9,8},{10,11... | collective-permute-start | bytes 3932168 | tf_op jit(solution)/shard_map/ppermute | solution.py:256
  61.1 22.4 %collective-permute-start.21 = (bf16[256,1024]{1,0:T(8,128)(2,1)}, bf16[256,1024]{1,0:T(8,128)(2,1)S(1)}, u32[]{:S(2)}, u32[]{:S(2)}) collective-permute-start(bf16[256,1024]{1,0:T(8,128)(2,1)} %collective-permute-done.6.refs_6_), channel_id=1, source_target_pairs={{0,8},{1,57},{8,16},{9,1},{16,24},{17,9},{24,32},{25,17},{32,40},{... | collective-permute-start | bytes 1572872 | tf_op jit(solution)/shard_map/ppermute | solution.py:271
  61.1 24.3 %collective-permute-start.22 = (bf16[256,1024]{1,0:T(8,128)(2,1)}, bf16[256,1024]{1,0:T(8,128)(2,1)S(1)}, u32[]{:S(2)}, u32[]{:S(2)}) collective-permute-start(bf16[256,1024]{1,0:T(8,128)(2,1)} %collective-permute-done.7.refs_7_), channel_id=1, source_target_pairs={{0,56},{1,9},{8,0},{9,17},{16,8},{17,25},{24,16},{25,33},{32,24},{... | collective-permute-start | bytes 1572872 | tf_op jit(solution)/shard_map/ppermute | solution.py:271
  64.3 1.1 copy-start.2
  65.4 1.1 copy-start.4
  66.5 1.1 copy-start.6
  71.0 25.6 %collective-permute-start.13 = (bf16[2064,128]{1,0:T(8,128)(2,1)S(1)}, bf16[2064,128]{1,0:T(8,128)(2,1)S(1)}, u32[]{:S(2)}, u32[]{:S(2)}) collective-permute-start(bf16[2064,128]{1,0:T(8,128)(2,1)S(1)} %shard_map.50), channel_id=1, source_target_pairs={{0,8},{1,57},{8,16},{9,1},{16,24},{17,9},{24,32},{25,17},{32,40},{... | collective-permute-start | bytes 1585160 | tf_op jit(solution)/shard_map/ppermute | solution.py:271
  74.3 28.2 %collective-permute-start.17 = (bf16[2064,128]{1,0:T(8,128)(2,1)S(1)}, bf16[2064,128]{1,0:T(8,128)(2,1)S(1)}, u32[]{:S(2)}, u32[]{:S(2)}) collective-permute-start(bf16[2064,128]{1,0:T(8,128)(2,1)S(1)} %shard_map.51), channel_id=1, source_target_pairs={{0,56},{1,9},{8,0},{9,17},{16,8},{17,25},{24,16},{25,33},{32,24},{... | collective-permute-start | bytes 1585160 | tf_op jit(solution)/shard_map/ppermute | solution.py:271
  83.5 10.7 %collective-permute-start.23 = (bf16[256,1024]{1,0:T(8,128)(2,1)S(1)}, bf16[256,1024]{1,0:T(8,128)(2,1)S(1)}, u32[]{:S(2)}, u32[]{:S(2)}) collective-permute-start(bf16[256,1024]{1,0:T(8,128)(2,1)S(1)} %collective-permute-done.21.refs_8_), channel_id=1, source_target_pairs={{0,8},{1,57},{8,16},{9,1},{16,24},{17,9},{24,32},{25,17},{32,40},{... | collective-permute-start | bytes 1572872 | tf_op jit(solution)/shard_map/ppermute | solution.py:271
  84.5 9.8 %copy-start.9 = (bf16[128,1024]{1,0:T(8,128)(2,1)S(1)}, bf16[128,1024]{1,0:T(8,128)(2,1)}, u32[]{:S(2)}) copy-start(bf16[128,1024]{1,0:T(8,128)(2,1)} %copy-done.7) | copy-start | bytes 786436
  84.5 9.8 %copy-start.12 = (bf16[128,1024]{1,0:T(8,128)(2,1)S(1)}, bf16[128,1024]{1,0:T(8,128)(2,1)}, u32[]{:S(2)}) copy-start(bf16[128,1024]{1,0:T(8,128)(2,1)} %copy-done.10) | copy-start | bytes 786436
  84.5 9.7 %copy-start.14 = (bf16[128,1024]{1,0:T(8,128)(2,1)S(1)}, bf16[128,1024]{1,0:T(8,128)(2,1)}, u32[]{:S(2)}) copy-start(bf16[128,1024]{1,0:T(8,128)(2,1)} %copy-done.13) | copy-start | bytes 786436
  84.5 9.7 %copy-start.16 = (bf16[128,1024]{1,0:T(8,128)(2,1)S(1)}, bf16[128,1024]{1,0:T(8,128)(2,1)}, u32[]{:S(2)}) copy-start(bf16[128,1024]{1,0:T(8,128)(2,1)} %copy-done.15) | copy-start | bytes 786436
  97.5 10.5 %collective-permute-start.14 = (bf16[2064,128]{1,0:T(8,128)(2,1)S(1)}, bf16[2064,128]{1,0:T(8,128)(2,1)S(1)}, u32[]{:S(2)}, u32[]{:S(2)}) collective-permute-start(bf16[2064,128]{1,0:T(8,128)(2,1)S(1)} %shard_map.54), channel_id=1, source_target_pairs={{0,8},{1,57},{8,16},{9,1},{16,24},{17,9},{24,32},{25,17},{32,40},{... | collective-permute-start | bytes 1585160 | tf_op jit(solution)/shard_map/ppermute | solution.py:271
  99.9 11.5 %collective-permute-start.24 = (bf16[2576,128]{1,0:T(8,128)(2,1)S(1)}, bf16[2576,128]{1,0:T(8,128)(2,1)S(1)}, u32[]{:S(2)}, u32[]{:S(2)}) collective-permute-start(bf16[2576,128]{1,0:T(8,128)(2,1)S(1)} %shard_map.63), channel_id=1, source_target_pairs={{0,64},{1,193},{64,128},{65,1},{128,192},{129,65},{192,0},{193,129... | collective-permute-start | bytes 1978376 | tf_op jit(solution)/shard_map/ppermute | solution.py:271
  103.5 15.6 %collective-permute-start.18 = (bf16[2064,128]{1,0:T(8,128)(2,1)S(1)}, bf16[2064,128]{1,0:T(8,128)(2,1)S(1)}, u32[]{:S(2)}, u32[]{:S(2)}) collective-permute-start(bf16[2064,128]{1,0:T(8,128)(2,1)S(1)} %shard_map.57), channel_id=1, source_target_pairs={{0,56},{1,9},{8,0},{9,17},{16,8},{17,25},{24,16},{25,33},{32,24},{... | collective-permute-start | bytes 1585160 | tf_op jit(solution)/shard_map/ppermute | solution.py:271
  109.0 14.8 %collective-permute-start.15 = (bf16[2064,128]{1,0:T(8,128)(2,1)S(1)}, bf16[2064,128]{1,0:T(8,128)(2,1)S(1)}, u32[]{:S(2)}, u32[]{:S(2)}) collective-permute-start(bf16[2064,128]{1,0:T(8,128)(2,1)S(1)} %shard_map.55), channel_id=1, source_target_pairs={{0,8},{1,57},{8,16},{9,1},{16,24},{17,9},{24,32},{25,17},{32,40},{... | collective-permute-start | bytes 1585160 | tf_op jit(solution)/shard_map/ppermute | solution.py:271
  111.3 16.1 %collective-permute-start.26 = (bf16[2576,128]{1,0:T(8,128)(2,1)S(1)}, bf16[2576,128]{1,0:T(8,128)(2,1)S(1)}, u32[]{:S(2)}, u32[]{:S(2)}) collective-permute-start(bf16[2576,128]{1,0:T(8,128)(2,1)S(1)} %shard_map.65), channel_id=1, source_target_pairs={{0,192},{1,65},{64,0},{65,129},{128,64},{129,193},{192,128},{193,1... | collective-permute-start | bytes 1978376 | tf_op jit(solution)/shard_map/ppermute | solution.py:271
  112.5 14.9 %collective-permute-start.25 = (bf16[2576,128]{1,0:T(8,128)(2,1)S(1)}, bf16[2576,128]{1,0:T(8,128)(2,1)S(1)}, u32[]{:S(2)}, u32[]{:S(2)}) collective-permute-start(bf16[2576,128]{1,0:T(8,128)(2,1)S(1)} %shard_map.64), channel_id=1, source_target_pairs={{0,64},{1,193},{64,128},{65,1},{128,192},{129,65},{192,0},{193,129... | collective-permute-start | bytes 1978376 | tf_op jit(solution)/shard_map/ppermute | solution.py:271
  120.0 15.4 %collective-permute-start.19 = (bf16[2064,128]{1,0:T(8,128)(2,1)S(1)}, bf16[2064,128]{1,0:T(8,128)(2,1)S(1)}, u32[]{:S(2)}, u32[]{:S(2)}) collective-permute-start(bf16[2064,128]{1,0:T(8,128)(2,1)S(1)} %shard_map.58), channel_id=1, source_target_pairs={{0,56},{1,9},{8,0},{9,17},{16,8},{17,25},{24,16},{25,33},{32,24},{... | collective-permute-start | bytes 1585160 | tf_op jit(solution)/shard_map/ppermute | solution.py:271
  124.6 10.7 %collective-permute-start.16 = (bf16[2064,128]{1,0:T(8,128)(2,1)S(1)}, bf16[2064,128]{1,0:T(8,128)(2,1)S(1)}, u32[]{:S(2)}, u32[]{:S(2)}) collective-permute-start(bf16[2064,128]{1,0:T(8,128)(2,1)S(1)} %shard_map.56), channel_id=1, source_target_pairs={{0,8},{1,57},{8,16},{9,1},{16,24},{17,9},{24,32},{25,17},{32,40},{... | collective-permute-start | bytes 1585160 | tf_op jit(solution)/shard_map/ppermute | solution.py:271
  129.5 10.3 %collective-permute-start.27 = (bf16[1296,128]{1,0:T(8,128)(2,1)}, bf16[1296,128]{1,0:T(8,128)(2,1)S(1)}, u32[]{:S(2)}, u32[]{:S(2)}) collective-permute-start(bf16[1296,128]{1,0:T(8,128)(2,1)} %get-tuple-element.69), channel_id=1, source_target_pairs={{0,4},{4,0},{1,5},{5,1},{2,6},{6,2},{3,7},{7,3},{8,12},{12,8},{9,1... | collective-permute-start | bytes 995336 | tf_op jit(solution)/shard_map/ppermute | solution.py:256
  137.0 9.0 %collective-permute-start.20 = (bf16[128,1024]{1,0:T(8,128)(2,1)}, bf16[128,1024]{1,0:T(8,128)(2,1)S(1)}, u32[]{:S(2)}, u32[]{:S(2)}) collective-permute-start(bf16[128,1024]{1,0:T(8,128)(2,1)} %shard_map.60), channel_id=1, source_target_pairs={{0,4},{4,0},{1,5},{5,1},{2,6},{6,2},{3,7},{7,3},{8,12},{12,8},{9,1... | collective-permute-start | bytes 786440 | tf_op jit(solution)/shard_map/ppermute | solution.py:256

commit v4 on v3

--- a/solution.py
+++ b/solution.py
@@ -103,9 +103,8 @@
         out_ref[:, pl.ds(got_at, half)] = got_ref[:, at]
 
 
-def first_kernel(at_ref, own_ref, got_ref, rest_ref, *refs):
-    ws, (out_ref, other_ref, v_ref) = refs[:-3], refs[-3:]
-    width, half = own_ref.shape[1], ws[0].shape[0]
+def first_kernel(at_ref, own_ref, got_ref, rest_ref, w_ref, out_ref, other_ref, v_ref):
+    width = own_ref.shape[1]
 
     @pl.when(at_ref[2] == 1)
     def _():
@@ -115,10 +114,7 @@
     def _():
         other_ref[...] = rest_ref[...]
 
-    for j, w in enumerate(ws):
-        v_ref[:, j * half : (j + 1) * half] = dot(own_ref[...], w[:, :width], ((1,), (1,))) + dot(
-            other_ref[...], w[:, width:], ((1,), (1,))
-        )
+    v_ref[...] = dot(own_ref[...], w_ref[:, :width], ((1,), (1,))) + dot(other_ref[...], w_ref[:, width:], ((1,), (1,)))
 
     def body(r, amax):
         for j in range(v_ref.shape[1] // LANES):
@@ -129,10 +125,10 @@
     write_coded(v_ref, v_ref.shape[1] // LANES, amax, out_ref)
 
 
-def first_sum(i, rows, core, own, got, rest, ws):
+def first_sum(i, rows, core, own, got, rest, w_all):
     per = got.shape[0] // rows
     width = own.shape[1]
-    shape = (rows, len(ws) * ws[0].shape[0])
+    shape = (rows, w_all.shape[0])
     out = coded_shape(*shape)
     vmem = pl.BlockSpec(memory_space=pltpu.VMEM)
     part = pl.BlockSpec((rows, width), lambda j, at: (at[1], 0))
@@ -142,7 +138,7 @@
         grid_spec=pltpu.PrefetchScalarGridSpec(
             num_scalar_prefetch=1,
             grid=(1,),
-            in_specs=[pl.BlockSpec((rows, width), lambda j, at: (at[0], 0)), part, part] + [vmem] * len(ws),
+            in_specs=[pl.BlockSpec((rows, width), lambda j, at: (at[0], 0)), part, part, vmem],
             out_specs=whole(out.shape),
             scratch_shapes=[pltpu.VMEM((rows, width), BF16), pltpu.VMEM(shape, F32)],
         ),
@@ -151,7 +147,7 @@
         cost_estimate=pl.CostEstimate(
             flops=4 * width * shape[0] * shape[1], bytes_accessed=4 * out.size, transcendentals=0
         ),
-    )(jnp.stack([jnp.int32(k) for k in at]), own, got, rest, *ws)
+    )(jnp.stack([jnp.int32(k) for k in at]), own, got, rest, w_all)
 
 
 def owned_kernel(idx_ref, f_ref, b_ref, own_ref, mine_ref, out_ref, v_ref):
@@ -225,7 +221,7 @@
         copy.wait()
 
 
-def placed(arrays, pieces, shape):
+def placed(arrays, pieces, shape, far=0):
     fixed = [p[:4] for p in pieces]
     size = 2 * shape[0] * shape[1]
     return pl.pallas_call(
@@ -233,7 +229,7 @@
         grid_spec=pltpu.PrefetchScalarGridSpec(
             num_scalar_prefetch=1,
             grid=(1,),
-            in_specs=[pl.BlockSpec(memory_space=pltpu.VMEM)] * len(arrays),
+            in_specs=[pl.BlockSpec(memory_space=pltpu.VMEM if i >= far else pltpu.HBM) for i in range(len(arrays))],
             out_specs=pl.BlockSpec(memory_space=pltpu.VMEM),
             scratch_shapes=[pltpu.SemaphoreType.DMA((len(pieces),))],
         ),
@@ -271,7 +267,7 @@
     return lax.ppermute(a, (axis, "c"), perm)
 
 
-def gathered(parts, axis, order, joint, before, out=()):
+def gathered(parts, axis, order, joint, before, known={}):
     n, me = lax.axis_size(axis), lax.axis_index(axis)
     step = 1 - 2 * lax.axis_index("c")
     count, (rows, width) = len(parts), parts[0].shape
@@ -282,13 +278,11 @@
             ahead, back = [jnp.concatenate(ahead)], [jnp.concatenate(back)]
         if k in before:
             held = before[k](blocks)
-            if k < n - n // 2:
-                ahead, back, *_ = after(*ahead, *back, *held)
-                ahead, back = [ahead], [back]
-            else:
-                ahead = [after(*ahead, *held)[0]]
-        if k == 1 and count == 2:
-            ahead, back = blocks[-1], blocks[1] = [[f, ring(parts[1], axis, w)] for f, w in zip(out, (1, -1))]
+            m = len(ahead)
+            tied = after(*ahead, *back, *held)
+            ahead, back = list(tied[:m]), list(tied[m : 2 * m])
+        if k in known:
+            ahead, back = blocks[-k], blocks[k] = known[k]
             continue
         ahead = blocks[-k] = [ring(p, axis, 1) for p in ahead]
         if k < n - n // 2:
@@ -345,30 +339,29 @@
 
     w_mine = lax.dynamic_slice_in_dim(weight[0], h * half, half, 0)
     w_sent = lax.dynamic_slice_in_dim(weight[0], (1 - h) * half, half, 0)
-    out = [ring(acts_mine, "z", 1), ring(acts_mine, "z", -1)]
-    *_, acts_got, w_got = after(*out, acts_got, swap(w_sent, "yl"))
+    out = [(ring(acts_mine, "z", 1), ring(acts_mine, "z", -1))]
+    out.append((ring(out[0][0], "z", 1), ring(out[0][1], "z", -1)))
+    *_, acts_got, w_got = after(*out[1], acts_got, swap(w_sent, "yl"))
+    other = ring(acts_got, "z", 1), ring(acts_got, "z", -1)
+    known = {1: tuple([a, b] for a, b in zip(out[0], other))}
+    known[2] = tuple([a, ring(b, "z", way)] for a, b, way in zip(out[1], other, (1, -1)))
     w_pair = jnp.concatenate([w_mine, w_got], axis=1)
-    *_, blocks = gathered([w_pair], "x", (0,), 0, {2: lambda b: b[1]})
+    *_, blocks = gathered([w_pair], "x", (0,), 0, {2: lambda b: [known[2][0][1], known[2][1][1]]})
     near = [0, -1, 1, -2]
     ws = [blocks[k][0] for k in near]
+    pieces = [(i, 0, half, 0, i * half) for i in range(owners)]
+    w_all = placed(ws, pieces, (owners * half, 2 * width), owners - 1)
 
     part = tokens // 2
     g_sent = lax.dynamic_slice_in_dim(out_grad, c * part, part, 0)
     g_got = y_ring(after(acts_got, w_got, g_sent)[2])
-    first, gs = [], []
-
-    def first_sums(blocks):
-        got = after(*blocks[-2], *blocks[2], ws[-1], g_got)[-1]
-        gs.extend([out_grad, got, swap(got, "c")])
-        first.extend(first_sum(block_at("z", k), 2 * own_tokens, c, *gs, ws) for k in (4, -3))
-        return first
-
-    before = {2: lambda b: [w_got], 3: lambda b: [ws[-1]], 4: first_sums}
-    arrays, acts_pieces, shape, blocks = gathered([acts_mine, acts_got], "z", (h, 1 - h), 2, before, out)
-
-    ws = after(*first, *ws)[2:]
-    pieces = [(i, 0, half, 0, i * half) for i in range(owners)]
-    w_all = placed(ws, pieces, (owners * half, 2 * width))
+
+    before = {3: lambda b: ws[1:3]}
+    arrays, acts_pieces, shape, blocks = gathered([acts_mine, acts_got], "z", (h, 1 - h), 3, before, known)
+    g_got = after(*blocks[-3], *blocks[3], ws[-1], g_got)[-1]
+    gs = [out_grad, g_got, swap(g_got, "c")]
+
+    first = [first_sum(block_at("z", k), 2 * own_tokens, c, *gs, w_all) for k in (4, -3)]
     pieces = [(0, 0, tokens, 0, 0), (1, 0, part, width, c * part), (2, 0, part, width, (1 - c) * part)]
     g_pair = placed(after(*first, *gs)[2:], pieces, (tokens, 2 * width))
 

time: 150 us -> 150 us (level); the launches traced: 147 us -> 149 us
  starting transfers between devices: 46.4 us -> 53.3 us
  waiting for transfers between devices: 49 us -> 42.1 us
  local copies, waits for them, and re-layouts: 9.33 us -> 11.3 us
    ppermute x22 -> x24, waiting for transfers between devices: 41.8 us -> 32.4 us  [ring(): return lax.ppermute(a, (axis, 'c'), perm)]
    ppermute x5, starting transfers between devices: 6.04 us -> 12.6 us  [swap(): return lax.ppermute(a, axis, [(0, 1), (1, 0)])]
    ppermute x5, waiting for transfers between devices: 7.21 us -> 9.69 us  [swap(): return lax.ppermute(a, axis, [(0, 1), (1, 0)])]
    unnamed x34 -> x50, local copies, waits for them, and re-layouts: 5.82 us -> 7.8 us
    ppermute x22 -> x24, starting transfers between devices: 38.7 us -> 39.1 us  [ring(): return lax.ppermute(a, (axis, 'c'), perm)]
  transfers between devices with their start and end apart: 28 -> 30, of which waited for: 10 -> 13; matrix products, arithmetic and copies ran while one was open for 8% -> 10% of each run, Pallas kernels for 18% -> 17%
where the time goes in v4:
time: 150 us; the launch traced here: 149 us
  starting transfers between devices  53.3 us (36%)
  waiting for transfers between devices  42.1 us (28%)
  Pallas kernels  27.2 us (18%)
  matrix products  11.5 us (8%)
  local copies, waits for them, and re-layouts  11.3 us (8%)
  other arithmetic  2.47 us (2%)
    ppermute x24, starting transfers between devices, ring(): return lax.ppermute(a, (axis, 'c'), perm)  39.1 us
    ppermute x24, waiting for transfers between devices, ring(): return lax.ppermute(a, (axis, 'c'), perm)  32.4 us
    pallas_call x13, Pallas kernels, call(): pl.pallas_call(kernel, grid_spec=pltpu.PrefetchScalarGridSpec(num_scalar_...  14.5 us
    ppermute x5, starting transfers between devices, swap(): return lax.ppermute(a, axis, [(0, 1), (1, 0)])  12.6 us
    dot_general x10, matrix products, dot(): return lax.dot_general(a, b, (dims, ((), ())), preferred_element_type=F32)  11.5 us
    ppermute x5, waiting for transfers between devices, swap(): return lax.ppermute(a, axis, [(0, 1), (1, 0)])  9.69 us
    unnamed x50, local copies, waits for them, and re-layouts  7.8 us
    pallas_call x2, Pallas kernels, first_sum(): pl.pallas_call(first_kernel, grid_spec=pltpu.PrefetchScalarGridSpec(num_s...  6.43 us
  transfers between devices with their start and end apart: 30, of which 13 were waited for; matrix products, arithmetic and copies ran while one was open for 10% of the time, Pallas kernels for 17%

profile of v4, /device:TPU:4, one launch (start us, length us, event | category | flops | bytes accessed | tf_op | source)
XLA Modules:
  0.0 149.3 jit_solution(6336574461908502341)
XLA Ops:
  0.6 1.3 fusion.30
  2.7 1.9 %collective-permute-start = (bf16[128,1024]{1,0:T(8,128)(2,1)S(1)}, bf16[128,1024]{1,0:T(8,128)(2,1)}, u32[]{:S(2)}, u32[]{:S(2)}) collective-permute-start(bf16[128,1024]{1,0:T(8,128)(2,1)S(1)} %get-tuple-element.45.refs_0_), channel_id=1, source_target_pairs={{0,8},{1,57},{8,16},{9,1},{16,24},{17,9},{24,32},{25,17},{32,40},{... | collective-permute-start | bytes 786440 | tf_op jit(solution)/shard_map/ppermute | solution.py:267
  4.7 3.9 %collective-permute-start.2 = (bf16[128,1024]{1,0:T(8,128)(2,1)S(1)}, bf16[128,1024]{1,0:T(8,128)(2,1)}, u32[]{:S(2)}, u32[]{:S(2)}) collective-permute-start(bf16[128,1024]{1,0:T(8,128)(2,1)S(1)} %get-tuple-element.45.refs_0_), channel_id=1, source_target_pairs={{0,56},{1,9},{8,0},{9,17},{16,8},{17,25},{24,16},{25,33},{32,24},{... | collective-permute-start | bytes 786440 | tf_op jit(solution)/shard_map/ppermute | solution.py:267
  8.6 2.0 %dynamic-slice_bitcast_fusion = (bf16[256,640]{1,0:T(8,128)(2,1)}, bf16[256,640]{1,0:T(8,128)(2,1)}) fusion(bf16[1,512,640]{2,1,0:T(8,128)(2,1)} %param.5, s32[]{:T(128)S(6)} %select_n.63, s32[]{:T(128)S(6)} %select_n.62), kind=kLoop, calls=%fused_computation.23 | loop fusion | bytes 1310728 | tf_op jit(solution)/shard_map/dynamic_slice | solution.py:340
  10.6 1.6 %collective-permute-start.5 = (bf16[256,640]{1,0:T(8,128)(2,1)}, bf16[256,640]{1,0:T(8,128)(2,1)}, u32[]{:S(2)}, u32[]{:S(2)}) collective-permute-start(bf16[256,640]{1,0:T(8,128)(2,1)} %get-tuple-element.61), channel_id=1, source_target_pairs={{0,4},{4,0},{1,5},{5,1},{2,6},{6,2},{3,7},{7,3},{8,12},{12,8},{9,1... | collective-permute-start | bytes 983048 | tf_op jit(solution)/shard_map/ppermute | solution.py:252
  12.6 1.4 collective-permute-done.refs_2_
  14.2 3.8 %collective-permute-start.3 = (bf16[128,1024]{1,0:T(8,128)(2,1)}, bf16[128,1024]{1,0:T(8,128)(2,1)S(1)}, u32[]{:S(2)}, u32[]{:S(2)}) collective-permute-start(bf16[128,1024]{1,0:T(8,128)(2,1)} %collective-permute-done.2.refs_4_), channel_id=1, source_target_pairs={{0,56},{1,9},{8,0},{9,17},{16,8},{17,25},{24,16},{25,33},{32,24},{... | collective-permute-start | bytes 786440 | tf_op jit(solution)/shard_map/ppermute | solution.py:267
  18.0 7.7 %collective-permute-done.4.refs_1_ = bf16[128,1024]{1,0:T(8,128)(2,1)} collective-permute-done((bf16[128,1024]{1,0:T(8,128)(2,1)}, bf16[128,1024]{1,0:T(8,128)(2,1)}, u32[]{:S(2)}, u32[]{:S(2)}) %collective-permute-start.4) | collective-permute-done | bytes 262176 | tf_op jit(solution)/shard_map/ppermute | solution.py:252
  27.1 1.2 pad_maximum_fusion.refs_0_
  28.3 1.3 collective-permute-start.10
  30.5 1.7 %collective-permute-start.15 = (bf16[1024,640]{1,0:T(8,128)(2,1)S(1)}, bf16[1024,640]{1,0:T(8,128)(2,1)}, u32[]{:S(2)}, u32[]{:S(2)}) collective-permute-start(bf16[1024,640]{1,0:T(8,128)(2,1)S(1)} %constant_dynamic-slice_fusion), channel_id=1, source_target_pairs={{0,4},{1,7},{4,2},{5,1},{2,6},{3,5},{6,0},{7,3},{8,12},{9,15},{12,... | collective-permute-start | bytes 3932168 | tf_op jit(solution)/shard_map/ppermute | solution.py:261
  32.2 3.2 %collective-permute-start.8 = (bf16[128,1024]{1,0:T(8,128)(2,1)}, bf16[128,1024]{1,0:T(8,128)(2,1)S(1)}, u32[]{:S(2)}, u32[]{:S(2)}) collective-permute-start(bf16[128,1024]{1,0:T(8,128)(2,1)} %collective-permute-done.4.refs_1_), channel_id=1, source_target_pairs={{0,56},{1,9},{8,0},{9,17},{16,8},{17,25},{24,16},{25,33},{32,24},{... | collective-permute-start | bytes 786440 | tf_op jit(solution)/shard_map/ppermute | solution.py:267
  35.4 5.3 %collective-permute-done.6.refs_3_ = bf16[128,1024]{1,0:T(8,128)(2,1)S(1)} collective-permute-done((bf16[128,1024]{1,0:T(8,128)(2,1)}, bf16[128,1024]{1,0:T(8,128)(2,1)S(1)}, u32[]{:S(2)}, u32[]{:S(2)}) %collective-permute-start.6) | collective-permute-done | bytes 262176 | tf_op jit(solution)/shard_map/ppermute | solution.py:267
  41.5 3.6 %collective-permute-start.9 = (bf16[128,1024]{1,0:T(8,128)(2,1)S(1)}, bf16[128,1024]{1,0:T(8,128)(2,1)S(1)}, u32[]{:S(2)}, u32[]{:S(2)}) collective-permute-start(bf16[128,1024]{1,0:T(8,128)(2,1)S(1)} %collective-permute-done.8.refs_5_), channel_id=1, source_target_pairs={{0,56},{1,9},{8,0},{9,17},{16,8},{17,25},{24,16},{25,33},{32,24},{... | collective-permute-start | bytes 786440 | tf_op jit(solution)/shard_map/ppermute | solution.py:267
  45.7 2.5 %collective-permute-done.7.refs_7_ = bf16[128,1024]{1,0:T(8,128)(2,1)S(1)} collective-permute-done((bf16[128,1024]{1,0:T(8,128)(2,1)S(1)}, bf16[128,1024]{1,0:T(8,128)(2,1)S(1)}, u32[]{:S(2)}, u32[]{:S(2)}) %collective-permute-start.7) | collective-permute-done | bytes 262176 | tf_op jit(solution)/shard_map/ppermute | solution.py:267
  48.3 1.8 %collective-permute-done.9.refs_9_ = bf16[128,1024]{1,0:T(8,128)(2,1)S(1)} collective-permute-done((bf16[128,1024]{1,0:T(8,128)(2,1)S(1)}, bf16[128,1024]{1,0:T(8,128)(2,1)S(1)}, u32[]{:S(2)}, u32[]{:S(2)}) %collective-permute-start.9) | collective-permute-done | bytes 262176 | tf_op jit(solution)/shard_map/ppermute | solution.py:267
  50.1 3.2 %collective-permute-start.14 = (bf16[256,1280]{1,0:T(8,128)(2,1)S(1)}, bf16[256,1280]{1,0:T(8,128)(2,1)S(1)}, u32[]{:S(2)}, u32[]{:S(2)}) collective-permute-start(bf16[256,1280]{1,0:T(8,128)(2,1)S(1)} %collective-permute-done.10.refs_1_), channel_id=1, source_target_pairs={{0,64},{1,193},{64,128},{65,1},{128,192},{129,65},{192,0},{193,129... | collective-permute-start | bytes 1966088 | tf_op jit(solution)/shard_map/ppermute | solution.py:267
  53.5 3.9 %collective-permute-start.13 = (bf16[256,1024]{1,0:T(8,128)(2,1)S(1)}, bf16[256,1024]{1,0:T(8,128)(2,1)S(1)}, u32[]{:S(2)}, u32[]{:S(2)}) collective-permute-start(bf16[256,1024]{1,0:T(8,128)(2,1)S(1)} %pad_maximum_fusion.2), channel_id=1, source_target_pairs={{0,56},{1,9},{8,0},{9,17},{16,8},{17,25},{24,16},{25,33},{32,24},{... | collective-permute-start | bytes 1572872 | tf_op jit(solution)/shard_map/ppermute | solution.py:267
  57.4 11.0 %collective-permute-done.12.refs_10_ = bf16[256,1024]{1,0:T(8,128)(2,1)S(1)} collective-permute-done((bf16[256,1024]{1,0:T(8,128)(2,1)S(1)}, bf16[256,1024]{1,0:T(8,128)(2,1)S(1)}, u32[]{:S(2)}, u32[]{:S(2)}) %collective-permute-start.12) | collective-permute-done | bytes 524320 | tf_op jit(solution)/shard_map/ppermute | solution.py:267
  70.8 1.1 copy-done.12
  71.9 1.1 copy-done.14
  73.0 1.1 copy-done.16
  74.1 1.4 shard_map.50.w_ref
  75.5 3.2 %shard_map.51 = bf16[2064,128]{1,0:T(8,128)(2,1)S(1)} custom-call(s32[3]{0:T(128)S(1)} %pad_add_fusion.1.at_ref, bf16[2048,640]{1,0:T(8,128)(2,1)S(1)} %copy-done, bf16[1024,640]{1,0:T(8,128)(2,1)} %collective-permute-done.15.got_ref.refs_1_, bf16[1024,640]{1,0:T(8,128)(2,1)} %collective-permute-done.16.rest_ref.refs_2_, bf16[1024,1280]{1,0:T(8,128)(2,1)S(1)} %shard_map.50.w_ref), custom_call_target="tpu_custom_call" | custom-call | flops 671088640 | bytes 1056768 | tf_op jit(solution)/shard_map/pallas_call | solution.py:136
  78.8 3.2 %shard_map.52 = bf16[2064,128]{1,0:T(8,128)(2,1)S(1)} custom-call(s32[3]{0:T(128)S(1)} %pad_add_fusion.3.at_ref, bf16[2048,640]{1,0:T(8,128)(2,1)S(1)} %copy-done, bf16[1024,640]{1,0:T(8,128)(2,1)} %collective-permute-done.15.got_ref.refs_1_, bf16[1024,640]{1,0:T(8,128)(2,1)} %collective-permute-done.16.rest_ref.refs_2_, bf16[1024,1280]{1,0:T(8,128)(2,1)S(1)} %shard_map.50.w_ref), custom_call_target="tpu_custom_call" | custom-call | flops 671088640 | bytes 1056768 | tf_op jit(solution)/shard_map/pallas_call | solution.py:136
  82.1 3.3 %collective-permute-start.21 = (bf16[2064,128]{1,0:T(8,128)(2,1)S(1)}, bf16[2064,128]{1,0:T(8,128)(2,1)S(1)}, u32[]{:S(2)}, u32[]{:S(2)}) collective-permute-start(bf16[2064,128]{1,0:T(8,128)(2,1)S(1)} %shard_map.52), channel_id=1, source_target_pairs={{0,56},{1,9},{8,0},{9,17},{16,8},{17,25},{24,16},{25,33},{32,24},{... | collective-permute-start | bytes 1585160 | tf_op jit(solution)/shard_map/ppermute | solution.py:267
  85.4 2.7 %shard_map.53 = bf16[2048,1280]{1,0:T(8,128)(2,1)S(1)} custom-call(s32[3]{0:T(128)S(1)} %pad_add_fusion.2.at_ref, bf16[2048,640]{1,0:T(8,128)(2,1)S(1)} %copy-done, bf16[1024,640]{1,0:T(8,128)(2,1)} %collective-permute-done.15.got_ref.refs_1_, bf16[1024,640]{1,0:T(8,128)(2,1)} %collective-permute-done.16.rest_ref.refs_2_), custom_call_target="tpu_custom_call" | custom-call | bytes 10485760 | tf_op jit(solution)/shard_map/pallas_call | solution.py:227
  88.2 2.1 %shard_map.62 = bf16[2048,1024]{1,0:T(8,128)(2,1)S(1)} custom-call(s32[16]{0:T(128)S(1)} %stack.151.at_ref, bf16[128,1024]{1,0:T(8,128)(2,1)S(1)} %get-tuple-element.45.refs_0_, bf16[128,1024]{1,0:T(8,128)(2,1)} %collective-permute-done.4.refs_1_, bf16[128,1024]{1,0:T(8,128)(2,1)} %collective-permute-done.refs_2_, bf16[128,1024]{1,0:T(8,128)(2,1)S(1)} %copy-done.22, ...), custom_call_target="tpu_custom_call" | custom-call | bytes 8388608 | tf_op jit(solution)/shard_map/pallas_call | solution.py:227
  90.4 1.6 %fusion.6.refs_0_ = f32[256,1280]{1,0:T(8,128)S(1)} fusion(bf16[2048,1280]{1,0:T(8,128)(2,1)S(1)} %shard_map.53, bf16[2048,1024]{1,0:T(8,128)(2,1)S(1)} %shard_map.62, s32[]{:T(128)S(6)} %select_n.72), kind=kOutput, calls=%fused_computation.6 | convolution fusion | flops 1342177280 | bytes 7602180 | tf_op jit(solution)/shard_map/dot_general | solution.py:318
  92.6 1.2 collective-permute-start.26
  93.8 1.6 %fusion.4.refs_1_ = f32[256,1280]{1,0:T(8,128)S(1)} fusion(bf16[2048,1280]{1,0:T(8,128)(2,1)S(1)} %shard_map.53, bf16[2048,1024]{1,0:T(8,128)(2,1)S(1)} %shard_map.62, s32[]{:T(128)S(6)} %select_n.73), kind=kOutput, calls=%fused_computation.4 | convolution fusion | flops 1342177280 | bytes 7602180 | tf_op jit(solution)/shard_map/dot_general | solution.py:318
  96.3 1.6 %fusion.2.refs_0_ = f32[256,1280]{1,0:T(8,128)S(1)} fusion(bf16[2048,1280]{1,0:T(8,128)(2,1)S(1)} %shard_map.53, bf16[2048,1024]{1,0:T(8,128)(2,1)S(1)} %shard_map.62, s32[]{:T(128)S(6)} %select_n.74), kind=kOutput, calls=%fused_computation.2 | convolution fusion | flops 1342177280 | bytes 7602180 | tf_op jit(solution)/shard_map/dot_general | solution.py:318
  100.6 1.0 collective-permute-start.28
  103.4 3.3 %collective-permute-start.22 = (bf16[2064,128]{1,0:T(8,128)(2,1)S(1)}, bf16[2064,128]{1,0:T(8,128)(2,1)S(1)}, u32[]{:S(2)}, u32[]{:S(2)}) collective-permute-start(bf16[2064,128]{1,0:T(8,128)(2,1)S(1)} %shard_map.57), channel_id=1, source_target_pairs={{0,56},{1,9},{8,0},{9,17},{16,8},{17,25},{24,16},{25,33},{32,24},{... | collective-permute-start | bytes 1585160 | tf_op jit(solution)/shard_map/ppermute | solution.py:267
  106.7 3.9 %collective-permute-done.18.refs_0_ = bf16[2064,128]{1,0:T(8,128)(2,1)S(1)} collective-permute-done((bf16[2064,128]{1,0:T(8,128)(2,1)S(1)}, bf16[2064,128]{1,0:T(8,128)(2,1)S(1)}, u32[]{:S(2)}, u32[]{:S(2)}) %collective-permute-start.18) | collective-permute-done | bytes 528416 | tf_op jit(solution)/shard_map/ppermute | solution.py:267
  112.5 1.1 shard_map.64
  114.6 2.6 %collective-permute-done.22.refs_0_ = bf16[2064,128]{1,0:T(8,128)(2,1)S(1)} collective-permute-done((bf16[2064,128]{1,0:T(8,128)(2,1)S(1)}, bf16[2064,128]{1,0:T(8,128)(2,1)S(1)}, u32[]{:S(2)}, u32[]{:S(2)}) %collective-permute-start.22) | collective-permute-done | bytes 528416 | tf_op jit(solution)/shard_map/ppermute | solution.py:267
  118.1 3.8 %collective-permute-start.23 = (bf16[2064,128]{1,0:T(8,128)(2,1)S(1)}, bf16[2064,128]{1,0:T(8,128)(2,1)S(1)}, u32[]{:S(2)}, u32[]{:S(2)}) collective-permute-start(bf16[2064,128]{1,0:T(8,128)(2,1)S(1)} %shard_map.58), channel_id=1, source_target_pairs={{0,56},{1,9},{8,0},{9,17},{16,8},{17,25},{24,16},{25,33},{32,24},{... | collective-permute-start | bytes 1585160 | tf_op jit(solution)/shard_map/ppermute | solution.py:267
  121.9 2.4 %collective-permute-done.19.refs_0_ = bf16[2064,128]{1,0:T(8,128)(2,1)S(1)} collective-permute-done((bf16[2064,128]{1,0:T(8,128)(2,1)S(1)}, bf16[2064,128]{1,0:T(8,128)(2,1)S(1)}, u32[]{:S(2)}, u32[]{:S(2)}) %collective-permute-start.19) | collective-permute-done | bytes 528416 | tf_op jit(solution)/shard_map/ppermute | solution.py:267
  125.3 1.6 %fusion.own_ref = f32[256,1280]{1,0:T(8,128)S(1)} fusion(bf16[2048,1280]{1,0:T(8,128)(2,1)S(1)} %shard_map.53, bf16[2048,1024]{1,0:T(8,128)(2,1)S(1)} %shard_map.62, s32[]{:T(128)S(6)} %select_n.75), kind=kOutput, calls=%fused_computation | convolution fusion | flops 1342177280 | bytes 7602180 | tf_op jit(solution)/shard_map/dot_general | solution.py:318
  126.9 2.0 %shard_map.66 = (f32[256,640]{1,0:T(8,128)S(1)}, bf16[1296,128]{1,0:T(8,128)(2,1)}) custom-call(s32[1]{0:T(128)} %constant.82.clone.1.idx_ref, bf16[2576,128]{1,0:T(8,128)(2,1)S(1)} %collective-permute-done.27.f_ref, bf16[2576,128]{1,0:T(8,128)(2,1)S(1)} %collective-permute-done.28.b_ref, f32[256,1280]{1,0:T(8,128)S(1)} %fusion.own_ref), custom_call_target="tpu_custom_call" | custom-call | flops 42139648 | bytes 5267456 | tf_op jit(solution)/shard_map/pallas_call | solution.py:196
  128.9 6.0 %collective-permute-start.29 = (bf16[1296,128]{1,0:T(8,128)(2,1)}, bf16[1296,128]{1,0:T(8,128)(2,1)S(1)}, u32[]{:S(2)}, u32[]{:S(2)}) collective-permute-start(bf16[1296,128]{1,0:T(8,128)(2,1)} %get-tuple-element.59), channel_id=1, source_target_pairs={{0,4},{4,0},{1,5},{5,1},{2,6},{6,2},{3,7},{7,3},{8,12},{12,8},{9,1... | collective-permute-start | bytes 995336 | tf_op jit(solution)/shard_map/ppermute | solution.py:252
  135.8 1.3 collective-permute-done.20.f_ref
  137.1 1.7 %shard_map.60 = bf16[128,1024]{1,0:T(8,128)(2,1)} custom-call(s32[2]{0:T(128)S(1)} %pad_add_fusion.4.idx_ref, bf16[2064,128]{1,0:T(8,128)(2,1)S(1)} %collective-permute-done.20.f_ref, bf16[2064,128]{1,0:T(8,128)(2,1)S(1)} %collective-permute-done.23.b_ref, f32[256,1024]{1,0:T(8,128)S(1)} %fusion.8.own_ref), custom_call_target="tpu_custom_call" | custom-call | flops 29491200 | bytes 3686400 | tf_op jit(solution)/shard_map/pallas_call | solution.py:196
  138.8 4.6 %collective-permute-start.24 = (bf16[128,1024]{1,0:T(8,128)(2,1)}, bf16[128,1024]{1,0:T(8,128)(2,1)S(1)}, u32[]{:S(2)}, u32[]{:S(2)}) collective-permute-start(bf16[128,1024]{1,0:T(8,128)(2,1)} %shard_map.60), channel_id=1, source_target_pairs={{0,4},{4,0},{1,5},{5,1},{2,6},{6,2},{3,7},{7,3},{8,12},{12,8},{9,1... | collective-permute-start | bytes 786440 | tf_op jit(solution)/shard_map/ppermute | solution.py:252
  143.6 1.4 shard_map.67
  146.0 2.0 %collective-permute-done.24.got_ref = bf16[128,1024]{1,0:T(8,128)(2,1)S(1)} collective-permute-done((bf16[128,1024]{1,0:T(8,128)(2,1)}, bf16[128,1024]{1,0:T(8,128)(2,1)S(1)}, u32[]{:S(2)}, u32[]{:S(2)}) %collective-permute-start.24) | collective-permute-done | bytes 262176 | tf_op jit(solution)/shard_map/ppermute | solution.py:252
  147.9 1.4 shard_map.61
  (105 shorter events, 20.6 us)
Async XLA Ops:
  0.6 29.8 %copy-start = (bf16[2048,640]{1,0:T(8,128)(2,1)S(1)}, bf16[2048,640]{1,0:T(8,128)(2,1)}, u32[]{:S(2)}) copy-start(bf16[2048,640]{1,0:T(8,128)(2,1)} %refs_0_) | copy-start | bytes 7864324
  2.7 11.2 %collective-permute-start = (bf16[128,1024]{1,0:T(8,128)(2,1)S(1)}, bf16[128,1024]{1,0:T(8,128)(2,1)}, u32[]{:S(2)}, u32[]{:S(2)}) collective-permute-start(bf16[128,1024]{1,0:T(8,128)(2,1)S(1)} %get-tuple-element.45.refs_0_), channel_id=1, source_target_pairs={{0,8},{1,57},{8,16},{9,1},{16,24},{17,9},{24,32},{25,17},{32,40},{... | collective-permute-start | bytes 786440 | tf_op jit(solution)/shard_map/ppermute | solution.py:267
  4.7 9.5 %collective-permute-start.2 = (bf16[128,1024]{1,0:T(8,128)(2,1)S(1)}, bf16[128,1024]{1,0:T(8,128)(2,1)}, u32[]{:S(2)}, u32[]{:S(2)}) collective-permute-start(bf16[128,1024]{1,0:T(8,128)(2,1)S(1)} %get-tuple-element.45.refs_0_), channel_id=1, source_target_pairs={{0,56},{1,9},{8,0},{9,17},{16,8},{17,25},{24,16},{25,33},{32,24},{... | collective-permute-start | bytes 786440 | tf_op jit(solution)/shard_map/ppermute | solution.py:267
  10.6 15.1 %collective-permute-start.5 = (bf16[256,640]{1,0:T(8,128)(2,1)}, bf16[256,640]{1,0:T(8,128)(2,1)}, u32[]{:S(2)}, u32[]{:S(2)}) collective-permute-start(bf16[256,640]{1,0:T(8,128)(2,1)} %get-tuple-element.61), channel_id=1, source_target_pairs={{0,4},{4,0},{1,5},{5,1},{2,6},{6,2},{3,7},{7,3},{8,12},{12,8},{9,1... | collective-permute-start | bytes 983048 | tf_op jit(solution)/shard_map/ppermute | solution.py:252
  12.1 13.5 %collective-permute-start.4 = (bf16[128,1024]{1,0:T(8,128)(2,1)}, bf16[128,1024]{1,0:T(8,128)(2,1)}, u32[]{:S(2)}, u32[]{:S(2)}) collective-permute-start(bf16[128,1024]{1,0:T(8,128)(2,1)} %get-tuple-element.33), channel_id=1, source_target_pairs={{0,4},{4,0},{1,5},{5,1},{2,6},{6,2},{3,7},{7,3},{8,12},{12,8},{9,1... | collective-permute-start | bytes 786440 | tf_op jit(solution)/shard_map/ppermute | solution.py:252
  14.0 11.7 %collective-permute-start.1 = (bf16[128,1024]{1,0:T(8,128)(2,1)}, bf16[128,1024]{1,0:T(8,128)(2,1)S(1)}, u32[]{:S(2)}, u32[]{:S(2)}) collective-permute-start(bf16[128,1024]{1,0:T(8,128)(2,1)} %collective-permute-done.refs_2_), channel_id=1, source_target_pairs={{0,8},{1,57},{8,16},{9,1},{16,24},{17,9},{24,32},{25,17},{32,40},{... | collective-permute-start | bytes 786440 | tf_op jit(solution)/shard_map/ppermute | solution.py:267
  14.2 11.5 %collective-permute-start.3 = (bf16[128,1024]{1,0:T(8,128)(2,1)}, bf16[128,1024]{1,0:T(8,128)(2,1)S(1)}, u32[]{:S(2)}, u32[]{:S(2)}) collective-permute-start(bf16[128,1024]{1,0:T(8,128)(2,1)} %collective-permute-done.2.refs_4_), channel_id=1, source_target_pairs={{0,56},{1,9},{8,0},{9,17},{16,8},{17,25},{24,16},{25,33},{32,24},{... | collective-permute-start | bytes 786440 | tf_op jit(solution)/shard_map/ppermute | solution.py:267
  27.1 26.2 %copy-start.2 = (bf16[128,1024]{1,0:T(8,128)(2,1)S(1)}, bf16[128,1024]{1,0:T(8,128)(2,1)}, u32[]{:S(2)}) copy-start(bf16[128,1024]{1,0:T(8,128)(2,1)} %copy-done.1) | copy-start | bytes 786436
  27.1 26.2 %copy-start.5 = (bf16[128,1024]{1,0:T(8,128)(2,1)S(1)}, bf16[128,1024]{1,0:T(8,128)(2,1)}, u32[]{:S(2)}) copy-start(bf16[128,1024]{1,0:T(8,128)(2,1)} %copy-done.4) | copy-start | bytes 786436
  28.3 21.8 %collective-permute-start.10 = (bf16[256,1280]{1,0:T(8,128)(2,1)S(1)}, bf16[256,1280]{1,0:T(8,128)(2,1)S(1)}, u32[]{:S(2)}, u32[]{:S(2)}) collective-permute-start(bf16[256,1280]{1,0:T(8,128)(2,1)S(1)} %pad_maximum_fusion.refs_0_), channel_id=1, source_target_pairs={{0,64},{1,193},{64,128},{65,1},{128,192},{129,65},{192,0},{193,129... | collective-permute-start | bytes 1966088 | tf_op jit(solution)/shard_map/ppermute | solution.py:267
  29.6 20.5 %collective-permute-start.11 = (bf16[256,1280]{1,0:T(8,128)(2,1)S(1)}, bf16[256,1280]{1,0:T(8,128)(2,1)S(1)}, u32[]{:S(2)}, u32[]{:S(2)}) collective-permute-start(bf16[256,1280]{1,0:T(8,128)(2,1)S(1)} %pad_maximum_fusion.refs_0_), channel_id=1, source_target_pairs={{0,192},{1,65},{64,0},{65,129},{128,64},{129,193},{192,128},{193,1... | collective-permute-start | bytes 1966088 | tf_op jit(solution)/shard_map/ppermute | solution.py:267
  30.5 39.6 %collective-permute-start.15 = (bf16[1024,640]{1,0:T(8,128)(2,1)S(1)}, bf16[1024,640]{1,0:T(8,128)(2,1)}, u32[]{:S(2)}, u32[]{:S(2)}) collective-permute-start(bf16[1024,640]{1,0:T(8,128)(2,1)S(1)} %constant_dynamic-slice_fusion), channel_id=1, source_target_pairs={{0,4},{1,7},{4,2},{5,1},{2,6},{3,5},{6,0},{7,3},{8,12},{9,15},{12,... | collective-permute-start | bytes 3932168 | tf_op jit(solution)/shard_map/ppermute | solution.py:261
  32.2 8.5 %collective-permute-start.6 = (bf16[128,1024]{1,0:T(8,128)(2,1)}, bf16[128,1024]{1,0:T(8,128)(2,1)S(1)}, u32[]{:S(2)}, u32[]{:S(2)}) collective-permute-start(bf16[128,1024]{1,0:T(8,128)(2,1)} %collective-permute-done.4.refs_1_), channel_id=1, source_target_pairs={{0,8},{1,57},{8,16},{9,1},{16,24},{17,9},{24,32},{25,17},{32,40},{... | collective-permute-start | bytes 786440 | tf_op jit(solution)/shard_map/ppermute | solution.py:267
  32.2 9.3 %collective-permute-start.8 = (bf16[128,1024]{1,0:T(8,128)(2,1)}, bf16[128,1024]{1,0:T(8,128)(2,1)S(1)}, u32[]{:S(2)}, u32[]{:S(2)}) collective-permute-start(bf16[128,1024]{1,0:T(8,128)(2,1)} %collective-permute-done.4.refs_1_), channel_id=1, source_target_pairs={{0,56},{1,9},{8,0},{9,17},{16,8},{17,25},{24,16},{25,33},{32,24},{... | collective-permute-start | bytes 786440 | tf_op jit(solution)/shard_map/ppermute | solution.py:267
  40.7 7.6 %collective-permute-start.7 = (bf16[128,1024]{1,0:T(8,128)(2,1)S(1)}, bf16[128,1024]{1,0:T(8,128)(2,1)S(1)}, u32[]{:S(2)}, u32[]{:S(2)}) collective-permute-start(bf16[128,1024]{1,0:T(8,128)(2,1)S(1)} %collective-permute-done.6.refs_3_), channel_id=1, source_target_pairs={{0,8},{1,57},{8,16},{9,1},{16,24},{17,9},{24,32},{25,17},{32,40},{... | collective-permute-start | bytes 786440 | tf_op jit(solution)/shard_map/ppermute | solution.py:267
  41.5 8.6 %collective-permute-start.9 = (bf16[128,1024]{1,0:T(8,128)(2,1)S(1)}, bf16[128,1024]{1,0:T(8,128)(2,1)S(1)}, u32[]{:S(2)}, u32[]{:S(2)}) collective-permute-start(bf16[128,1024]{1,0:T(8,128)(2,1)S(1)} %collective-permute-done.8.refs_5_), channel_id=1, source_target_pairs={{0,56},{1,9},{8,0},{9,17},{16,8},{17,25},{24,16},{25,33},{32,24},{... | collective-permute-start | bytes 786440 | tf_op jit(solution)/shard_map/ppermute | solution.py:267
  48.3 5.1 %copy-start.7 = (bf16[128,1024]{1,0:T(8,128)(2,1)}, bf16[128,1024]{1,0:T(8,128)(2,1)S(1)}, u32[]{:S(2)}) copy-start(bf16[128,1024]{1,0:T(8,128)(2,1)S(1)} %collective-permute-done.7.refs_7_) | copy-start | bytes 786436
  50.0 3.4 %copy-start.9 = (bf16[128,1024]{1,0:T(8,128)(2,1)}, bf16[128,1024]{1,0:T(8,128)(2,1)S(1)}, u32[]{:S(2)}) copy-start(bf16[128,1024]{1,0:T(8,128)(2,1)S(1)} %collective-permute-done.9.refs_9_) | copy-start | bytes 786436
  50.1 7.3 %copy-start.11 = (bf16[256,1280]{1,0:T(8,128)(2,1)}, bf16[256,1280]{1,0:T(8,128)(2,1)S(1)}, u32[]{:S(2)}) copy-start(bf16[256,1280]{1,0:T(8,128)(2,1)S(1)} %collective-permute-done.10.refs_1_) | copy-start | bytes 1966084
  50.1 19.2 %copy-start.13 = (bf16[256,1280]{1,0:T(8,128)(2,1)}, bf16[256,1280]{1,0:T(8,128)(2,1)S(1)}, u32[]{:S(2)}) copy-start(bf16[256,1280]{1,0:T(8,128)(2,1)S(1)} %collective-permute-done.11.refs_2_) | copy-start | bytes 1966084
  50.1 19.2 %collective-permute-start.14 = (bf16[256,1280]{1,0:T(8,128)(2,1)S(1)}, bf16[256,1280]{1,0:T(8,128)(2,1)S(1)}, u32[]{:S(2)}, u32[]{:S(2)}) collective-permute-start(bf16[256,1280]{1,0:T(8,128)(2,1)S(1)} %collective-permute-done.10.refs_1_), channel_id=1, source_target_pairs={{0,64},{1,193},{64,128},{65,1},{128,192},{129,65},{192,0},{193,129... | collective-permute-start | bytes 1966088 | tf_op jit(solution)/shard_map/ppermute | solution.py:267
  53.3 15.1 %collective-permute-start.12 = (bf16[256,1024]{1,0:T(8,128)(2,1)S(1)}, bf16[256,1024]{1,0:T(8,128)(2,1)S(1)}, u32[]{:S(2)}, u32[]{:S(2)}) collective-permute-start(bf16[256,1024]{1,0:T(8,128)(2,1)S(1)} %pad_maximum_fusion.1), channel_id=1, source_target_pairs={{0,8},{1,57},{8,16},{9,1},{16,24},{17,9},{24,32},{25,17},{32,40},{... | collective-permute-start | bytes 1572872 | tf_op jit(solution)/shard_map/ppermute | solution.py:267
  53.5 15.0 %collective-permute-start.13 = (bf16[256,1024]{1,0:T(8,128)(2,1)S(1)}, bf16[256,1024]{1,0:T(8,128)(2,1)S(1)}, u32[]{:S(2)}, u32[]{:S(2)}) collective-permute-start(bf16[256,1024]{1,0:T(8,128)(2,1)S(1)} %pad_maximum_fusion.2), channel_id=1, source_target_pairs={{0,56},{1,9},{8,0},{9,17},{16,8},{17,25},{24,16},{25,33},{32,24},{... | collective-permute-start | bytes 1572872 | tf_op jit(solution)/shard_map/ppermute | solution.py:267
  68.4 1.7 %copy-start.17 = (bf16[256,1024]{1,0:T(8,128)(2,1)}, bf16[256,1024]{1,0:T(8,128)(2,1)S(1)}, u32[]{:S(2)}) copy-start(bf16[256,1024]{1,0:T(8,128)(2,1)S(1)} %collective-permute-done.12.refs_10_) | copy-start | bytes 1572868
  70.1 5.4 %collective-permute-start.16 = (bf16[1024,640]{1,0:T(8,128)(2,1)}, bf16[1024,640]{1,0:T(8,128)(2,1)}, u32[]{:S(2)}, u32[]{:S(2)}) collective-permute-start(bf16[1024,640]{1,0:T(8,128)(2,1)} %collective-permute-done.15.got_ref.refs_1_), channel_id=1, source_target_pairs={{0,1},{1,0},{2,3},{3,2},{4,5},{5,4},{6,7},{7,6},{8,9},{9,8},{10,11... | collective-permute-start | bytes 3932168 | tf_op jit(solution)/shard_map/ppermute | solution.py:252
  70.4 15.0 %collective-permute-start.25 = (bf16[256,1024]{1,0:T(8,128)(2,1)}, bf16[256,1024]{1,0:T(8,128)(2,1)S(1)}, u32[]{:S(2)}, u32[]{:S(2)}) collective-permute-start(bf16[256,1024]{1,0:T(8,128)(2,1)} %copy-done.17), channel_id=1, source_target_pairs={{0,8},{1,57},{8,16},{9,1},{16,24},{17,9},{24,32},{25,17},{32,40},{... | collective-permute-start | bytes 1572872 | tf_op jit(solution)/shard_map/ppermute | solution.py:267
  70.8 1.1 copy-start.12
  71.9 1.1 copy-start.14
  78.7 19.1 %collective-permute-start.17 = (bf16[2064,128]{1,0:T(8,128)(2,1)S(1)}, bf16[2064,128]{1,0:T(8,128)(2,1)S(1)}, u32[]{:S(2)}, u32[]{:S(2)}) collective-permute-start(bf16[2064,128]{1,0:T(8,128)(2,1)S(1)} %shard_map.51), channel_id=1, source_target_pairs={{0,8},{1,57},{8,16},{9,1},{16,24},{17,9},{24,32},{25,17},{32,40},{... | collective-permute-start | bytes 1585160 | tf_op jit(solution)/shard_map/ppermute | solution.py:267
  82.0 6.1 %copy-start.3 = (bf16[128,1024]{1,0:T(8,128)(2,1)S(1)}, bf16[128,1024]{1,0:T(8,128)(2,1)}, u32[]{:S(2)}) copy-start(bf16[128,1024]{1,0:T(8,128)(2,1)} %copy-done.1) | copy-start | bytes 786436
  82.0 6.1 %copy-start.6 = (bf16[128,1024]{1,0:T(8,128)(2,1)S(1)}, bf16[128,1024]{1,0:T(8,128)(2,1)}, u32[]{:S(2)}) copy-start(bf16[128,1024]{1,0:T(8,128)(2,1)} %copy-done.4) | copy-start | bytes 786436
  82.1 6.1 %copy-start.8 = (bf16[128,1024]{1,0:T(8,128)(2,1)S(1)}, bf16[128,1024]{1,0:T(8,128)(2,1)}, u32[]{:S(2)}) copy-start(bf16[128,1024]{1,0:T(8,128)(2,1)} %copy-done.7) | copy-start | bytes 786436
  82.1 6.1 %copy-start.10 = (bf16[128,1024]{1,0:T(8,128)(2,1)S(1)}, bf16[128,1024]{1,0:T(8,128)(2,1)}, u32[]{:S(2)}) copy-start(bf16[128,1024]{1,0:T(8,128)(2,1)} %copy-done.9) | copy-start | bytes 786436
  82.1 6.1 %copy-start.18 = (bf16[256,1024]{1,0:T(8,128)(2,1)S(1)}, bf16[256,1024]{1,0:T(8,128)(2,1)}, u32[]{:S(2)}) copy-start(bf16[256,1024]{1,0:T(8,128)(2,1)} %copy-done.17) | copy-start | bytes 1572868
  82.1 6.1 %copy-start.20 = (bf16[256,1024]{1,0:T(8,128)(2,1)S(1)}, bf16[256,1024]{1,0:T(8,128)(2,1)}, u32[]{:S(2)}) copy-start(bf16[256,1024]{1,0:T(8,128)(2,1)} %copy-done.19) | copy-start | bytes 1572868
  82.1 6.1 %copy-start.22 = (bf16[128,1024]{1,0:T(8,128)(2,1)S(1)}, bf16[128,1024]{1,0:T(8,128)(2,1)}, u32[]{:S(2)}) copy-start(bf16[128,1024]{1,0:T(8,128)(2,1)} %copy-done.21) | copy-start | bytes 786436
  82.1 6.1 %copy-start.24 = (bf16[128,1024]{1,0:T(8,128)(2,1)S(1)}, bf16[128,1024]{1,0:T(8,128)(2,1)}, u32[]{:S(2)}) copy-start(bf16[128,1024]{1,0:T(8,128)(2,1)} %copy-done.23) | copy-start | bytes 786436
  82.1 20.4 %collective-permute-start.21 = (bf16[2064,128]{1,0:T(8,128)(2,1)S(1)}, bf16[2064,128]{1,0:T(8,128)(2,1)S(1)}, u32[]{:S(2)}, u32[]{:S(2)}) collective-permute-start(bf16[2064,128]{1,0:T(8,128)(2,1)S(1)} %shard_map.52), channel_id=1, source_target_pairs={{0,56},{1,9},{8,0},{9,17},{16,8},{17,25},{24,16},{25,33},{32,24},{... | collective-permute-start | bytes 1585160 | tf_op jit(solution)/shard_map/ppermute | solution.py:267
  92.6 19.9 %collective-permute-start.26 = (bf16[2576,128]{1,0:T(8,128)(2,1)S(1)}, bf16[2576,128]{1,0:T(8,128)(2,1)S(1)}, u32[]{:S(2)}, u32[]{:S(2)}) collective-permute-start(bf16[2576,128]{1,0:T(8,128)(2,1)S(1)} %shard_map.63), channel_id=1, source_target_pairs={{0,64},{1,193},{64,128},{65,1},{128,192},{129,65},{192,0},{193,129... | collective-permute-start | bytes 1978376 | tf_op jit(solution)/shard_map/ppermute | solution.py:267
  98.8 11.9 %collective-permute-start.18 = (bf16[2064,128]{1,0:T(8,128)(2,1)S(1)}, bf16[2064,128]{1,0:T(8,128)(2,1)S(1)}, u32[]{:S(2)}, u32[]{:S(2)}) collective-permute-start(bf16[2064,128]{1,0:T(8,128)(2,1)S(1)} %shard_map.54), channel_id=1, source_target_pairs={{0,8},{1,57},{8,16},{9,1},{16,24},{17,9},{24,32},{25,17},{32,40},{... | collective-permute-start | bytes 1585160 | tf_op jit(solution)/shard_map/ppermute | solution.py:267
  100.6 26.3 %collective-permute-start.28 = (bf16[2576,128]{1,0:T(8,128)(2,1)S(1)}, bf16[2576,128]{1,0:T(8,128)(2,1)S(1)}, u32[]{:S(2)}, u32[]{:S(2)}) collective-permute-start(bf16[2576,128]{1,0:T(8,128)(2,1)S(1)} %shard_map.65), channel_id=1, source_target_pairs={{0,192},{1,65},{64,0},{65,129},{128,64},{129,193},{192,128},{193,1... | collective-permute-start | bytes 1978376 | tf_op jit(solution)/shard_map/ppermute | solution.py:267
  103.4 13.8 %collective-permute-start.22 = (bf16[2064,128]{1,0:T(8,128)(2,1)S(1)}, bf16[2064,128]{1,0:T(8,128)(2,1)S(1)}, u32[]{:S(2)}, u32[]{:S(2)}) collective-permute-start(bf16[2064,128]{1,0:T(8,128)(2,1)S(1)} %shard_map.57), channel_id=1, source_target_pairs={{0,56},{1,9},{8,0},{9,17},{16,8},{17,25},{24,16},{25,33},{32,24},{... | collective-permute-start | bytes 1585160 | tf_op jit(solution)/shard_map/ppermute | solution.py:267
  111.5 12.7 %collective-permute-start.19 = (bf16[2064,128]{1,0:T(8,128)(2,1)S(1)}, bf16[2064,128]{1,0:T(8,128)(2,1)S(1)}, u32[]{:S(2)}, u32[]{:S(2)}) collective-permute-start(bf16[2064,128]{1,0:T(8,128)(2,1)S(1)} %shard_map.55), channel_id=1, source_target_pairs={{0,8},{1,57},{8,16},{9,1},{16,24},{17,9},{24,32},{25,17},{32,40},{... | collective-permute-start | bytes 1585160 | tf_op jit(solution)/shard_map/ppermute | solution.py:267
  113.7 13.2 %collective-permute-start.27 = (bf16[2576,128]{1,0:T(8,128)(2,1)S(1)}, bf16[2576,128]{1,0:T(8,128)(2,1)S(1)}, u32[]{:S(2)}, u32[]{:S(2)}) collective-permute-start(bf16[2576,128]{1,0:T(8,128)(2,1)S(1)} %shard_map.64), channel_id=1, source_target_pairs={{0,64},{1,193},{64,128},{65,1},{128,192},{129,65},{192,0},{193,129... | collective-permute-start | bytes 1978376 | tf_op jit(solution)/shard_map/ppermute | solution.py:267
  118.1 17.7 %collective-permute-start.23 = (bf16[2064,128]{1,0:T(8,128)(2,1)S(1)}, bf16[2064,128]{1,0:T(8,128)(2,1)S(1)}, u32[]{:S(2)}, u32[]{:S(2)}) collective-permute-start(bf16[2064,128]{1,0:T(8,128)(2,1)S(1)} %shard_map.58), channel_id=1, source_target_pairs={{0,56},{1,9},{8,0},{9,17},{16,8},{17,25},{24,16},{25,33},{32,24},{... | collective-permute-start | bytes 1585160 | tf_op jit(solution)/shard_map/ppermute | solution.py:267
  125.2 11.9 %collective-permute-start.20 = (bf16[2064,128]{1,0:T(8,128)(2,1)S(1)}, bf16[2064,128]{1,0:T(8,128)(2,1)S(1)}, u32[]{:S(2)}, u32[]{:S(2)}) collective-permute-start(bf16[2064,128]{1,0:T(8,128)(2,1)S(1)} %shard_map.56), channel_id=1, source_target_pairs={{0,8},{1,57},{8,16},{9,1},{16,24},{17,9},{24,32},{25,17},{32,40},{... | collective-permute-start | bytes 1585160 | tf_op jit(solution)/shard_map/ppermute | solution.py:267
  128.9 14.6 %collective-permute-start.29 = (bf16[1296,128]{1,0:T(8,128)(2,1)}, bf16[1296,128]{1,0:T(8,128)(2,1)S(1)}, u32[]{:S(2)}, u32[]{:S(2)}) collective-permute-start(bf16[1296,128]{1,0:T(8,128)(2,1)} %get-tuple-element.59), channel_id=1, source_target_pairs={{0,4},{4,0},{1,5},{5,1},{2,6},{6,2},{3,7},{7,3},{8,12},{12,8},{9,1... | collective-permute-start | bytes 995336 | tf_op jit(solution)/shard_map/ppermute | solution.py:252
  138.8 9.2 %collective-permute-start.24 = (bf16[128,1024]{1,0:T(8,128)(2,1)}, bf16[128,1024]{1,0:T(8,128)(2,1)S(1)}, u32[]{:S(2)}, u32[]{:S(2)}) collective-permute-start(bf16[128,1024]{1,0:T(8,128)(2,1)} %shard_map.60), channel_id=1, source_target_pairs={{0,4},{4,0},{1,5},{5,1},{2,6},{6,2},{3,7},{7,3},{8,12},{12,8},{9,1... | collective-permute-start | bytes 786440 | tf_op jit(solution)/shard_map/ppermute | solution.py:252
  (7 other events, 5.6 us)

commit v5 on v4

--- a/solution.py
+++ b/solution.py
@@ -103,18 +103,8 @@
         out_ref[:, pl.ds(got_at, half)] = got_ref[:, at]
 
 
-def first_kernel(at_ref, own_ref, got_ref, rest_ref, w_ref, out_ref, other_ref, v_ref):
-    width = own_ref.shape[1]
-
-    @pl.when(at_ref[2] == 1)
-    def _():
-        other_ref[...] = got_ref[...]
-
-    @pl.when(at_ref[2] != 1)
-    def _():
-        other_ref[...] = rest_ref[...]
-
-    v_ref[...] = dot(own_ref[...], w_ref[:, :width], ((1,), (1,))) + dot(other_ref[...], w_ref[:, width:], ((1,), (1,)))
+def first_kernel(at_ref, g_ref, w_ref, out_ref, v_ref):
+    v_ref[...] = dot(g_ref[...], w_ref[...], ((1,), (1,)))
 
     def body(r, amax):
         for j in range(v_ref.shape[1] // LANES):
@@ -125,29 +115,28 @@
     write_coded(v_ref, v_ref.shape[1] // LANES, amax, out_ref)
 
 
-def first_sum(i, rows, core, own, got, rest, w_all):
-    per = got.shape[0] // rows
-    width = own.shape[1]
+def first_sum(i, rows, g_pair, w_all):
+    width = g_pair.shape[1]
     shape = (rows, w_all.shape[0])
     out = coded_shape(*shape)
-    vmem = pl.BlockSpec(memory_space=pltpu.VMEM)
-    part = pl.BlockSpec((rows, width), lambda j, at: (at[1], 0))
-    at = [i, lax.rem(i, per), jnp.where(lax.div(i, per) == core, 1, 0)]
     return pl.pallas_call(
         first_kernel,
         grid_spec=pltpu.PrefetchScalarGridSpec(
             num_scalar_prefetch=1,
             grid=(1,),
-            in_specs=[pl.BlockSpec((rows, width), lambda j, at: (at[0], 0)), part, part, vmem],
+            in_specs=[
+                pl.BlockSpec((rows, width), lambda j, at: (at[0], 0)),
+                pl.BlockSpec(memory_space=pltpu.VMEM),
+            ],
             out_specs=whole(out.shape),
-            scratch_shapes=[pltpu.VMEM((rows, width), BF16), pltpu.VMEM(shape, F32)],
+            scratch_shapes=[pltpu.VMEM(shape, F32)],
         ),
         out_shape=out,
         compiler_params=pltpu.CompilerParams(vmem_limit_bytes=10 * MIB),
         cost_estimate=pl.CostEstimate(
-            flops=4 * width * shape[0] * shape[1], bytes_accessed=4 * out.size, transcendentals=0
+            flops=2 * width * shape[0] * shape[1], bytes_accessed=4 * out.size, transcendentals=0
         ),
-    )(jnp.stack([jnp.int32(k) for k in at]), own, got, rest, w_all)
+    )(jnp.stack([jnp.int32(i)]), g_pair, w_all)
 
 
 def owned_kernel(idx_ref, f_ref, b_ref, own_ref, mine_ref, out_ref, v_ref):
@@ -229,7 +218,7 @@
         grid_spec=pltpu.PrefetchScalarGridSpec(
             num_scalar_prefetch=1,
             grid=(1,),
-            in_specs=[pl.BlockSpec(memory_space=pltpu.VMEM if i >= far else pltpu.HBM) for i in range(len(arrays))],
+            in_specs=[pl.BlockSpec(memory_space=pltpu.VMEM if i >= far else pl.ANY) for i in range(len(arrays))],
             out_specs=pl.BlockSpec(memory_space=pltpu.VMEM),
             scratch_shapes=[pltpu.SemaphoreType.DMA((len(pieces),))],
         ),
@@ -356,14 +345,19 @@
     g_sent = lax.dynamic_slice_in_dim(out_grad, c * part, part, 0)
     g_got = y_ring(after(acts_got, w_got, g_sent)[2])
 
-    before = {3: lambda b: ws[1:3]}
+    pairs = []
+
+    def g_pair_of(blocks):
+        got = after(blocks[-2][1], blocks[2][1], *ws[1:3], g_got)[-1]
+        pieces = [(0, 0, tokens, 0, 0), (1, 0, part, width, c * part), (2, 0, part, width, (1 - c) * part)]
+        pairs.append(placed([out_grad, got, swap(got, "c")], pieces, (tokens, 2 * width)))
+        return pairs
+
+    before = {3: lambda b: ws[1:3], 4: g_pair_of}
     arrays, acts_pieces, shape, blocks = gathered([acts_mine, acts_got], "z", (h, 1 - h), 3, before, known)
-    g_got = after(*blocks[-3], *blocks[3], ws[-1], g_got)[-1]
-    gs = [out_grad, g_got, swap(g_got, "c")]
-
-    first = [first_sum(block_at("z", k), 2 * own_tokens, c, *gs, w_all) for k in (4, -3)]
-    pieces = [(0, 0, tokens, 0, 0), (1, 0, part, width, c * part), (2, 0, part, width, (1 - c) * part)]
-    g_pair = placed(after(*first, *gs)[2:], pieces, (tokens, 2 * width))
+    (g_pair,) = pairs
+
+    first = [first_sum(block_at("z", k), 2 * own_tokens, g_pair, w_all) for k in (4, -3)]
 
     def of_tokens(i):
         count = 2 * own_tokens

time: 150 us -> 150 us (level); the launches traced: 149 us -> 147 us
  waiting for transfers between devices: 42.1 us -> 47.8 us
  local copies, waits for them, and re-layouts: 11.3 us -> 7 us
  starting transfers between devices: 53.3 us -> 49.5 us
  other arithmetic: 2.47 us -> 4.2 us
    ppermute x5, starting transfers between devices: 12.6 us -> 6.87 us  [swap(): return lax.ppermute(a, axis, [(0, 1), (1, 0)])]
    unnamed x50 -> x32, local copies, waits for them, and re-layouts: 7.8 us -> 3.49 us
    pallas_call x2, Pallas kernels: 6.43 us -> 2.87 us  [first_sum(): pl.pallas_call(first_kernel, grid_spec=pltpu.PrefetchScalarGridSpec(num_s...]
    ppermute x5, waiting for transfers between devices: 9.69 us -> 12.7 us  [swap(): return lax.ppermute(a, axis, [(0, 1), (1, 0)])]
    ppermute x24, waiting for transfers between devices: 32.4 us -> 35.1 us  [ring(): return lax.ppermute(a, (axis, 'c'), perm)]
    concatenate x2, other arithmetic: 0.07 us -> 2.13 us  [gathered(): ahead, back = ([jnp.concatenate(ahead)], [jnp.concatenate(back)])]
    ppermute x24, starting transfers between devices: 39.1 us -> 41 us  [ring(): return lax.ppermute(a, (axis, 'c'), perm)]
    pallas_call x3, Pallas kernels: 6.29 us -> 7.84 us  [placed(): pl.pallas_call(functools.partial(placed_kernel, fixed), grid_spec=pltpu.P...]
  transfers between devices with their start and end apart: 30 -> 30, of which waited for: 13 -> 14; matrix products, arithmetic and copies ran while one was open for 10% -> 12% of each run, Pallas kernels for 17% -> 16%
where the time goes in v5:
time: 150 us; the launch traced here: 147 us
  starting transfers between devices  49.5 us (33%)
  waiting for transfers between devices  47.8 us (32%)
  Pallas kernels  26.2 us (17%)
  matrix products  11.5 us (8%)
  local copies, waits for them, and re-layouts  7 us (5%)
  other arithmetic  4.2 us (3%)
    ppermute x24, starting transfers between devices, ring(): return lax.ppermute(a, (axis, 'c'), perm)  41 us
    ppermute x24, waiting for transfers between devices, ring(): return lax.ppermute(a, (axis, 'c'), perm)  35.1 us
    pallas_call x13, Pallas kernels, call(): pl.pallas_call(kernel, grid_spec=pltpu.PrefetchScalarGridSpec(num_scalar_...  15.5 us
    ppermute x5, waiting for transfers between devices, swap(): return lax.ppermute(a, axis, [(0, 1), (1, 0)])  12.7 us
    dot_general x10, matrix products, dot(): return lax.dot_general(a, b, (dims, ((), ())), preferred_element_type=F32)  11.5 us
    pallas_call x3, Pallas kernels, placed(): pl.pallas_call(functools.partial(placed_kernel, fixed), grid_spec=pltpu.P...  7.84 us
    ppermute x5, starting transfers between devices, swap(): return lax.ppermute(a, axis, [(0, 1), (1, 0)])  6.87 us
    unnamed x32, local copies, waits for them, and re-layouts  3.49 us
  transfers between devices with their start and end apart: 30, of which 14 were waited for; matrix products, arithmetic and copies ran while one was open for 12% of the time, Pallas kernels for 16%

profile of v5, /device:TPU:4, one launch (start us, length us, event | category | flops | bytes accessed | tf_op | source)
XLA Modules:
  0.0 147.3 jit_solution(10251044753338735610)
XLA Ops:
  0.6 1.3 fusion.30
  2.7 1.9 %collective-permute-start = (bf16[128,1024]{1,0:T(8,128)(2,1)S(1)}, bf16[128,1024]{1,0:T(8,128)(2,1)}, u32[]{:S(2)}, u32[]{:S(2)}) collective-permute-start(bf16[128,1024]{1,0:T(8,128)(2,1)S(1)} %get-tuple-element.41.refs_0_), channel_id=1, source_target_pairs={{0,8},{1,57},{8,16},{9,1},{16,24},{17,9},{24,32},{25,17},{32,40},{... | collective-permute-start | bytes 786440 | tf_op jit(solution)/shard_map/ppermute | solution.py:256
  4.6 3.9 %collective-permute-start.2 = (bf16[128,1024]{1,0:T(8,128)(2,1)S(1)}, bf16[128,1024]{1,0:T(8,128)(2,1)}, u32[]{:S(2)}, u32[]{:S(2)}) collective-permute-start(bf16[128,1024]{1,0:T(8,128)(2,1)S(1)} %get-tuple-element.41.refs_0_), channel_id=1, source_target_pairs={{0,56},{1,9},{8,0},{9,17},{16,8},{17,25},{24,16},{25,33},{32,24},{... | collective-permute-start | bytes 786440 | tf_op jit(solution)/shard_map/ppermute | solution.py:256
  8.6 2.0 %dynamic-slice_bitcast_fusion = (bf16[256,640]{1,0:T(8,128)(2,1)}, bf16[256,640]{1,0:T(8,128)(2,1)}) fusion(bf16[1,512,640]{2,1,0:T(8,128)(2,1)} %param.5, s32[]{:T(128)S(6)} %select_n.55, s32[]{:T(128)S(6)} %select_n.54), kind=kLoop, calls=%fused_computation.23 | loop fusion | bytes 1310728 | tf_op jit(solution)/shard_map/dynamic_slice | solution.py:329
  10.5 1.6 %collective-permute-start.5 = (bf16[256,640]{1,0:T(8,128)(2,1)}, bf16[256,640]{1,0:T(8,128)(2,1)}, u32[]{:S(2)}, u32[]{:S(2)}) collective-permute-start(bf16[256,640]{1,0:T(8,128)(2,1)} %get-tuple-element.57), channel_id=1, source_target_pairs={{0,4},{4,0},{1,5},{5,1},{2,6},{6,2},{3,7},{7,3},{8,12},{12,8},{9,1... | collective-permute-start | bytes 983048 | tf_op jit(solution)/shard_map/ppermute | solution.py:241
  12.6 1.4 collective-permute-done.refs_2_
  14.2 3.8 %collective-permute-start.3 = (bf16[128,1024]{1,0:T(8,128)(2,1)}, bf16[128,1024]{1,0:T(8,128)(2,1)S(1)}, u32[]{:S(2)}, u32[]{:S(2)}) collective-permute-start(bf16[128,1024]{1,0:T(8,128)(2,1)} %collective-permute-done.2.refs_4_), channel_id=1, source_target_pairs={{0,56},{1,9},{8,0},{9,17},{16,8},{17,25},{24,16},{25,33},{32,24},{... | collective-permute-start | bytes 786440 | tf_op jit(solution)/shard_map/ppermute | solution.py:256
  18.1 7.6 %collective-permute-done.4.refs_1_ = bf16[128,1024]{1,0:T(8,128)(2,1)} collective-permute-done((bf16[128,1024]{1,0:T(8,128)(2,1)}, bf16[128,1024]{1,0:T(8,128)(2,1)}, u32[]{:S(2)}, u32[]{:S(2)}) %collective-permute-start.4) | collective-permute-done | bytes 262176 | tf_op jit(solution)/shard_map/ppermute | solution.py:241
  25.7 1.7 %collective-permute-start.12 = (bf16[1024,640]{1,0:T(8,128)(2,1)S(1)}, bf16[1024,640]{1,0:T(8,128)(2,1)}, u32[]{:S(2)}, u32[]{:S(2)}) collective-permute-start(bf16[1024,640]{1,0:T(8,128)(2,1)S(1)} %constant_dynamic-slice_fusion), channel_id=1, source_target_pairs={{0,4},{1,7},{4,2},{5,1},{2,6},{3,5},{6,0},{7,3},{8,12},{9,15},{12,... | collective-permute-start | bytes 3932168 | tf_op jit(solution)/shard_map/ppermute | solution.py:250
  28.4 1.3 collective-permute-start.10
  30.5 3.2 %collective-permute-start.8 = (bf16[128,1024]{1,0:T(8,128)(2,1)}, bf16[128,1024]{1,0:T(8,128)(2,1)S(1)}, u32[]{:S(2)}, u32[]{:S(2)}) collective-permute-start(bf16[128,1024]{1,0:T(8,128)(2,1)} %collective-permute-done.4.refs_1_), channel_id=1, source_target_pairs={{0,56},{1,9},{8,0},{9,17},{16,8},{17,25},{24,16},{25,33},{32,24},{... | collective-permute-start | bytes 786440 | tf_op jit(solution)/shard_map/ppermute | solution.py:256
  33.7 5.3 %collective-permute-done.6.refs_3_ = bf16[128,1024]{1,0:T(8,128)(2,1)S(1)} collective-permute-done((bf16[128,1024]{1,0:T(8,128)(2,1)}, bf16[128,1024]{1,0:T(8,128)(2,1)S(1)}, u32[]{:S(2)}, u32[]{:S(2)}) %collective-permute-start.6) | collective-permute-done | bytes 262176 | tf_op jit(solution)/shard_map/ppermute | solution.py:256
  39.8 3.6 %collective-permute-start.9 = (bf16[128,1024]{1,0:T(8,128)(2,1)S(1)}, bf16[128,1024]{1,0:T(8,128)(2,1)S(1)}, u32[]{:S(2)}, u32[]{:S(2)}) collective-permute-start(bf16[128,1024]{1,0:T(8,128)(2,1)S(1)} %collective-permute-done.8.refs_5_), channel_id=1, source_target_pairs={{0,56},{1,9},{8,0},{9,17},{16,8},{17,25},{24,16},{25,33},{32,24},{... | collective-permute-start | bytes 786440 | tf_op jit(solution)/shard_map/ppermute | solution.py:256
  44.1 2.5 %collective-permute-done.7.refs_7_ = bf16[128,1024]{1,0:T(8,128)(2,1)S(1)} collective-permute-done((bf16[128,1024]{1,0:T(8,128)(2,1)S(1)}, bf16[128,1024]{1,0:T(8,128)(2,1)S(1)}, u32[]{:S(2)}, u32[]{:S(2)}) %collective-permute-start.7) | collective-permute-done | bytes 262176 | tf_op jit(solution)/shard_map/ppermute | solution.py:256
  46.6 1.8 %collective-permute-done.9.refs_9_ = bf16[128,1024]{1,0:T(8,128)(2,1)S(1)} collective-permute-done((bf16[128,1024]{1,0:T(8,128)(2,1)S(1)}, bf16[128,1024]{1,0:T(8,128)(2,1)S(1)}, u32[]{:S(2)}, u32[]{:S(2)}) %collective-permute-start.9) | collective-permute-done | bytes 262176 | tf_op jit(solution)/shard_map/ppermute | solution.py:256
  49.3 1.1 collective-permute-start.13
  50.5 3.1 %collective-permute-start.14 = (bf16[256,1280]{1,0:T(8,128)(2,1)}, bf16[256,1280]{1,0:T(8,128)(2,1)}, u32[]{:S(2)}, u32[]{:S(2)}) collective-permute-start(bf16[256,1280]{1,0:T(8,128)(2,1)} %collective-permute-done.10.refs_1_), channel_id=1, source_target_pairs={{0,64},{1,193},{64,128},{65,1},{128,192},{129,65},{192,0},{193,129... | collective-permute-start | bytes 1966088 | tf_op jit(solution)/shard_map/ppermute | solution.py:256
  53.8 1.1 pad_maximum_fusion.1
  54.9 1.1 pad_maximum_fusion.2
  56.2 3.2 %collective-permute-start.24 = (bf16[256,1024]{1,0:T(8,128)(2,1)S(1)}, bf16[256,1024]{1,0:T(8,128)(2,1)S(1)}, u32[]{:S(2)}, u32[]{:S(2)}) collective-permute-start(bf16[256,1024]{1,0:T(8,128)(2,1)S(1)} %pad_maximum_fusion.2), channel_id=1, source_target_pairs={{0,56},{1,9},{8,0},{9,17},{16,8},{17,25},{24,16},{25,33},{32,24},{... | collective-permute-start | bytes 1572872 | tf_op jit(solution)/shard_map/ppermute | solution.py:256
  59.5 2.5 %collective-permute-done.14.refs_3_ = bf16[256,1280]{1,0:T(8,128)(2,1)} collective-permute-done((bf16[256,1280]{1,0:T(8,128)(2,1)}, bf16[256,1280]{1,0:T(8,128)(2,1)}, u32[]{:S(2)}, u32[]{:S(2)}) %collective-permute-start.14) | collective-permute-done | bytes 655392 | tf_op jit(solution)/shard_map/ppermute | solution.py:256
  62.0 1.1 copy-done.10
  63.1 3.0 %shard_map.51.w_ref = bf16[1024,1280]{1,0:T(8,128)(2,1)S(1)} custom-call(s32[4]{0:T(128)S(1)} %iota_multiply_fusion.at_ref, bf16[256,1280]{1,0:T(8,128)(2,1)S(1)} %pad_maximum_fusion.refs_0_, bf16[256,1280]{1,0:T(8,128)(2,1)} %collective-permute-done.10.refs_1_, bf16[256,1280]{1,0:T(8,128)(2,1)S(1)} %copy-done.10, ...), custom_call_target="tpu_custom_call" | custom-call | bytes 5242880 | tf_op jit(solution)/shard_map/pallas_call | solution.py:216
  66.0 2.7 %shard_map.50.g_ref = bf16[2048,1280]{1,0:T(8,128)(2,1)S(1)} custom-call(s32[3]{0:T(128)S(1)} %pad_add_fusion.1.at_ref, bf16[2048,640]{1,0:T(8,128)(2,1)S(1)} %copy-done, bf16[1024,640]{1,0:T(8,128)(2,1)} %collective-permute-done.12.refs_1_, bf16[1024,640]{1,0:T(8,128)(2,1)} %collective-permute-done.13.refs_2_), custom_call_target="tpu_custom_call" | custom-call | bytes 10485760 | tf_op jit(solution)/shard_map/pallas_call | solution.py:216
  68.8 1.4 shard_map.52
  70.3 1.4 shard_map.56
  71.8 3.3 %collective-permute-start.19 = (bf16[2064,128]{1,0:T(8,128)(2,1)S(1)}, bf16[2064,128]{1,0:T(8,128)(2,1)S(1)}, u32[]{:S(2)}, u32[]{:S(2)}) collective-permute-start(bf16[2064,128]{1,0:T(8,128)(2,1)S(1)} %shard_map.56), channel_id=1, source_target_pairs={{0,56},{1,9},{8,0},{9,17},{16,8},{17,25},{24,16},{25,33},{32,24},{... | collective-permute-start | bytes 1585160 | tf_op jit(solution)/shard_map/ppermute | solution.py:256
  78.7 13.3 %collective-permute-done.25.refs_12_ = bf16[256,1024]{1,0:T(8,128)(2,1)S(1)} collective-permute-done((bf16[256,1024]{1,0:T(8,128)(2,1)S(1)}, bf16[256,1024]{1,0:T(8,128)(2,1)S(1)}, u32[]{:S(2)}, u32[]{:S(2)}) %collective-permute-start.25) | collective-permute-done | bytes 524320 | tf_op jit(solution)/shard_map/ppermute | solution.py:256
  92.1 2.1 %shard_map.62 = bf16[2048,1024]{1,0:T(8,128)(2,1)S(1)} custom-call(s32[16]{0:T(128)S(1)} %stack.127.at_ref, bf16[128,1024]{1,0:T(8,128)(2,1)S(1)} %get-tuple-element.41.refs_0_, bf16[128,1024]{1,0:T(8,128)(2,1)} %collective-permute-done.4.refs_1_, bf16[128,1024]{1,0:T(8,128)(2,1)} %collective-permute-done.refs_2_, bf16[128,1024]{1,0:T(8,128)(2,1)S(1)} %copy-done.12, ...), custom_call_target="tpu_custom_call" | custom-call | bytes 8388608 | tf_op jit(solution)/shard_map/pallas_call | solution.py:216
  95.2 1.6 %fusion.6.refs_0_ = f32[256,1280]{1,0:T(8,128)S(1)} fusion(bf16[2048,1280]{1,0:T(8,128)(2,1)S(1)} %shard_map.50.g_ref, bf16[2048,1024]{1,0:T(8,128)(2,1)S(1)} %shard_map.62, s32[]{:T(128)S(6)} %select_n.63), kind=kOutput, calls=%fused_computation.6 | convolution fusion | flops 1342177280 | bytes 7602180 | tf_op jit(solution)/shard_map/dot_general | solution.py:307
  97.5 2.6 %collective-permute-start.26 = (bf16[2576,128]{1,0:T(8,128)(2,1)S(1)}, bf16[2576,128]{1,0:T(8,128)(2,1)S(1)}, u32[]{:S(2)}, u32[]{:S(2)}) collective-permute-start(bf16[2576,128]{1,0:T(8,128)(2,1)S(1)} %shard_map.63), channel_id=1, source_target_pairs={{0,64},{1,193},{64,128},{65,1},{128,192},{129,65},{192,0},{193,129... | collective-permute-start | bytes 1978376 | tf_op jit(solution)/shard_map/ppermute | solution.py:256
  100.0 1.6 %fusion.4.refs_1_ = f32[256,1280]{1,0:T(8,128)S(1)} fusion(bf16[2048,1280]{1,0:T(8,128)(2,1)S(1)} %shard_map.50.g_ref, bf16[2048,1024]{1,0:T(8,128)(2,1)S(1)} %shard_map.62, s32[]{:T(128)S(6)} %select_n.64), kind=kOutput, calls=%fused_computation.4 | convolution fusion | flops 1342177280 | bytes 7602180 | tf_op jit(solution)/shard_map/dot_general | solution.py:307
  102.6 3.5 %collective-permute-start.20 = (bf16[2064,128]{1,0:T(8,128)(2,1)S(1)}, bf16[2064,128]{1,0:T(8,128)(2,1)S(1)}, u32[]{:S(2)}, u32[]{:S(2)}) collective-permute-start(bf16[2064,128]{1,0:T(8,128)(2,1)S(1)} %shard_map.57), channel_id=1, source_target_pairs={{0,56},{1,9},{8,0},{9,17},{16,8},{17,25},{24,16},{25,33},{32,24},{... | collective-permute-start | bytes 1585160 | tf_op jit(solution)/shard_map/ppermute | solution.py:256
  107.1 1.6 %fusion.2.refs_0_ = f32[256,1280]{1,0:T(8,128)S(1)} fusion(bf16[2048,1280]{1,0:T(8,128)(2,1)S(1)} %shard_map.50.g_ref, bf16[2048,1024]{1,0:T(8,128)(2,1)S(1)} %shard_map.62, s32[]{:T(128)S(6)} %select_n.65), kind=kOutput, calls=%fused_computation.2 | convolution fusion | flops 1342177280 | bytes 7602180 | tf_op jit(solution)/shard_map/dot_general | solution.py:307
  109.4 1.1 shard_map.64
  110.6 2.2 %collective-permute-start.27 = (bf16[2576,128]{1,0:T(8,128)(2,1)S(1)}, bf16[2576,128]{1,0:T(8,128)(2,1)S(1)}, u32[]{:S(2)}, u32[]{:S(2)}) collective-permute-start(bf16[2576,128]{1,0:T(8,128)(2,1)S(1)} %shard_map.64), channel_id=1, source_target_pairs={{0,64},{1,193},{64,128},{65,1},{128,192},{129,65},{192,0},{193,129... | collective-permute-start | bytes 1978376 | tf_op jit(solution)/shard_map/ppermute | solution.py:256
  113.6 4.7 %collective-permute-done.20.refs_0_ = bf16[2064,128]{1,0:T(8,128)(2,1)S(1)} collective-permute-done((bf16[2064,128]{1,0:T(8,128)(2,1)S(1)}, bf16[2064,128]{1,0:T(8,128)(2,1)S(1)}, u32[]{:S(2)}, u32[]{:S(2)}) %collective-permute-start.20) | collective-permute-done | bytes 528416 | tf_op jit(solution)/shard_map/ppermute | solution.py:256
  119.2 3.8 %collective-permute-start.21 = (bf16[2064,128]{1,0:T(8,128)(2,1)S(1)}, bf16[2064,128]{1,0:T(8,128)(2,1)S(1)}, u32[]{:S(2)}, u32[]{:S(2)}) collective-permute-start(bf16[2064,128]{1,0:T(8,128)(2,1)S(1)} %shard_map.58), channel_id=1, source_target_pairs={{0,56},{1,9},{8,0},{9,17},{16,8},{17,25},{24,16},{25,33},{32,24},{... | collective-permute-start | bytes 1585160 | tf_op jit(solution)/shard_map/ppermute | solution.py:256
  124.0 1.6 %fusion.own_ref = f32[256,1280]{1,0:T(8,128)S(1)} fusion(bf16[2048,1280]{1,0:T(8,128)(2,1)S(1)} %shard_map.50.g_ref, bf16[2048,1024]{1,0:T(8,128)(2,1)S(1)} %shard_map.62, s32[]{:T(128)S(6)} %select_n.66), kind=kOutput, calls=%fused_computation | convolution fusion | flops 1342177280 | bytes 7602180 | tf_op jit(solution)/shard_map/dot_general | solution.py:307
  126.4 2.0 %shard_map.66 = (f32[256,640]{1,0:T(8,128)S(1)}, bf16[1296,128]{1,0:T(8,128)(2,1)}) custom-call(s32[1]{0:T(128)} %constant.74.clone.1.idx_ref, bf16[2576,128]{1,0:T(8,128)(2,1)S(1)} %collective-permute-done.27.f_ref, bf16[2576,128]{1,0:T(8,128)(2,1)S(1)} %collective-permute-done.28.b_ref, f32[256,1280]{1,0:T(8,128)S(1)} %fusion.own_ref), custom_call_target="tpu_custom_call" | custom-call | flops 42139648 | bytes 5267456 | tf_op jit(solution)/shard_map/pallas_call | solution.py:185
  128.5 2.7 %collective-permute-start.29 = (bf16[1296,128]{1,0:T(8,128)(2,1)}, bf16[1296,128]{1,0:T(8,128)(2,1)S(1)}, u32[]{:S(2)}, u32[]{:S(2)}) collective-permute-start(bf16[1296,128]{1,0:T(8,128)(2,1)} %get-tuple-element.55), channel_id=1, source_target_pairs={{0,4},{4,0},{1,5},{5,1},{2,6},{6,2},{3,7},{7,3},{8,12},{12,8},{9,1... | collective-permute-start | bytes 995336 | tf_op jit(solution)/shard_map/ppermute | solution.py:241
  132.0 2.6 %collective-permute-done.21.b_ref = bf16[2064,128]{1,0:T(8,128)(2,1)S(1)} collective-permute-done((bf16[2064,128]{1,0:T(8,128)(2,1)S(1)}, bf16[2064,128]{1,0:T(8,128)(2,1)S(1)}, u32[]{:S(2)}, u32[]{:S(2)}) %collective-permute-start.21) | collective-permute-done | bytes 528416 | tf_op jit(solution)/shard_map/ppermute | solution.py:256
  134.6 1.7 %shard_map.60 = bf16[128,1024]{1,0:T(8,128)(2,1)} custom-call(s32[2]{0:T(128)S(1)} %pad_add_fusion.2.idx_ref, bf16[2064,128]{1,0:T(8,128)(2,1)S(1)} %collective-permute-done.18.f_ref, bf16[2064,128]{1,0:T(8,128)(2,1)S(1)} %collective-permute-done.21.b_ref, f32[256,1024]{1,0:T(8,128)S(1)} %fusion.8.own_ref), custom_call_target="tpu_custom_call" | custom-call | flops 29491200 | bytes 3686400 | tf_op jit(solution)/shard_map/pallas_call | solution.py:185
  136.2 1.1 collective-permute-start.22
  138.4 1.5 %collective-permute-done.29.got_ref = bf16[1296,128]{1,0:T(8,128)(2,1)S(1)} collective-permute-done((bf16[1296,128]{1,0:T(8,128)(2,1)}, bf16[1296,128]{1,0:T(8,128)(2,1)S(1)}, u32[]{:S(2)}, u32[]{:S(2)}) %collective-permute-start.29) | collective-permute-done | bytes 331808 | tf_op jit(solution)/shard_map/ppermute | solution.py:241
  139.9 1.4 shard_map.67
  141.4 3.6 %collective-permute-done.22.got_ref = bf16[128,1024]{1,0:T(8,128)(2,1)} collective-permute-done((bf16[128,1024]{1,0:T(8,128)(2,1)}, bf16[128,1024]{1,0:T(8,128)(2,1)}, u32[]{:S(2)}, u32[]{:S(2)}) %collective-permute-start.22) | collective-permute-done | bytes 262176 | tf_op jit(solution)/shard_map/ppermute | solution.py:241
  145.0 2.3 %shard_map.61 = bf16[128,2048]{1,0:T(8,128)(2,1)} custom-call(s32[5]{0:T(128)S(1)} %stack.102.at_ref, bf16[128,1024]{1,0:T(8,128)(2,1)S(1)} %shard_map.59.mine_ref, bf16[128,1024]{1,0:T(8,128)(2,1)} %collective-permute-done.22.got_ref), custom_call_target="tpu_custom_call" | custom-call | flops 16777216 | bytes 2097152 | tf_op jit(solution)/shard_map/pallas_call | solution.py:185
  (85 shorter events, 20.0 us)
Async XLA Ops:
  0.6 17.3 %copy-start = (bf16[2048,640]{1,0:T(8,128)(2,1)S(1)}, bf16[2048,640]{1,0:T(8,128)(2,1)}, u32[]{:S(2)}) copy-start(bf16[2048,640]{1,0:T(8,128)(2,1)} %refs_0_) | copy-start | bytes 7864324
  2.7 11.2 %collective-permute-start = (bf16[128,1024]{1,0:T(8,128)(2,1)S(1)}, bf16[128,1024]{1,0:T(8,128)(2,1)}, u32[]{:S(2)}, u32[]{:S(2)}) collective-permute-start(bf16[128,1024]{1,0:T(8,128)(2,1)S(1)} %get-tuple-element.41.refs_0_), channel_id=1, source_target_pairs={{0,8},{1,57},{8,16},{9,1},{16,24},{17,9},{24,32},{25,17},{32,40},{... | collective-permute-start | bytes 786440 | tf_op jit(solution)/shard_map/ppermute | solution.py:256
  4.6 9.5 %collective-permute-start.2 = (bf16[128,1024]{1,0:T(8,128)(2,1)S(1)}, bf16[128,1024]{1,0:T(8,128)(2,1)}, u32[]{:S(2)}, u32[]{:S(2)}) collective-permute-start(bf16[128,1024]{1,0:T(8,128)(2,1)S(1)} %get-tuple-element.41.refs_0_), channel_id=1, source_target_pairs={{0,56},{1,9},{8,0},{9,17},{16,8},{17,25},{24,16},{25,33},{32,24},{... | collective-permute-start | bytes 786440 | tf_op jit(solution)/shard_map/ppermute | solution.py:256
  10.5 15.1 %collective-permute-start.5 = (bf16[256,640]{1,0:T(8,128)(2,1)}, bf16[256,640]{1,0:T(8,128)(2,1)}, u32[]{:S(2)}, u32[]{:S(2)}) collective-permute-start(bf16[256,640]{1,0:T(8,128)(2,1)} %get-tuple-element.57), channel_id=1, source_target_pairs={{0,4},{4,0},{1,5},{5,1},{2,6},{6,2},{3,7},{7,3},{8,12},{12,8},{9,1... | collective-permute-start | bytes 983048 | tf_op jit(solution)/shard_map/ppermute | solution.py:241
  12.1 13.5 %collective-permute-start.4 = (bf16[128,1024]{1,0:T(8,128)(2,1)}, bf16[128,1024]{1,0:T(8,128)(2,1)}, u32[]{:S(2)}, u32[]{:S(2)}) collective-permute-start(bf16[128,1024]{1,0:T(8,128)(2,1)} %get-tuple-element.31), channel_id=1, source_target_pairs={{0,4},{4,0},{1,5},{5,1},{2,6},{6,2},{3,7},{7,3},{8,12},{12,8},{9,1... | collective-permute-start | bytes 786440 | tf_op jit(solution)/shard_map/ppermute | solution.py:241
  14.0 11.7 %collective-permute-start.1 = (bf16[128,1024]{1,0:T(8,128)(2,1)}, bf16[128,1024]{1,0:T(8,128)(2,1)S(1)}, u32[]{:S(2)}, u32[]{:S(2)}) collective-permute-start(bf16[128,1024]{1,0:T(8,128)(2,1)} %collective-permute-done.refs_2_), channel_id=1, source_target_pairs={{0,8},{1,57},{8,16},{9,1},{16,24},{17,9},{24,32},{25,17},{32,40},{... | collective-permute-start | bytes 786440 | tf_op jit(solution)/shard_map/ppermute | solution.py:256
  14.2 11.5 %collective-permute-start.3 = (bf16[128,1024]{1,0:T(8,128)(2,1)}, bf16[128,1024]{1,0:T(8,128)(2,1)S(1)}, u32[]{:S(2)}, u32[]{:S(2)}) collective-permute-start(bf16[128,1024]{1,0:T(8,128)(2,1)} %collective-permute-done.2.refs_4_), channel_id=1, source_target_pairs={{0,56},{1,9},{8,0},{9,17},{16,8},{17,25},{24,16},{25,33},{32,24},{... | collective-permute-start | bytes 786440 | tf_op jit(solution)/shard_map/ppermute | solution.py:256
  17.9 9.4 %copy-start.15 = (bf16[256,640]{1,0:T(8,128)(2,1)S(1)}, bf16[256,640]{1,0:T(8,128)(2,1)}, u32[]{:S(2)}) copy-start(bf16[256,640]{1,0:T(8,128)(2,1)} %get-tuple-element.56) | copy-start | bytes 983044
  25.7 1.7 %copy-start.1 = (bf16[128,1024]{1,0:T(8,128)(2,1)}, bf16[128,1024]{1,0:T(8,128)(2,1)S(1)}, u32[]{:S(2)}) copy-start(bf16[128,1024]{1,0:T(8,128)(2,1)S(1)} %collective-permute-done.1.refs_6_) | copy-start | bytes 786436
  25.7 1.7 %copy-start.3 = (bf16[128,1024]{1,0:T(8,128)(2,1)}, bf16[128,1024]{1,0:T(8,128)(2,1)S(1)}, u32[]{:S(2)}) copy-start(bf16[128,1024]{1,0:T(8,128)(2,1)S(1)} %collective-permute-done.3.refs_8_) | copy-start | bytes 786436
  25.7 23.6 %collective-permute-start.12 = (bf16[1024,640]{1,0:T(8,128)(2,1)S(1)}, bf16[1024,640]{1,0:T(8,128)(2,1)}, u32[]{:S(2)}, u32[]{:S(2)}) collective-permute-start(bf16[1024,640]{1,0:T(8,128)(2,1)S(1)} %constant_dynamic-slice_fusion), channel_id=1, source_target_pairs={{0,4},{1,7},{4,2},{5,1},{2,6},{3,5},{6,0},{7,3},{8,12},{9,15},{12,... | collective-permute-start | bytes 3932168 | tf_op jit(solution)/shard_map/ppermute | solution.py:250
  28.4 20.0 %collective-permute-start.10 = (bf16[256,1280]{1,0:T(8,128)(2,1)S(1)}, bf16[256,1280]{1,0:T(8,128)(2,1)}, u32[]{:S(2)}, u32[]{:S(2)}) collective-permute-start(bf16[256,1280]{1,0:T(8,128)(2,1)S(1)} %pad_maximum_fusion.refs_0_), channel_id=1, source_target_pairs={{0,64},{1,193},{64,128},{65,1},{128,192},{129,65},{192,0},{193,129... | collective-permute-start | bytes 1966088 | tf_op jit(solution)/shard_map/ppermute | solution.py:256
  29.6 18.7 %collective-permute-start.11 = (bf16[256,1280]{1,0:T(8,128)(2,1)S(1)}, bf16[256,1280]{1,0:T(8,128)(2,1)S(1)}, u32[]{:S(2)}, u32[]{:S(2)}) collective-permute-start(bf16[256,1280]{1,0:T(8,128)(2,1)S(1)} %pad_maximum_fusion.refs_0_), channel_id=1, source_target_pairs={{0,192},{1,65},{64,0},{65,129},{128,64},{129,193},{192,128},{193,1... | collective-permute-start | bytes 1966088 | tf_op jit(solution)/shard_map/ppermute | solution.py:256
  30.5 8.5 %collective-permute-start.6 = (bf16[128,1024]{1,0:T(8,128)(2,1)}, bf16[128,1024]{1,0:T(8,128)(2,1)S(1)}, u32[]{:S(2)}, u32[]{:S(2)}) collective-permute-start(bf16[128,1024]{1,0:T(8,128)(2,1)} %collective-permute-done.4.refs_1_), channel_id=1, source_target_pairs={{0,8},{1,57},{8,16},{9,1},{16,24},{17,9},{24,32},{25,17},{32,40},{... | collective-permute-start | bytes 786440 | tf_op jit(solution)/shard_map/ppermute | solution.py:256
  30.5 9.3 %collective-permute-start.8 = (bf16[128,1024]{1,0:T(8,128)(2,1)}, bf16[128,1024]{1,0:T(8,128)(2,1)S(1)}, u32[]{:S(2)}, u32[]{:S(2)}) collective-permute-start(bf16[128,1024]{1,0:T(8,128)(2,1)} %collective-permute-done.4.refs_1_), channel_id=1, source_target_pairs={{0,56},{1,9},{8,0},{9,17},{16,8},{17,25},{24,16},{25,33},{32,24},{... | collective-permute-start | bytes 786440 | tf_op jit(solution)/shard_map/ppermute | solution.py:256
  39.0 7.6 %collective-permute-start.7 = (bf16[128,1024]{1,0:T(8,128)(2,1)S(1)}, bf16[128,1024]{1,0:T(8,128)(2,1)S(1)}, u32[]{:S(2)}, u32[]{:S(2)}) collective-permute-start(bf16[128,1024]{1,0:T(8,128)(2,1)S(1)} %collective-permute-done.6.refs_3_), channel_id=1, source_target_pairs={{0,8},{1,57},{8,16},{9,1},{16,24},{17,9},{24,32},{25,17},{32,40},{... | collective-permute-start | bytes 786440 | tf_op jit(solution)/shard_map/ppermute | solution.py:256
  39.0 0.7 copy-start.11
  39.8 8.6 %collective-permute-start.9 = (bf16[128,1024]{1,0:T(8,128)(2,1)S(1)}, bf16[128,1024]{1,0:T(8,128)(2,1)S(1)}, u32[]{:S(2)}, u32[]{:S(2)}) collective-permute-start(bf16[128,1024]{1,0:T(8,128)(2,1)S(1)} %collective-permute-done.8.refs_5_), channel_id=1, source_target_pairs={{0,56},{1,9},{8,0},{9,17},{16,8},{17,25},{24,16},{25,33},{32,24},{... | collective-permute-start | bytes 786440 | tf_op jit(solution)/shard_map/ppermute | solution.py:256
  43.4 0.7 copy-start.13
  46.6 1.8 %copy-start.5 = (bf16[128,1024]{1,0:T(8,128)(2,1)}, bf16[128,1024]{1,0:T(8,128)(2,1)S(1)}, u32[]{:S(2)}) copy-start(bf16[128,1024]{1,0:T(8,128)(2,1)S(1)} %collective-permute-done.7.refs_7_) | copy-start | bytes 786436
  48.4 1.0 copy-start.7
  48.4 0.9 copy-start.9
  49.3 16.7 %collective-permute-start.13 = (bf16[1024,640]{1,0:T(8,128)(2,1)}, bf16[1024,640]{1,0:T(8,128)(2,1)}, u32[]{:S(2)}, u32[]{:S(2)}) collective-permute-start(bf16[1024,640]{1,0:T(8,128)(2,1)} %collective-permute-done.12.refs_1_), channel_id=1, source_target_pairs={{0,1},{1,0},{2,3},{3,2},{4,5},{5,4},{6,7},{7,6},{8,9},{9,8},{10,11... | collective-permute-start | bytes 3932168 | tf_op jit(solution)/shard_map/ppermute | solution.py:241
  50.5 11.5 %collective-permute-start.14 = (bf16[256,1280]{1,0:T(8,128)(2,1)}, bf16[256,1280]{1,0:T(8,128)(2,1)}, u32[]{:S(2)}, u32[]{:S(2)}) collective-permute-start(bf16[256,1280]{1,0:T(8,128)(2,1)} %collective-permute-done.10.refs_1_), channel_id=1, source_target_pairs={{0,64},{1,193},{64,128},{65,1},{128,192},{129,65},{192,0},{193,129... | collective-permute-start | bytes 1966088 | tf_op jit(solution)/shard_map/ppermute | solution.py:256
  56.0 20.9 %collective-permute-start.23 = (bf16[256,1024]{1,0:T(8,128)(2,1)S(1)}, bf16[256,1024]{1,0:T(8,128)(2,1)S(1)}, u32[]{:S(2)}, u32[]{:S(2)}) collective-permute-start(bf16[256,1024]{1,0:T(8,128)(2,1)S(1)} %pad_maximum_fusion.1), channel_id=1, source_target_pairs={{0,8},{1,57},{8,16},{9,1},{16,24},{17,9},{24,32},{25,17},{32,40},{... | collective-permute-start | bytes 1572872 | tf_op jit(solution)/shard_map/ppermute | solution.py:256
  56.2 20.6 %collective-permute-start.24 = (bf16[256,1024]{1,0:T(8,128)(2,1)S(1)}, bf16[256,1024]{1,0:T(8,128)(2,1)S(1)}, u32[]{:S(2)}, u32[]{:S(2)}) collective-permute-start(bf16[256,1024]{1,0:T(8,128)(2,1)S(1)} %pad_maximum_fusion.2), channel_id=1, source_target_pairs={{0,56},{1,9},{8,0},{9,17},{16,8},{17,25},{24,16},{25,33},{32,24},{... | collective-permute-start | bytes 1572872 | tf_op jit(solution)/shard_map/ppermute | solution.py:256
  62.0 1.1 copy-start.10
  70.2 24.0 %collective-permute-start.15 = (bf16[2064,128]{1,0:T(8,128)(2,1)S(1)}, bf16[2064,128]{1,0:T(8,128)(2,1)S(1)}, u32[]{:S(2)}, u32[]{:S(2)}) collective-permute-start(bf16[2064,128]{1,0:T(8,128)(2,1)S(1)} %shard_map.52), channel_id=1, source_target_pairs={{0,8},{1,57},{8,16},{9,1},{16,24},{17,9},{24,32},{25,17},{32,40},{... | collective-permute-start | bytes 1585160 | tf_op jit(solution)/shard_map/ppermute | solution.py:256
  71.8 29.9 %collective-permute-start.19 = (bf16[2064,128]{1,0:T(8,128)(2,1)S(1)}, bf16[2064,128]{1,0:T(8,128)(2,1)S(1)}, u32[]{:S(2)}, u32[]{:S(2)}) collective-permute-start(bf16[2064,128]{1,0:T(8,128)(2,1)S(1)} %shard_map.56), channel_id=1, source_target_pairs={{0,56},{1,9},{8,0},{9,17},{16,8},{17,25},{24,16},{25,33},{32,24},{... | collective-permute-start | bytes 1585160 | tf_op jit(solution)/shard_map/ppermute | solution.py:256
  76.8 15.2 %collective-permute-start.25 = (bf16[256,1024]{1,0:T(8,128)(2,1)S(1)}, bf16[256,1024]{1,0:T(8,128)(2,1)S(1)}, u32[]{:S(2)}, u32[]{:S(2)}) collective-permute-start(bf16[256,1024]{1,0:T(8,128)(2,1)S(1)} %collective-permute-done.23.refs_10_), channel_id=1, source_target_pairs={{0,8},{1,57},{8,16},{9,1},{16,24},{17,9},{24,32},{25,17},{32,40},{... | collective-permute-start | bytes 1572872 | tf_op jit(solution)/shard_map/ppermute | solution.py:256
  77.8 14.2 %copy-start.2 = (bf16[128,1024]{1,0:T(8,128)(2,1)S(1)}, bf16[128,1024]{1,0:T(8,128)(2,1)}, u32[]{:S(2)}) copy-start(bf16[128,1024]{1,0:T(8,128)(2,1)} %copy-done.1) | copy-start | bytes 786436
  77.8 14.2 %copy-start.4 = (bf16[128,1024]{1,0:T(8,128)(2,1)S(1)}, bf16[128,1024]{1,0:T(8,128)(2,1)}, u32[]{:S(2)}) copy-start(bf16[128,1024]{1,0:T(8,128)(2,1)} %copy-done.3) | copy-start | bytes 786436
  77.8 14.2 %copy-start.6 = (bf16[128,1024]{1,0:T(8,128)(2,1)S(1)}, bf16[128,1024]{1,0:T(8,128)(2,1)}, u32[]{:S(2)}) copy-start(bf16[128,1024]{1,0:T(8,128)(2,1)} %copy-done.5) | copy-start | bytes 786436
  77.8 14.2 %copy-start.8 = (bf16[128,1024]{1,0:T(8,128)(2,1)S(1)}, bf16[128,1024]{1,0:T(8,128)(2,1)}, u32[]{:S(2)}) copy-start(bf16[128,1024]{1,0:T(8,128)(2,1)} %copy-done.7) | copy-start | bytes 786436
  77.8 14.2 %copy-start.12 = (bf16[128,1024]{1,0:T(8,128)(2,1)S(1)}, bf16[128,1024]{1,0:T(8,128)(2,1)}, u32[]{:S(2)}) copy-start(bf16[128,1024]{1,0:T(8,128)(2,1)} %copy-done.11) | copy-start | bytes 786436
  77.8 14.2 %copy-start.14 = (bf16[128,1024]{1,0:T(8,128)(2,1)S(1)}, bf16[128,1024]{1,0:T(8,128)(2,1)}, u32[]{:S(2)}) copy-start(bf16[128,1024]{1,0:T(8,128)(2,1)} %copy-done.13) | copy-start | bytes 786436
  95.2 10.9 %collective-permute-start.16 = (bf16[2064,128]{1,0:T(8,128)(2,1)S(1)}, bf16[2064,128]{1,0:T(8,128)(2,1)S(1)}, u32[]{:S(2)}, u32[]{:S(2)}) collective-permute-start(bf16[2064,128]{1,0:T(8,128)(2,1)S(1)} %shard_map.53), channel_id=1, source_target_pairs={{0,8},{1,57},{8,16},{9,1},{16,24},{17,9},{24,32},{25,17},{32,40},{... | collective-permute-start | bytes 1585160 | tf_op jit(solution)/shard_map/ppermute | solution.py:256
  97.5 12.0 %collective-permute-start.26 = (bf16[2576,128]{1,0:T(8,128)(2,1)S(1)}, bf16[2576,128]{1,0:T(8,128)(2,1)S(1)}, u32[]{:S(2)}, u32[]{:S(2)}) collective-permute-start(bf16[2576,128]{1,0:T(8,128)(2,1)S(1)} %shard_map.63), channel_id=1, source_target_pairs={{0,64},{1,193},{64,128},{65,1},{128,192},{129,65},{192,0},{193,129... | collective-permute-start | bytes 1978376 | tf_op jit(solution)/shard_map/ppermute | solution.py:256
  102.6 15.8 %collective-permute-start.20 = (bf16[2064,128]{1,0:T(8,128)(2,1)S(1)}, bf16[2064,128]{1,0:T(8,128)(2,1)S(1)}, u32[]{:S(2)}, u32[]{:S(2)}) collective-permute-start(bf16[2064,128]{1,0:T(8,128)(2,1)S(1)} %shard_map.57), channel_id=1, source_target_pairs={{0,56},{1,9},{8,0},{9,17},{16,8},{17,25},{24,16},{25,33},{32,24},{... | collective-permute-start | bytes 1585160 | tf_op jit(solution)/shard_map/ppermute | solution.py:256
  107.0 16.0 %collective-permute-start.17 = (bf16[2064,128]{1,0:T(8,128)(2,1)S(1)}, bf16[2064,128]{1,0:T(8,128)(2,1)S(1)}, u32[]{:S(2)}, u32[]{:S(2)}) collective-permute-start(bf16[2064,128]{1,0:T(8,128)(2,1)S(1)} %shard_map.54), channel_id=1, source_target_pairs={{0,8},{1,57},{8,16},{9,1},{16,24},{17,9},{24,32},{25,17},{32,40},{... | collective-permute-start | bytes 1585160 | tf_op jit(solution)/shard_map/ppermute | solution.py:256
  109.3 16.3 %collective-permute-start.28 = (bf16[2576,128]{1,0:T(8,128)(2,1)S(1)}, bf16[2576,128]{1,0:T(8,128)(2,1)S(1)}, u32[]{:S(2)}, u32[]{:S(2)}) collective-permute-start(bf16[2576,128]{1,0:T(8,128)(2,1)S(1)} %shard_map.65), channel_id=1, source_target_pairs={{0,192},{1,65},{64,0},{65,129},{128,64},{129,193},{192,128},{193,1... | collective-permute-start | bytes 1978376 | tf_op jit(solution)/shard_map/ppermute | solution.py:256
  110.6 15.9 %collective-permute-start.27 = (bf16[2576,128]{1,0:T(8,128)(2,1)S(1)}, bf16[2576,128]{1,0:T(8,128)(2,1)S(1)}, u32[]{:S(2)}, u32[]{:S(2)}) collective-permute-start(bf16[2576,128]{1,0:T(8,128)(2,1)S(1)} %shard_map.64), channel_id=1, source_target_pairs={{0,64},{1,193},{64,128},{65,1},{128,192},{129,65},{192,0},{193,129... | collective-permute-start | bytes 1978376 | tf_op jit(solution)/shard_map/ppermute | solution.py:256
  119.2 15.3 %collective-permute-start.21 = (bf16[2064,128]{1,0:T(8,128)(2,1)S(1)}, bf16[2064,128]{1,0:T(8,128)(2,1)S(1)}, u32[]{:S(2)}, u32[]{:S(2)}) collective-permute-start(bf16[2064,128]{1,0:T(8,128)(2,1)S(1)} %shard_map.58), channel_id=1, source_target_pairs={{0,56},{1,9},{8,0},{9,17},{16,8},{17,25},{24,16},{25,33},{32,24},{... | collective-permute-start | bytes 1585160 | tf_op jit(solution)/shard_map/ppermute | solution.py:256
  123.9 10.6 %collective-permute-start.18 = (bf16[2064,128]{1,0:T(8,128)(2,1)S(1)}, bf16[2064,128]{1,0:T(8,128)(2,1)S(1)}, u32[]{:S(2)}, u32[]{:S(2)}) collective-permute-start(bf16[2064,128]{1,0:T(8,128)(2,1)S(1)} %shard_map.55), channel_id=1, source_target_pairs={{0,8},{1,57},{8,16},{9,1},{16,24},{17,9},{24,32},{25,17},{32,40},{... | collective-permute-start | bytes 1585160 | tf_op jit(solution)/shard_map/ppermute | solution.py:256
  128.5 11.5 %collective-permute-start.29 = (bf16[1296,128]{1,0:T(8,128)(2,1)}, bf16[1296,128]{1,0:T(8,128)(2,1)S(1)}, u32[]{:S(2)}, u32[]{:S(2)}) collective-permute-start(bf16[1296,128]{1,0:T(8,128)(2,1)} %get-tuple-element.55), channel_id=1, source_target_pairs={{0,4},{4,0},{1,5},{5,1},{2,6},{6,2},{3,7},{7,3},{8,12},{12,8},{9,1... | collective-permute-start | bytes 995336 | tf_op jit(solution)/shard_map/ppermute | solution.py:241
  136.2 8.7 %collective-permute-start.22 = (bf16[128,1024]{1,0:T(8,128)(2,1)}, bf16[128,1024]{1,0:T(8,128)(2,1)}, u32[]{:S(2)}, u32[]{:S(2)}) collective-permute-start(bf16[128,1024]{1,0:T(8,128)(2,1)} %shard_map.60), channel_id=1, source_target_pairs={{0,4},{4,0},{1,5},{5,1},{2,6},{6,2},{3,7},{7,3},{8,12},{12,8},{9,1... | collective-permute-start | bytes 786440 | tf_op jit(solution)/shard_map/ppermute | solution.py:241

commit v6 on v5

--- a/solution.py
+++ b/solution.py
@@ -294,13 +294,16 @@
 def scattered(share, axis, first):
     n, me = lax.axis_size(axis), lax.axis_index(axis)
     step = 1 - 2 * lax.axis_index("c")
-    came = []
+    came, second = [], []
     for way, hops, got in ((1, n // 2, first[0]), (-1, n - n // 2 - 1, first[1])):
         got = ring(got, axis, way)
         for k in range(hops - 1, 0, -1):
-            got = ring(hop([got], share(lax.rem(me + way * step * k + n, n))), axis, way)
+            sent = hop([got], share(lax.rem(me + way * step * k + n, n)))
+            if k == hops - 1:
+                second.append(sent)
+            got = ring(sent, axis, way)
         came.append(got)
-    return came
+    return came, second
 
 
 def dot(a, b, dims):
@@ -363,8 +366,8 @@
         count = 2 * own_tokens
         return dot(lax.dynamic_slice_in_dim(g_pair, i * count, count, 0), w_all, ((1,), (1,)))
 
-    acts_all = placed(after(*first, *arrays)[2:], acts_pieces, shape)
-    came = scattered(of_tokens, "z", first)
+    came, second = scattered(of_tokens, "z", first)
+    acts_all = placed(after(*second, *arrays)[2:], acts_pieces, shape)
     mine = of_tokens(lax.axis_index("z"))
 
     def finished(of):
@@ -379,7 +382,7 @@
         acts = lax.dynamic_slice_in_dim(acts_all, i * half, half, 1)
         return dot(acts, g_pair, ((0,), (0,)))
 
-    came = scattered(of_rows, "x", [hop([], of_rows(block_at("x", k))) for k in (2, -1)])
+    came, _ = scattered(of_rows, "x", [hop([], of_rows(block_at("x", k))) for k in (2, -1)])
     mine = of_rows(lax.axis_index("x"))
     shapes = [jax.ShapeDtypeStruct((half, width), F32), coded_shape(half, width)]
     owned, coded = call(owned_kernel, [jnp.int32(0)], came + [mine], None, shapes, [(half, width)])

time: 150 us -> 146 us (0.973)
  waiting for transfers between devices: 47.8 us -> 41.6 us
  starting transfers between devices: 49.5 us -> 51.2 us
    ppermute x24, waiting for transfers between devices: 35.1 us -> 29 us  [ring(): return lax.ppermute(a, (axis, 'c'), perm)]
    ppermute x5, starting transfers between devices: 6.87 us -> 8.54 us  [swap(): return lax.ppermute(a, axis, [(0, 1), (1, 0)])]
  transfers between devices with their start and end apart: 30 -> 30, of which waited for: 14 -> 14; matrix products, arithmetic and copies ran while one was open for 12% -> 12% of each run, Pallas kernels for 16% -> 17%
where the time goes in v6:
time: 146 us; the launch traced here: 143 us
  starting transfers between devices  51.2 us (35%)
  waiting for transfers between devices  41.6 us (28%)
  Pallas kernels  26.2 us (18%)
  matrix products  11.5 us (8%)
  local copies, waits for them, and re-layouts  7 us (5%)
  other arithmetic  4.2 us (3%)
    ppermute x24, starting transfers between devices, ring(): return lax.ppermute(a, (axis, 'c'), perm)  41 us
    ppermute x24, waiting for transfers between devices, ring(): return lax.ppermute(a, (axis, 'c'), perm)  29 us
    pallas_call x13, Pallas kernels, call(): pl.pallas_call(kernel, grid_spec=pltpu.PrefetchScalarGridSpec(num_scalar_...  15.5 us
    ppermute x5, waiting for transfers between devices, swap(): return lax.ppermute(a, axis, [(0, 1), (1, 0)])  12.6 us
    dot_general x10, matrix products, dot(): return lax.dot_general(a, b, (dims, ((), ())), preferred_element_type=F32)  11.5 us
    ppermute x5, starting transfers between devices, swap(): return lax.ppermute(a, axis, [(0, 1), (1, 0)])  8.54 us
    pallas_call x3, Pallas kernels, placed(): pl.pallas_call(functools.partial(placed_kernel, fixed), grid_spec=pltpu.P...  7.84 us
    unnamed x32, local copies, waits for them, and re-layouts  3.49 us
  transfers between devices with their start and end apart: 30, of which 14 were waited for; matrix products, arithmetic and copies ran while one was open for 12% of the time, Pallas kernels for 17%

profile of v6, /device:TPU:4, one launch (start us, length us, event | category | flops | bytes accessed | tf_op | source)
XLA Modules:
  0.0 142.8 jit_solution(5090789632882162960)
XLA Ops:
  0.6 1.3 fusion.30
  2.7 1.9 %collective-permute-start = (bf16[128,1024]{1,0:T(8,128)(2,1)S(1)}, bf16[128,1024]{1,0:T(8,128)(2,1)}, u32[]{:S(2)}, u32[]{:S(2)}) collective-permute-start(bf16[128,1024]{1,0:T(8,128)(2,1)S(1)} %get-tuple-element.41.refs_0_), channel_id=1, source_target_pairs={{0,8},{1,57},{8,16},{9,1},{16,24},{17,9},{24,32},{25,17},{32,40},{... | collective-permute-start | bytes 786440 | tf_op jit(solution)/shard_map/ppermute | solution.py:256
  4.6 3.9 %collective-permute-start.2 = (bf16[128,1024]{1,0:T(8,128)(2,1)S(1)}, bf16[128,1024]{1,0:T(8,128)(2,1)}, u32[]{:S(2)}, u32[]{:S(2)}) collective-permute-start(bf16[128,1024]{1,0:T(8,128)(2,1)S(1)} %get-tuple-element.41.refs_0_), channel_id=1, source_target_pairs={{0,56},{1,9},{8,0},{9,17},{16,8},{17,25},{24,16},{25,33},{32,24},{... | collective-permute-start | bytes 786440 | tf_op jit(solution)/shard_map/ppermute | solution.py:256
  8.6 2.0 %dynamic-slice_bitcast_fusion = (bf16[256,640]{1,0:T(8,128)(2,1)}, bf16[256,640]{1,0:T(8,128)(2,1)}) fusion(bf16[1,512,640]{2,1,0:T(8,128)(2,1)} %param.5, s32[]{:T(128)S(6)} %select_n.55, s32[]{:T(128)S(6)} %select_n.54), kind=kLoop, calls=%fused_computation.23 | loop fusion | bytes 1310728 | tf_op jit(solution)/shard_map/dynamic_slice | solution.py:332
  10.5 1.6 %collective-permute-start.5 = (bf16[256,640]{1,0:T(8,128)(2,1)}, bf16[256,640]{1,0:T(8,128)(2,1)}, u32[]{:S(2)}, u32[]{:S(2)}) collective-permute-start(bf16[256,640]{1,0:T(8,128)(2,1)} %get-tuple-element.57), channel_id=1, source_target_pairs={{0,4},{4,0},{1,5},{5,1},{2,6},{6,2},{3,7},{7,3},{8,12},{12,8},{9,1... | collective-permute-start | bytes 983048 | tf_op jit(solution)/shard_map/ppermute | solution.py:241
  12.6 1.4 collective-permute-done.refs_2_
  14.2 3.8 %collective-permute-start.3 = (bf16[128,1024]{1,0:T(8,128)(2,1)}, bf16[128,1024]{1,0:T(8,128)(2,1)S(1)}, u32[]{:S(2)}, u32[]{:S(2)}) collective-permute-start(bf16[128,1024]{1,0:T(8,128)(2,1)} %collective-permute-done.2.refs_4_), channel_id=1, source_target_pairs={{0,56},{1,9},{8,0},{9,17},{16,8},{17,25},{24,16},{25,33},{32,24},{... | collective-permute-start | bytes 786440 | tf_op jit(solution)/shard_map/ppermute | solution.py:256
  18.1 7.6 %collective-permute-done.4.refs_1_ = bf16[128,1024]{1,0:T(8,128)(2,1)} collective-permute-done((bf16[128,1024]{1,0:T(8,128)(2,1)}, bf16[128,1024]{1,0:T(8,128)(2,1)}, u32[]{:S(2)}, u32[]{:S(2)}) %collective-permute-start.4) | collective-permute-done | bytes 262176 | tf_op jit(solution)/shard_map/ppermute | solution.py:241
  25.7 1.7 %collective-permute-start.12 = (bf16[1024,640]{1,0:T(8,128)(2,1)S(1)}, bf16[1024,640]{1,0:T(8,128)(2,1)}, u32[]{:S(2)}, u32[]{:S(2)}) collective-permute-start(bf16[1024,640]{1,0:T(8,128)(2,1)S(1)} %constant_dynamic-slice_fusion), channel_id=1, source_target_pairs={{0,4},{1,7},{4,2},{5,1},{2,6},{3,5},{6,0},{7,3},{8,12},{9,15},{12,... | collective-permute-start | bytes 3932168 | tf_op jit(solution)/shard_map/ppermute | solution.py:250
  28.4 1.3 collective-permute-start.10
  30.5 3.2 %collective-permute-start.8 = (bf16[128,1024]{1,0:T(8,128)(2,1)}, bf16[128,1024]{1,0:T(8,128)(2,1)S(1)}, u32[]{:S(2)}, u32[]{:S(2)}) collective-permute-start(bf16[128,1024]{1,0:T(8,128)(2,1)} %collective-permute-done.4.refs_1_), channel_id=1, source_target_pairs={{0,56},{1,9},{8,0},{9,17},{16,8},{17,25},{24,16},{25,33},{32,24},{... | collective-permute-start | bytes 786440 | tf_op jit(solution)/shard_map/ppermute | solution.py:256
  33.7 5.3 %collective-permute-done.6.refs_3_ = bf16[128,1024]{1,0:T(8,128)(2,1)S(1)} collective-permute-done((bf16[128,1024]{1,0:T(8,128)(2,1)}, bf16[128,1024]{1,0:T(8,128)(2,1)S(1)}, u32[]{:S(2)}, u32[]{:S(2)}) %collective-permute-start.6) | collective-permute-done | bytes 262176 | tf_op jit(solution)/shard_map/ppermute | solution.py:256
  39.8 3.6 %collective-permute-start.9 = (bf16[128,1024]{1,0:T(8,128)(2,1)S(1)}, bf16[128,1024]{1,0:T(8,128)(2,1)S(1)}, u32[]{:S(2)}, u32[]{:S(2)}) collective-permute-start(bf16[128,1024]{1,0:T(8,128)(2,1)S(1)} %collective-permute-done.8.refs_5_), channel_id=1, source_target_pairs={{0,56},{1,9},{8,0},{9,17},{16,8},{17,25},{24,16},{25,33},{32,24},{... | collective-permute-start | bytes 786440 | tf_op jit(solution)/shard_map/ppermute | solution.py:256
  44.1 2.5 %collective-permute-done.7.refs_7_ = bf16[128,1024]{1,0:T(8,128)(2,1)S(1)} collective-permute-done((bf16[128,1024]{1,0:T(8,128)(2,1)S(1)}, bf16[128,1024]{1,0:T(8,128)(2,1)S(1)}, u32[]{:S(2)}, u32[]{:S(2)}) %collective-permute-start.7) | collective-permute-done | bytes 262176 | tf_op jit(solution)/shard_map/ppermute | solution.py:256
  46.6 1.8 %collective-permute-done.9.refs_9_ = bf16[128,1024]{1,0:T(8,128)(2,1)S(1)} collective-permute-done((bf16[128,1024]{1,0:T(8,128)(2,1)S(1)}, bf16[128,1024]{1,0:T(8,128)(2,1)S(1)}, u32[]{:S(2)}, u32[]{:S(2)}) %collective-permute-start.9) | collective-permute-done | bytes 262176 | tf_op jit(solution)/shard_map/ppermute | solution.py:256
  49.3 1.1 collective-permute-start.13
  50.5 3.1 %collective-permute-start.14 = (bf16[256,1280]{1,0:T(8,128)(2,1)}, bf16[256,1280]{1,0:T(8,128)(2,1)}, u32[]{:S(2)}, u32[]{:S(2)}) collective-permute-start(bf16[256,1280]{1,0:T(8,128)(2,1)} %collective-permute-done.10.refs_1_), channel_id=1, source_target_pairs={{0,64},{1,193},{64,128},{65,1},{128,192},{129,65},{192,0},{193,129... | collective-permute-start | bytes 1966088 | tf_op jit(solution)/shard_map/ppermute | solution.py:256
  53.8 1.1 pad_maximum_fusion.1
  56.2 3.2 %collective-permute-start.24 = (bf16[256,1024]{1,0:T(8,128)(2,1)S(1)}, bf16[256,1024]{1,0:T(8,128)(2,1)S(1)}, u32[]{:S(2)}, u32[]{:S(2)}) collective-permute-start(bf16[256,1024]{1,0:T(8,128)(2,1)S(1)} %pad_maximum_fusion.2), channel_id=1, source_target_pairs={{0,56},{1,9},{8,0},{9,17},{16,8},{17,25},{24,16},{25,33},{32,24},{... | collective-permute-start | bytes 1572872 | tf_op jit(solution)/shard_map/ppermute | solution.py:256
  59.5 2.5 %collective-permute-done.14.refs_3_ = bf16[256,1280]{1,0:T(8,128)(2,1)} collective-permute-done((bf16[256,1280]{1,0:T(8,128)(2,1)}, bf16[256,1280]{1,0:T(8,128)(2,1)}, u32[]{:S(2)}, u32[]{:S(2)}) %collective-permute-start.14) | collective-permute-done | bytes 655392 | tf_op jit(solution)/shard_map/ppermute | solution.py:256
  62.0 1.1 copy-done.10
  63.1 3.0 %shard_map.51.w_ref = bf16[1024,1280]{1,0:T(8,128)(2,1)S(1)} custom-call(s32[4]{0:T(128)S(1)} %iota_multiply_fusion.at_ref, bf16[256,1280]{1,0:T(8,128)(2,1)S(1)} %pad_maximum_fusion.refs_0_, bf16[256,1280]{1,0:T(8,128)(2,1)} %collective-permute-done.10.refs_1_, bf16[256,1280]{1,0:T(8,128)(2,1)S(1)} %copy-done.10, ...), custom_call_target="tpu_custom_call" | custom-call | bytes 5242880 | tf_op jit(solution)/shard_map/pallas_call | solution.py:216
  66.0 2.7 %shard_map.50.g_ref = bf16[2048,1280]{1,0:T(8,128)(2,1)S(1)} custom-call(s32[3]{0:T(128)S(1)} %pad_add_fusion.1.at_ref, bf16[2048,640]{1,0:T(8,128)(2,1)S(1)} %copy-done, bf16[1024,640]{1,0:T(8,128)(2,1)} %collective-permute-done.12.refs_1_, bf16[1024,640]{1,0:T(8,128)(2,1)} %collective-permute-done.13.refs_2_), custom_call_target="tpu_custom_call" | custom-call | bytes 10485760 | tf_op jit(solution)/shard_map/pallas_call | solution.py:216
  68.8 1.4 %shard_map.52 = bf16[2064,128]{1,0:T(8,128)(2,1)S(1)} custom-call(s32[1]{0:T(128)} %bitcast.5.at_ref, bf16[2048,1280]{1,0:T(8,128)(2,1)S(1)} %shard_map.50.g_ref, bf16[1024,1280]{1,0:T(8,128)(2,1)S(1)} %shard_map.51.w_ref), custom_call_target="tpu_custom_call" | custom-call | flops 671088640 | bytes 1056768 | tf_op jit(solution)/shard_map/pallas_call | solution.py:122
  70.3 1.4 %shard_map.56 = bf16[2064,128]{1,0:T(8,128)(2,1)S(1)} custom-call(s32[1]{0:T(128)} %bitcast.10.at_ref, bf16[2048,1280]{1,0:T(8,128)(2,1)S(1)} %shard_map.50.g_ref, bf16[1024,1280]{1,0:T(8,128)(2,1)S(1)} %shard_map.51.w_ref), custom_call_target="tpu_custom_call" | custom-call | flops 671088640 | bytes 1056768 | tf_op jit(solution)/shard_map/pallas_call | solution.py:122
  71.8 3.3 %collective-permute-start.19 = (bf16[2064,128]{1,0:T(8,128)(2,1)S(1)}, bf16[2064,128]{1,0:T(8,128)(2,1)S(1)}, u32[]{:S(2)}, u32[]{:S(2)}) collective-permute-start(bf16[2064,128]{1,0:T(8,128)(2,1)S(1)} %shard_map.56), channel_id=1, source_target_pairs={{0,56},{1,9},{8,0},{9,17},{16,8},{17,25},{24,16},{25,33},{32,24},{... | collective-permute-start | bytes 1585160 | tf_op jit(solution)/shard_map/ppermute | solution.py:256
  78.7 4.5 %collective-permute-done.15.refs_0_ = bf16[2064,128]{1,0:T(8,128)(2,1)S(1)} collective-permute-done((bf16[2064,128]{1,0:T(8,128)(2,1)S(1)}, bf16[2064,128]{1,0:T(8,128)(2,1)S(1)}, u32[]{:S(2)}, u32[]{:S(2)}) %collective-permute-start.15) | collective-permute-done | bytes 528416 | tf_op jit(solution)/shard_map/ppermute | solution.py:256
  84.2 3.3 %collective-permute-done.19.refs_0_ = bf16[2064,128]{1,0:T(8,128)(2,1)S(1)} collective-permute-done((bf16[2064,128]{1,0:T(8,128)(2,1)S(1)}, bf16[2064,128]{1,0:T(8,128)(2,1)S(1)}, u32[]{:S(2)}, u32[]{:S(2)}) %collective-permute-start.19) | collective-permute-done | bytes 528416 | tf_op jit(solution)/shard_map/ppermute | solution.py:256
  88.4 3.8 %collective-permute-start.20 = (bf16[2064,128]{1,0:T(8,128)(2,1)S(1)}, bf16[2064,128]{1,0:T(8,128)(2,1)S(1)}, u32[]{:S(2)}, u32[]{:S(2)}) collective-permute-start(bf16[2064,128]{1,0:T(8,128)(2,1)S(1)} %shard_map.57), channel_id=1, source_target_pairs={{0,56},{1,9},{8,0},{9,17},{16,8},{17,25},{24,16},{25,33},{32,24},{... | collective-permute-start | bytes 1585160 | tf_op jit(solution)/shard_map/ppermute | solution.py:256
  92.3 2.1 %shard_map.62 = bf16[2048,1024]{1,0:T(8,128)(2,1)S(1)} custom-call(s32[16]{0:T(128)S(1)} %stack.127.at_ref, bf16[128,1024]{1,0:T(8,128)(2,1)S(1)} %get-tuple-element.41.refs_0_, bf16[128,1024]{1,0:T(8,128)(2,1)} %collective-permute-done.4.refs_1_, bf16[128,1024]{1,0:T(8,128)(2,1)} %collective-permute-done.refs_2_, bf16[128,1024]{1,0:T(8,128)(2,1)S(1)} %copy-done.12, ...), custom_call_target="tpu_custom_call" | custom-call | bytes 8388608 | tf_op jit(solution)/shard_map/pallas_call | solution.py:216
  94.4 1.6 %fusion.6.refs_0_ = f32[256,1280]{1,0:T(8,128)S(1)} fusion(bf16[2048,1280]{1,0:T(8,128)(2,1)S(1)} %shard_map.50.g_ref, bf16[2048,1024]{1,0:T(8,128)(2,1)S(1)} %shard_map.62, s32[]{:T(128)S(6)} %select_n.63), kind=kOutput, calls=%fused_computation.6 | convolution fusion | flops 1342177280 | bytes 7602180 | tf_op jit(solution)/shard_map/dot_general | solution.py:310
  96.7 2.8 %collective-permute-start.26 = (bf16[2576,128]{1,0:T(8,128)(2,1)S(1)}, bf16[2576,128]{1,0:T(8,128)(2,1)S(1)}, u32[]{:S(2)}, u32[]{:S(2)}) collective-permute-start(bf16[2576,128]{1,0:T(8,128)(2,1)S(1)} %shard_map.63), channel_id=1, source_target_pairs={{0,64},{1,193},{64,128},{65,1},{128,192},{129,65},{192,0},{193,129... | collective-permute-start | bytes 1978376 | tf_op jit(solution)/shard_map/ppermute | solution.py:256
  99.4 1.6 %fusion.4.refs_1_ = f32[256,1280]{1,0:T(8,128)S(1)} fusion(bf16[2048,1280]{1,0:T(8,128)(2,1)S(1)} %shard_map.50.g_ref, bf16[2048,1024]{1,0:T(8,128)(2,1)S(1)} %shard_map.62, s32[]{:T(128)S(6)} %select_n.64), kind=kOutput, calls=%fused_computation.4 | convolution fusion | flops 1342177280 | bytes 7602180 | tf_op jit(solution)/shard_map/dot_general | solution.py:310
  102.1 1.6 %fusion.2.refs_0_ = f32[256,1280]{1,0:T(8,128)S(1)} fusion(bf16[2048,1280]{1,0:T(8,128)(2,1)S(1)} %shard_map.50.g_ref, bf16[2048,1024]{1,0:T(8,128)(2,1)S(1)} %shard_map.62, s32[]{:T(128)S(6)} %select_n.65), kind=kOutput, calls=%fused_computation.2 | convolution fusion | flops 1342177280 | bytes 7602180 | tf_op jit(solution)/shard_map/dot_general | solution.py:310
  104.7 2.9 %collective-permute-done.26.refs_0_ = bf16[2576,128]{1,0:T(8,128)(2,1)S(1)} collective-permute-done((bf16[2576,128]{1,0:T(8,128)(2,1)S(1)}, bf16[2576,128]{1,0:T(8,128)(2,1)S(1)}, u32[]{:S(2)}, u32[]{:S(2)}) %collective-permute-start.26) | collective-permute-done | bytes 659488 | tf_op jit(solution)/shard_map/ppermute | solution.py:256
  107.6 1.1 shard_map.64
  108.7 2.6 %collective-permute-start.27 = (bf16[2576,128]{1,0:T(8,128)(2,1)S(1)}, bf16[2576,128]{1,0:T(8,128)(2,1)S(1)}, u32[]{:S(2)}, u32[]{:S(2)}) collective-permute-start(bf16[2576,128]{1,0:T(8,128)(2,1)S(1)} %shard_map.64), channel_id=1, source_target_pairs={{0,64},{1,193},{64,128},{65,1},{128,192},{129,65},{192,0},{193,129... | collective-permute-start | bytes 1978376 | tf_op jit(solution)/shard_map/ppermute | solution.py:256
  113.1 2.6 %collective-permute-start.21 = (bf16[2064,128]{1,0:T(8,128)(2,1)S(1)}, bf16[2064,128]{1,0:T(8,128)(2,1)S(1)}, u32[]{:S(2)}, u32[]{:S(2)}) collective-permute-start(bf16[2064,128]{1,0:T(8,128)(2,1)S(1)} %shard_map.58), channel_id=1, source_target_pairs={{0,56},{1,9},{8,0},{9,17},{16,8},{17,25},{24,16},{25,33},{32,24},{... | collective-permute-start | bytes 1585160 | tf_op jit(solution)/shard_map/ppermute | solution.py:256
  116.7 1.6 %fusion.own_ref = f32[256,1280]{1,0:T(8,128)S(1)} fusion(bf16[2048,1280]{1,0:T(8,128)(2,1)S(1)} %shard_map.50.g_ref, bf16[2048,1024]{1,0:T(8,128)(2,1)S(1)} %shard_map.62, s32[]{:T(128)S(6)} %select_n.66), kind=kOutput, calls=%fused_computation | convolution fusion | flops 1342177280 | bytes 7602180 | tf_op jit(solution)/shard_map/dot_general | solution.py:310
  118.3 4.5 %collective-permute-done.27.f_ref = bf16[2576,128]{1,0:T(8,128)(2,1)S(1)} collective-permute-done((bf16[2576,128]{1,0:T(8,128)(2,1)S(1)}, bf16[2576,128]{1,0:T(8,128)(2,1)S(1)}, u32[]{:S(2)}, u32[]{:S(2)}) %collective-permute-start.27) | collective-permute-done | bytes 659488 | tf_op jit(solution)/shard_map/ppermute | solution.py:256
  122.9 2.0 %shard_map.66 = (f32[256,640]{1,0:T(8,128)S(1)}, bf16[1296,128]{1,0:T(8,128)(2,1)}) custom-call(s32[1]{0:T(128)} %constant.74.clone.1.idx_ref, bf16[2576,128]{1,0:T(8,128)(2,1)S(1)} %collective-permute-done.27.f_ref, bf16[2576,128]{1,0:T(8,128)(2,1)S(1)} %collective-permute-done.28.b_ref, f32[256,1280]{1,0:T(8,128)S(1)} %fusion.own_ref), custom_call_target="tpu_custom_call" | custom-call | flops 42139648 | bytes 5267456 | tf_op jit(solution)/shard_map/pallas_call | solution.py:185
  124.9 2.6 %collective-permute-start.29 = (bf16[1296,128]{1,0:T(8,128)(2,1)}, bf16[1296,128]{1,0:T(8,128)(2,1)S(1)}, u32[]{:S(2)}, u32[]{:S(2)}) collective-permute-start(bf16[1296,128]{1,0:T(8,128)(2,1)} %get-tuple-element.55), channel_id=1, source_target_pairs={{0,4},{4,0},{1,5},{5,1},{2,6},{6,2},{3,7},{7,3},{8,12},{12,8},{9,1... | collective-permute-start | bytes 995336 | tf_op jit(solution)/shard_map/ppermute | solution.py:241
  128.4 1.7 %shard_map.60 = bf16[128,1024]{1,0:T(8,128)(2,1)} custom-call(s32[2]{0:T(128)S(1)} %pad_add_fusion.2.idx_ref, bf16[2064,128]{1,0:T(8,128)(2,1)S(1)} %collective-permute-done.18.f_ref, bf16[2064,128]{1,0:T(8,128)(2,1)S(1)} %collective-permute-done.21.b_ref, f32[256,1024]{1,0:T(8,128)S(1)} %fusion.8.own_ref), custom_call_target="tpu_custom_call" | custom-call | flops 29491200 | bytes 3686400 | tf_op jit(solution)/shard_map/pallas_call | solution.py:185
  130.0 2.8 %collective-permute-start.22 = (bf16[128,1024]{1,0:T(8,128)(2,1)}, bf16[128,1024]{1,0:T(8,128)(2,1)}, u32[]{:S(2)}, u32[]{:S(2)}) collective-permute-start(bf16[128,1024]{1,0:T(8,128)(2,1)} %shard_map.60), channel_id=1, source_target_pairs={{0,4},{4,0},{1,5},{5,1},{2,6},{6,2},{3,7},{7,3},{8,12},{12,8},{9,1... | collective-permute-start | bytes 786440 | tf_op jit(solution)/shard_map/ppermute | solution.py:241
  134.0 2.4 %collective-permute-done.29.got_ref = bf16[1296,128]{1,0:T(8,128)(2,1)S(1)} collective-permute-done((bf16[1296,128]{1,0:T(8,128)(2,1)}, bf16[1296,128]{1,0:T(8,128)(2,1)S(1)}, u32[]{:S(2)}, u32[]{:S(2)}) %collective-permute-start.29) | collective-permute-done | bytes 331808 | tf_op jit(solution)/shard_map/ppermute | solution.py:241
  136.4 1.4 %shard_map.67 = f32[512,640]{1,0:T(8,128)} custom-call(s32[1]{0:T(128)} %bitcast.h_ref, f32[256,640]{1,0:T(8,128)S(1)} %get-tuple-element.54.mine_ref, bf16[1296,128]{1,0:T(8,128)(2,1)S(1)} %collective-permute-done.29.got_ref), custom_call_target="tpu_custom_call" | custom-call | flops 21037056 | bytes 2629632 | tf_op jit(solution)/shard_map/pallas_call | solution.py:185
  137.8 2.6 %collective-permute-done.22.got_ref = bf16[128,1024]{1,0:T(8,128)(2,1)} collective-permute-done((bf16[128,1024]{1,0:T(8,128)(2,1)}, bf16[128,1024]{1,0:T(8,128)(2,1)}, u32[]{:S(2)}, u32[]{:S(2)}) %collective-permute-start.22) | collective-permute-done | bytes 262176 | tf_op jit(solution)/shard_map/ppermute | solution.py:241
  140.4 2.3 %shard_map.61 = bf16[128,2048]{1,0:T(8,128)(2,1)} custom-call(s32[5]{0:T(128)S(1)} %stack.102.at_ref, bf16[128,1024]{1,0:T(8,128)(2,1)S(1)} %shard_map.59.mine_ref, bf16[128,1024]{1,0:T(8,128)(2,1)} %collective-permute-done.22.got_ref), custom_call_target="tpu_custom_call" | custom-call | flops 16777216 | bytes 2097152 | tf_op jit(solution)/shard_map/pallas_call | solution.py:185
  (85 shorter events, 20.5 us)
Async XLA Ops:
  0.6 17.3 %copy-start = (bf16[2048,640]{1,0:T(8,128)(2,1)S(1)}, bf16[2048,640]{1,0:T(8,128)(2,1)}, u32[]{:S(2)}) copy-start(bf16[2048,640]{1,0:T(8,128)(2,1)} %refs_0_) | copy-start | bytes 7864324
  2.7 11.2 %collective-permute-start = (bf16[128,1024]{1,0:T(8,128)(2,1)S(1)}, bf16[128,1024]{1,0:T(8,128)(2,1)}, u32[]{:S(2)}, u32[]{:S(2)}) collective-permute-start(bf16[128,1024]{1,0:T(8,128)(2,1)S(1)} %get-tuple-element.41.refs_0_), channel_id=1, source_target_pairs={{0,8},{1,57},{8,16},{9,1},{16,24},{17,9},{24,32},{25,17},{32,40},{... | collective-permute-start | bytes 786440 | tf_op jit(solution)/shard_map/ppermute | solution.py:256
  4.6 9.5 %collective-permute-start.2 = (bf16[128,1024]{1,0:T(8,128)(2,1)S(1)}, bf16[128,1024]{1,0:T(8,128)(2,1)}, u32[]{:S(2)}, u32[]{:S(2)}) collective-permute-start(bf16[128,1024]{1,0:T(8,128)(2,1)S(1)} %get-tuple-element.41.refs_0_), channel_id=1, source_target_pairs={{0,56},{1,9},{8,0},{9,17},{16,8},{17,25},{24,16},{25,33},{32,24},{... | collective-permute-start | bytes 786440 | tf_op jit(solution)/shard_map/ppermute | solution.py:256
  10.5 15.1 %collective-permute-start.5 = (bf16[256,640]{1,0:T(8,128)(2,1)}, bf16[256,640]{1,0:T(8,128)(2,1)}, u32[]{:S(2)}, u32[]{:S(2)}) collective-permute-start(bf16[256,640]{1,0:T(8,128)(2,1)} %get-tuple-element.57), channel_id=1, source_target_pairs={{0,4},{4,0},{1,5},{5,1},{2,6},{6,2},{3,7},{7,3},{8,12},{12,8},{9,1... | collective-permute-start | bytes 983048 | tf_op jit(solution)/shard_map/ppermute | solution.py:241
  12.1 13.5 %collective-permute-start.4 = (bf16[128,1024]{1,0:T(8,128)(2,1)}, bf16[128,1024]{1,0:T(8,128)(2,1)}, u32[]{:S(2)}, u32[]{:S(2)}) collective-permute-start(bf16[128,1024]{1,0:T(8,128)(2,1)} %get-tuple-element.31), channel_id=1, source_target_pairs={{0,4},{4,0},{1,5},{5,1},{2,6},{6,2},{3,7},{7,3},{8,12},{12,8},{9,1... | collective-permute-start | bytes 786440 | tf_op jit(solution)/shard_map/ppermute | solution.py:241
  14.0 11.7 %collective-permute-start.1 = (bf16[128,1024]{1,0:T(8,128)(2,1)}, bf16[128,1024]{1,0:T(8,128)(2,1)S(1)}, u32[]{:S(2)}, u32[]{:S(2)}) collective-permute-start(bf16[128,1024]{1,0:T(8,128)(2,1)} %collective-permute-done.refs_2_), channel_id=1, source_target_pairs={{0,8},{1,57},{8,16},{9,1},{16,24},{17,9},{24,32},{25,17},{32,40},{... | collective-permute-start | bytes 786440 | tf_op jit(solution)/shard_map/ppermute | solution.py:256
  14.2 11.5 %collective-permute-start.3 = (bf16[128,1024]{1,0:T(8,128)(2,1)}, bf16[128,1024]{1,0:T(8,128)(2,1)S(1)}, u32[]{:S(2)}, u32[]{:S(2)}) collective-permute-start(bf16[128,1024]{1,0:T(8,128)(2,1)} %collective-permute-done.2.refs_4_), channel_id=1, source_target_pairs={{0,56},{1,9},{8,0},{9,17},{16,8},{17,25},{24,16},{25,33},{32,24},{... | collective-permute-start | bytes 786440 | tf_op jit(solution)/shard_map/ppermute | solution.py:256
  17.9 9.4 %copy-start.15 = (bf16[256,640]{1,0:T(8,128)(2,1)S(1)}, bf16[256,640]{1,0:T(8,128)(2,1)}, u32[]{:S(2)}) copy-start(bf16[256,640]{1,0:T(8,128)(2,1)} %get-tuple-element.56) | copy-start | bytes 983044
  25.7 1.7 %copy-start.1 = (bf16[128,1024]{1,0:T(8,128)(2,1)}, bf16[128,1024]{1,0:T(8,128)(2,1)S(1)}, u32[]{:S(2)}) copy-start(bf16[128,1024]{1,0:T(8,128)(2,1)S(1)} %collective-permute-done.1.refs_6_) | copy-start | bytes 786436
  25.7 1.7 %copy-start.3 = (bf16[128,1024]{1,0:T(8,128)(2,1)}, bf16[128,1024]{1,0:T(8,128)(2,1)S(1)}, u32[]{:S(2)}) copy-start(bf16[128,1024]{1,0:T(8,128)(2,1)S(1)} %collective-permute-done.3.refs_8_) | copy-start | bytes 786436
  25.7 23.6 %collective-permute-start.12 = (bf16[1024,640]{1,0:T(8,128)(2,1)S(1)}, bf16[1024,640]{1,0:T(8,128)(2,1)}, u32[]{:S(2)}, u32[]{:S(2)}) collective-permute-start(bf16[1024,640]{1,0:T(8,128)(2,1)S(1)} %constant_dynamic-slice_fusion), channel_id=1, source_target_pairs={{0,4},{1,7},{4,2},{5,1},{2,6},{3,5},{6,0},{7,3},{8,12},{9,15},{12,... | collective-permute-start | bytes 3932168 | tf_op jit(solution)/shard_map/ppermute | solution.py:250
  28.4 20.0 %collective-permute-start.10 = (bf16[256,1280]{1,0:T(8,128)(2,1)S(1)}, bf16[256,1280]{1,0:T(8,128)(2,1)}, u32[]{:S(2)}, u32[]{:S(2)}) collective-permute-start(bf16[256,1280]{1,0:T(8,128)(2,1)S(1)} %pad_maximum_fusion.refs_0_), channel_id=1, source_target_pairs={{0,64},{1,193},{64,128},{65,1},{128,192},{129,65},{192,0},{193,129... | collective-permute-start | bytes 1966088 | tf_op jit(solution)/shard_map/ppermute | solution.py:256
  29.6 18.7 %collective-permute-start.11 = (bf16[256,1280]{1,0:T(8,128)(2,1)S(1)}, bf16[256,1280]{1,0:T(8,128)(2,1)S(1)}, u32[]{:S(2)}, u32[]{:S(2)}) collective-permute-start(bf16[256,1280]{1,0:T(8,128)(2,1)S(1)} %pad_maximum_fusion.refs_0_), channel_id=1, source_target_pairs={{0,192},{1,65},{64,0},{65,129},{128,64},{129,193},{192,128},{193,1... | collective-permute-start | bytes 1966088 | tf_op jit(solution)/shard_map/ppermute | solution.py:256
  30.5 8.5 %collective-permute-start.6 = (bf16[128,1024]{1,0:T(8,128)(2,1)}, bf16[128,1024]{1,0:T(8,128)(2,1)S(1)}, u32[]{:S(2)}, u32[]{:S(2)}) collective-permute-start(bf16[128,1024]{1,0:T(8,128)(2,1)} %collective-permute-done.4.refs_1_), channel_id=1, source_target_pairs={{0,8},{1,57},{8,16},{9,1},{16,24},{17,9},{24,32},{25,17},{32,40},{... | collective-permute-start | bytes 786440 | tf_op jit(solution)/shard_map/ppermute | solution.py:256
  30.5 9.3 %collective-permute-start.8 = (bf16[128,1024]{1,0:T(8,128)(2,1)}, bf16[128,1024]{1,0:T(8,128)(2,1)S(1)}, u32[]{:S(2)}, u32[]{:S(2)}) collective-permute-start(bf16[128,1024]{1,0:T(8,128)(2,1)} %collective-permute-done.4.refs_1_), channel_id=1, source_target_pairs={{0,56},{1,9},{8,0},{9,17},{16,8},{17,25},{24,16},{25,33},{32,24},{... | collective-permute-start | bytes 786440 | tf_op jit(solution)/shard_map/ppermute | solution.py:256
  39.0 7.6 %collective-permute-start.7 = (bf16[128,1024]{1,0:T(8,128)(2,1)S(1)}, bf16[128,1024]{1,0:T(8,128)(2,1)S(1)}, u32[]{:S(2)}, u32[]{:S(2)}) collective-permute-start(bf16[128,1024]{1,0:T(8,128)(2,1)S(1)} %collective-permute-done.6.refs_3_), channel_id=1, source_target_pairs={{0,8},{1,57},{8,16},{9,1},{16,24},{17,9},{24,32},{25,17},{32,40},{... | collective-permute-start | bytes 786440 | tf_op jit(solution)/shard_map/ppermute | solution.py:256
  39.0 0.7 copy-start.11
  39.8 8.6 %collective-permute-start.9 = (bf16[128,1024]{1,0:T(8,128)(2,1)S(1)}, bf16[128,1024]{1,0:T(8,128)(2,1)S(1)}, u32[]{:S(2)}, u32[]{:S(2)}) collective-permute-start(bf16[128,1024]{1,0:T(8,128)(2,1)S(1)} %collective-permute-done.8.refs_5_), channel_id=1, source_target_pairs={{0,56},{1,9},{8,0},{9,17},{16,8},{17,25},{24,16},{25,33},{32,24},{... | collective-permute-start | bytes 786440 | tf_op jit(solution)/shard_map/ppermute | solution.py:256
  43.4 0.7 copy-start.13
  46.6 1.8 %copy-start.5 = (bf16[128,1024]{1,0:T(8,128)(2,1)}, bf16[128,1024]{1,0:T(8,128)(2,1)S(1)}, u32[]{:S(2)}) copy-start(bf16[128,1024]{1,0:T(8,128)(2,1)S(1)} %collective-permute-done.7.refs_7_) | copy-start | bytes 786436
  48.4 1.0 copy-start.7
  48.4 0.9 copy-start.9
  49.3 16.7 %collective-permute-start.13 = (bf16[1024,640]{1,0:T(8,128)(2,1)}, bf16[1024,640]{1,0:T(8,128)(2,1)}, u32[]{:S(2)}, u32[]{:S(2)}) collective-permute-start(bf16[1024,640]{1,0:T(8,128)(2,1)} %collective-permute-done.12.refs_1_), channel_id=1, source_target_pairs={{0,1},{1,0},{2,3},{3,2},{4,5},{5,4},{6,7},{7,6},{8,9},{9,8},{10,11... | collective-permute-start | bytes 3932168 | tf_op jit(solution)/shard_map/ppermute | solution.py:241
  50.5 11.5 %collective-permute-start.14 = (bf16[256,1280]{1,0:T(8,128)(2,1)}, bf16[256,1280]{1,0:T(8,128)(2,1)}, u32[]{:S(2)}, u32[]{:S(2)}) collective-permute-start(bf16[256,1280]{1,0:T(8,128)(2,1)} %collective-permute-done.10.refs_1_), channel_id=1, source_target_pairs={{0,64},{1,193},{64,128},{65,1},{128,192},{129,65},{192,0},{193,129... | collective-permute-start | bytes 1966088 | tf_op jit(solution)/shard_map/ppermute | solution.py:256
  56.0 20.9 %collective-permute-start.23 = (bf16[256,1024]{1,0:T(8,128)(2,1)S(1)}, bf16[256,1024]{1,0:T(8,128)(2,1)S(1)}, u32[]{:S(2)}, u32[]{:S(2)}) collective-permute-start(bf16[256,1024]{1,0:T(8,128)(2,1)S(1)} %pad_maximum_fusion.1), channel_id=1, source_target_pairs={{0,8},{1,57},{8,16},{9,1},{16,24},{17,9},{24,32},{25,17},{32,40},{... | collective-permute-start | bytes 1572872 | tf_op jit(solution)/shard_map/ppermute | solution.py:256
  56.2 20.6 %collective-permute-start.24 = (bf16[256,1024]{1,0:T(8,128)(2,1)S(1)}, bf16[256,1024]{1,0:T(8,128)(2,1)S(1)}, u32[]{:S(2)}, u32[]{:S(2)}) collective-permute-start(bf16[256,1024]{1,0:T(8,128)(2,1)S(1)} %pad_maximum_fusion.2), channel_id=1, source_target_pairs={{0,56},{1,9},{8,0},{9,17},{16,8},{17,25},{24,16},{25,33},{32,24},{... | collective-permute-start | bytes 1572872 | tf_op jit(solution)/shard_map/ppermute | solution.py:256
  62.0 1.1 copy-start.10
  70.2 13.0 %collective-permute-start.15 = (bf16[2064,128]{1,0:T(8,128)(2,1)S(1)}, bf16[2064,128]{1,0:T(8,128)(2,1)S(1)}, u32[]{:S(2)}, u32[]{:S(2)}) collective-permute-start(bf16[2064,128]{1,0:T(8,128)(2,1)S(1)} %shard_map.52), channel_id=1, source_target_pairs={{0,8},{1,57},{8,16},{9,1},{16,24},{17,9},{24,32},{25,17},{32,40},{... | collective-permute-start | bytes 1585160 | tf_op jit(solution)/shard_map/ppermute | solution.py:256
  71.8 15.8 %collective-permute-start.19 = (bf16[2064,128]{1,0:T(8,128)(2,1)S(1)}, bf16[2064,128]{1,0:T(8,128)(2,1)S(1)}, u32[]{:S(2)}, u32[]{:S(2)}) collective-permute-start(bf16[2064,128]{1,0:T(8,128)(2,1)S(1)} %shard_map.56), channel_id=1, source_target_pairs={{0,56},{1,9},{8,0},{9,17},{16,8},{17,25},{24,16},{25,33},{32,24},{... | collective-permute-start | bytes 1585160 | tf_op jit(solution)/shard_map/ppermute | solution.py:256
  76.8 15.4 %collective-permute-start.25 = (bf16[256,1024]{1,0:T(8,128)(2,1)S(1)}, bf16[256,1024]{1,0:T(8,128)(2,1)S(1)}, u32[]{:S(2)}, u32[]{:S(2)}) collective-permute-start(bf16[256,1024]{1,0:T(8,128)(2,1)S(1)} %collective-permute-done.23.refs_10_), channel_id=1, source_target_pairs={{0,8},{1,57},{8,16},{9,1},{16,24},{17,9},{24,32},{25,17},{32,40},{... | collective-permute-start | bytes 1572872 | tf_op jit(solution)/shard_map/ppermute | solution.py:256
  78.7 13.6 %copy-start.2 = (bf16[128,1024]{1,0:T(8,128)(2,1)S(1)}, bf16[128,1024]{1,0:T(8,128)(2,1)}, u32[]{:S(2)}) copy-start(bf16[128,1024]{1,0:T(8,128)(2,1)} %copy-done.1) | copy-start | bytes 786436
  78.7 13.5 %copy-start.4 = (bf16[128,1024]{1,0:T(8,128)(2,1)S(1)}, bf16[128,1024]{1,0:T(8,128)(2,1)}, u32[]{:S(2)}) copy-start(bf16[128,1024]{1,0:T(8,128)(2,1)} %copy-done.3) | copy-start | bytes 786436
  78.7 13.5 %copy-start.6 = (bf16[128,1024]{1,0:T(8,128)(2,1)S(1)}, bf16[128,1024]{1,0:T(8,128)(2,1)}, u32[]{:S(2)}) copy-start(bf16[128,1024]{1,0:T(8,128)(2,1)} %copy-done.5) | copy-start | bytes 786436
  78.7 13.5 %copy-start.8 = (bf16[128,1024]{1,0:T(8,128)(2,1)S(1)}, bf16[128,1024]{1,0:T(8,128)(2,1)}, u32[]{:S(2)}) copy-start(bf16[128,1024]{1,0:T(8,128)(2,1)} %copy-done.7) | copy-start | bytes 786436
  78.7 13.5 %copy-start.12 = (bf16[128,1024]{1,0:T(8,128)(2,1)S(1)}, bf16[128,1024]{1,0:T(8,128)(2,1)}, u32[]{:S(2)}) copy-start(bf16[128,1024]{1,0:T(8,128)(2,1)} %copy-done.11) | copy-start | bytes 786436
  78.7 13.5 %copy-start.14 = (bf16[128,1024]{1,0:T(8,128)(2,1)S(1)}, bf16[128,1024]{1,0:T(8,128)(2,1)}, u32[]{:S(2)}) copy-start(bf16[128,1024]{1,0:T(8,128)(2,1)} %copy-done.13) | copy-start | bytes 786436
  84.1 16.9 %collective-permute-start.16 = (bf16[2064,128]{1,0:T(8,128)(2,1)S(1)}, bf16[2064,128]{1,0:T(8,128)(2,1)S(1)}, u32[]{:S(2)}, u32[]{:S(2)}) collective-permute-start(bf16[2064,128]{1,0:T(8,128)(2,1)S(1)} %shard_map.53), channel_id=1, source_target_pairs={{0,8},{1,57},{8,16},{9,1},{16,24},{17,9},{24,32},{25,17},{32,40},{... | collective-permute-start | bytes 1585160 | tf_op jit(solution)/shard_map/ppermute | solution.py:256
  88.4 23.7 %collective-permute-start.20 = (bf16[2064,128]{1,0:T(8,128)(2,1)S(1)}, bf16[2064,128]{1,0:T(8,128)(2,1)S(1)}, u32[]{:S(2)}, u32[]{:S(2)}) collective-permute-start(bf16[2064,128]{1,0:T(8,128)(2,1)S(1)} %shard_map.57), channel_id=1, source_target_pairs={{0,56},{1,9},{8,0},{9,17},{16,8},{17,25},{24,16},{25,33},{32,24},{... | collective-permute-start | bytes 1585160 | tf_op jit(solution)/shard_map/ppermute | solution.py:256
  96.7 10.9 %collective-permute-start.26 = (bf16[2576,128]{1,0:T(8,128)(2,1)S(1)}, bf16[2576,128]{1,0:T(8,128)(2,1)S(1)}, u32[]{:S(2)}, u32[]{:S(2)}) collective-permute-start(bf16[2576,128]{1,0:T(8,128)(2,1)S(1)} %shard_map.63), channel_id=1, source_target_pairs={{0,64},{1,193},{64,128},{65,1},{128,192},{129,65},{192,0},{193,129... | collective-permute-start | bytes 1978376 | tf_op jit(solution)/shard_map/ppermute | solution.py:256
  102.0 13.7 %collective-permute-start.17 = (bf16[2064,128]{1,0:T(8,128)(2,1)S(1)}, bf16[2064,128]{1,0:T(8,128)(2,1)S(1)}, u32[]{:S(2)}, u32[]{:S(2)}) collective-permute-start(bf16[2064,128]{1,0:T(8,128)(2,1)S(1)} %shard_map.54), channel_id=1, source_target_pairs={{0,8},{1,57},{8,16},{9,1},{16,24},{17,9},{24,32},{25,17},{32,40},{... | collective-permute-start | bytes 1585160 | tf_op jit(solution)/shard_map/ppermute | solution.py:256
  104.3 14.0 %collective-permute-start.28 = (bf16[2576,128]{1,0:T(8,128)(2,1)S(1)}, bf16[2576,128]{1,0:T(8,128)(2,1)S(1)}, u32[]{:S(2)}, u32[]{:S(2)}) collective-permute-start(bf16[2576,128]{1,0:T(8,128)(2,1)S(1)} %shard_map.65), channel_id=1, source_target_pairs={{0,192},{1,65},{64,0},{65,129},{128,64},{129,193},{192,128},{193,1... | collective-permute-start | bytes 1978376 | tf_op jit(solution)/shard_map/ppermute | solution.py:256
  108.7 14.1 %collective-permute-start.27 = (bf16[2576,128]{1,0:T(8,128)(2,1)S(1)}, bf16[2576,128]{1,0:T(8,128)(2,1)S(1)}, u32[]{:S(2)}, u32[]{:S(2)}) collective-permute-start(bf16[2576,128]{1,0:T(8,128)(2,1)S(1)} %shard_map.64), channel_id=1, source_target_pairs={{0,64},{1,193},{64,128},{65,1},{128,192},{129,65},{192,0},{193,129... | collective-permute-start | bytes 1978376 | tf_op jit(solution)/shard_map/ppermute | solution.py:256
  113.1 15.3 %collective-permute-start.21 = (bf16[2064,128]{1,0:T(8,128)(2,1)S(1)}, bf16[2064,128]{1,0:T(8,128)(2,1)S(1)}, u32[]{:S(2)}, u32[]{:S(2)}) collective-permute-start(bf16[2064,128]{1,0:T(8,128)(2,1)S(1)} %shard_map.58), channel_id=1, source_target_pairs={{0,56},{1,9},{8,0},{9,17},{16,8},{17,25},{24,16},{25,33},{32,24},{... | collective-permute-start | bytes 1585160 | tf_op jit(solution)/shard_map/ppermute | solution.py:256
  116.6 11.7 %collective-permute-start.18 = (bf16[2064,128]{1,0:T(8,128)(2,1)S(1)}, bf16[2064,128]{1,0:T(8,128)(2,1)S(1)}, u32[]{:S(2)}, u32[]{:S(2)}) collective-permute-start(bf16[2064,128]{1,0:T(8,128)(2,1)S(1)} %shard_map.55), channel_id=1, source_target_pairs={{0,8},{1,57},{8,16},{9,1},{16,24},{17,9},{24,32},{25,17},{32,40},{... | collective-permute-start | bytes 1585160 | tf_op jit(solution)/shard_map/ppermute | solution.py:256
  124.9 11.5 %collective-permute-start.29 = (bf16[1296,128]{1,0:T(8,128)(2,1)}, bf16[1296,128]{1,0:T(8,128)(2,1)S(1)}, u32[]{:S(2)}, u32[]{:S(2)}) collective-permute-start(bf16[1296,128]{1,0:T(8,128)(2,1)} %get-tuple-element.55), channel_id=1, source_target_pairs={{0,4},{4,0},{1,5},{5,1},{2,6},{6,2},{3,7},{7,3},{8,12},{12,8},{9,1... | collective-permute-start | bytes 995336 | tf_op jit(solution)/shard_map/ppermute | solution.py:241
  130.0 10.4 %collective-permute-start.22 = (bf16[128,1024]{1,0:T(8,128)(2,1)}, bf16[128,1024]{1,0:T(8,128)(2,1)}, u32[]{:S(2)}, u32[]{:S(2)}) collective-permute-start(bf16[128,1024]{1,0:T(8,128)(2,1)} %shard_map.60), channel_id=1, source_target_pairs={{0,4},{4,0},{1,5},{5,1},{2,6},{6,2},{3,7},{7,3},{8,12},{12,8},{9,1... | collective-permute-start | bytes 786440 | tf_op jit(solution)/shard_map/ppermute | solution.py:241

commit v7 on v6

--- a/solution.py
+++ b/solution.py
@@ -341,8 +341,6 @@
     *_, blocks = gathered([w_pair], "x", (0,), 0, {2: lambda b: [known[2][0][1], known[2][1][1]]})
     near = [0, -1, 1, -2]
     ws = [blocks[k][0] for k in near]
-    pieces = [(i, 0, half, 0, i * half) for i in range(owners)]
-    w_all = placed(ws, pieces, (owners * half, 2 * width), owners - 1)
 
     part = tokens // 2
     g_sent = lax.dynamic_slice_in_dim(out_grad, c * part, part, 0)
@@ -360,6 +358,8 @@
     arrays, acts_pieces, shape, blocks = gathered([acts_mine, acts_got], "z", (h, 1 - h), 3, before, known)
     (g_pair,) = pairs
 
+    pieces = [(i, 0, half, 0, i * half) for i in range(owners)]
+    w_all = placed(ws[:-1] + [after(g_pair, ws[-1])[1]], pieces, (owners * half, 2 * width), owners - 1)
     first = [first_sum(block_at("z", k), 2 * own_tokens, g_pair, w_all) for k in (4, -3)]
 
     def of_tokens(i):

time: 146 us -> 140 us (0.959)
  starting transfers between devices: 51.2 us -> 46.6 us
  waiting for transfers between devices: 41.6 us -> 43.5 us
    ppermute x5, starting transfers between devices: 8.54 us -> 4.69 us  [swap(): return lax.ppermute(a, axis, [(0, 1), (1, 0)])]
    ppermute x5, waiting for transfers between devices: 12.6 us -> 15.4 us  [swap(): return lax.ppermute(a, axis, [(0, 1), (1, 0)])]
    unnamed x32 -> x24, local copies, waits for them, and re-layouts: 3.49 us -> 2.28 us
  transfers between devices with their start and end apart: 30 -> 30, of which waited for: 14 -> 16; matrix products, arithmetic and copies ran while one was open for 12% -> 12% of each run, Pallas kernels for 17% -> 17%
where the time goes in v7:
time: 140 us; the launch traced here: 138 us
  starting transfers between devices  46.6 us (33%)
  waiting for transfers between devices  43.5 us (31%)
  Pallas kernels  25.4 us (18%)
  matrix products  11.5 us (8%)
  local copies, waits for them, and re-layouts  5.78 us (4%)
  other arithmetic  4.21 us (3%)
    ppermute x24, starting transfers between devices, ring(): return lax.ppermute(a, (axis, 'c'), perm)  40.3 us
    ppermute x24, waiting for transfers between devices, ring(): return lax.ppermute(a, (axis, 'c'), perm)  28.1 us
    ppermute x5, waiting for transfers between devices, swap(): return lax.ppermute(a, axis, [(0, 1), (1, 0)])  15.4 us
    pallas_call x13, Pallas kernels, call(): pl.pallas_call(kernel, grid_spec=pltpu.PrefetchScalarGridSpec(num_scalar_...  14.5 us
    dot_general x10, matrix products, dot(): return lax.dot_general(a, b, (dims, ((), ())), preferred_element_type=F32)  11.5 us
    pallas_call x3, Pallas kernels, placed(): pl.pallas_call(functools.partial(placed_kernel, fixed), grid_spec=pltpu.P...  7.99 us
    ppermute x5, starting transfers between devices, swap(): return lax.ppermute(a, axis, [(0, 1), (1, 0)])  4.69 us
    pallas_call x2, Pallas kernels, first_sum(): pl.pallas_call(first_kernel, grid_spec=pltpu.PrefetchScalarGridSpec(num_s...  2.87 us
  transfers between devices with their start and end apart: 30, of which 16 were waited for; matrix products, arithmetic and copies ran while one was open for 12% of the time, Pallas kernels for 17%

profile of v7, /device:TPU:4, one launch (start us, length us, event | category | flops | bytes accessed | tf_op | source)
XLA Modules:
  0.0 138.1 jit_solution(13837847936340392840)
XLA Ops:
  0.6 1.3 fusion.30
  2.7 1.9 %collective-permute-start = (bf16[128,1024]{1,0:T(8,128)(2,1)S(1)}, bf16[128,1024]{1,0:T(8,128)(2,1)S(1)}, u32[]{:S(2)}, u32[]{:S(2)}) collective-permute-start(bf16[128,1024]{1,0:T(8,128)(2,1)S(1)} %get-tuple-element.43.refs_0_), channel_id=1, source_target_pairs={{0,8},{1,57},{8,16},{9,1},{16,24},{17,9},{24,32},{25,17},{32,40},{... | collective-permute-start | bytes 786440 | tf_op jit(solution)/shard_map/ppermute | solution.py:256
  4.6 3.9 %collective-permute-start.2 = (bf16[128,1024]{1,0:T(8,128)(2,1)S(1)}, bf16[128,1024]{1,0:T(8,128)(2,1)S(1)}, u32[]{:S(2)}, u32[]{:S(2)}) collective-permute-start(bf16[128,1024]{1,0:T(8,128)(2,1)S(1)} %get-tuple-element.43.refs_0_), channel_id=1, source_target_pairs={{0,56},{1,9},{8,0},{9,17},{16,8},{17,25},{24,16},{25,33},{32,24},{... | collective-permute-start | bytes 786440 | tf_op jit(solution)/shard_map/ppermute | solution.py:256
  8.6 2.0 %dynamic-slice_bitcast_fusion = (bf16[256,640]{1,0:T(8,128)(2,1)}, bf16[256,640]{1,0:T(8,128)(2,1)}) fusion(bf16[1,512,640]{2,1,0:T(8,128)(2,1)} %param.5, s32[]{:T(128)S(6)} %select_n.55, s32[]{:T(128)S(6)} %select_n.54), kind=kLoop, calls=%fused_computation.23 | loop fusion | bytes 1310728 | tf_op jit(solution)/shard_map/dynamic_slice | solution.py:332
  10.5 1.6 %collective-permute-start.5 = (bf16[256,640]{1,0:T(8,128)(2,1)}, bf16[256,640]{1,0:T(8,128)(2,1)}, u32[]{:S(2)}, u32[]{:S(2)}) collective-permute-start(bf16[256,640]{1,0:T(8,128)(2,1)} %get-tuple-element.59), channel_id=1, source_target_pairs={{0,4},{4,0},{1,5},{5,1},{2,6},{6,2},{3,7},{7,3},{8,12},{12,8},{9,1... | collective-permute-start | bytes 983048 | tf_op jit(solution)/shard_map/ppermute | solution.py:241
  12.6 1.3 collective-permute-done.refs_2_
  14.2 3.7 %collective-permute-start.3 = (bf16[128,1024]{1,0:T(8,128)(2,1)S(1)}, bf16[128,1024]{1,0:T(8,128)(2,1)}, u32[]{:S(2)}, u32[]{:S(2)}) collective-permute-start(bf16[128,1024]{1,0:T(8,128)(2,1)S(1)} %collective-permute-done.2.refs_4_), channel_id=1, source_target_pairs={{0,56},{1,9},{8,0},{9,17},{16,8},{17,25},{24,16},{25,33},{32,24},{... | collective-permute-start | bytes 786440 | tf_op jit(solution)/shard_map/ppermute | solution.py:256
  18.0 7.7 %collective-permute-done.4.refs_1_ = bf16[128,1024]{1,0:T(8,128)(2,1)} collective-permute-done((bf16[128,1024]{1,0:T(8,128)(2,1)}, bf16[128,1024]{1,0:T(8,128)(2,1)}, u32[]{:S(2)}, u32[]{:S(2)}) %collective-permute-start.4) | collective-permute-done | bytes 262176 | tf_op jit(solution)/shard_map/ppermute | solution.py:241
  25.7 1.7 %collective-permute-start.12 = (bf16[1024,640]{1,0:T(8,128)(2,1)S(1)}, bf16[1024,640]{1,0:T(8,128)(2,1)}, u32[]{:S(2)}, u32[]{:S(2)}) collective-permute-start(bf16[1024,640]{1,0:T(8,128)(2,1)S(1)} %constant_dynamic-slice_fusion), channel_id=1, source_target_pairs={{0,4},{1,7},{4,2},{5,1},{2,6},{3,5},{6,0},{7,3},{8,12},{9,15},{12,... | collective-permute-start | bytes 3932168 | tf_op jit(solution)/shard_map/ppermute | solution.py:250
  27.3 1.0 pad_maximum_fusion.refs_0_
  28.4 1.3 collective-permute-start.10
  30.5 3.2 %collective-permute-start.8 = (bf16[128,1024]{1,0:T(8,128)(2,1)}, bf16[128,1024]{1,0:T(8,128)(2,1)S(1)}, u32[]{:S(2)}, u32[]{:S(2)}) collective-permute-start(bf16[128,1024]{1,0:T(8,128)(2,1)} %collective-permute-done.4.refs_1_), channel_id=1, source_target_pairs={{0,56},{1,9},{8,0},{9,17},{16,8},{17,25},{24,16},{25,33},{32,24},{... | collective-permute-start | bytes 786440 | tf_op jit(solution)/shard_map/ppermute | solution.py:256
  33.7 5.3 %collective-permute-done.6.refs_3_ = bf16[128,1024]{1,0:T(8,128)(2,1)S(1)} collective-permute-done((bf16[128,1024]{1,0:T(8,128)(2,1)}, bf16[128,1024]{1,0:T(8,128)(2,1)S(1)}, u32[]{:S(2)}, u32[]{:S(2)}) %collective-permute-start.6) | collective-permute-done | bytes 262176 | tf_op jit(solution)/shard_map/ppermute | solution.py:256
  39.8 3.6 %collective-permute-start.9 = (bf16[128,1024]{1,0:T(8,128)(2,1)S(1)}, bf16[128,1024]{1,0:T(8,128)(2,1)}, u32[]{:S(2)}, u32[]{:S(2)}) collective-permute-start(bf16[128,1024]{1,0:T(8,128)(2,1)S(1)} %collective-permute-done.8.refs_5_), channel_id=1, source_target_pairs={{0,56},{1,9},{8,0},{9,17},{16,8},{17,25},{24,16},{25,33},{32,24},{... | collective-permute-start | bytes 786440 | tf_op jit(solution)/shard_map/ppermute | solution.py:256
  44.0 2.6 %collective-permute-done.7.refs_7_ = bf16[128,1024]{1,0:T(8,128)(2,1)} collective-permute-done((bf16[128,1024]{1,0:T(8,128)(2,1)S(1)}, bf16[128,1024]{1,0:T(8,128)(2,1)}, u32[]{:S(2)}, u32[]{:S(2)}) %collective-permute-start.7) | collective-permute-done | bytes 262176 | tf_op jit(solution)/shard_map/ppermute | solution.py:256
  46.7 1.7 %collective-permute-done.9.refs_9_ = bf16[128,1024]{1,0:T(8,128)(2,1)} collective-permute-done((bf16[128,1024]{1,0:T(8,128)(2,1)S(1)}, bf16[128,1024]{1,0:T(8,128)(2,1)}, u32[]{:S(2)}, u32[]{:S(2)}) %collective-permute-start.9) | collective-permute-done | bytes 262176 | tf_op jit(solution)/shard_map/ppermute | solution.py:256
  49.2 1.2 collective-permute-start.13
  50.4 3.1 %collective-permute-start.14 = (bf16[256,1280]{1,0:T(8,128)(2,1)}, bf16[256,1280]{1,0:T(8,128)(2,1)}, u32[]{:S(2)}, u32[]{:S(2)}) collective-permute-start(bf16[256,1280]{1,0:T(8,128)(2,1)} %collective-permute-done.10.refs_1_), channel_id=1, source_target_pairs={{0,64},{1,193},{64,128},{65,1},{128,192},{129,65},{192,0},{193,129... | collective-permute-start | bytes 1966088 | tf_op jit(solution)/shard_map/ppermute | solution.py:256
  53.8 1.1 pad_maximum_fusion.1
  54.9 1.1 pad_maximum_fusion.2
  56.2 3.2 %collective-permute-start.24 = (bf16[256,1024]{1,0:T(8,128)(2,1)S(1)}, bf16[256,1024]{1,0:T(8,128)(2,1)S(1)}, u32[]{:S(2)}, u32[]{:S(2)}) collective-permute-start(bf16[256,1024]{1,0:T(8,128)(2,1)S(1)} %pad_maximum_fusion.2), channel_id=1, source_target_pairs={{0,56},{1,9},{8,0},{9,17},{16,8},{17,25},{24,16},{25,33},{32,24},{... | collective-permute-start | bytes 1572872 | tf_op jit(solution)/shard_map/ppermute | solution.py:256
  59.4 2.7 %shard_map.50.g_ref = bf16[2048,1280]{1,0:T(8,128)(2,1)S(1)} custom-call(s32[3]{0:T(128)S(1)} %pad_add_fusion.1.at_ref, bf16[2048,640]{1,0:T(8,128)(2,1)S(1)} %copy-done, bf16[1024,640]{1,0:T(8,128)(2,1)} %collective-permute-done.12.refs_1_, bf16[1024,640]{1,0:T(8,128)(2,1)} %collective-permute-done.13.refs_2_), custom_call_target="tpu_custom_call" | custom-call | bytes 10485760 | tf_op jit(solution)/shard_map/pallas_call | solution.py:216
  62.2 3.0 %shard_map.51.w_ref = bf16[1024,1280]{1,0:T(8,128)(2,1)S(1)} custom-call(s32[4]{0:T(128)S(1)} %iota_multiply_fusion.at_ref, bf16[256,1280]{1,0:T(8,128)(2,1)S(1)} %pad_maximum_fusion.refs_0_, bf16[256,1280]{1,0:T(8,128)(2,1)} %collective-permute-done.10.refs_1_, bf16[256,1280]{1,0:T(8,128)(2,1)S(1)} %copy-done.2, ...), custom_call_target="tpu_custom_call" | custom-call | bytes 5242880 | tf_op jit(solution)/shard_map/pallas_call | solution.py:216
  65.2 1.4 %shard_map.52 = bf16[2064,128]{1,0:T(8,128)(2,1)S(1)} custom-call(s32[1]{0:T(128)} %bitcast.5.at_ref, bf16[2048,1280]{1,0:T(8,128)(2,1)S(1)} %shard_map.50.g_ref, bf16[1024,1280]{1,0:T(8,128)(2,1)S(1)} %shard_map.51.w_ref), custom_call_target="tpu_custom_call" | custom-call | flops 671088640 | bytes 1056768 | tf_op jit(solution)/shard_map/pallas_call | solution.py:122
  66.7 1.4 %shard_map.56 = bf16[2064,128]{1,0:T(8,128)(2,1)S(1)} custom-call(s32[1]{0:T(128)} %bitcast.10.at_ref, bf16[2048,1280]{1,0:T(8,128)(2,1)S(1)} %shard_map.50.g_ref, bf16[1024,1280]{1,0:T(8,128)(2,1)S(1)} %shard_map.51.w_ref), custom_call_target="tpu_custom_call" | custom-call | flops 671088640 | bytes 1056768 | tf_op jit(solution)/shard_map/pallas_call | solution.py:122
  68.1 3.3 %collective-permute-start.19 = (bf16[2064,128]{1,0:T(8,128)(2,1)S(1)}, bf16[2064,128]{1,0:T(8,128)(2,1)S(1)}, u32[]{:S(2)}, u32[]{:S(2)}) collective-permute-start(bf16[2064,128]{1,0:T(8,128)(2,1)S(1)} %shard_map.56), channel_id=1, source_target_pairs={{0,56},{1,9},{8,0},{9,17},{16,8},{17,25},{24,16},{25,33},{32,24},{... | collective-permute-start | bytes 1585160 | tf_op jit(solution)/shard_map/ppermute | solution.py:256
  75.1 4.8 %collective-permute-done.15.refs_0_ = bf16[2064,128]{1,0:T(8,128)(2,1)S(1)} collective-permute-done((bf16[2064,128]{1,0:T(8,128)(2,1)S(1)}, bf16[2064,128]{1,0:T(8,128)(2,1)S(1)}, u32[]{:S(2)}, u32[]{:S(2)}) %collective-permute-start.15) | collective-permute-done | bytes 528416 | tf_op jit(solution)/shard_map/ppermute | solution.py:256
  80.9 3.0 %collective-permute-done.19.refs_0_ = bf16[2064,128]{1,0:T(8,128)(2,1)S(1)} collective-permute-done((bf16[2064,128]{1,0:T(8,128)(2,1)S(1)}, bf16[2064,128]{1,0:T(8,128)(2,1)S(1)}, u32[]{:S(2)}, u32[]{:S(2)}) %collective-permute-start.19) | collective-permute-done | bytes 528416 | tf_op jit(solution)/shard_map/ppermute | solution.py:256
  84.8 3.8 %collective-permute-start.20 = (bf16[2064,128]{1,0:T(8,128)(2,1)S(1)}, bf16[2064,128]{1,0:T(8,128)(2,1)S(1)}, u32[]{:S(2)}, u32[]{:S(2)}) collective-permute-start(bf16[2064,128]{1,0:T(8,128)(2,1)S(1)} %shard_map.57), channel_id=1, source_target_pairs={{0,56},{1,9},{8,0},{9,17},{16,8},{17,25},{24,16},{25,33},{32,24},{... | collective-permute-start | bytes 1585160 | tf_op jit(solution)/shard_map/ppermute | solution.py:256
  88.6 2.3 %shard_map.62 = bf16[2048,1024]{1,0:T(8,128)(2,1)S(1)} custom-call(s32[16]{0:T(128)S(1)} %stack.127.at_ref, bf16[128,1024]{1,0:T(8,128)(2,1)S(1)} %get-tuple-element.43.refs_0_, bf16[128,1024]{1,0:T(8,128)(2,1)} %collective-permute-done.4.refs_1_, bf16[128,1024]{1,0:T(8,128)(2,1)S(1)} %copy-done.4, bf16[128,1024]{1,0:T(8,128)(2,1)S(1)} %copy-done.8, ...), custom_call_target="tpu_custom_call" | custom-call | bytes 8388608 | tf_op jit(solution)/shard_map/pallas_call | solution.py:216
  90.9 1.6 %fusion.6.refs_0_ = f32[256,1280]{1,0:T(8,128)S(1)} fusion(bf16[2048,1280]{1,0:T(8,128)(2,1)S(1)} %shard_map.50.g_ref, bf16[2048,1024]{1,0:T(8,128)(2,1)S(1)} %shard_map.62, s32[]{:T(128)S(6)} %select_n.63), kind=kOutput, calls=%fused_computation.6 | convolution fusion | flops 1342177280 | bytes 7602180 | tf_op jit(solution)/shard_map/dot_general | solution.py:310
  93.2 2.5 %collective-permute-start.26 = (bf16[2576,128]{1,0:T(8,128)(2,1)S(1)}, bf16[2576,128]{1,0:T(8,128)(2,1)S(1)}, u32[]{:S(2)}, u32[]{:S(2)}) collective-permute-start(bf16[2576,128]{1,0:T(8,128)(2,1)S(1)} %shard_map.63), channel_id=1, source_target_pairs={{0,64},{1,193},{64,128},{65,1},{128,192},{129,65},{192,0},{193,129... | collective-permute-start | bytes 1978376 | tf_op jit(solution)/shard_map/ppermute | solution.py:256
  95.7 1.6 %fusion.4.refs_1_ = f32[256,1280]{1,0:T(8,128)S(1)} fusion(bf16[2048,1280]{1,0:T(8,128)(2,1)S(1)} %shard_map.50.g_ref, bf16[2048,1024]{1,0:T(8,128)(2,1)S(1)} %shard_map.62, s32[]{:T(128)S(6)} %select_n.64), kind=kOutput, calls=%fused_computation.4 | convolution fusion | flops 1342177280 | bytes 7602180 | tf_op jit(solution)/shard_map/dot_general | solution.py:310
  98.4 1.6 %fusion.2.refs_0_ = f32[256,1280]{1,0:T(8,128)S(1)} fusion(bf16[2048,1280]{1,0:T(8,128)(2,1)S(1)} %shard_map.50.g_ref, bf16[2048,1024]{1,0:T(8,128)(2,1)S(1)} %shard_map.62, s32[]{:T(128)S(6)} %select_n.65), kind=kOutput, calls=%fused_computation.2 | convolution fusion | flops 1342177280 | bytes 7602180 | tf_op jit(solution)/shard_map/dot_general | solution.py:310
  100.8 3.6 %collective-permute-done.26.refs_0_ = bf16[2576,128]{1,0:T(8,128)(2,1)S(1)} collective-permute-done((bf16[2576,128]{1,0:T(8,128)(2,1)S(1)}, bf16[2576,128]{1,0:T(8,128)(2,1)S(1)}, u32[]{:S(2)}, u32[]{:S(2)}) %collective-permute-start.26) | collective-permute-done | bytes 659488 | tf_op jit(solution)/shard_map/ppermute | solution.py:256
  104.4 1.1 shard_map.64
  105.5 2.0 %collective-permute-start.27 = (bf16[2576,128]{1,0:T(8,128)(2,1)S(1)}, bf16[2576,128]{1,0:T(8,128)(2,1)S(1)}, u32[]{:S(2)}, u32[]{:S(2)}) collective-permute-start(bf16[2576,128]{1,0:T(8,128)(2,1)S(1)} %shard_map.64), channel_id=1, source_target_pairs={{0,64},{1,193},{64,128},{65,1},{128,192},{129,65},{192,0},{193,129... | collective-permute-start | bytes 1978376 | tf_op jit(solution)/shard_map/ppermute | solution.py:256
  108.4 0.9 shard_map.58
  109.3 3.1 %collective-permute-start.21 = (bf16[2064,128]{1,0:T(8,128)(2,1)S(1)}, bf16[2064,128]{1,0:T(8,128)(2,1)S(1)}, u32[]{:S(2)}, u32[]{:S(2)}) collective-permute-start(bf16[2064,128]{1,0:T(8,128)(2,1)S(1)} %shard_map.58), channel_id=1, source_target_pairs={{0,56},{1,9},{8,0},{9,17},{16,8},{17,25},{24,16},{25,33},{32,24},{... | collective-permute-start | bytes 1585160 | tf_op jit(solution)/shard_map/ppermute | solution.py:256
  113.4 1.6 %fusion.own_ref = f32[256,1280]{1,0:T(8,128)S(1)} fusion(bf16[2048,1280]{1,0:T(8,128)(2,1)S(1)} %shard_map.50.g_ref, bf16[2048,1024]{1,0:T(8,128)(2,1)S(1)} %shard_map.62, s32[]{:T(128)S(6)} %select_n.66), kind=kOutput, calls=%fused_computation | convolution fusion | flops 1342177280 | bytes 7602180 | tf_op jit(solution)/shard_map/dot_general | solution.py:310
  115.0 4.0 %collective-permute-done.27.f_ref = bf16[2576,128]{1,0:T(8,128)(2,1)S(1)} collective-permute-done((bf16[2576,128]{1,0:T(8,128)(2,1)S(1)}, bf16[2576,128]{1,0:T(8,128)(2,1)S(1)}, u32[]{:S(2)}, u32[]{:S(2)}) %collective-permute-start.27) | collective-permute-done | bytes 659488 | tf_op jit(solution)/shard_map/ppermute | solution.py:256
  119.0 2.0 %shard_map.66 = (f32[256,640]{1,0:T(8,128)S(1)}, bf16[1296,128]{1,0:T(8,128)(2,1)}) custom-call(s32[1]{0:T(128)} %constant.74.clone.1.idx_ref, bf16[2576,128]{1,0:T(8,128)(2,1)S(1)} %collective-permute-done.27.f_ref, bf16[2576,128]{1,0:T(8,128)(2,1)S(1)} %collective-permute-done.28.b_ref, f32[256,1280]{1,0:T(8,128)S(1)} %fusion.own_ref), custom_call_target="tpu_custom_call" | custom-call | flops 42139648 | bytes 5267456 | tf_op jit(solution)/shard_map/pallas_call | solution.py:185
  123.9 1.7 %shard_map.60 = bf16[128,1024]{1,0:T(8,128)(2,1)} custom-call(s32[2]{0:T(128)S(1)} %pad_add_fusion.2.idx_ref, bf16[2064,128]{1,0:T(8,128)(2,1)S(1)} %collective-permute-done.18.f_ref, bf16[2064,128]{1,0:T(8,128)(2,1)S(1)} %collective-permute-done.21.b_ref, f32[256,1024]{1,0:T(8,128)S(1)} %fusion.8.own_ref), custom_call_target="tpu_custom_call" | custom-call | flops 29491200 | bytes 3686400 | tf_op jit(solution)/shard_map/pallas_call | solution.py:185
  126.5 1.0 shard_map.59.mine_ref
  127.5 4.4 %collective-permute-done.29.got_ref = bf16[1296,128]{1,0:T(8,128)(2,1)S(1)} collective-permute-done((bf16[1296,128]{1,0:T(8,128)(2,1)}, bf16[1296,128]{1,0:T(8,128)(2,1)S(1)}, u32[]{:S(2)}, u32[]{:S(2)}) %collective-permute-start.29) | collective-permute-done | bytes 331808 | tf_op jit(solution)/shard_map/ppermute | solution.py:241
  131.9 1.4 %shard_map.67 = f32[512,640]{1,0:T(8,128)} custom-call(s32[1]{0:T(128)} %bitcast.h_ref, f32[256,640]{1,0:T(8,128)S(1)} %get-tuple-element.56.mine_ref, bf16[1296,128]{1,0:T(8,128)(2,1)S(1)} %collective-permute-done.29.got_ref), custom_call_target="tpu_custom_call" | custom-call | flops 21037056 | bytes 2629632 | tf_op jit(solution)/shard_map/pallas_call | solution.py:185
  133.3 3.3 %collective-permute-done.22.got_ref = bf16[128,1024]{1,0:T(8,128)(2,1)S(1)} collective-permute-done((bf16[128,1024]{1,0:T(8,128)(2,1)}, bf16[128,1024]{1,0:T(8,128)(2,1)S(1)}, u32[]{:S(2)}, u32[]{:S(2)}) %collective-permute-start.22) | collective-permute-done | bytes 262176 | tf_op jit(solution)/shard_map/ppermute | solution.py:241
  136.7 1.4 %shard_map.61 = bf16[128,2048]{1,0:T(8,128)(2,1)} custom-call(s32[5]{0:T(128)S(1)} %stack.102.at_ref, bf16[128,1024]{1,0:T(8,128)(2,1)S(1)} %shard_map.59.mine_ref, bf16[128,1024]{1,0:T(8,128)(2,1)S(1)} %collective-permute-done.22.got_ref), custom_call_target="tpu_custom_call" | custom-call | flops 16777216 | bytes 2097152 | tf_op jit(solution)/shard_map/pallas_call | solution.py:185
  (77 shorter events, 19.2 us)
Async XLA Ops:
  0.6 17.2 %copy-start = (bf16[2048,640]{1,0:T(8,128)(2,1)S(1)}, bf16[2048,640]{1,0:T(8,128)(2,1)}, u32[]{:S(2)}) copy-start(bf16[2048,640]{1,0:T(8,128)(2,1)} %refs_0_) | copy-start | bytes 7864324
  2.7 11.1 %collective-permute-start = (bf16[128,1024]{1,0:T(8,128)(2,1)S(1)}, bf16[128,1024]{1,0:T(8,128)(2,1)S(1)}, u32[]{:S(2)}, u32[]{:S(2)}) collective-permute-start(bf16[128,1024]{1,0:T(8,128)(2,1)S(1)} %get-tuple-element.43.refs_0_), channel_id=1, source_target_pairs={{0,8},{1,57},{8,16},{9,1},{16,24},{17,9},{24,32},{25,17},{32,40},{... | collective-permute-start | bytes 786440 | tf_op jit(solution)/shard_map/ppermute | solution.py:256
  4.6 9.5 %collective-permute-start.2 = (bf16[128,1024]{1,0:T(8,128)(2,1)S(1)}, bf16[128,1024]{1,0:T(8,128)(2,1)S(1)}, u32[]{:S(2)}, u32[]{:S(2)}) collective-permute-start(bf16[128,1024]{1,0:T(8,128)(2,1)S(1)} %get-tuple-element.43.refs_0_), channel_id=1, source_target_pairs={{0,56},{1,9},{8,0},{9,17},{16,8},{17,25},{24,16},{25,33},{32,24},{... | collective-permute-start | bytes 786440 | tf_op jit(solution)/shard_map/ppermute | solution.py:256
  10.5 15.1 %collective-permute-start.5 = (bf16[256,640]{1,0:T(8,128)(2,1)}, bf16[256,640]{1,0:T(8,128)(2,1)}, u32[]{:S(2)}, u32[]{:S(2)}) collective-permute-start(bf16[256,640]{1,0:T(8,128)(2,1)} %get-tuple-element.59), channel_id=1, source_target_pairs={{0,4},{4,0},{1,5},{5,1},{2,6},{6,2},{3,7},{7,3},{8,12},{12,8},{9,1... | collective-permute-start | bytes 983048 | tf_op jit(solution)/shard_map/ppermute | solution.py:241
  12.1 13.5 %collective-permute-start.4 = (bf16[128,1024]{1,0:T(8,128)(2,1)}, bf16[128,1024]{1,0:T(8,128)(2,1)}, u32[]{:S(2)}, u32[]{:S(2)}) collective-permute-start(bf16[128,1024]{1,0:T(8,128)(2,1)} %get-tuple-element.32), channel_id=1, source_target_pairs={{0,4},{4,0},{1,5},{5,1},{2,6},{6,2},{3,7},{7,3},{8,12},{12,8},{9,1... | collective-permute-start | bytes 786440 | tf_op jit(solution)/shard_map/ppermute | solution.py:241
  13.9 13.5 %copy-start.3 = (bf16[128,1024]{1,0:T(8,128)(2,1)}, bf16[128,1024]{1,0:T(8,128)(2,1)S(1)}, u32[]{:S(2)}) copy-start(bf16[128,1024]{1,0:T(8,128)(2,1)S(1)} %collective-permute-done.refs_2_) | copy-start | bytes 786436
  13.9 11.8 %collective-permute-start.1 = (bf16[128,1024]{1,0:T(8,128)(2,1)S(1)}, bf16[128,1024]{1,0:T(8,128)(2,1)}, u32[]{:S(2)}, u32[]{:S(2)}) collective-permute-start(bf16[128,1024]{1,0:T(8,128)(2,1)S(1)} %collective-permute-done.refs_2_), channel_id=1, source_target_pairs={{0,8},{1,57},{8,16},{9,1},{16,24},{17,9},{24,32},{25,17},{32,40},{... | collective-permute-start | bytes 786440 | tf_op jit(solution)/shard_map/ppermute | solution.py:256
  14.2 13.2 %copy-start.5 = (bf16[128,1024]{1,0:T(8,128)(2,1)}, bf16[128,1024]{1,0:T(8,128)(2,1)S(1)}, u32[]{:S(2)}) copy-start(bf16[128,1024]{1,0:T(8,128)(2,1)S(1)} %collective-permute-done.2.refs_4_) | copy-start | bytes 786436
  14.2 11.5 %collective-permute-start.3 = (bf16[128,1024]{1,0:T(8,128)(2,1)S(1)}, bf16[128,1024]{1,0:T(8,128)(2,1)}, u32[]{:S(2)}, u32[]{:S(2)}) collective-permute-start(bf16[128,1024]{1,0:T(8,128)(2,1)S(1)} %collective-permute-done.2.refs_4_), channel_id=1, source_target_pairs={{0,56},{1,9},{8,0},{9,17},{16,8},{17,25},{24,16},{25,33},{32,24},{... | collective-permute-start | bytes 786440 | tf_op jit(solution)/shard_map/ppermute | solution.py:256
  17.8 9.5 %copy-start.11 = (bf16[256,640]{1,0:T(8,128)(2,1)S(1)}, bf16[256,640]{1,0:T(8,128)(2,1)}, u32[]{:S(2)}) copy-start(bf16[256,640]{1,0:T(8,128)(2,1)} %get-tuple-element.58) | copy-start | bytes 983044
  25.7 23.5 %collective-permute-start.12 = (bf16[1024,640]{1,0:T(8,128)(2,1)S(1)}, bf16[1024,640]{1,0:T(8,128)(2,1)}, u32[]{:S(2)}, u32[]{:S(2)}) collective-permute-start(bf16[1024,640]{1,0:T(8,128)(2,1)S(1)} %constant_dynamic-slice_fusion), channel_id=1, source_target_pairs={{0,4},{1,7},{4,2},{5,1},{2,6},{3,5},{6,0},{7,3},{8,12},{9,15},{12,... | collective-permute-start | bytes 3932168 | tf_op jit(solution)/shard_map/ppermute | solution.py:250
  28.4 20.0 %collective-permute-start.10 = (bf16[256,1280]{1,0:T(8,128)(2,1)S(1)}, bf16[256,1280]{1,0:T(8,128)(2,1)}, u32[]{:S(2)}, u32[]{:S(2)}) collective-permute-start(bf16[256,1280]{1,0:T(8,128)(2,1)S(1)} %pad_maximum_fusion.refs_0_), channel_id=1, source_target_pairs={{0,64},{1,193},{64,128},{65,1},{128,192},{129,65},{192,0},{193,129... | collective-permute-start | bytes 1966088 | tf_op jit(solution)/shard_map/ppermute | solution.py:256
  29.6 18.7 %collective-permute-start.11 = (bf16[256,1280]{1,0:T(8,128)(2,1)S(1)}, bf16[256,1280]{1,0:T(8,128)(2,1)S(1)}, u32[]{:S(2)}, u32[]{:S(2)}) collective-permute-start(bf16[256,1280]{1,0:T(8,128)(2,1)S(1)} %pad_maximum_fusion.refs_0_), channel_id=1, source_target_pairs={{0,192},{1,65},{64,0},{65,129},{128,64},{129,193},{192,128},{193,1... | collective-permute-start | bytes 1966088 | tf_op jit(solution)/shard_map/ppermute | solution.py:256
  30.5 8.5 %collective-permute-start.6 = (bf16[128,1024]{1,0:T(8,128)(2,1)}, bf16[128,1024]{1,0:T(8,128)(2,1)S(1)}, u32[]{:S(2)}, u32[]{:S(2)}) collective-permute-start(bf16[128,1024]{1,0:T(8,128)(2,1)} %collective-permute-done.4.refs_1_), channel_id=1, source_target_pairs={{0,8},{1,57},{8,16},{9,1},{16,24},{17,9},{24,32},{25,17},{32,40},{... | collective-permute-start | bytes 786440 | tf_op jit(solution)/shard_map/ppermute | solution.py:256
  30.5 9.3 %collective-permute-start.8 = (bf16[128,1024]{1,0:T(8,128)(2,1)}, bf16[128,1024]{1,0:T(8,128)(2,1)S(1)}, u32[]{:S(2)}, u32[]{:S(2)}) collective-permute-start(bf16[128,1024]{1,0:T(8,128)(2,1)} %collective-permute-done.4.refs_1_), channel_id=1, source_target_pairs={{0,56},{1,9},{8,0},{9,17},{16,8},{17,25},{24,16},{25,33},{32,24},{... | collective-permute-start | bytes 786440 | tf_op jit(solution)/shard_map/ppermute | solution.py:256
  39.0 7.7 %collective-permute-start.7 = (bf16[128,1024]{1,0:T(8,128)(2,1)S(1)}, bf16[128,1024]{1,0:T(8,128)(2,1)}, u32[]{:S(2)}, u32[]{:S(2)}) collective-permute-start(bf16[128,1024]{1,0:T(8,128)(2,1)S(1)} %collective-permute-done.6.refs_3_), channel_id=1, source_target_pairs={{0,8},{1,57},{8,16},{9,1},{16,24},{17,9},{24,32},{25,17},{32,40},{... | collective-permute-start | bytes 786440 | tf_op jit(solution)/shard_map/ppermute | solution.py:256
  39.0 0.7 copy-start.7
  39.8 8.6 %collective-permute-start.9 = (bf16[128,1024]{1,0:T(8,128)(2,1)S(1)}, bf16[128,1024]{1,0:T(8,128)(2,1)}, u32[]{:S(2)}, u32[]{:S(2)}) collective-permute-start(bf16[128,1024]{1,0:T(8,128)(2,1)S(1)} %collective-permute-done.8.refs_5_), channel_id=1, source_target_pairs={{0,56},{1,9},{8,0},{9,17},{16,8},{17,25},{24,16},{25,33},{32,24},{... | collective-permute-start | bytes 786440 | tf_op jit(solution)/shard_map/ppermute | solution.py:256
  43.3 0.7 copy-start.9
  48.4 0.8 copy-start.1
  49.2 10.2 %collective-permute-start.13 = (bf16[1024,640]{1,0:T(8,128)(2,1)}, bf16[1024,640]{1,0:T(8,128)(2,1)}, u32[]{:S(2)}, u32[]{:S(2)}) collective-permute-start(bf16[1024,640]{1,0:T(8,128)(2,1)} %collective-permute-done.12.refs_1_), channel_id=1, source_target_pairs={{0,1},{1,0},{2,3},{3,2},{4,5},{5,4},{6,7},{7,6},{8,9},{9,8},{10,11... | collective-permute-start | bytes 3932168 | tf_op jit(solution)/shard_map/ppermute | solution.py:241
  50.4 11.7 %collective-permute-start.14 = (bf16[256,1280]{1,0:T(8,128)(2,1)}, bf16[256,1280]{1,0:T(8,128)(2,1)}, u32[]{:S(2)}, u32[]{:S(2)}) collective-permute-start(bf16[256,1280]{1,0:T(8,128)(2,1)} %collective-permute-done.10.refs_1_), channel_id=1, source_target_pairs={{0,64},{1,193},{64,128},{65,1},{128,192},{129,65},{192,0},{193,129... | collective-permute-start | bytes 1966088 | tf_op jit(solution)/shard_map/ppermute | solution.py:256
  55.9 6.3 %copy-start.2 = (bf16[256,1280]{1,0:T(8,128)(2,1)S(1)}, bf16[256,1280]{1,0:T(8,128)(2,1)}, u32[]{:S(2)}) copy-start(bf16[256,1280]{1,0:T(8,128)(2,1)} %copy-done.1) | copy-start | bytes 1966084
  55.9 17.2 %collective-permute-start.23 = (bf16[256,1024]{1,0:T(8,128)(2,1)S(1)}, bf16[256,1024]{1,0:T(8,128)(2,1)S(1)}, u32[]{:S(2)}, u32[]{:S(2)}) collective-permute-start(bf16[256,1024]{1,0:T(8,128)(2,1)S(1)} %pad_maximum_fusion.1), channel_id=1, source_target_pairs={{0,8},{1,57},{8,16},{9,1},{16,24},{17,9},{24,32},{25,17},{32,40},{... | collective-permute-start | bytes 1572872 | tf_op jit(solution)/shard_map/ppermute | solution.py:256
  56.2 17.0 %collective-permute-start.24 = (bf16[256,1024]{1,0:T(8,128)(2,1)S(1)}, bf16[256,1024]{1,0:T(8,128)(2,1)S(1)}, u32[]{:S(2)}, u32[]{:S(2)}) collective-permute-start(bf16[256,1024]{1,0:T(8,128)(2,1)S(1)} %pad_maximum_fusion.2), channel_id=1, source_target_pairs={{0,56},{1,9},{8,0},{9,17},{16,8},{17,25},{24,16},{25,33},{32,24},{... | collective-permute-start | bytes 1572872 | tf_op jit(solution)/shard_map/ppermute | solution.py:256
  66.6 13.2 %collective-permute-start.15 = (bf16[2064,128]{1,0:T(8,128)(2,1)S(1)}, bf16[2064,128]{1,0:T(8,128)(2,1)S(1)}, u32[]{:S(2)}, u32[]{:S(2)}) collective-permute-start(bf16[2064,128]{1,0:T(8,128)(2,1)S(1)} %shard_map.52), channel_id=1, source_target_pairs={{0,8},{1,57},{8,16},{9,1},{16,24},{17,9},{24,32},{25,17},{32,40},{... | collective-permute-start | bytes 1585160 | tf_op jit(solution)/shard_map/ppermute | solution.py:256
  68.1 15.8 %collective-permute-start.19 = (bf16[2064,128]{1,0:T(8,128)(2,1)S(1)}, bf16[2064,128]{1,0:T(8,128)(2,1)S(1)}, u32[]{:S(2)}, u32[]{:S(2)}) collective-permute-start(bf16[2064,128]{1,0:T(8,128)(2,1)S(1)} %shard_map.56), channel_id=1, source_target_pairs={{0,56},{1,9},{8,0},{9,17},{16,8},{17,25},{24,16},{25,33},{32,24},{... | collective-permute-start | bytes 1585160 | tf_op jit(solution)/shard_map/ppermute | solution.py:256
  73.2 15.4 %collective-permute-start.25 = (bf16[256,1024]{1,0:T(8,128)(2,1)S(1)}, bf16[256,1024]{1,0:T(8,128)(2,1)S(1)}, u32[]{:S(2)}, u32[]{:S(2)}) collective-permute-start(bf16[256,1024]{1,0:T(8,128)(2,1)S(1)} %collective-permute-done.23.refs_10_), channel_id=1, source_target_pairs={{0,8},{1,57},{8,16},{9,1},{16,24},{17,9},{24,32},{25,17},{32,40},{... | collective-permute-start | bytes 1572872 | tf_op jit(solution)/shard_map/ppermute | solution.py:256
  75.0 13.6 %copy-start.4 = (bf16[128,1024]{1,0:T(8,128)(2,1)S(1)}, bf16[128,1024]{1,0:T(8,128)(2,1)}, u32[]{:S(2)}) copy-start(bf16[128,1024]{1,0:T(8,128)(2,1)} %copy-done.3) | copy-start | bytes 786436
  75.1 13.5 %copy-start.6 = (bf16[128,1024]{1,0:T(8,128)(2,1)S(1)}, bf16[128,1024]{1,0:T(8,128)(2,1)}, u32[]{:S(2)}) copy-start(bf16[128,1024]{1,0:T(8,128)(2,1)} %copy-done.5) | copy-start | bytes 786436
  75.1 13.5 %copy-start.8 = (bf16[128,1024]{1,0:T(8,128)(2,1)S(1)}, bf16[128,1024]{1,0:T(8,128)(2,1)}, u32[]{:S(2)}) copy-start(bf16[128,1024]{1,0:T(8,128)(2,1)} %copy-done.7) | copy-start | bytes 786436
  75.1 13.5 %copy-start.10 = (bf16[128,1024]{1,0:T(8,128)(2,1)S(1)}, bf16[128,1024]{1,0:T(8,128)(2,1)}, u32[]{:S(2)}) copy-start(bf16[128,1024]{1,0:T(8,128)(2,1)} %copy-done.9) | copy-start | bytes 786436
  80.8 16.7 %collective-permute-start.16 = (bf16[2064,128]{1,0:T(8,128)(2,1)S(1)}, bf16[2064,128]{1,0:T(8,128)(2,1)S(1)}, u32[]{:S(2)}, u32[]{:S(2)}) collective-permute-start(bf16[2064,128]{1,0:T(8,128)(2,1)S(1)} %shard_map.53), channel_id=1, source_target_pairs={{0,8},{1,57},{8,16},{9,1},{16,24},{17,9},{24,32},{25,17},{32,40},{... | collective-permute-start | bytes 1585160 | tf_op jit(solution)/shard_map/ppermute | solution.py:256
  84.8 23.6 %collective-permute-start.20 = (bf16[2064,128]{1,0:T(8,128)(2,1)S(1)}, bf16[2064,128]{1,0:T(8,128)(2,1)S(1)}, u32[]{:S(2)}, u32[]{:S(2)}) collective-permute-start(bf16[2064,128]{1,0:T(8,128)(2,1)S(1)} %shard_map.57), channel_id=1, source_target_pairs={{0,56},{1,9},{8,0},{9,17},{16,8},{17,25},{24,16},{25,33},{32,24},{... | collective-permute-start | bytes 1585160 | tf_op jit(solution)/shard_map/ppermute | solution.py:256
  93.2 11.3 %collective-permute-start.26 = (bf16[2576,128]{1,0:T(8,128)(2,1)S(1)}, bf16[2576,128]{1,0:T(8,128)(2,1)S(1)}, u32[]{:S(2)}, u32[]{:S(2)}) collective-permute-start(bf16[2576,128]{1,0:T(8,128)(2,1)S(1)} %shard_map.63), channel_id=1, source_target_pairs={{0,64},{1,193},{64,128},{65,1},{128,192},{129,65},{192,0},{193,129... | collective-permute-start | bytes 1978376 | tf_op jit(solution)/shard_map/ppermute | solution.py:256
  98.3 14.1 %collective-permute-start.17 = (bf16[2064,128]{1,0:T(8,128)(2,1)S(1)}, bf16[2064,128]{1,0:T(8,128)(2,1)S(1)}, u32[]{:S(2)}, u32[]{:S(2)}) collective-permute-start(bf16[2064,128]{1,0:T(8,128)(2,1)S(1)} %shard_map.54), channel_id=1, source_target_pairs={{0,8},{1,57},{8,16},{9,1},{16,24},{17,9},{24,32},{25,17},{32,40},{... | collective-permute-start | bytes 1585160 | tf_op jit(solution)/shard_map/ppermute | solution.py:256
  100.7 14.4 %collective-permute-start.28 = (bf16[2576,128]{1,0:T(8,128)(2,1)S(1)}, bf16[2576,128]{1,0:T(8,128)(2,1)S(1)}, u32[]{:S(2)}, u32[]{:S(2)}) collective-permute-start(bf16[2576,128]{1,0:T(8,128)(2,1)S(1)} %shard_map.65), channel_id=1, source_target_pairs={{0,192},{1,65},{64,0},{65,129},{128,64},{129,193},{192,128},{193,1... | collective-permute-start | bytes 1978376 | tf_op jit(solution)/shard_map/ppermute | solution.py:256
  105.5 13.5 %collective-permute-start.27 = (bf16[2576,128]{1,0:T(8,128)(2,1)S(1)}, bf16[2576,128]{1,0:T(8,128)(2,1)S(1)}, u32[]{:S(2)}, u32[]{:S(2)}) collective-permute-start(bf16[2576,128]{1,0:T(8,128)(2,1)S(1)} %shard_map.64), channel_id=1, source_target_pairs={{0,64},{1,193},{64,128},{65,1},{128,192},{129,65},{192,0},{193,129... | collective-permute-start | bytes 1978376 | tf_op jit(solution)/shard_map/ppermute | solution.py:256
  109.3 13.6 %collective-permute-start.21 = (bf16[2064,128]{1,0:T(8,128)(2,1)S(1)}, bf16[2064,128]{1,0:T(8,128)(2,1)S(1)}, u32[]{:S(2)}, u32[]{:S(2)}) collective-permute-start(bf16[2064,128]{1,0:T(8,128)(2,1)S(1)} %shard_map.58), channel_id=1, source_target_pairs={{0,56},{1,9},{8,0},{9,17},{16,8},{17,25},{24,16},{25,33},{32,24},{... | collective-permute-start | bytes 1585160 | tf_op jit(solution)/shard_map/ppermute | solution.py:256
  113.3 10.5 %collective-permute-start.18 = (bf16[2064,128]{1,0:T(8,128)(2,1)S(1)}, bf16[2064,128]{1,0:T(8,128)(2,1)S(1)}, u32[]{:S(2)}, u32[]{:S(2)}) collective-permute-start(bf16[2064,128]{1,0:T(8,128)(2,1)S(1)} %shard_map.55), channel_id=1, source_target_pairs={{0,8},{1,57},{8,16},{9,1},{16,24},{17,9},{24,32},{25,17},{32,40},{... | collective-permute-start | bytes 1585160 | tf_op jit(solution)/shard_map/ppermute | solution.py:256
  121.0 10.9 %collective-permute-start.29 = (bf16[1296,128]{1,0:T(8,128)(2,1)}, bf16[1296,128]{1,0:T(8,128)(2,1)S(1)}, u32[]{:S(2)}, u32[]{:S(2)}) collective-permute-start(bf16[1296,128]{1,0:T(8,128)(2,1)} %get-tuple-element.57), channel_id=1, source_target_pairs={{0,4},{4,0},{1,5},{5,1},{2,6},{6,2},{3,7},{7,3},{8,12},{12,8},{9,1... | collective-permute-start | bytes 995336 | tf_op jit(solution)/shard_map/ppermute | solution.py:241
  125.5 11.1 %collective-permute-start.22 = (bf16[128,1024]{1,0:T(8,128)(2,1)}, bf16[128,1024]{1,0:T(8,128)(2,1)S(1)}, u32[]{:S(2)}, u32[]{:S(2)}) collective-permute-start(bf16[128,1024]{1,0:T(8,128)(2,1)} %shard_map.60), channel_id=1, source_target_pairs={{0,4},{4,0},{1,5},{5,1},{2,6},{6,2},{3,7},{7,3},{8,12},{12,8},{9,1... | collective-permute-start | bytes 786440 | tf_op jit(solution)/shard_map/ppermute | solution.py:241

commit v8 on v7

--- a/solution.py
+++ b/solution.py
@@ -103,8 +103,9 @@
         out_ref[:, pl.ds(got_at, half)] = got_ref[:, at]
 
 
-def first_kernel(at_ref, g_ref, w_ref, out_ref, v_ref):
-    v_ref[...] = dot(g_ref[...], w_ref[...], ((1,), (1,)))
+def first_kernel(at_ref, g_ref, near_ref, last_ref, out_ref, v_ref):
+    v_ref[:, : near_ref.shape[0]] = dot(g_ref[...], near_ref[...], ((1,), (1,)))
+    v_ref[:, near_ref.shape[0] :] = dot(g_ref[...], last_ref[...], ((1,), (1,)))
 
     def body(r, amax):
         for j in range(v_ref.shape[1] // LANES):
@@ -115,9 +116,9 @@
     write_coded(v_ref, v_ref.shape[1] // LANES, amax, out_ref)
 
 
-def first_sum(i, rows, g_pair, w_all):
+def first_sum(i, rows, g_pair, near, last):
     width = g_pair.shape[1]
-    shape = (rows, w_all.shape[0])
+    shape = (rows, near.shape[0] + last.shape[0])
     out = coded_shape(*shape)
     return pl.pallas_call(
         first_kernel,
@@ -126,6 +127,7 @@
             grid=(1,),
             in_specs=[
                 pl.BlockSpec((rows, width), lambda j, at: (at[0], 0)),
+                pl.BlockSpec(memory_space=pltpu.VMEM),
                 pl.BlockSpec(memory_space=pltpu.VMEM),
             ],
             out_specs=whole(out.shape),
@@ -136,7 +138,7 @@
         cost_estimate=pl.CostEstimate(
             flops=2 * width * shape[0] * shape[1], bytes_accessed=4 * out.size, transcendentals=0
         ),
-    )(jnp.stack([jnp.int32(i)]), g_pair, w_all)
+    )(jnp.stack([jnp.int32(i)]), g_pair, near, last)
 
 
 def owned_kernel(idx_ref, f_ref, b_ref, own_ref, mine_ref, out_ref, v_ref):
@@ -358,9 +360,11 @@
     arrays, acts_pieces, shape, blocks = gathered([acts_mine, acts_got], "z", (h, 1 - h), 3, before, known)
     (g_pair,) = pairs
 
-    pieces = [(i, 0, half, 0, i * half) for i in range(owners)]
-    w_all = placed(ws[:-1] + [after(g_pair, ws[-1])[1]], pieces, (owners * half, 2 * width), owners - 1)
-    first = [first_sum(block_at("z", k), 2 * own_tokens, g_pair, w_all) for k in (4, -3)]
+    pieces = [(i, 0, half, 0, i * half) for i in range(owners - 1)]
+    w_near = placed(ws[:-1], pieces, ((owners - 1) * half, 2 * width), owners - 1)
+    *_, w_last = after(g_pair, w_near, ws[-1])
+    first = [first_sum(block_at("z", k), 2 * own_tokens, g_pair, w_near, w_last) for k in (4, -3)]
+    w_all = jnp.concatenate(after(*first, w_near, w_last)[2:])
 
     def of_tokens(i):
         count = 2 * own_tokens

time: 140 us -> 145 us (1.036)
  the two profiles are of different devices: /device:TPU:4 before, /device:TPU:1 now
where the time goes in v8:
time: 145 us; the launch traced here: 144 us
  starting transfers between devices  50.2 us (35%)
  waiting for transfers between devices  43.2 us (30%)
  Pallas kernels  25.1 us (17%)
  matrix products  11.5 us (8%)
  local copies, waits for them, and re-layouts  9.03 us (6%)
  other arithmetic  4.2 us (3%)
    ppermute x24, starting transfers between devices, ring(): return lax.ppermute(a, (axis, 'c'), perm)  44.6 us
    ppermute x24, waiting for transfers between devices, ring(): return lax.ppermute(a, (axis, 'c'), perm)  27.9 us
    pallas_call x13, Pallas kernels, call(): pl.pallas_call(kernel, grid_spec=pltpu.PrefetchScalarGridSpec(num_scalar_...  15.5 us
    ppermute x5, waiting for transfers between devices, swap(): return lax.ppermute(a, axis, [(0, 1), (1, 0)])  15.3 us
    dot_general x10, matrix products, dot(): return lax.dot_general(a, b, (dims, ((), ())), preferred_element_type=F32)  11.5 us
    pallas_call x3, Pallas kernels, placed(): pl.pallas_call(functools.partial(placed_kernel, fixed), grid_spec=pltpu.P...  6.75 us
    unnamed x37, local copies, waits for them, and re-layouts  5.48 us
    ppermute x5, starting transfers between devices, swap(): return lax.ppermute(a, axis, [(0, 1), (1, 0)])  2.94 us
  transfers between devices with their start and end apart: 30, of which 12 were waited for; matrix products, arithmetic and copies ran while one was open for 12% of the time, Pallas kernels for 16%

profile of v8, /device:TPU:1, one launch (start us, length us, event | category | flops | bytes accessed | tf_op | source)
XLA Modules:
  0.0 144.4 jit_solution(5443379874040395159)
XLA Ops:
  0.6 1.3 fusion.30
  2.7 6.4 %collective-permute-start = (bf16[128,1024]{1,0:T(8,128)(2,1)S(1)}, bf16[128,1024]{1,0:T(8,128)(2,1)}, u32[]{:S(2)}, u32[]{:S(2)}) collective-permute-start(bf16[128,1024]{1,0:T(8,128)(2,1)S(1)} %get-tuple-element.47.refs_0_), channel_id=1, source_target_pairs={{0,8},{1,57},{8,16},{9,1},{16,24},{17,9},{24,32},{25,17},{32,40},{... | collective-permute-start | bytes 786440 | tf_op jit(solution)/shard_map/ppermute | solution.py:258
  9.1 2.0 %dynamic-slice_bitcast_fusion = (bf16[256,640]{1,0:T(8,128)(2,1)}, bf16[256,640]{1,0:T(8,128)(2,1)}) fusion(bf16[1,512,640]{2,1,0:T(8,128)(2,1)} %param.5, s32[]{:T(128)S(6)} %select_n.55, s32[]{:T(128)S(6)} %select_n.54), kind=kLoop, calls=%fused_computation.23 | loop fusion | bytes 1310728 | tf_op jit(solution)/shard_map/dynamic_slice | solution.py:334
  11.1 1.3 collective-permute-start.5
  12.6 1.5 %collective-permute-done.refs_2_ = bf16[128,1024]{1,0:T(8,128)(2,1)} collective-permute-done((bf16[128,1024]{1,0:T(8,128)(2,1)S(1)}, bf16[128,1024]{1,0:T(8,128)(2,1)}, u32[]{:S(2)}, u32[]{:S(2)}) %collective-permute-start) | collective-permute-done | bytes 262176 | tf_op jit(solution)/shard_map/ppermute | solution.py:258
  14.1 3.5 %collective-permute-start.1 = (bf16[128,1024]{1,0:T(8,128)(2,1)}, bf16[128,1024]{1,0:T(8,128)(2,1)S(1)}, u32[]{:S(2)}, u32[]{:S(2)}) collective-permute-start(bf16[128,1024]{1,0:T(8,128)(2,1)} %collective-permute-done.refs_2_), channel_id=1, source_target_pairs={{0,8},{1,57},{8,16},{9,1},{16,24},{17,9},{24,32},{25,17},{32,40},{... | collective-permute-start | bytes 786440 | tf_op jit(solution)/shard_map/ppermute | solution.py:258
  17.8 7.5 %collective-permute-done.4.refs_1_ = bf16[128,1024]{1,0:T(8,128)(2,1)} collective-permute-done((bf16[128,1024]{1,0:T(8,128)(2,1)}, bf16[128,1024]{1,0:T(8,128)(2,1)}, u32[]{:S(2)}, u32[]{:S(2)}) %collective-permute-start.4) | collective-permute-done | bytes 262176 | tf_op jit(solution)/shard_map/ppermute | solution.py:243
  25.6 2.7 %collective-permute-start.12 = (bf16[1024,640]{1,0:T(8,128)(2,1)S(1)}, bf16[1024,640]{1,0:T(8,128)(2,1)}, u32[]{:S(2)}, u32[]{:S(2)}) collective-permute-start(bf16[1024,640]{1,0:T(8,128)(2,1)S(1)} %constant_dynamic-slice_fusion), channel_id=1, source_target_pairs={{0,4},{1,7},{4,2},{5,1},{2,6},{3,5},{6,0},{7,3},{8,12},{9,15},{12,... | collective-permute-start | bytes 3932168 | tf_op jit(solution)/shard_map/ppermute | solution.py:252
  28.4 1.0 pad_maximum_fusion.refs_0_
  29.4 2.6 %collective-permute-start.10 = (bf16[256,1280]{1,0:T(8,128)(2,1)S(1)}, bf16[256,1280]{1,0:T(8,128)(2,1)}, u32[]{:S(2)}, u32[]{:S(2)}) collective-permute-start(bf16[256,1280]{1,0:T(8,128)(2,1)S(1)} %pad_maximum_fusion.refs_0_), channel_id=1, source_target_pairs={{0,64},{1,193},{64,128},{65,1},{128,192},{129,65},{192,0},{193,129... | collective-permute-start | bytes 1966088 | tf_op jit(solution)/shard_map/ppermute | solution.py:258
  32.8 3.5 %collective-permute-start.6 = (bf16[128,1024]{1,0:T(8,128)(2,1)}, bf16[128,1024]{1,0:T(8,128)(2,1)S(1)}, u32[]{:S(2)}, u32[]{:S(2)}) collective-permute-start(bf16[128,1024]{1,0:T(8,128)(2,1)} %collective-permute-done.4.refs_1_), channel_id=1, source_target_pairs={{0,8},{1,57},{8,16},{9,1},{16,24},{17,9},{24,32},{25,17},{32,40},{... | collective-permute-start | bytes 786440 | tf_op jit(solution)/shard_map/ppermute | solution.py:258
  36.3 5.3 %collective-permute-done.6.refs_3_ = bf16[128,1024]{1,0:T(8,128)(2,1)S(1)} collective-permute-done((bf16[128,1024]{1,0:T(8,128)(2,1)}, bf16[128,1024]{1,0:T(8,128)(2,1)S(1)}, u32[]{:S(2)}, u32[]{:S(2)}) %collective-permute-start.6) | collective-permute-done | bytes 262176 | tf_op jit(solution)/shard_map/ppermute | solution.py:258
  41.6 3.4 %collective-permute-start.7 = (bf16[128,1024]{1,0:T(8,128)(2,1)S(1)}, bf16[128,1024]{1,0:T(8,128)(2,1)S(1)}, u32[]{:S(2)}, u32[]{:S(2)}) collective-permute-start(bf16[128,1024]{1,0:T(8,128)(2,1)S(1)} %collective-permute-done.6.refs_3_), channel_id=1, source_target_pairs={{0,8},{1,57},{8,16},{9,1},{16,24},{17,9},{24,32},{25,17},{32,40},{... | collective-permute-start | bytes 786440 | tf_op jit(solution)/shard_map/ppermute | solution.py:258
  46.4 2.7 %collective-permute-done.7.refs_7_ = bf16[128,1024]{1,0:T(8,128)(2,1)S(1)} collective-permute-done((bf16[128,1024]{1,0:T(8,128)(2,1)S(1)}, bf16[128,1024]{1,0:T(8,128)(2,1)S(1)}, u32[]{:S(2)}, u32[]{:S(2)}) %collective-permute-start.7) | collective-permute-done | bytes 262176 | tf_op jit(solution)/shard_map/ppermute | solution.py:258
  49.1 3.3 %collective-permute-done.9.refs_9_ = bf16[128,1024]{1,0:T(8,128)(2,1)S(1)} collective-permute-done((bf16[128,1024]{1,0:T(8,128)(2,1)S(1)}, bf16[128,1024]{1,0:T(8,128)(2,1)S(1)}, u32[]{:S(2)}, u32[]{:S(2)}) %collective-permute-start.9) | collective-permute-done | bytes 262176 | tf_op jit(solution)/shard_map/ppermute | solution.py:258
  53.4 3.3 %collective-permute-start.14 = (bf16[256,1280]{1,0:T(8,128)(2,1)}, bf16[256,1280]{1,0:T(8,128)(2,1)S(1)}, u32[]{:S(2)}, u32[]{:S(2)}) collective-permute-start(bf16[256,1280]{1,0:T(8,128)(2,1)} %collective-permute-done.10.refs_1_), channel_id=1, source_target_pairs={{0,64},{1,193},{64,128},{65,1},{128,192},{129,65},{192,0},{193,129... | collective-permute-start | bytes 1966088 | tf_op jit(solution)/shard_map/ppermute | solution.py:258
  56.9 1.1 pad_maximum_fusion.1
  58.0 1.1 pad_maximum_fusion.2
  59.1 3.0 %collective-permute-start.23 = (bf16[256,1024]{1,0:T(8,128)(2,1)S(1)}, bf16[256,1024]{1,0:T(8,128)(2,1)S(1)}, u32[]{:S(2)}, u32[]{:S(2)}) collective-permute-start(bf16[256,1024]{1,0:T(8,128)(2,1)S(1)} %pad_maximum_fusion.1), channel_id=1, source_target_pairs={{0,8},{1,57},{8,16},{9,1},{16,24},{17,9},{24,32},{25,17},{32,40},{... | collective-permute-start | bytes 1572872 | tf_op jit(solution)/shard_map/ppermute | solution.py:258
  62.0 1.1 copy-done.2
  63.1 1.1 copy-done.12
  64.2 1.9 %shard_map.51.near_ref = bf16[768,1280]{1,0:T(8,128)(2,1)S(1)} custom-call(s32[3]{0:T(128)S(1)} %iota_multiply_fusion.at_ref, bf16[256,1280]{1,0:T(8,128)(2,1)S(1)} %copy-done.2, bf16[256,1280]{1,0:T(8,128)(2,1)} %collective-permute-done.10.refs_1_, bf16[256,1280]{1,0:T(8,128)(2,1)S(1)} %copy-done.12), custom_call_target="tpu_custom_call" | custom-call | bytes 3932160 | tf_op jit(solution)/shard_map/pallas_call | solution.py:218
  66.1 2.7 %shard_map.50.g_ref = bf16[2048,1280]{1,0:T(8,128)(2,1)S(1)} custom-call(s32[3]{0:T(128)S(1)} %pad_add_fusion.1.at_ref, bf16[2048,640]{1,0:T(8,128)(2,1)S(1)} %copy-done, bf16[1024,640]{1,0:T(8,128)(2,1)} %collective-permute-done.12.refs_1_, bf16[1024,640]{1,0:T(8,128)(2,1)} %collective-permute-done.13.refs_2_), custom_call_target="tpu_custom_call" | custom-call | bytes 10485760 | tf_op jit(solution)/shard_map/pallas_call | solution.py:218
  68.9 1.4 shard_map.52
  70.3 2.8 %collective-permute-start.15 = (bf16[2064,128]{1,0:T(8,128)(2,1)S(1)}, bf16[2064,128]{1,0:T(8,128)(2,1)S(1)}, u32[]{:S(2)}, u32[]{:S(2)}) collective-permute-start(bf16[2064,128]{1,0:T(8,128)(2,1)S(1)} %shard_map.52), channel_id=1, source_target_pairs={{0,8},{1,57},{8,16},{9,1},{16,24},{17,9},{24,32},{25,17},{32,40},{... | collective-permute-start | bytes 1585160 | tf_op jit(solution)/shard_map/ppermute | solution.py:258
  73.0 1.4 shard_map.53
  76.5 2.7 %collective-permute-start.25 = (bf16[256,1024]{1,0:T(8,128)(2,1)S(1)}, bf16[256,1024]{1,0:T(8,128)(2,1)S(1)}, u32[]{:S(2)}, u32[]{:S(2)}) collective-permute-start(bf16[256,1024]{1,0:T(8,128)(2,1)S(1)} %collective-permute-done.23.refs_10_), channel_id=1, source_target_pairs={{0,8},{1,57},{8,16},{9,1},{16,24},{17,9},{24,32},{25,17},{32,40},{... | collective-permute-start | bytes 1572872 | tf_op jit(solution)/shard_map/ppermute | solution.py:258
  81.1 3.5 %collective-permute-done.15.refs_0_ = bf16[2064,128]{1,0:T(8,128)(2,1)S(1)} collective-permute-done((bf16[2064,128]{1,0:T(8,128)(2,1)S(1)}, bf16[2064,128]{1,0:T(8,128)(2,1)S(1)}, u32[]{:S(2)}, u32[]{:S(2)}) %collective-permute-start.15) | collective-permute-done | bytes 528416 | tf_op jit(solution)/shard_map/ppermute | solution.py:258
  85.5 3.5 %collective-permute-start.16 = (bf16[2064,128]{1,0:T(8,128)(2,1)S(1)}, bf16[2064,128]{1,0:T(8,128)(2,1)S(1)}, u32[]{:S(2)}, u32[]{:S(2)}) collective-permute-start(bf16[2064,128]{1,0:T(8,128)(2,1)S(1)} %shard_map.54), channel_id=1, source_target_pairs={{0,8},{1,57},{8,16},{9,1},{16,24},{17,9},{24,32},{25,17},{32,40},{... | collective-permute-start | bytes 1585160 | tf_op jit(solution)/shard_map/ppermute | solution.py:258
  90.5 2.1 %shard_map.62 = bf16[2048,1024]{1,0:T(8,128)(2,1)S(1)} custom-call(s32[16]{0:T(128)S(1)} %stack.127.at_ref, bf16[128,1024]{1,0:T(8,128)(2,1)S(1)} %get-tuple-element.47.refs_0_, bf16[128,1024]{1,0:T(8,128)(2,1)} %collective-permute-done.4.refs_1_, bf16[128,1024]{1,0:T(8,128)(2,1)} %collective-permute-done.refs_2_, bf16[128,1024]{1,0:T(8,128)(2,1)S(1)} %copy-done.14, ...), custom_call_target="tpu_custom_call" | custom-call | bytes 8388608 | tf_op jit(solution)/shard_map/pallas_call | solution.py:218
  92.7 1.6 %fusion.6.refs_0_ = f32[256,1280]{1,0:T(8,128)S(1)} fusion(bf16[2048,1280]{1,0:T(8,128)(2,1)S(1)} %shard_map.50.g_ref, bf16[2048,1024]{1,0:T(8,128)(2,1)S(1)} %shard_map.62, s32[]{:T(128)S(6)} %select_n.63), kind=kOutput, calls=%fused_computation.6 | convolution fusion | flops 1342177280 | bytes 7602180 | tf_op jit(solution)/shard_map/dot_general | solution.py:312
  95.7 1.6 %fusion.4.refs_1_ = f32[256,1280]{1,0:T(8,128)S(1)} fusion(bf16[2048,1280]{1,0:T(8,128)(2,1)S(1)} %shard_map.50.g_ref, bf16[2048,1024]{1,0:T(8,128)(2,1)S(1)} %shard_map.62, s32[]{:T(128)S(6)} %select_n.64), kind=kOutput, calls=%fused_computation.4 | convolution fusion | flops 1342177280 | bytes 7602180 | tf_op jit(solution)/shard_map/dot_general | solution.py:312
  97.2 4.1 %collective-permute-done.16.refs_0_ = bf16[2064,128]{1,0:T(8,128)(2,1)S(1)} collective-permute-done((bf16[2064,128]{1,0:T(8,128)(2,1)S(1)}, bf16[2064,128]{1,0:T(8,128)(2,1)S(1)}, u32[]{:S(2)}, u32[]{:S(2)}) %collective-permute-start.16) | collective-permute-done | bytes 528416 | tf_op jit(solution)/shard_map/ppermute | solution.py:258
  102.3 3.4 %collective-permute-start.17 = (bf16[2064,128]{1,0:T(8,128)(2,1)S(1)}, bf16[2064,128]{1,0:T(8,128)(2,1)S(1)}, u32[]{:S(2)}, u32[]{:S(2)}) collective-permute-start(bf16[2064,128]{1,0:T(8,128)(2,1)S(1)} %shard_map.55), channel_id=1, source_target_pairs={{0,8},{1,57},{8,16},{9,1},{16,24},{17,9},{24,32},{25,17},{32,40},{... | collective-permute-start | bytes 1585160 | tf_op jit(solution)/shard_map/ppermute | solution.py:258
  105.7 1.6 %fusion.2.refs_0_ = f32[256,1280]{1,0:T(8,128)S(1)} fusion(bf16[2048,1280]{1,0:T(8,128)(2,1)S(1)} %shard_map.50.g_ref, bf16[2048,1024]{1,0:T(8,128)(2,1)S(1)} %shard_map.62, s32[]{:T(128)S(6)} %select_n.65), kind=kOutput, calls=%fused_computation.2 | convolution fusion | flops 1342177280 | bytes 7602180 | tf_op jit(solution)/shard_map/dot_general | solution.py:312
  108.0 1.1 shard_map.64
  109.1 2.8 %collective-permute-start.27 = (bf16[2576,128]{1,0:T(8,128)(2,1)S(1)}, bf16[2576,128]{1,0:T(8,128)(2,1)S(1)}, u32[]{:S(2)}, u32[]{:S(2)}) collective-permute-start(bf16[2576,128]{1,0:T(8,128)(2,1)S(1)} %shard_map.64), channel_id=1, source_target_pairs={{0,64},{1,193},{64,128},{65,1},{128,192},{129,65},{192,0},{193,129... | collective-permute-start | bytes 1978376 | tf_op jit(solution)/shard_map/ppermute | solution.py:258
  114.7 2.7 %collective-permute-start.18 = (bf16[2064,128]{1,0:T(8,128)(2,1)S(1)}, bf16[2064,128]{1,0:T(8,128)(2,1)S(1)}, u32[]{:S(2)}, u32[]{:S(2)}) collective-permute-start(bf16[2064,128]{1,0:T(8,128)(2,1)S(1)} %shard_map.56), channel_id=1, source_target_pairs={{0,8},{1,57},{8,16},{9,1},{16,24},{17,9},{24,32},{25,17},{32,40},{... | collective-permute-start | bytes 1585160 | tf_op jit(solution)/shard_map/ppermute | solution.py:258
  117.5 1.6 %fusion.own_ref = f32[256,1280]{1,0:T(8,128)S(1)} fusion(bf16[2048,1280]{1,0:T(8,128)(2,1)S(1)} %shard_map.50.g_ref, bf16[2048,1024]{1,0:T(8,128)(2,1)S(1)} %shard_map.62, s32[]{:T(128)S(6)} %select_n.66), kind=kOutput, calls=%fused_computation | convolution fusion | flops 1342177280 | bytes 7602180 | tf_op jit(solution)/shard_map/dot_general | solution.py:312
  119.0 6.6 %collective-permute-done.28.b_ref = bf16[2576,128]{1,0:T(8,128)(2,1)S(1)} collective-permute-done((bf16[2576,128]{1,0:T(8,128)(2,1)S(1)}, bf16[2576,128]{1,0:T(8,128)(2,1)S(1)}, u32[]{:S(2)}, u32[]{:S(2)}) %collective-permute-start.28) | collective-permute-done | bytes 659488 | tf_op jit(solution)/shard_map/ppermute | solution.py:258
  125.6 2.0 %shard_map.66 = (f32[256,640]{1,0:T(8,128)S(1)}, bf16[1296,128]{1,0:T(8,128)(2,1)}) custom-call(s32[1]{0:T(128)} %constant.74.clone.1.idx_ref, bf16[2576,128]{1,0:T(8,128)(2,1)S(1)} %collective-permute-done.27.f_ref, bf16[2576,128]{1,0:T(8,128)(2,1)S(1)} %collective-permute-done.28.b_ref, f32[256,1280]{1,0:T(8,128)S(1)} %fusion.own_ref), custom_call_target="tpu_custom_call" | custom-call | flops 42139648 | bytes 5267456 | tf_op jit(solution)/shard_map/pallas_call | solution.py:187
  128.5 1.7 %shard_map.60 = bf16[128,1024]{1,0:T(8,128)(2,1)} custom-call(s32[2]{0:T(128)S(1)} %pad_add_fusion.2.idx_ref, bf16[2064,128]{1,0:T(8,128)(2,1)S(1)} %collective-permute-done.18.f_ref, bf16[2064,128]{1,0:T(8,128)(2,1)S(1)} %collective-permute-done.21.b_ref, f32[256,1024]{1,0:T(8,128)S(1)} %fusion.8.own_ref), custom_call_target="tpu_custom_call" | custom-call | flops 29491200 | bytes 3686400 | tf_op jit(solution)/shard_map/pallas_call | solution.py:187
  130.2 1.5 %collective-permute-start.22 = (bf16[128,1024]{1,0:T(8,128)(2,1)}, bf16[128,1024]{1,0:T(8,128)(2,1)}, u32[]{:S(2)}, u32[]{:S(2)}) collective-permute-start(bf16[128,1024]{1,0:T(8,128)(2,1)} %shard_map.60), channel_id=1, source_target_pairs={{0,4},{4,0},{1,5},{5,1},{2,6},{6,2},{3,7},{7,3},{8,12},{12,8},{9,1... | collective-permute-start | bytes 786440 | tf_op jit(solution)/shard_map/ppermute | solution.py:243
  131.8 1.0 shard_map.59.mine_ref
  132.8 3.5 %collective-permute-done.29.got_ref = bf16[1296,128]{1,0:T(8,128)(2,1)S(1)} collective-permute-done((bf16[1296,128]{1,0:T(8,128)(2,1)}, bf16[1296,128]{1,0:T(8,128)(2,1)S(1)}, u32[]{:S(2)}, u32[]{:S(2)}) %collective-permute-start.29) | collective-permute-done | bytes 331808 | tf_op jit(solution)/shard_map/ppermute | solution.py:243
  136.3 1.4 shard_map.67
  137.7 4.3 %collective-permute-done.22.got_ref = bf16[128,1024]{1,0:T(8,128)(2,1)} collective-permute-done((bf16[128,1024]{1,0:T(8,128)(2,1)}, bf16[128,1024]{1,0:T(8,128)(2,1)}, u32[]{:S(2)}, u32[]{:S(2)}) %collective-permute-start.22) | collective-permute-done | bytes 262176 | tf_op jit(solution)/shard_map/ppermute | solution.py:243
  142.0 2.3 %shard_map.61 = bf16[128,2048]{1,0:T(8,128)(2,1)} custom-call(s32[5]{0:T(128)S(1)} %stack.102.at_ref, bf16[128,1024]{1,0:T(8,128)(2,1)S(1)} %shard_map.59.mine_ref, bf16[128,1024]{1,0:T(8,128)(2,1)} %collective-permute-done.22.got_ref), custom_call_target="tpu_custom_call" | custom-call | flops 16777216 | bytes 2097152 | tf_op jit(solution)/shard_map/pallas_call | solution.py:187
  (91 shorter events, 17.9 us)
Async XLA Ops:
  0.6 17.0 %copy-start = (bf16[2048,640]{1,0:T(8,128)(2,1)S(1)}, bf16[2048,640]{1,0:T(8,128)(2,1)}, u32[]{:S(2)}) copy-start(bf16[2048,640]{1,0:T(8,128)(2,1)} %refs_0_) | copy-start | bytes 7864324
  2.7 11.4 %collective-permute-start = (bf16[128,1024]{1,0:T(8,128)(2,1)S(1)}, bf16[128,1024]{1,0:T(8,128)(2,1)}, u32[]{:S(2)}, u32[]{:S(2)}) collective-permute-start(bf16[128,1024]{1,0:T(8,128)(2,1)S(1)} %get-tuple-element.47.refs_0_), channel_id=1, source_target_pairs={{0,8},{1,57},{8,16},{9,1},{16,24},{17,9},{24,32},{25,17},{32,40},{... | collective-permute-start | bytes 786440 | tf_op jit(solution)/shard_map/ppermute | solution.py:258
  9.1 8.5 %collective-permute-start.2 = (bf16[128,1024]{1,0:T(8,128)(2,1)S(1)}, bf16[128,1024]{1,0:T(8,128)(2,1)}, u32[]{:S(2)}, u32[]{:S(2)}) collective-permute-start(bf16[128,1024]{1,0:T(8,128)(2,1)S(1)} %get-tuple-element.47.refs_0_), channel_id=1, source_target_pairs={{0,56},{1,9},{8,0},{9,17},{16,8},{17,25},{24,16},{25,33},{32,24},{... | collective-permute-start | bytes 786440 | tf_op jit(solution)/shard_map/ppermute | solution.py:258
  11.1 14.2 %collective-permute-start.5 = (bf16[256,640]{1,0:T(8,128)(2,1)}, bf16[256,640]{1,0:T(8,128)(2,1)}, u32[]{:S(2)}, u32[]{:S(2)}) collective-permute-start(bf16[256,640]{1,0:T(8,128)(2,1)} %get-tuple-element.63), channel_id=1, source_target_pairs={{0,4},{4,0},{1,5},{5,1},{2,6},{6,2},{3,7},{7,3},{8,12},{12,8},{9,1... | collective-permute-start | bytes 983048 | tf_op jit(solution)/shard_map/ppermute | solution.py:243
  12.4 12.9 %collective-permute-start.4 = (bf16[128,1024]{1,0:T(8,128)(2,1)}, bf16[128,1024]{1,0:T(8,128)(2,1)}, u32[]{:S(2)}, u32[]{:S(2)}) collective-permute-start(bf16[128,1024]{1,0:T(8,128)(2,1)} %get-tuple-element.34), channel_id=1, source_target_pairs={{0,4},{4,0},{1,5},{5,1},{2,6},{6,2},{3,7},{7,3},{8,12},{12,8},{9,1... | collective-permute-start | bytes 786440 | tf_op jit(solution)/shard_map/ppermute | solution.py:243
  14.1 11.2 %collective-permute-start.1 = (bf16[128,1024]{1,0:T(8,128)(2,1)}, bf16[128,1024]{1,0:T(8,128)(2,1)S(1)}, u32[]{:S(2)}, u32[]{:S(2)}) collective-permute-start(bf16[128,1024]{1,0:T(8,128)(2,1)} %collective-permute-done.refs_2_), channel_id=1, source_target_pairs={{0,8},{1,57},{8,16},{9,1},{16,24},{17,9},{24,32},{25,17},{32,40},{... | collective-permute-start | bytes 786440 | tf_op jit(solution)/shard_map/ppermute | solution.py:258
  17.6 8.0 %collective-permute-start.3 = (bf16[128,1024]{1,0:T(8,128)(2,1)}, bf16[128,1024]{1,0:T(8,128)(2,1)S(1)}, u32[]{:S(2)}, u32[]{:S(2)}) collective-permute-start(bf16[128,1024]{1,0:T(8,128)(2,1)} %collective-permute-done.2.refs_4_), channel_id=1, source_target_pairs={{0,56},{1,9},{8,0},{9,17},{16,8},{17,25},{24,16},{25,33},{32,24},{... | collective-permute-start | bytes 786440 | tf_op jit(solution)/shard_map/ppermute | solution.py:258
  17.6 10.8 %copy-start.17 = (bf16[256,640]{1,0:T(8,128)(2,1)S(1)}, bf16[256,640]{1,0:T(8,128)(2,1)}, u32[]{:S(2)}) copy-start(bf16[256,640]{1,0:T(8,128)(2,1)} %get-tuple-element.62) | copy-start | bytes 983044
  25.3 3.1 %copy-start.3 = (bf16[128,1024]{1,0:T(8,128)(2,1)}, bf16[128,1024]{1,0:T(8,128)(2,1)S(1)}, u32[]{:S(2)}) copy-start(bf16[128,1024]{1,0:T(8,128)(2,1)S(1)} %collective-permute-done.1.refs_6_) | copy-start | bytes 786436
  25.6 2.7 %copy-start.5 = (bf16[128,1024]{1,0:T(8,128)(2,1)}, bf16[128,1024]{1,0:T(8,128)(2,1)S(1)}, u32[]{:S(2)}) copy-start(bf16[128,1024]{1,0:T(8,128)(2,1)S(1)} %collective-permute-done.3.refs_8_) | copy-start | bytes 786436
  25.6 27.7 %collective-permute-start.12 = (bf16[1024,640]{1,0:T(8,128)(2,1)S(1)}, bf16[1024,640]{1,0:T(8,128)(2,1)}, u32[]{:S(2)}, u32[]{:S(2)}) collective-permute-start(bf16[1024,640]{1,0:T(8,128)(2,1)S(1)} %constant_dynamic-slice_fusion), channel_id=1, source_target_pairs={{0,4},{1,7},{4,2},{5,1},{2,6},{3,5},{6,0},{7,3},{8,12},{9,15},{12,... | collective-permute-start | bytes 3932168 | tf_op jit(solution)/shard_map/ppermute | solution.py:252
  29.4 23.0 %collective-permute-start.10 = (bf16[256,1280]{1,0:T(8,128)(2,1)S(1)}, bf16[256,1280]{1,0:T(8,128)(2,1)}, u32[]{:S(2)}, u32[]{:S(2)}) collective-permute-start(bf16[256,1280]{1,0:T(8,128)(2,1)S(1)} %pad_maximum_fusion.refs_0_), channel_id=1, source_target_pairs={{0,64},{1,193},{64,128},{65,1},{128,192},{129,65},{192,0},{193,129... | collective-permute-start | bytes 1966088 | tf_op jit(solution)/shard_map/ppermute | solution.py:258
  32.0 20.5 %collective-permute-start.11 = (bf16[256,1280]{1,0:T(8,128)(2,1)S(1)}, bf16[256,1280]{1,0:T(8,128)(2,1)S(1)}, u32[]{:S(2)}, u32[]{:S(2)}) collective-permute-start(bf16[256,1280]{1,0:T(8,128)(2,1)S(1)} %pad_maximum_fusion.refs_0_), channel_id=1, source_target_pairs={{0,192},{1,65},{64,0},{65,129},{128,64},{129,193},{192,128},{193,1... | collective-permute-start | bytes 1966088 | tf_op jit(solution)/shard_map/ppermute | solution.py:258
  32.0 0.8 copy-start.1
  32.8 8.8 %collective-permute-start.6 = (bf16[128,1024]{1,0:T(8,128)(2,1)}, bf16[128,1024]{1,0:T(8,128)(2,1)S(1)}, u32[]{:S(2)}, u32[]{:S(2)}) collective-permute-start(bf16[128,1024]{1,0:T(8,128)(2,1)} %collective-permute-done.4.refs_1_), channel_id=1, source_target_pairs={{0,8},{1,57},{8,16},{9,1},{16,24},{17,9},{24,32},{25,17},{32,40},{... | collective-permute-start | bytes 786440 | tf_op jit(solution)/shard_map/ppermute | solution.py:258
  36.3 9.4 %collective-permute-start.8 = (bf16[128,1024]{1,0:T(8,128)(2,1)}, bf16[128,1024]{1,0:T(8,128)(2,1)S(1)}, u32[]{:S(2)}, u32[]{:S(2)}) collective-permute-start(bf16[128,1024]{1,0:T(8,128)(2,1)} %collective-permute-done.4.refs_1_), channel_id=1, source_target_pairs={{0,56},{1,9},{8,0},{9,17},{16,8},{17,25},{24,16},{25,33},{32,24},{... | collective-permute-start | bytes 786440 | tf_op jit(solution)/shard_map/ppermute | solution.py:258
  41.6 7.6 %collective-permute-start.7 = (bf16[128,1024]{1,0:T(8,128)(2,1)S(1)}, bf16[128,1024]{1,0:T(8,128)(2,1)S(1)}, u32[]{:S(2)}, u32[]{:S(2)}) collective-permute-start(bf16[128,1024]{1,0:T(8,128)(2,1)S(1)} %collective-permute-done.6.refs_3_), channel_id=1, source_target_pairs={{0,8},{1,57},{8,16},{9,1},{16,24},{17,9},{24,32},{25,17},{32,40},{... | collective-permute-start | bytes 786440 | tf_op jit(solution)/shard_map/ppermute | solution.py:258
  45.0 0.7 copy-start.13
  45.7 6.8 %collective-permute-start.9 = (bf16[128,1024]{1,0:T(8,128)(2,1)S(1)}, bf16[128,1024]{1,0:T(8,128)(2,1)S(1)}, u32[]{:S(2)}, u32[]{:S(2)}) collective-permute-start(bf16[128,1024]{1,0:T(8,128)(2,1)S(1)} %collective-permute-done.8.refs_5_), channel_id=1, source_target_pairs={{0,56},{1,9},{8,0},{9,17},{16,8},{17,25},{24,16},{25,33},{32,24},{... | collective-permute-start | bytes 786440 | tf_op jit(solution)/shard_map/ppermute | solution.py:258
  45.7 0.7 copy-start.15
  49.1 4.2 %copy-start.7 = (bf16[128,1024]{1,0:T(8,128)(2,1)}, bf16[128,1024]{1,0:T(8,128)(2,1)S(1)}, u32[]{:S(2)}) copy-start(bf16[128,1024]{1,0:T(8,128)(2,1)S(1)} %collective-permute-done.7.refs_7_) | copy-start | bytes 786436
  52.5 0.9 copy-start.9
  52.5 0.9 copy-start.11
  53.3 12.8 %collective-permute-start.13 = (bf16[1024,640]{1,0:T(8,128)(2,1)}, bf16[1024,640]{1,0:T(8,128)(2,1)}, u32[]{:S(2)}, u32[]{:S(2)}) collective-permute-start(bf16[1024,640]{1,0:T(8,128)(2,1)} %collective-permute-done.12.refs_1_), channel_id=1, source_target_pairs={{0,1},{1,0},{2,3},{3,2},{4,5},{5,4},{6,7},{7,6},{8,9},{9,8},{10,11... | collective-permute-start | bytes 3932168 | tf_op jit(solution)/shard_map/ppermute | solution.py:243
  53.4 15.5 %collective-permute-start.14 = (bf16[256,1280]{1,0:T(8,128)(2,1)}, bf16[256,1280]{1,0:T(8,128)(2,1)S(1)}, u32[]{:S(2)}, u32[]{:S(2)}) collective-permute-start(bf16[256,1280]{1,0:T(8,128)(2,1)} %collective-permute-done.10.refs_1_), channel_id=1, source_target_pairs={{0,64},{1,193},{64,128},{65,1},{128,192},{129,65},{192,0},{193,129... | collective-permute-start | bytes 1966088 | tf_op jit(solution)/shard_map/ppermute | solution.py:258
  59.1 17.4 %collective-permute-start.23 = (bf16[256,1024]{1,0:T(8,128)(2,1)S(1)}, bf16[256,1024]{1,0:T(8,128)(2,1)S(1)}, u32[]{:S(2)}, u32[]{:S(2)}) collective-permute-start(bf16[256,1024]{1,0:T(8,128)(2,1)S(1)} %pad_maximum_fusion.1), channel_id=1, source_target_pairs={{0,8},{1,57},{8,16},{9,1},{16,24},{17,9},{24,32},{25,17},{32,40},{... | collective-permute-start | bytes 1572872 | tf_op jit(solution)/shard_map/ppermute | solution.py:258
  62.0 14.5 %collective-permute-start.24 = (bf16[256,1024]{1,0:T(8,128)(2,1)S(1)}, bf16[256,1024]{1,0:T(8,128)(2,1)S(1)}, u32[]{:S(2)}, u32[]{:S(2)}) collective-permute-start(bf16[256,1024]{1,0:T(8,128)(2,1)S(1)} %pad_maximum_fusion.2), channel_id=1, source_target_pairs={{0,56},{1,9},{8,0},{9,17},{16,8},{17,25},{24,16},{25,33},{32,24},{... | collective-permute-start | bytes 1572872 | tf_op jit(solution)/shard_map/ppermute | solution.py:258
  62.0 1.1 copy-start.2
  63.1 1.1 copy-start.12
  70.3 14.2 %collective-permute-start.15 = (bf16[2064,128]{1,0:T(8,128)(2,1)S(1)}, bf16[2064,128]{1,0:T(8,128)(2,1)S(1)}, u32[]{:S(2)}, u32[]{:S(2)}) collective-permute-start(bf16[2064,128]{1,0:T(8,128)(2,1)S(1)} %shard_map.52), channel_id=1, source_target_pairs={{0,8},{1,57},{8,16},{9,1},{16,24},{17,9},{24,32},{25,17},{32,40},{... | collective-permute-start | bytes 1585160 | tf_op jit(solution)/shard_map/ppermute | solution.py:258
  74.5 14.5 %collective-permute-start.19 = (bf16[2064,128]{1,0:T(8,128)(2,1)S(1)}, bf16[2064,128]{1,0:T(8,128)(2,1)S(1)}, u32[]{:S(2)}, u32[]{:S(2)}) collective-permute-start(bf16[2064,128]{1,0:T(8,128)(2,1)S(1)} %shard_map.53), channel_id=1, source_target_pairs={{0,56},{1,9},{8,0},{9,17},{16,8},{17,25},{24,16},{25,33},{32,24},{... | collective-permute-start | bytes 1585160 | tf_op jit(solution)/shard_map/ppermute | solution.py:258
  76.5 14.0 %collective-permute-start.25 = (bf16[256,1024]{1,0:T(8,128)(2,1)S(1)}, bf16[256,1024]{1,0:T(8,128)(2,1)S(1)}, u32[]{:S(2)}, u32[]{:S(2)}) collective-permute-start(bf16[256,1024]{1,0:T(8,128)(2,1)S(1)} %collective-permute-done.23.refs_10_), channel_id=1, source_target_pairs={{0,8},{1,57},{8,16},{9,1},{16,24},{17,9},{24,32},{25,17},{32,40},{... | collective-permute-start | bytes 1572872 | tf_op jit(solution)/shard_map/ppermute | solution.py:258
  81.0 9.5 %copy-start.4 = (bf16[128,1024]{1,0:T(8,128)(2,1)S(1)}, bf16[128,1024]{1,0:T(8,128)(2,1)}, u32[]{:S(2)}) copy-start(bf16[128,1024]{1,0:T(8,128)(2,1)} %copy-done.3) | copy-start | bytes 786436
  81.0 9.5 %copy-start.6 = (bf16[128,1024]{1,0:T(8,128)(2,1)S(1)}, bf16[128,1024]{1,0:T(8,128)(2,1)}, u32[]{:S(2)}) copy-start(bf16[128,1024]{1,0:T(8,128)(2,1)} %copy-done.5) | copy-start | bytes 786436
  81.0 9.5 %copy-start.8 = (bf16[128,1024]{1,0:T(8,128)(2,1)S(1)}, bf16[128,1024]{1,0:T(8,128)(2,1)}, u32[]{:S(2)}) copy-start(bf16[128,1024]{1,0:T(8,128)(2,1)} %copy-done.7) | copy-start | bytes 786436
  81.1 9.5 %copy-start.10 = (bf16[128,1024]{1,0:T(8,128)(2,1)S(1)}, bf16[128,1024]{1,0:T(8,128)(2,1)}, u32[]{:S(2)}) copy-start(bf16[128,1024]{1,0:T(8,128)(2,1)} %copy-done.9) | copy-start | bytes 786436
  81.1 9.4 %copy-start.14 = (bf16[128,1024]{1,0:T(8,128)(2,1)S(1)}, bf16[128,1024]{1,0:T(8,128)(2,1)}, u32[]{:S(2)}) copy-start(bf16[128,1024]{1,0:T(8,128)(2,1)} %copy-done.13) | copy-start | bytes 786436
  81.1 9.4 %copy-start.16 = (bf16[128,1024]{1,0:T(8,128)(2,1)S(1)}, bf16[128,1024]{1,0:T(8,128)(2,1)}, u32[]{:S(2)}) copy-start(bf16[128,1024]{1,0:T(8,128)(2,1)} %copy-done.15) | copy-start | bytes 786436
  85.5 15.9 %collective-permute-start.16 = (bf16[2064,128]{1,0:T(8,128)(2,1)S(1)}, bf16[2064,128]{1,0:T(8,128)(2,1)S(1)}, u32[]{:S(2)}, u32[]{:S(2)}) collective-permute-start(bf16[2064,128]{1,0:T(8,128)(2,1)S(1)} %shard_map.54), channel_id=1, source_target_pairs={{0,8},{1,57},{8,16},{9,1},{16,24},{17,9},{24,32},{25,17},{32,40},{... | collective-permute-start | bytes 1585160 | tf_op jit(solution)/shard_map/ppermute | solution.py:258
  89.9 22.9 %collective-permute-start.20 = (bf16[2064,128]{1,0:T(8,128)(2,1)S(1)}, bf16[2064,128]{1,0:T(8,128)(2,1)S(1)}, u32[]{:S(2)}, u32[]{:S(2)}) collective-permute-start(bf16[2064,128]{1,0:T(8,128)(2,1)S(1)} %shard_map.57), channel_id=1, source_target_pairs={{0,56},{1,9},{8,0},{9,17},{16,8},{17,25},{24,16},{25,33},{32,24},{... | collective-permute-start | bytes 1585160 | tf_op jit(solution)/shard_map/ppermute | solution.py:258
  94.9 13.1 %collective-permute-start.26 = (bf16[2576,128]{1,0:T(8,128)(2,1)S(1)}, bf16[2576,128]{1,0:T(8,128)(2,1)S(1)}, u32[]{:S(2)}, u32[]{:S(2)}) collective-permute-start(bf16[2576,128]{1,0:T(8,128)(2,1)S(1)} %shard_map.63), channel_id=1, source_target_pairs={{0,64},{1,193},{64,128},{65,1},{128,192},{129,65},{192,0},{193,129... | collective-permute-start | bytes 1978376 | tf_op jit(solution)/shard_map/ppermute | solution.py:258
  102.3 11.5 %collective-permute-start.17 = (bf16[2064,128]{1,0:T(8,128)(2,1)S(1)}, bf16[2064,128]{1,0:T(8,128)(2,1)S(1)}, u32[]{:S(2)}, u32[]{:S(2)}) collective-permute-start(bf16[2064,128]{1,0:T(8,128)(2,1)S(1)} %shard_map.55), channel_id=1, source_target_pairs={{0,8},{1,57},{8,16},{9,1},{16,24},{17,9},{24,32},{25,17},{32,40},{... | collective-permute-start | bytes 1585160 | tf_op jit(solution)/shard_map/ppermute | solution.py:258
  107.9 17.7 %collective-permute-start.28 = (bf16[2576,128]{1,0:T(8,128)(2,1)S(1)}, bf16[2576,128]{1,0:T(8,128)(2,1)S(1)}, u32[]{:S(2)}, u32[]{:S(2)}) collective-permute-start(bf16[2576,128]{1,0:T(8,128)(2,1)S(1)} %shard_map.65), channel_id=1, source_target_pairs={{0,192},{1,65},{64,0},{65,129},{128,64},{129,193},{192,128},{193,1... | collective-permute-start | bytes 1978376 | tf_op jit(solution)/shard_map/ppermute | solution.py:258
  109.1 16.5 %collective-permute-start.27 = (bf16[2576,128]{1,0:T(8,128)(2,1)S(1)}, bf16[2576,128]{1,0:T(8,128)(2,1)S(1)}, u32[]{:S(2)}, u32[]{:S(2)}) collective-permute-start(bf16[2576,128]{1,0:T(8,128)(2,1)S(1)} %shard_map.64), channel_id=1, source_target_pairs={{0,64},{1,193},{64,128},{65,1},{128,192},{129,65},{192,0},{193,129... | collective-permute-start | bytes 1978376 | tf_op jit(solution)/shard_map/ppermute | solution.py:258
  113.7 14.8 %collective-permute-start.21 = (bf16[2064,128]{1,0:T(8,128)(2,1)S(1)}, bf16[2064,128]{1,0:T(8,128)(2,1)S(1)}, u32[]{:S(2)}, u32[]{:S(2)}) collective-permute-start(bf16[2064,128]{1,0:T(8,128)(2,1)S(1)} %shard_map.58), channel_id=1, source_target_pairs={{0,56},{1,9},{8,0},{9,17},{16,8},{17,25},{24,16},{25,33},{32,24},{... | collective-permute-start | bytes 1585160 | tf_op jit(solution)/shard_map/ppermute | solution.py:258
  114.7 13.8 %collective-permute-start.18 = (bf16[2064,128]{1,0:T(8,128)(2,1)S(1)}, bf16[2064,128]{1,0:T(8,128)(2,1)S(1)}, u32[]{:S(2)}, u32[]{:S(2)}) collective-permute-start(bf16[2064,128]{1,0:T(8,128)(2,1)S(1)} %shard_map.56), channel_id=1, source_target_pairs={{0,8},{1,57},{8,16},{9,1},{16,24},{17,9},{24,32},{25,17},{32,40},{... | collective-permute-start | bytes 1585160 | tf_op jit(solution)/shard_map/ppermute | solution.py:258
  127.6 8.7 %collective-permute-start.29 = (bf16[1296,128]{1,0:T(8,128)(2,1)}, bf16[1296,128]{1,0:T(8,128)(2,1)S(1)}, u32[]{:S(2)}, u32[]{:S(2)}) collective-permute-start(bf16[1296,128]{1,0:T(8,128)(2,1)} %get-tuple-element.61), channel_id=1, source_target_pairs={{0,4},{4,0},{1,5},{5,1},{2,6},{6,2},{3,7},{7,3},{8,12},{12,8},{9,1... | collective-permute-start | bytes 995336 | tf_op jit(solution)/shard_map/ppermute | solution.py:243
  130.2 11.8 %collective-permute-start.22 = (bf16[128,1024]{1,0:T(8,128)(2,1)}, bf16[128,1024]{1,0:T(8,128)(2,1)}, u32[]{:S(2)}, u32[]{:S(2)}) collective-permute-start(bf16[128,1024]{1,0:T(8,128)(2,1)} %shard_map.60), channel_id=1, source_target_pairs={{0,4},{4,0},{1,5},{5,1},{2,6},{6,2},{3,7},{7,3},{8,12},{12,8},{9,1... | collective-permute-start | bytes 786440 | tf_op jit(solution)/shard_map/ppermute | solution.py:243
